TPU v7x, 32 devices: a whole 2x2x4 slice. The times are simulated.
32 devices in a mesh: dp: 8 (over y, x, core), tensor: 4 (over z).
Axes of the slice: x: 2, y: 2, z: 4, core: 2. Of those that a mesh axis runs over, the one named last changes fastest.
Arguments:
- tokens: bfloat16 [1024, 8, 1024], P('tensor', 'dp'), may hold values from -6 to 6
- lengths: int32 [8], replicated, may hold values from 1 to 1024, 5120 in all
- order: int32 [8], replicated, may hold values from 0 to 7, each once
- norm_mix: bfloat16 [2, 1024], replicated, may hold values from 0.5 to 1.5
- w_query: bfloat16 [2, 1024, 1024], P(None, 'dp', 'tensor'), may hold values from -0.1875 to 0.1875
- w_key: bfloat16 [2, 1024, 1024], P(None, 'dp', 'tensor'), may hold values from -0.1875 to 0.1875
- w_value: bfloat16 [2, 1024, 2048], P(None, 'dp', 'tensor'), may hold values from -0.1875 to 0.1875
- w_gate: bfloat16 [2, 1024, 2048], P(None, 'dp', 'tensor'), may hold values from -0.1875 to 0.1875
- w_decay: bfloat16 [2, 1024, 4, 2], P(None, 'dp', 'tensor'), may hold values from -0.1875 to 0.1875
- conv_filter: bfloat16 [2, 4, 4, 1024], P(None, None, 'tensor', 'dp'), may hold values from -3 to 3
- log_rate: bfloat16 [2, 4], replicated, may hold values from 0 to 2.6875
- step_bias: bfloat16 [2, 4], replicated, may hold values from -6 to -2
- norm_heads: bfloat16 [2, 512], replicated, may hold values from 0.5 to 1.5
- w_out: bfloat16 [2, 2048, 1024], P(None, 'tensor', 'dp'), may hold values from -0.25 to 0.25
- norm_ffn: bfloat16 [2, 1024], replicated, may hold values from 0.5 to 1.5
- w_ffn_gate: bfloat16 [2, 1024, 2816], P(None, 'dp', 'tensor'), may hold values from -0.1875 to 0.1875
- w_ffn_up: bfloat16 [2, 1024, 2816], P(None, 'dp', 'tensor'), may hold values from -0.1875 to 0.1875
- w_ffn_down: bfloat16 [2, 2816, 1024], P(None, 'tensor', 'dp'), may hold values from -0.109375 to 0.109375
- cotangent: bfloat16 [1024, 8, 1024], P('tensor', 'dp'), may hold values from -6 to 6
Outputs:
- mixed: bfloat16 [1024, 8, 1024], P('tensor', 'dp')
- grad_tokens: float32 [1024, 8, 1024], P('tensor', 'dp')
- grad_norm_mix: float32 [2, 1024], replicated
- grad_w_query: float32 [2, 1024, 1024], P(None, 'dp', 'tensor')
- grad_w_key: float32 [2, 1024, 1024], P(None, 'dp', 'tensor')
- grad_w_value: float32 [2, 1024, 2048], P(None, 'dp', 'tensor')
- grad_w_gate: float32 [2, 1024, 2048], P(None, 'dp', 'tensor')
- grad_w_decay: float32 [2, 1024, 4, 2], P(None, 'dp', 'tensor')
- grad_conv_filter: float32 [2, 4, 4, 1024], P(None, None, 'tensor', 'dp')
- grad_log_rate: float32 [2, 4], replicated
- grad_step_bias: float32 [2, 4], replicated
- grad_norm_heads: float32 [2, 512], replicated
- grad_w_out: float32 [2, 2048, 1024], P(None, 'tensor', 'dp')
- grad_norm_ffn: float32 [2, 1024], replicated
- feedforward_gate_weight_gradient: float32 [2, 1024, 2816], P(None, 'dp', 'tensor')
- grad_w_ffn_up: float32 [2, 1024, 2816], P(None, 'dp', 'tensor')
- grad_w_ffn_down: float32 [2, 2816, 1024], P(None, 'tensor', 'dp')
Inputs may be any that keep to these rules, and one draw needn't show every extreme that they name: lengths sum to 5120 and one slot is full; a slot's sequence takes its first time positions. `order`: each slot appears once.
All inputs are finite; a program needn't handle non-finite values.
Results may differ from a plain program's by a relative error of at most 0.035.
Values may be sent and summed in bfloat16 or wider, within the bound.
A program may use at most 320 MiB of HBM per device.

v0:
```python
import jax
import jax.numpy as jnp
from jax import lax
from jax.sharding import PartitionSpec as P

GROUP = 64


def precise_product(left_side, right_side):
    return jnp.dot(left_side, right_side, precision=lax.Precision.HIGHEST)


def block_step(memory, inputs):
    queries, key_rows, values, write_rate, log_decay = inputs
    length = queries.shape[0]
    row_ids = jnp.arange(length)
    strictly = row_ids[:, None] > row_ids[None, :]
    inclusive = row_ids[:, None] >= row_ids[None, :]
    spread = log_decay[:, None] - log_decay[None, :]
    below_decay = jnp.exp(jnp.where(strictly, spread, 0.0)) * strictly.astype(jnp.float32)
    within = jnp.exp(jnp.where(inclusive, spread, 0.0)) * inclusive.astype(jnp.float32)
    coupling = write_rate[:, None] * precise_product(key_rows, key_rows.T) * below_decay
    unit_lower = jnp.eye(length, dtype=jnp.float32) + coupling
    growth = jnp.exp(log_decay)[:, None]
    key_terms = jax.scipy.linalg.solve_triangular(
        unit_lower, write_rate[:, None] * key_rows * growth, lower=True, unit_diagonal=True
    )
    value_terms = jax.scipy.linalg.solve_triangular(
        unit_lower, write_rate[:, None] * values, lower=True, unit_diagonal=True
    )
    corrected = value_terms - precise_product(key_terms, memory)
    output = precise_product(queries * growth, memory) + precise_product(
        precise_product(queries, key_rows.T) * within, corrected
    )
    final_decay = log_decay[-1]
    memory = jnp.exp(final_decay) * memory + precise_product(
        (key_rows * jnp.exp(final_decay - log_decay)[:, None]).T, corrected
    )
    return (memory, output)


def delta_sequence(queries, key_rows, values, write_rate, log_step):
    length = queries.shape[0]
    blocks = length // GROUP
    key_size = key_rows.shape[1]
    value_size = values.shape[1]
    inputs = (
        queries.reshape(blocks, GROUP, key_size),
        key_rows.reshape(blocks, GROUP, key_size),
        values.reshape(blocks, GROUP, value_size),
        write_rate.reshape(blocks, GROUP),
        jnp.cumsum(log_step.reshape(blocks, GROUP), axis=1),
    )
    initial = jnp.zeros((key_size, value_size), jnp.float32)
    final_memory, outputs = lax.scan(jax.checkpoint(block_step), initial, inputs)
    return outputs.reshape(length, value_size)


def causal_filter(signal, filter_taps):
    tap_count = filter_taps.shape[0]
    length = signal.shape[0]
    padded = jnp.pad(signal, ((tap_count - 1, 0), (0, 0), (0, 0), (0, 0)))
    result = jnp.zeros_like(signal)
    for tap_index in range(tap_count):
        result = result + padded[tap_index : tap_index + length] * filter_taps[tap_index]
    return result


def unit_rows(vector):
    return vector * lax.rsqrt(jnp.sum(vector * vector, axis=-1, keepdims=True) + 1e-06)


def norm_rows(values, gain_row):
    return values * lax.rsqrt(jnp.mean(values * values, axis=-1, keepdims=True) + 1e-06) * gain_row


def delta_mixer(
    query_in, key_in, value_in, gate_in, rate_in, filter_taps, rate_param, bias_param, gain_row
):
    length, slot_count = (query_in.shape[0], query_in.shape[1])
    head_count = filter_taps.shape[1]
    key_size = query_in.shape[2] // head_count
    value_size = value_in.shape[2] // head_count
    joined = jnp.concatenate(
        [
            query_in.reshape(length, slot_count, head_count, key_size),
            key_in.reshape(length, slot_count, head_count, key_size),
            value_in.reshape(length, slot_count, head_count, value_size),
        ],
        axis=3,
    )
    filtered = jax.nn.silu(causal_filter(joined, filter_taps))
    queries = unit_rows(filtered[..., :key_size]) * key_size ** (-0.5)
    key_rows = unit_rows(filtered[..., key_size : 2 * key_size])
    values = filtered[..., 2 * key_size :]
    rate_pairs = rate_in.reshape(length, slot_count, head_count, 2)
    write_rate = jax.nn.sigmoid(rate_pairs[..., 0])
    log_step = -jnp.exp(rate_param) * jax.nn.softplus(rate_pairs[..., 1] + bias_param)
    axes_order = (1, 2, 0, 3)
    outputs = jax.vmap(jax.vmap(delta_sequence))(
        queries.transpose(axes_order),
        key_rows.transpose(axes_order),
        values.transpose(axes_order),
        write_rate.transpose((1, 2, 0)),
        log_step.transpose((1, 2, 0)),
    )
    outputs = outputs.transpose((2, 0, 1, 3))
    scaled = (
        outputs * lax.rsqrt(jnp.mean(outputs * outputs, axis=-1, keepdims=True) + 1e-05) * gain_row
    )
    gated_rows = scaled * jax.nn.silu(gate_in.reshape(length, slot_count, head_count, value_size))
    return gated_rows.reshape(length, slot_count, head_count * value_size)


def swiglu_rows(paired):
    gate_part, up_part = jnp.split(paired, 2, axis=2)
    return jax.nn.silu(gate_part) * up_part


def join_weights(gathered):
    (
        weight_query,
        weight_key,
        weight_value,
        weight_gate,
        weight_decay,
        filter_taps,
        weight_out,
        weight_up_gate,
        weight_up,
        down_projection_weight,
    ) = gathered
    width_model = weight_query.shape[0]
    weight_in = jnp.concatenate(
        [
            weight_query,
            weight_key,
            weight_value,
            weight_gate,
            weight_decay.reshape(width_model, -1),
        ],
        axis=1,
    )
    weight_pair = jnp.concatenate([weight_up_gate, weight_up], axis=1)
    first_cut = weight_query.shape[1]
    second_cut = first_cut + weight_key.shape[1]
    third_cut = second_cut + weight_value.shape[1]
    fourth_cut = third_cut + weight_gate.shape[1]
    return (weight_in, weight_pair, [first_cut, second_cut, third_cut, fourth_cut])


def gather_rows(values):
    return lax.all_gather(values, "tensor", axis=0, tiled=True)


def gather_grads(values):
    return lax.all_gather(values, "tensor", axis=0, tiled=True)


def sum_products(values, weight, rows_local):

    def product_rows(first_row, row_count):
        return jnp.einsum("lsc,cd->lsd", values, weight, preferred_element_type=jnp.float32)

    return lax.psum_scatter(
        product_rows(jnp.int32(0), rows_local * lax.axis_size("tensor")).astype(jnp.bfloat16),
        "tensor",
        scatter_dimension=0,
        tiled=True,
    ).astype(jnp.float32)


def sum_back(values, weight, rows_local):

    def product_rows(first_row, row_count):
        return jnp.einsum("lsc,dc->lsd", values, weight, preferred_element_type=jnp.float32)

    return lax.psum_scatter(
        product_rows(jnp.int32(0), rows_local * lax.axis_size("tensor")).astype(jnp.bfloat16),
        "tensor",
        scatter_dimension=0,
        tiled=True,
    ).astype(jnp.float32)


def forward_layer(residual, gathered, gain_mix, gain_heads, gain_ffn, rate_local, bias_local):
    weight_in, weight_pair, cut_points = join_weights(gathered)
    filter_taps = gathered[5].astype(jnp.float32)
    weight_out = gathered[6]
    down_projection_weight = gathered[9]
    rows_local = residual.shape[0]
    normed, norm_back = jax.vjp(norm_rows, residual, gain_mix)
    rows_in = gather_rows(normed.astype(jnp.bfloat16))
    projected = jnp.einsum("lsd,dc->lsc", rows_in, weight_in, preferred_element_type=jnp.float32)

    def mixer_local(projected_in, filter_in, rate_param, bias_param, gain_param):
        query_in, key_in, value_in, gate_in, rate_in = jnp.split(projected_in, cut_points, axis=2)
        return delta_mixer(
            query_in,
            key_in,
            value_in,
            gate_in,
            rate_in,
            filter_in,
            rate_param,
            bias_param,
            gain_param,
        )

    mixer_output, mixer_back = jax.vjp(
        mixer_local, projected, filter_taps, rate_local, bias_local, gain_heads
    )
    mixer_low = mixer_output.astype(jnp.bfloat16)
    residual = residual + sum_products(mixer_low, weight_out, rows_local)
    normed_ffn, ffn_norm_back = jax.vjp(norm_rows, residual, gain_ffn)
    rows_ffn = gather_rows(normed_ffn.astype(jnp.bfloat16))
    paired = jnp.einsum("lsd,dc->lsc", rows_ffn, weight_pair, preferred_element_type=jnp.float32)
    hidden, swiglu_back = jax.vjp(swiglu_rows, paired)
    hidden_reduced = hidden.astype(jnp.bfloat16)
    residual = residual + sum_products(hidden_reduced, down_projection_weight, rows_local)
    record = (
        norm_back,
        rows_in,
        mixer_back,
        mixer_low,
        ffn_norm_back,
        rows_ffn,
        swiglu_back,
        hidden_reduced,
    )
    return (residual, record)


def shards(
    tokens,
    lengths,
    order,
    norm_mix,
    w_query,
    w_key,
    w_value,
    w_gate,
    w_decay,
    conv_filter,
    log_rate,
    step_bias,
    norm_heads,
    w_out,
    norm_ffn,
    w_ffn_gate,
    w_ffn_up,
    w_ffn_down,
    cotangent,
):
    layer_count = w_query.shape[0]
    local_heads = w_decay.shape[2]
    head_count_total = log_rate.shape[1]
    device_part = lax.axis_index("tensor")
    dp_place = lax.axis_index("dp")
    rows_local = tokens.shape[0]
    slots_local = tokens.shape[1]
    slot_total = order.shape[0]
    spread_in = lax.all_to_all(tokens, "dp", split_axis=2, concat_axis=1, tiled=True)
    picked = jnp.take(spread_in, order, axis=1)
    dealt = lax.all_to_all(picked, "dp", split_axis=1, concat_axis=2, tiled=True)
    residual = dealt.astype(jnp.float32)
    saved = []
    kept_weights = []
    for layer_index in range(layer_count):
        gathered = (
            lax.all_gather(w_query[layer_index], "dp", axis=0, tiled=True),
            lax.all_gather(w_key[layer_index], "dp", axis=0, tiled=True),
            lax.all_gather(w_value[layer_index], "dp", axis=0, tiled=True),
            lax.all_gather(w_gate[layer_index], "dp", axis=0, tiled=True),
            lax.all_gather(w_decay[layer_index], "dp", axis=0, tiled=True),
            lax.all_gather(conv_filter[layer_index], "dp", axis=2, tiled=True),
            lax.all_gather(w_out[layer_index], "dp", axis=1, tiled=True),
            lax.all_gather(w_ffn_gate[layer_index], "dp", axis=0, tiled=True),
            lax.all_gather(w_ffn_up[layer_index], "dp", axis=0, tiled=True),
            lax.all_gather(w_ffn_down[layer_index], "dp", axis=1, tiled=True),
        )
        kept_weights.append(gathered)
        rate_local = lax.dynamic_slice_in_dim(
            log_rate[layer_index].astype(jnp.float32), device_part * local_heads, local_heads
        )
        bias_local = lax.dynamic_slice_in_dim(
            step_bias[layer_index].astype(jnp.float32), device_part * local_heads, local_heads
        )
        residual, record = forward_layer(
            residual,
            gathered,
            norm_mix[layer_index].astype(jnp.float32),
            norm_heads[layer_index].astype(jnp.float32),
            norm_ffn[layer_index].astype(jnp.float32),
            rate_local,
            bias_local,
        )
        saved.append(record)
    my_slots = lax.dynamic_slice_in_dim(order, dp_place * slots_local, slots_local)
    my_lengths = jnp.take(lengths, my_slots)
    positions = device_part * rows_local + jnp.arange(rows_local)
    valid_mask = (positions[:, None] < my_lengths[None, :]).astype(jnp.float32)
    gradient = cotangent.astype(jnp.float32) * valid_mask[:, :, None]
    weight_grads = [None] * layer_count
    small_terms = [None] * layer_count
    for layer_index in reversed(range(layer_count)):
        gathered = (
            lax.all_gather(w_query[layer_index], "dp", axis=0, tiled=True),
            lax.all_gather(w_key[layer_index], "dp", axis=0, tiled=True),
            lax.all_gather(w_value[layer_index], "dp", axis=0, tiled=True),
            lax.all_gather(w_gate[layer_index], "dp", axis=0, tiled=True),
            lax.all_gather(w_decay[layer_index], "dp", axis=0, tiled=True),
            lax.all_gather(conv_filter[layer_index], "dp", axis=2, tiled=True),
            lax.all_gather(w_out[layer_index], "dp", axis=1, tiled=True),
            lax.all_gather(w_ffn_gate[layer_index], "dp", axis=0, tiled=True),
            lax.all_gather(w_ffn_up[layer_index], "dp", axis=0, tiled=True),
            lax.all_gather(w_ffn_down[layer_index], "dp", axis=1, tiled=True),
        )
        weight_in, weight_pair, cut_points = join_weights(gathered)
        weight_out = gathered[6]
        down_projection_weight = gathered[9]
        width_model = weight_in.shape[0]
        (
            norm_back,
            rows_in,
            mixer_back,
            mixer_low,
            ffn_norm_back,
            rows_ffn,
            swiglu_back,
            hidden_reduced,
        ) = saved[layer_index]
        feedforward_gradient_rows = gather_grads(gradient.astype(jnp.bfloat16))
        grad_hidden = jnp.einsum(
            "hti,pi->htp",
            feedforward_gradient_rows,
            down_projection_weight,
            preferred_element_type=jnp.float32,
        )
        grad_down = jnp.einsum(
            "kwy,kwx->yx",
            hidden_reduced,
            feedforward_gradient_rows,
            preferred_element_type=jnp.float32,
        )
        (grad_paired,) = swiglu_back(grad_hidden)
        paired_low = grad_paired.astype(jnp.bfloat16)
        grad_pair_weight = jnp.einsum(
            "lsd,lsc->dc", rows_ffn, paired_low, preferred_element_type=jnp.float32
        )
        grad_up_gate, grad_up = jnp.split(grad_pair_weight, 2, axis=1)
        grad_normed = sum_back(paired_low, weight_pair, rows_local)
        grad_residual, grad_gain_ffn = ffn_norm_back(grad_normed)
        gradient = gradient + grad_residual
        grad_rows_mix = gather_grads(gradient.astype(jnp.bfloat16))
        grad_mixer = jnp.einsum(
            "lsd,cd->lsc", grad_rows_mix, weight_out, preferred_element_type=jnp.float32
        )
        grad_out = jnp.einsum(
            "lsc,lsd->cd", mixer_low, grad_rows_mix, preferred_element_type=jnp.float32
        )
        grad_projected, grad_taps, grad_rate, grad_bias, grad_gain_heads = mixer_back(grad_mixer)
        projected_low = grad_projected.astype(jnp.bfloat16)
        grad_in_weight = jnp.einsum(
            "lsd,lsc->dc", rows_in, projected_low, preferred_element_type=jnp.float32
        )
        grad_normed = sum_back(projected_low, weight_in, rows_local)
        grad_residual, grad_gain_mix = norm_back(grad_normed)
        gradient = gradient + grad_residual
        grad_query, grad_key, grad_value, grad_gate, grad_decay = jnp.split(
            grad_in_weight, cut_points, axis=1
        )
        weight_grads[layer_index] = (
            lax.psum_scatter(grad_query, "dp", scatter_dimension=0, tiled=True),
            lax.psum_scatter(grad_key, "dp", scatter_dimension=0, tiled=True),
            lax.psum_scatter(grad_value, "dp", scatter_dimension=0, tiled=True),
            lax.psum_scatter(grad_gate, "dp", scatter_dimension=0, tiled=True),
            lax.psum_scatter(
                grad_decay.reshape(width_model, local_heads, 2),
                "dp",
                scatter_dimension=0,
                tiled=True,
            ),
            lax.psum_scatter(grad_taps, "dp", scatter_dimension=2, tiled=True),
            lax.psum_scatter(grad_out, "dp", scatter_dimension=1, tiled=True),
            lax.psum_scatter(grad_up_gate, "dp", scatter_dimension=0, tiled=True),
            lax.psum_scatter(grad_up, "dp", scatter_dimension=0, tiled=True),
            lax.psum_scatter(grad_down, "dp", scatter_dimension=1, tiled=True),
        )
        rate_full = lax.dynamic_update_slice_in_dim(
            jnp.zeros((head_count_total,), jnp.float32), grad_rate, device_part * local_heads, 0
        )
        bias_full = lax.dynamic_update_slice_in_dim(
            jnp.zeros((head_count_total,), jnp.float32), grad_bias, device_part * local_heads, 0
        )
        small_terms[layer_index] = lax.psum(
            (grad_gain_mix, grad_gain_heads, rate_full, bias_full, grad_gain_ffn), ("dp", "tensor")
        )
    spread_back = lax.all_to_all(
        gradient.astype(jnp.bfloat16), "dp", split_axis=2, concat_axis=1, tiled=True
    ).astype(gradient.dtype)
    inverse_order = (
        jnp.zeros((slot_total,), jnp.int32).at[order].set(jnp.arange(slot_total, dtype=jnp.int32))
    )
    homed = jnp.take(spread_back, inverse_order, axis=1)
    grad_home = lax.all_to_all(
        homed.astype(jnp.bfloat16), "dp", split_axis=1, concat_axis=2, tiled=True
    ).astype(homed.dtype)
    stacked = [
        jnp.stack([layer_terms[member] for layer_terms in small_terms]) for member in range(5)
    ]
    grad_members = [
        jnp.stack([layer_grads[member] for layer_grads in weight_grads]) for member in range(10)
    ]
    return (
        residual.astype(jnp.bfloat16),
        grad_home,
        stacked[0],
        grad_members[0],
        grad_members[1],
        grad_members[2],
        grad_members[3],
        grad_members[4],
        grad_members[5],
        stacked[2],
        stacked[3],
        stacked[1],
        grad_members[6],
        stacked[4],
        grad_members[7],
        grad_members[8],
        grad_members[9],
    )


def solution(mesh):
    return jax.shard_map(
        shards,
        mesh=mesh,
        in_specs=(
            P("tensor", "dp", None),
            P(),
            P(),
            P(),
            P(None, "dp", "tensor"),
            P(None, "dp", "tensor"),
            P(None, "dp", "tensor"),
            P(None, "dp", "tensor"),
            P(None, "dp", "tensor", None),
            P(None, None, "tensor", "dp"),
            P(),
            P(),
            P(),
            P(None, "tensor", "dp"),
            P(),
            P(None, "dp", "tensor"),
            P(None, "dp", "tensor"),
            P(None, "tensor", "dp"),
            P("tensor", "dp", None),
        ),
        out_specs=(
            P("tensor", "dp", None),
            P("tensor", "dp", None),
            P(),
            P(None, "dp", "tensor"),
            P(None, "dp", "tensor"),
            P(None, "dp", "tensor"),
            P(None, "dp", "tensor"),
            P(None, "dp", "tensor", None),
            P(None, None, "tensor", "dp"),
            P(),
            P(),
            P(),
            P(None, "tensor", "dp"),
            P(),
            P(None, "dp", "tensor"),
            P(None, "dp", "tensor"),
            P(None, "tensor", "dp"),
        ),
        check_vma=False,
    )
```

profile of v0, /device:TPU:0, one launch (start us, length us, event | category | flops | bytes accessed | tf_op | source)
XLA Modules:
  0.0 3127.1 jit_solution(17210678592108211237)
XLA Ops:
  22.8 8.9 all-to-all-done
  37.8 9.5 all-to-all-done.1
  51.9 10.0 all-gather
  62.8 9.8 all-gather.1
  80.6 9.0 all-gather.5
  96.1 15.7 all-gather.41.cloned.1.call-done
  150.0 225.1 %while.85 = (s32[]{:T(128)}, f32[1,1,256,512]{3,2,1,0:T(8,128)S(1)}, f32[16,1,1,64,512]{4,3,2,1,0:T(8,128)}, f32[16,1,1,256,512]{4,3,2,1,0:T(8,128)}, f32[16,1,1...) while((s32[]{:T(128)}, ...), condition=%wide.region_5.9_spmd.clone, body=%wide.region_4.8_spmd.clone.sunk | while | flops 391106688 | bytes 4958393 | solution.py:55
  389.9 41.0 %reduce-scatter.37.cloned.1.call-done = bf16[256,1,1024]{2,0,1:T(8,128)(2,1)} async-done(((bf16[1024,1,1024]{2,0,1:T(8,128)(2,1)}), bf16[256,1,1024]{2,0,1:T(8,128)(2,1)}) %reduce-scatter.37.cloned.1.call-update) | async-done | bytes 524304 | tf_op jit(solution)/shard_map/reduce_scatter | solution.py:165
  435.5 22.5 all-gather.65.cloned.1.call-done
  458.0 27.9 all-gather.63.cloned.1.call-done
  486.0 48.2 %all-gather.43.cloned.1.call-done = bf16[1024,1,1024]{2,0,1:T(8,128)(2,1)} async-done(((bf16[256,1,1024]{2,0,1:T(8,128)(2,1)}), bf16[1024,1,1024]{2,0,1:T(8,128)(2,1)}) %all-gather.43.cloned.1.call-update) | async-done | bytes 2097168 | tf_op jit(solution)/shard_map/all_gather | solution.py:153
  544.8 16.0 all-gather.67.cloned.1.call-done
  567.2 42.7 %reduce-scatter.39.cloned.1.call-done = bf16[256,1,1024]{2,0,1:T(8,128)(2,1)} async-done(((bf16[1024,1,1024]{2,0,1:T(8,128)(2,1)}), bf16[256,1,1024]{2,0,1:T(8,128)(2,1)}) %reduce-scatter.39.cloned.1.call-update) | async-done | bytes 524304 | tf_op jit(solution)/shard_map/reduce_scatter | solution.py:165
  612.8 10.0 all-gather.10
  623.7 12.0 all-gather.11
  643.5 9.1 all-gather.15
  663.5 45.1 %all-gather.45.cloned.1.call-done = bf16[1024,1,1024]{2,0,1:T(8,128)(2,1)} async-done(((bf16[256,1,1024]{2,0,1:T(8,128)(2,1)}), bf16[1024,1,1024]{2,0,1:T(8,128)(2,1)}) %all-gather.45.cloned.1.call-update) | async-done | bytes 2097168 | tf_op jit(solution)/shard_map/all_gather | solution.py:153
  744.3 267.1 %while.86 = (s32[]{:T(128)}, f32[1,1,256,512]{3,2,1,0:T(8,128)S(1)}, f32[16,1,1,64,512]{4,3,2,1,0:T(8,128)}, f32[16,1,1,256,512]{4,3,2,1,0:T(8,128)}, f32[16,1,1...) while((s32[]{:T(128)}, ...), condition=%wide.region_15.19_spmd.clone, body=%wide.region_14.18_spmd.clone.sunk | while | flops 391106688 | bytes 4941749 | solution.py:55
  1024.6 41.7 %reduce-scatter.41.cloned.1.call-done = bf16[256,1,1024]{2,0,1:T(8,128)(2,1)} async-done(((bf16[1024,1,1024]{2,0,1:T(8,128)(2,1)}), bf16[256,1,1024]{2,0,1:T(8,128)(2,1)}) %reduce-scatter.41.cloned.1.call-update) | async-done | bytes 524304 | tf_op jit(solution)/shard_map/reduce_scatter | solution.py:165
  1076.5 16.9 all-gather.77.cloned.1.call-done
  1093.4 27.8 all-gather.75.cloned.1.call-done
  1121.2 48.0 %all-gather.47.cloned.1.call-done = bf16[1024,1,1024]{2,0,1:T(8,128)(2,1)} async-done(((bf16[256,1,1024]{2,0,1:T(8,128)(2,1)}), bf16[1024,1,1024]{2,0,1:T(8,128)(2,1)}) %all-gather.47.cloned.1.call-update) | async-done | bytes 2097168 | tf_op jit(solution)/shard_map/all_gather | solution.py:153
  1177.6 18.3 all-gather.79.cloned.1.call-done
  1195.9 48.0 %all-gather.49.cloned.1.call-done = bf16[1024,1,1024]{2,0,1:T(8,128)(2,1)} async-done(((bf16[256,1,1024]{2,0,1:T(8,128)(2,1)}), bf16[1024,1,1024]{2,0,1:T(8,128)(2,1)}) %all-gather.49.cloned.1.call-update) | async-done | bytes 2097168 | tf_op jit(solution)/shard_map/all_gather | solution.py:157
  1258.2 42.7 %reduce-scatter.45.cloned.1.call-done = bf16[256,1,1024]{2,0,1:T(8,128)(2,1)} async-done(((bf16[1024,1,1024]{2,0,1:T(8,128)(2,1)}), bf16[256,1,1024]{2,0,1:T(8,128)(2,1)}) %reduce-scatter.45.cloned.1.call-update) | async-done | bytes 524304 | tf_op jit(solution)/shard_map/reduce_scatter | solution.py:178
  1308.0 43.2 %all-gather.51.cloned.1.call-done = bf16[1024,1,1024]{2,0,1:T(8,128)(2,1)} async-done(((bf16[256,1,1024]{2,0,1:T(8,128)(2,1)}), bf16[1024,1,1024]{2,0,1:T(8,128)(2,1)}) %all-gather.51.cloned.1.call-update) | async-done | bytes 2097168 | tf_op jit(solution)/shard_map/all_gather | solution.py:157
  1368.4 395.6 %while.87 = (s32[]{:T(128)}, f32[1,1,256,512]{2,3,1,0:T(8,128)S(1)}, f32[16,1,1,64,256]{4,3,2,1,0:T(8,128)}, f32[16,1,1,64,256]{4,3,2,1,0:T(8,128)}, f32[16,1,1,...) while((s32[]{:T(128)}, ...), condition=%wide.region_35.42_spmd.clone, body=%wide.region_24.41_spmd.clone.sunk | while | flops 951722560 | bytes 15191331 | solution.py:55
  1775.5 8.7 multiply_reduce_fusion.12
  1811.5 37.9 %reduce-scatter.47.cloned.1.call-done = bf16[256,1,1024]{2,0,1:T(8,128)(2,1)} async-done(((bf16[1024,1,1024]{2,0,1:T(8,128)(2,1)}), bf16[256,1,1024]{2,0,1:T(8,128)(2,1)}) %reduce-scatter.47.cloned.1.call-update) | async-done | bytes 524304 | tf_op jit(solution)/shard_map/reduce_scatter | solution.py:178
  1851.3 43.5 %reduce-scatter.43.cloned.1.call-done = bf16[256,1,1024]{2,0,1:T(8,128)(2,1)} async-done(((bf16[1024,1,1024]{2,0,1:T(8,128)(2,1)}), bf16[256,1,1024]{2,0,1:T(8,128)(2,1)}) %reduce-scatter.43.cloned.1.call-update) | async-done | bytes 524304 | tf_op jit(solution)/shard_map/reduce_scatter | solution.py:165
  1897.9 45.4 %all-gather.53.cloned.1.call-done = bf16[1024,1,1024]{2,0,1:T(8,128)(2,1)} async-done(((bf16[256,1,1024]{2,0,1:T(8,128)(2,1)}), bf16[1024,1,1024]{2,0,1:T(8,128)(2,1)}) %all-gather.53.cloned.1.call-update) | async-done | bytes 2097168 | tf_op jit(solution)/shard_map/all_gather | solution.py:157
  1958.4 42.7 %reduce-scatter.49.cloned.1.call-done = bf16[256,1,1024]{2,0,1:T(8,128)(2,1)} async-done(((bf16[1024,1,1024]{2,0,1:T(8,128)(2,1)}), bf16[256,1,1024]{2,0,1:T(8,128)(2,1)}) %reduce-scatter.49.cloned.1.call-update) | async-done | bytes 524304 | tf_op jit(solution)/shard_map/reduce_scatter | solution.py:178
  2005.3 8.6 fusion.420
  2071.5 406.5 %while.88 = (s32[]{:T(128)}, f32[1,1,256,512]{2,3,1,0:T(8,128)S(1)}, f32[16,1,1,64,256]{4,3,2,1,0:T(8,128)}, f32[16,1,1,64,256]{4,3,2,1,0:T(8,128)}, f32[16,1,1,...) while((s32[]{:T(128)}, ...), condition=%wide.region_55.62_spmd.clone, body=%wide.region_44.61_spmd.clone.sunk | while | flops 951722560 | bytes 15191331 | solution.py:55
  2490.8 8.5 multiply_reduce_fusion.16
  2572.2 16.4 reduce-scatter.89.cloned.1.call-done
  2590.2 38.0 %reduce-scatter.55.cloned.1.call-done = f32[128,256]{0,1:T(8,128)} async-done(((f32[1024,256]{0,1:T(8,128)}), f32[128,256]{0,1:T(8,128)}) %reduce-scatter.55.cloned.1.call-update) | async-done | bytes 131088 | tf_op jit(solution)/shard_map/reduce_scatter | solution.py:374
  2628.2 39.4 %reduce-scatter.53.cloned.1.call-done = f32[128,256]{0,1:T(8,128)} async-done(((f32[1024,256]{0,1:T(8,128)}), f32[128,256]{0,1:T(8,128)}) %reduce-scatter.53.cloned.1.call-update) | async-done | bytes 131088 | tf_op jit(solution)/shard_map/reduce_scatter | solution.py:374
  2669.5 44.5 %reduce-scatter.51.cloned.1.call-done = bf16[256,1,1024]{2,0,1:T(8,128)(2,1)} async-done(((bf16[1024,1,1024]{2,0,1:T(8,128)(2,1)}), bf16[256,1,1024]{2,0,1:T(8,128)(2,1)}) %reduce-scatter.51.cloned.1.call-update) | async-done | bytes 524304 | tf_op jit(solution)/shard_map/reduce_scatter | solution.py:178
  2728.7 24.4 reduce-scatter.59.cloned.1.call-done
  2753.1 39.2 %reduce-scatter.57.cloned.1.call-done = f32[128,256]{0,1:T(8,128)} async-done(((f32[1024,256]{0,1:T(8,128)}), f32[128,256]{0,1:T(8,128)}) %reduce-scatter.57.cloned.1.call-update) | async-done | bytes 131088 | tf_op jit(solution)/shard_map/reduce_scatter | solution.py:375
  2794.1 42.5 %reduce-scatter.63.cloned.1.call-done = f32[128,512]{0,1:T(8,128)} async-done(((f32[1024,512]{0,1:T(8,128)}), f32[128,512]{0,1:T(8,128)}) %reduce-scatter.63.cloned.1.call-update) | async-done | bytes 262160 | tf_op jit(solution)/shard_map/reduce_scatter | solution.py:376
  2836.6 44.9 %reduce-scatter.61.cloned.1.call-done = f32[128,512]{0,1:T(8,128)} async-done(((f32[1024,512]{0,1:T(8,128)}), f32[128,512]{0,1:T(8,128)}) %reduce-scatter.61.cloned.1.call-update) | async-done | bytes 262160 | tf_op jit(solution)/shard_map/reduce_scatter | solution.py:376
  2883.6 42.3 %reduce-scatter.67.cloned.1.call-done = f32[128,512]{0,1:T(8,128)} async-done(((f32[1024,512]{0,1:T(8,128)}), f32[128,512]{0,1:T(8,128)}) %reduce-scatter.67.cloned.1.call-update) | async-done | bytes 262160 | tf_op jit(solution)/shard_map/reduce_scatter | solution.py:377
  2925.9 44.7 %reduce-scatter.65.cloned.1.call-done = f32[128,512]{0,1:T(8,128)} async-done(((f32[1024,512]{0,1:T(8,128)}), f32[128,512]{0,1:T(8,128)}) %reduce-scatter.65.cloned.1.call-update) | async-done | bytes 262160 | tf_op jit(solution)/shard_map/reduce_scatter | solution.py:377
  2972.7 42.3 %reduce-scatter.71.cloned.1.call-done = f32[512,128]{1,0:T(8,128)} async-done(((f32[512,1024]{1,0:T(8,128)}), f32[512,128]{1,0:T(8,128)}) %reduce-scatter.71.cloned.1.call-update) | async-done | bytes 262160 | tf_op jit(solution)/shard_map/reduce_scatter | solution.py:385
  3015.1 44.7 %reduce-scatter.69.cloned.1.call-done = f32[512,128]{1,0:T(8,128)} async-done(((f32[512,1024]{1,0:T(8,128)}), f32[512,128]{1,0:T(8,128)}) %reduce-scatter.69.cloned.1.call-update) | async-done | bytes 262160 | tf_op jit(solution)/shard_map/reduce_scatter | solution.py:385
  3061.7 39.8 %all-reduce.30 = (f32[1,1024]{1,0:T(1,128)S(1)}, f32[1,1024]{1,0:T(1,128)S(1)}, f32[1,4]{1,0:T(1,128)S(1)}, f32[1,4]{1,0:T(1,128)S(1)}, f32[1,4]{1,0:T(1,128)S(1...) all-reduce(f32[1,1024]{1,0:T(1,128)S(1)} %bitcast.1824, ...), channel_id=1, replica_groups=mesh['dp'=8,'tensor'=4] {'dp','tensor'}, use_global_device_ids=true, to_apply=%region_64.71 | all-reduce | flops 5136 | bytes 41088 | tf_op jit(solution)/shard_map/psum | solution.py:396
  (2418 shorter events, 1687.8 us)
Async XLA Ops:
  7.2 83.4 %all-gather.57.cloned.1.call-start = ((), (), s32[]{:S(2)}) async-start(), calls=%async_computation.64 | async-start | bytes 1179648 | tf_op jit(solution)/shard_map/all_gather | solution.py:273
  21.9 71.1 %all-gather.59.cloned.1.call-start = ((), (), s32[]{:S(2)}) async-start(), calls=%async_computation.65 | async-start | bytes 1179648 | tf_op jit(solution)/shard_map/all_gather | solution.py:274
  37.7 74.1 %all-gather.41.cloned.1.call-start = ((), (), s32[]{:S(2)}) async-start(), calls=%async_computation.32 | async-start | bytes 2621440 | tf_op jit(solution)/shard_map/all_gather | solution.py:153
  49.1 334.8 %all-gather.61.cloned.1.call-start = ((), (), s32[]{:S(2)}) async-start(), calls=%async_computation.66 | async-start | bytes 1179648 | tf_op jit(solution)/shard_map/all_gather | solution.py:277
  49.9 381.0 %reduce-scatter.37.cloned.1.call-start = ((), (), s32[]{:S(2)}) async-start(), calls=%async_computation.33 | async-start | bytes 2621440 | tf_op jit(solution)/shard_map/reduce_scatter | solution.py:165
  389.0 97.0 %all-gather.63.cloned.1.call-start = ((), (), s32[]{:S(2)}) async-start(), calls=%async_computation.67 | async-start | bytes 1622016 | tf_op jit(solution)/shard_map/all_gather | solution.py:278
  389.9 144.3 %all-gather.43.cloned.1.call-start = ((), (), s32[]{:S(2)}) async-start(), calls=%async_computation.34 | async-start | bytes 2621440 | tf_op jit(solution)/shard_map/all_gather | solution.py:153
  434.2 126.6 %all-gather.67.cloned.1.call-start = ((), (), s32[]{:S(2)}) async-start(), calls=%async_computation.69 | async-start | bytes 1622016 | tf_op jit(solution)/shard_map/all_gather | solution.py:280
  435.1 174.8 %reduce-scatter.39.cloned.1.call-start = ((), (), s32[]{:S(2)}) async-start(), calls=%async_computation.35 | async-start | bytes 2621440 | tf_op jit(solution)/shard_map/reduce_scatter | solution.py:165
  565.8 88.7 %all-gather.69.cloned.1.call-start = ((), (), s32[]{:S(2)}) async-start(), calls=%async_computation.70 | async-start | bytes 1179648 | tf_op jit(solution)/shard_map/all_gather | solution.py:273
  566.6 93.9 %all-gather.71.cloned.1.call-start = ((), (), s32[]{:S(2)}) async-start(), calls=%async_computation.71 | async-start | bytes 1179648 | tf_op jit(solution)/shard_map/all_gather | solution.py:274
  567.2 141.4 %all-gather.45.cloned.1.call-start = ((), (), s32[]{:S(2)}) async-start(), calls=%async_computation.36 | async-start | bytes 2621440 | tf_op jit(solution)/shard_map/all_gather | solution.py:153
  612.2 407.1 %all-gather.73.cloned.1.call-start = ((), (), s32[]{:S(2)}) async-start(), calls=%async_computation.72 | async-start | bytes 1179648 | tf_op jit(solution)/shard_map/all_gather | solution.py:277
  612.8 453.5 %reduce-scatter.41.cloned.1.call-start = ((), (), s32[]{:S(2)}) async-start(), calls=%async_computation.37 | async-start | bytes 2621440 | tf_op jit(solution)/shard_map/reduce_scatter | solution.py:165
  1023.4 70.0 %all-gather.77.cloned.1.call-start = ((), (), s32[]{:S(2)}) async-start(), calls=%async_computation.74 | async-start | bytes 1622016 | tf_op jit(solution)/shard_map/all_gather | solution.py:279
  1024.0 97.2 %all-gather.75.cloned.1.call-start = ((), (), s32[]{:S(2)}) async-start(), calls=%async_computation.73 | async-start | bytes 1622016 | tf_op jit(solution)/shard_map/all_gather | solution.py:278
  1024.6 144.7 %all-gather.47.cloned.1.call-start = ((), (), s32[]{:S(2)}) async-start(), calls=%async_computation.38 | async-start | bytes 2621440 | tf_op jit(solution)/shard_map/all_gather | solution.py:153
  1069.6 126.3 %all-gather.79.cloned.1.call-start = ((), (), s32[]{:S(2)}) async-start(), calls=%async_computation.75 | async-start | bytes 1622016 | tf_op jit(solution)/shard_map/all_gather | solution.py:280
  1070.4 173.6 %all-gather.49.cloned.1.call-start = ((), (), s32[]{:S(2)}) async-start(), calls=%async_computation.40 | async-start | bytes 2621440 | tf_op jit(solution)/shard_map/all_gather | solution.py:157
  1076.2 224.6 %reduce-scatter.45.cloned.1.call-start = ((), (), s32[]{:S(2)}) async-start(), calls=%async_computation.41 | async-start | bytes 2621440 | tf_op jit(solution)/shard_map/reduce_scatter | solution.py:178
  1258.2 93.0 %all-gather.51.cloned.1.call-start = ((), (), s32[]{:S(2)}) async-start(), calls=%async_computation.42 | async-start | bytes 2621440 | tf_op jit(solution)/shard_map/all_gather | solution.py:157
  1305.7 543.7 %reduce-scatter.47.cloned.1.call-start = ((), (), s32[]{:S(2)}) async-start(), calls=%async_computation.43 | async-start | bytes 2621440 | tf_op jit(solution)/shard_map/reduce_scatter | solution.py:178
  1806.7 88.2 %reduce-scatter.43.cloned.1.call-start = ((), (), s32[]{:S(2)}) async-start(), calls=%async_computation.39 | async-start | bytes 2621440 | tf_op jit(solution)/shard_map/reduce_scatter | solution.py:165
  1811.5 131.8 %all-gather.53.cloned.1.call-start = ((), (), s32[]{:S(2)}) async-start(), calls=%async_computation.44 | async-start | bytes 2621440 | tf_op jit(solution)/shard_map/all_gather | solution.py:157
  1897.9 103.2 %reduce-scatter.49.cloned.1.call-start = ((), (), s32[]{:S(2)}) async-start(), calls=%async_computation.45 | async-start | bytes 2621440 | tf_op jit(solution)/shard_map/reduce_scatter | solution.py:178
  1958.4 96.6 %all-gather.55.cloned.1.call-start = ((), (), s32[]{:S(2)}) async-start(), calls=%async_computation.46 | async-start | bytes 2621440 | tf_op jit(solution)/shard_map/all_gather | solution.py:157
  2004.8 553.0 %reduce-scatter.87.cloned.1.call-start = ((), (), s32[]{:S(2)}) async-start(), calls=%async_computation.77 | async-start | bytes 589824
  2021.1 537.5 %reduce-scatter.91.cloned.1.call-start = ((), (), s32[]{:S(2)}) async-start(), calls=%async_computation.79 | async-start | bytes 589824
  2022.3 537.3 %reduce-scatter.75.cloned.1.call-start = ((), (), s32[]{:S(2)}) async-start(), calls=%async_computation.59 | async-start | bytes 3538944 | tf_op jit(solution)/shard_map/reduce_scatter | solution.py:386
  2028.9 530.7 %reduce-scatter.73.cloned.1.call-start = ((), (), s32[]{:S(2)}) async-start(), calls=%async_computation.58 | async-start | bytes 3538944 | tf_op jit(solution)/shard_map/reduce_scatter | solution.py:386
  2039.6 522.3 %reduce-scatter.79.cloned.1.call-start = ((), (), s32[]{:S(2)}) async-start(), calls=%async_computation.61 | async-start | bytes 3538944 | tf_op jit(solution)/shard_map/reduce_scatter | solution.py:387
  2040.4 521.5 %reduce-scatter.77.cloned.1.call-start = ((), (), s32[]{:S(2)}) async-start(), calls=%async_computation.60 | async-start | bytes 3538944 | tf_op jit(solution)/shard_map/reduce_scatter | solution.py:387
  2041.0 525.5 %reduce-scatter.83.cloned.1.call-start = ((), (), s32[]{:S(2)}) async-start(), calls=%async_computation.63 | async-start | bytes 3244032 | tf_op jit(solution)/shard_map/reduce_scatter | solution.py:388
  2046.0 520.5 %reduce-scatter.81.cloned.1.call-start = ((), (), s32[]{:S(2)}) async-start(), calls=%async_computation.62 | async-start | bytes 3244032 | tf_op jit(solution)/shard_map/reduce_scatter | solution.py:388
  2054.9 515.8 %reduce-scatter.85.cloned.1.call-start = ((), (), s32[]{:S(2)}) async-start(), calls=%async_computation.76 | async-start | bytes 589824
  2517.5 71.2 %reduce-scatter.89.cloned.1.call-start = ((), (), s32[]{:S(2)}) async-start(), calls=%async_computation.78 | async-start | bytes 589824
  2518.6 109.6 %reduce-scatter.55.cloned.1.call-start = ((), (), s32[]{:S(2)}) async-start(), calls=%async_computation.49 | async-start | bytes 1179648 | tf_op jit(solution)/shard_map/reduce_scatter | solution.py:374
  2521.8 145.8 %reduce-scatter.53.cloned.1.call-start = ((), (), s32[]{:S(2)}) async-start(), calls=%async_computation.48 | async-start | bytes 1179648 | tf_op jit(solution)/shard_map/reduce_scatter | solution.py:374
  2525.2 188.8 %reduce-scatter.51.cloned.1.call-start = ((), (), s32[]{:S(2)}) async-start(), calls=%async_computation.47 | async-start | bytes 2621440 | tf_op jit(solution)/shard_map/reduce_scatter | solution.py:178
  2533.8 219.2 %reduce-scatter.59.cloned.1.call-start = ((), (), s32[]{:S(2)}) async-start(), calls=%async_computation.51 | async-start | bytes 1179648 | tf_op jit(solution)/shard_map/reduce_scatter | solution.py:375
  2534.6 257.7 %reduce-scatter.57.cloned.1.call-start = ((), (), s32[]{:S(2)}) async-start(), calls=%async_computation.50 | async-start | bytes 1179648 | tf_op jit(solution)/shard_map/reduce_scatter | solution.py:375
  2535.3 301.3 %reduce-scatter.63.cloned.1.call-start = ((), (), s32[]{:S(2)}) async-start(), calls=%async_computation.53 | async-start | bytes 2359296 | tf_op jit(solution)/shard_map/reduce_scatter | solution.py:376
  2540.3 341.3 %reduce-scatter.61.cloned.1.call-start = ((), (), s32[]{:S(2)}) async-start(), calls=%async_computation.52 | async-start | bytes 2359296 | tf_op jit(solution)/shard_map/reduce_scatter | solution.py:376
  2545.2 380.7 %reduce-scatter.67.cloned.1.call-start = ((), (), s32[]{:S(2)}) async-start(), calls=%async_computation.55 | async-start | bytes 2359296 | tf_op jit(solution)/shard_map/reduce_scatter | solution.py:377
  2545.8 424.9 %reduce-scatter.65.cloned.1.call-start = ((), (), s32[]{:S(2)}) async-start(), calls=%async_computation.54 | async-start | bytes 2359296 | tf_op jit(solution)/shard_map/reduce_scatter | solution.py:377
  2546.4 468.6 %reduce-scatter.71.cloned.1.call-start = ((), (), s32[]{:S(2)}) async-start(), calls=%async_computation.57 | async-start | bytes 2359296 | tf_op jit(solution)/shard_map/reduce_scatter | solution.py:385
  2550.8 509.0 %reduce-scatter.69.cloned.1.call-start = ((), (), s32[]{:S(2)}) async-start(), calls=%async_computation.56 | async-start | bytes 2359296 | tf_op jit(solution)/shard_map/reduce_scatter | solution.py:385
  2725.0 376.4 %all-to-all-start.2 = ((bf16[8,2,16384]{2,1,0:T(2,128)(2,1)}), bf16[8,2,16384]{2,1,0:T(2,128)(2,1)S(1)}, u32[]{:S(2)}, u32[]{:S(2)}) async-start(bf16[8,2,16384]{2,1,0:T(2,128)(2,1)} %reshape.4231), calls=%async_computation.10 | async-start | bytes 1048576 | tf_op jit(solution)/shard_map/all_to_all | solution.py:399
  (121 other events, 4418.8 us)
Sparse Core Ops, SparseCore 0:
  10.5 26.1 all-gather.56
  39.2 24.1 all-gather.58
  65.6 46.1 all-gather.40
  114.1 22.2 all-gather.60
  388.2 42.6 reduce-scatter.36
  433.4 24.6 all-gather.64
  460.6 25.2 all-gather.62
  488.2 45.9 all-gather.42
  536.8 24.0 all-gather.66
  566.0 43.8 reduce-scatter.38
  612.3 24.2 all-gather.68
  638.3 22.0 all-gather.70
  662.6 45.9 all-gather.44
  710.9 22.2 all-gather.72
  1023.5 42.7 reduce-scatter.40
  1068.8 24.6 all-gather.76
  1095.9 25.2 all-gather.74
  1123.3 45.9 all-gather.46
  1171.9 24.0 all-gather.78
  1198.0 45.9 all-gather.48
  1258.3 42.5 reduce-scatter.44
  1305.8 45.2 all-gather.50
  1806.8 42.5 reduce-scatter.46
  1851.6 43.1 reduce-scatter.42
  1898.0 45.2 all-gather.52
  1958.5 42.5 reduce-scatter.48
  2004.9 45.2 all-gather.54
  2054.1 33.0 reduce-scatter.86
  2090.8 34.1 reduce-scatter.90
  2128.6 46.3 reduce-scatter.74
  2178.4 46.3 reduce-scatter.72
  2228.6 46.3 reduce-scatter.78
  2278.2 46.3 reduce-scatter.76
  2328.3 45.0 reduce-scatter.82
  2376.8 45.0 reduce-scatter.80
  2517.6 33.3 reduce-scatter.84
  2554.6 34.0 reduce-scatter.88
  2592.2 36.0 reduce-scatter.54
  2631.6 35.9 reduce-scatter.52
  2670.0 43.8 reduce-scatter.50
  2717.7 35.3 reduce-scatter.58
  2756.2 35.9 reduce-scatter.56
  2795.4 41.1 reduce-scatter.62
  2840.3 41.2 reduce-scatter.60
  2884.7 41.2 reduce-scatter.66
  2929.4 41.2 reduce-scatter.64
  2973.8 41.2 reduce-scatter.70
  3018.5 41.2 reduce-scatter.68
where the time goes:
time: 3150 us; the launch traced here: 3130 us
  waiting for transfers between devices  1220 us (39%)
  matrix products  705 us (22%)
  other arithmetic  628 us (20%)
  local copies, waits for them, and re-layouts  326 us (10%)
  blocking collectives  115 us (4%)
  loops' own time  94 us (3%)
    dot_general x672, matrix products, precise_product(): return jnp.dot(left_side, right_side, precision=lax.Precision.HIGHEST)  416 us
    reduce_scatter x4, waiting for transfers between devices, sum_products(): lax.psum_scatter(product_rows(jnp.int32(0), rows_local * lax.axis_size('t...  169 us
    reduce_scatter x4, waiting for transfers between devices, sum_back(): lax.psum_scatter(product_rows(jnp.int32(0), rows_local * lax.axis_size('t...  168 us
    another operation x96, other arithmetic, block_step(): jax.scipy.linalg.solve_triangular(unit_lower, write_rate[:, None] * key_r...  160 us
    all_gather x4, waiting for transfers between devices, gather_rows(): return lax.all_gather(values, 'tensor', axis=0, tiled=True)  157 us
    another operation x64, other arithmetic, block_step(): jax.scipy.linalg.solve_triangular(unit_lower, write_rate[:, None] * value...  157 us
    all_gather x4, waiting for transfers between devices, gather_grads(): return lax.all_gather(values, 'tensor', axis=0, tiled=True)  137 us
    another operation x4, loops' own time, delta_sequence(): lax.scan(jax.checkpoint(block_step), initial, inputs)  94 us
  transfers between devices with their start and end apart: 52, of which 36 were waited for; matrix products, arithmetic and copies ran while one was open for 37% of the time, Pallas kernels for 0%

commit v1 on v0

v1 whole, which is shorter than its diff:
```python
import functools
import jax
import jax.numpy as jnp
from jax import lax
from jax.experimental import pallas as pl
from jax.experimental.pallas import tpu as pltpu
from jax.sharding import PartitionSpec as P

CHUNK = 256
LANES = 128
KEY = 256
VAL = 512
CONV_CH = 2 * KEY + VAL
F32 = jnp.float32
BF16 = jnp.bfloat16
NN = (((1,), (0,)), ((), ()))
NT = (((1,), (1,)), ((), ()))
TN = (((0,), (0,)), ((), ()))


def mm(a, b, dims=NN):
    return lax.dot_general(
        a.astype(BF16), b.astype(BF16), dims, preferred_element_type=F32
    )


def split_low(a):
    high = a.astype(BF16)
    return high, (a - high.astype(F32)).astype(BF16)


def mm3(a, b, dims=NN):
    a_high, a_low = split_low(a)
    b_high, b_low = split_low(b)
    dot = functools.partial(
        lax.dot_general, dimension_numbers=dims, preferred_element_type=F32
    )
    return dot(a_high, b_high) + (dot(a_high, b_low) + dot(a_low, b_high))


def mm_exact_left(a, b, dims=NN):
    a = a.astype(BF16)
    high = b.astype(BF16)
    rest = b - high.astype(F32)
    mid = rest.astype(BF16)
    low = (rest - mid.astype(F32)).astype(BF16)
    dot = functools.partial(
        lax.dot_general, dimension_numbers=dims, preferred_element_type=F32
    )
    return dot(a, high) + (dot(a, mid) + dot(a, low))


def iotas():
    rows = lax.broadcasted_iota(jnp.int32, (CHUNK, CHUNK), 0)
    cols = lax.broadcasted_iota(jnp.int32, (CHUNK, CHUNK), 1)
    return rows, cols


def wide(col_block, width):
    return jnp.concatenate([col_block] * (width // LANES), axis=1)


def rates_of(rates, rate, bias):
    write = jax.nn.sigmoid(jnp.broadcast_to(rates[:, 0:1], (CHUNK, LANES)))
    logit = jnp.broadcast_to(rates[:, 1:2], (CHUNK, LANES)) + bias
    soft = jnp.maximum(logit, 0.0) + jnp.log1p(jnp.exp(-jnp.abs(logit)))
    return write, -rate * soft, jax.nn.sigmoid(logit)


def decay_terms(step, rows, cols):
    inclusive = (rows >= cols).astype(BF16)
    total = mm_exact_left(inclusive, step)
    spread = wide(total, CHUNK) - jnp.concatenate([total.T] * (CHUNK // LANES), axis=0)
    decay = jnp.where(rows >= cols, jnp.exp(jnp.minimum(spread, 0.0)), 0.0)
    last = jnp.broadcast_to(total[CHUNK - 1 : CHUNK, :], (CHUNK, LANES))
    return decay, jnp.exp(total), jnp.exp(last - total), jnp.exp(last)


def solve_unit(coupling, rows, cols, product):
    same = ((rows >> 1) == (cols >> 1)) & (rows != cols)
    inverse = jnp.where(rows == cols, 1.0, 0.0) - jnp.where(same, coupling, 0.0)
    for level in range(1, CHUNK.bit_length() - 1):
        between = ((rows >> (level + 1)) == (cols >> (level + 1))) & (
            (rows >> level) != (cols >> level)
        )
        part = jnp.where(between, coupling, 0.0)
        inverse = inverse - product(product(inverse, part), inverse)
    return inverse


def silu_of(x):
    gate = jax.nn.sigmoid(x)
    return x * gate, gate


def conv_rows(padded_ref, taps_ref, start):
    result = padded_ref[pl.ds(start, CHUNK), :] * taps_ref[0:1, :]
    for j in range(1, 4):
        result = result + padded_ref[pl.ds(start + j, CHUNK), :] * taps_ref[j : j + 1, :]
    return result


def forward_kernel(
    scalars_ref, x_ref, w_in_ref, w_aux_ref, w_out_ref, taps_ref, gain_ref,
    part_ref, heads_ref, proj_ref, gate_ref, rates_ref, inverse_ref, fresh_ref, o_ref, state_ref,
    padded, memory,
):
    @pl.when(pl.program_id(0) == 0)
    def _():
        memory[...] = jnp.zeros_like(memory)
        padded[0:8, :] = jnp.zeros((8, CONV_CH), F32)

    x = x_ref[...]
    proj = mm(x, w_in_ref[...])
    rates = mm(x, w_aux_ref[...])
    rates_ref[...] = rates
    qkv = proj[:, :CONV_CH]
    proj_ref[...] = qkv
    gate_in = proj[:, CONV_CH:]
    gate_ref[...] = gate_in
    padded[8 : 8 + CHUNK, :] = qkv
    conv = conv_rows(padded, taps_ref, 5)
    padded[0:8, :] = qkv[CHUNK - 8 :, :]
    act, _ = silu_of(conv)
    q, k, v = act[:, :KEY], act[:, KEY : 2 * KEY], act[:, 2 * KEY :]
    q = q * (lax.rsqrt(jnp.sum(q * q, axis=1, keepdims=True) + 1e-6) * KEY**-0.5)
    k = k * lax.rsqrt(jnp.sum(k * k, axis=1, keepdims=True) + 1e-6)
    rows, cols = iotas()
    write, step, _ = rates_of(rates, scalars_ref[0], scalars_ref[1])
    decay, growth, rest, final = decay_terms(step, rows, cols)
    coupling = jnp.where(rows > cols, wide(write, CHUNK) * mm3(k, k, NT) * decay, 0.0)
    inverse = solve_unit(coupling, rows, cols, mm3)
    inverse_ref[...] = inverse.astype(BF16)
    within = mm(q, k, NT) * decay
    state = memory[...]
    state_ref[...] = state
    low_state = state.astype(BF16)
    source = wide(write, VAL) * (v - wide(growth, VAL) * mm(k, low_state))
    fresh = mm3(inverse, source)
    fresh_ref[...] = fresh
    o = wide(growth, VAL) * mm(q, low_state) + mm(within, fresh)
    o_ref[...] = o
    memory[...] = wide(final, VAL) * state + mm(k * wide(rest, KEY), fresh, TN)
    scaled = o * lax.rsqrt(jnp.mean(o * o, axis=1, keepdims=True) + 1e-5) * gain_ref[...]
    heads = (scaled * silu_of(gate_in)[0]).astype(BF16)
    heads_ref[...] = heads
    part_ref[...] = mm(heads, w_out_ref[...], NT).astype(BF16)


def mixer_forward(x, pack, taps, gain, scalars):
    length, width = x.shape
    chunks = length // CHUNK
    row = lambda cols: pl.BlockSpec((CHUNK, cols), lambda i: (i, 0))
    fixed = lambda shape, at: pl.BlockSpec(shape, lambda i: (0, at), pipeline_mode=pl.Buffered(1))
    out = lambda cols, kind: jax.ShapeDtypeStruct((length, cols), kind)
    return pl.pallas_call(
        forward_kernel,
        grid=(chunks,),
        in_specs=[
            pl.BlockSpec(memory_space=pltpu.SMEM),
            row(width),
            fixed((width, 1536), 0),
            fixed((width, LANES), 16),
            fixed((width, VAL), 3),
            fixed((4, CONV_CH), 0),
            fixed((1, VAL), 0),
        ],
        out_specs=[
            row(width), row(VAL), row(CONV_CH), row(VAL), row(LANES), row(CHUNK), row(VAL), row(VAL),
            pl.BlockSpec((None, KEY, VAL), lambda i: (i, 0, 0)),
        ],
        out_shape=[
            out(width, BF16), out(VAL, BF16), out(CONV_CH, F32), out(VAL, F32), out(LANES, F32),
            out(CHUNK, BF16), out(VAL, F32), out(VAL, F32),
            jax.ShapeDtypeStruct((chunks, KEY, VAL), F32),
        ],
        scratch_shapes=[pltpu.VMEM((CHUNK + 8, CONV_CH), F32), pltpu.VMEM((KEY, VAL), F32)],
        compiler_params=pltpu.CompilerParams(
            dimension_semantics=("arbitrary",), vmem_limit_bytes=56 * 1024 * 1024
        ),
        name="mixer_forward",
    )(scalars, x, pack, pack, pack, taps, gain)


def unit_back(grad, vector, scale):
    inv = lax.rsqrt(jnp.sum(vector * vector, axis=1, keepdims=True) + 1e-6)
    dot = jnp.sum(grad * vector, axis=1, keepdims=True)
    return (grad - vector * (inv * inv * dot)) * (inv * scale)


def backward_kernel(
    scalars_ref, g_ref, w_in_ref, w_aux_ref, w_out_ref, taps_ref, gain_ref,
    proj_ref, halo_ref, gate_ref, rates_ref, inverse_ref, fresh_ref, o_ref, state_ref,
    part_ref, dproj_ref, drates_ref, dtaps_ref, dgain_ref, dscalars_ref,
    padded, dpadded, dmemory,
):
    at = pl.program_id(0)
    last = pl.num_programs(0) - 1

    @pl.when(at == 0)
    def _():
        dmemory[...] = jnp.zeros_like(dmemory)
        dpadded[CHUNK : CHUNK + 8, :] = jnp.zeros((8, CONV_CH), F32)
        dtaps_ref[...] = jnp.zeros_like(dtaps_ref)
        dgain_ref[...] = jnp.zeros_like(dgain_ref)
        dscalars_ref[...] = jnp.zeros_like(dscalars_ref)

    rows, cols = iotas()
    padded[8 : 8 + CHUNK, :] = proj_ref[...]
    padded[0:8, :] = jnp.where(at == last, 0.0, halo_ref[...])
    conv = conv_rows(padded, taps_ref, 5)
    act, sig = silu_of(conv)
    act_q, act_k, v = act[:, :KEY], act[:, KEY : 2 * KEY], act[:, 2 * KEY :]
    q = act_q * (lax.rsqrt(jnp.sum(act_q * act_q, axis=1, keepdims=True) + 1e-6) * KEY**-0.5)
    k = act_k * lax.rsqrt(jnp.sum(act_k * act_k, axis=1, keepdims=True) + 1e-6)
    rates = rates_ref[...]
    write, step, sig_decay = rates_of(rates, scalars_ref[0], scalars_ref[1])
    decay, growth, rest, final = decay_terms(step, rows, cols)
    growth_v = wide(growth, VAL)
    write_v = wide(write, VAL)
    low_q, low_k = q.astype(BF16), k.astype(BF16)
    below = rows > cols
    strict_decay = jnp.where(below, decay, 0.0)
    keys = mm(low_k, low_k, NT) * strict_decay * wide(write, CHUNK)
    within = mm(low_q, low_k, NT) * decay
    dheads = mm(g_ref[...], w_out_ref[...])
    o = o_ref[...]
    gate_in = gate_ref[...]
    gate, gate_sig = silu_of(gate_in)
    inv = lax.rsqrt(jnp.mean(o * o, axis=1, keepdims=True) + 1e-5)
    normal = o * inv
    gain = gain_ref[...]
    dgate = dheads * normal * gain * (gate_sig * (1.0 + gate_in * (1.0 - gate_sig)))
    dscaled = dheads * gate
    dgain_ref[...] += jnp.sum(dscaled * normal, axis=0, keepdims=True)
    dnormal = dscaled * gain
    do = inv * (dnormal - normal * jnp.mean(dnormal * normal, axis=1, keepdims=True))
    state = state_ref[...]
    low_state = state.astype(BF16)
    fresh = fresh_ref[...]
    low_fresh = fresh.astype(BF16)
    dstate = dmemory[...]
    low_dstate = dstate.astype(BF16)
    low_do = do.astype(BF16)
    k_rest = k * wide(rest, KEY)
    rest_dstate = mm(k_rest, low_dstate)
    dfresh = mm(within, low_do, TN) + rest_dstate
    dsource = mm(inverse_ref[...], dfresh, TN)
    low_dsource = dsource.astype(BF16)
    dv = write_v * dsource
    dread = -(growth_v * dv)
    low_dread = dread.astype(BF16)
    do_growth = growth_v * do
    low_do_growth = do_growth.astype(BF16)
    dwithin = mm(low_do, low_fresh, NT)
    dcoupling = -mm(low_dsource, low_fresh, NT)
    dkeys = dcoupling * strict_decay * wide(write, CHUNK)
    dpairs = dwithin * decay
    dq = mm(low_do_growth, low_state, NT) + mm(dpairs, low_k)
    dk = (
        mm(low_dread, low_state, NT)
        + mm(dpairs, low_q, TN)
        + mm(dkeys + dkeys.T, low_k)
        + wide(rest, KEY) * mm(low_fresh, low_dstate, NT)
    )
    dmemory[...] = (
        wide(final, VAL) * dstate + mm(low_q, low_do_growth, TN) + mm(low_k, low_dread, TN)
    )
    spread = dwithin * within + dcoupling * keys
    straddle = jnp.where(below, mm_exact_left((rows <= cols).astype(BF16), spread), 0.0)
    read_rows = jnp.sum(
        do_growth * mm(low_q, low_state) + dread * mm(low_k, low_state), axis=1, keepdims=True
    )
    rest_rows = jnp.sum(fresh * rest_dstate, axis=1, keepdims=True)
    carried = jnp.sum(dstate * state) * final[0:1, 0:1]
    suffix = mm_exact_left(
        (rows <= cols).astype(BF16), jnp.broadcast_to(read_rows, (CHUNK, LANES))
    ) + mm_exact_left((rows > cols).astype(BF16), jnp.broadcast_to(rest_rows, (CHUNK, LANES)))
    dstep = suffix + jnp.sum(straddle, axis=1, keepdims=True) + carried
    dlogit = dstep * (-scalars_ref[0]) * sig_decay
    dwrite = (1.0 - write) * jnp.sum(dsource * fresh, axis=1, keepdims=True)
    lane = lax.broadcasted_iota(jnp.int32, (CHUNK, LANES), 1)
    drates = jnp.where(lane == 0, dwrite, jnp.where(lane == 1, dlogit, 0.0))
    low_drates = drates.astype(BF16)
    drates_ref[...] = low_drates
    dscalars_ref[0:1, :] += jnp.sum(dstep * step, axis=0, keepdims=True)
    dscalars_ref[1:2, :] += jnp.sum(dlogit, axis=0, keepdims=True)
    dact = jnp.concatenate(
        [unit_back(dq, act_q, KEY**-0.5), unit_back(dk, act_k, 1.0), dv], axis=1
    )
    dconv = dact * (sig * (1.0 + conv * (1.0 - sig)))
    dpadded[0:CHUNK, :] = dconv
    dtaps_ref[...] += jnp.concatenate(
        [
            jnp.sum(dconv * padded[5 + j : 5 + j + CHUNK, :], axis=0, keepdims=True)
            for j in range(4)
        ],
        axis=0,
    )
    dqkv = dconv * taps_ref[3:4, :]
    for j in range(3):
        dqkv = dqkv + dpadded[pl.ds(3 - j, CHUNK), :] * taps_ref[j : j + 1, :]
    dpadded[CHUNK : CHUNK + 8, :] = dconv[0:8, :]
    low_dproj = jnp.concatenate([dqkv, dgate], axis=1).astype(BF16)
    dproj_ref[...] = low_dproj
    part_ref[...] = (
        mm(low_dproj, w_in_ref[...], NT) + mm(low_drates, w_aux_ref[...], NT)
    ).astype(BF16)


def mixer_backward(g, pack, taps, gain, scalars, saved):
    proj, gate_in, rates, inverse, fresh, o, states = saved
    length, width = g.shape
    chunks = length // CHUNK
    back = chunks - 1
    row = lambda cols: pl.BlockSpec((CHUNK, cols), lambda i: (back - i, 0))
    fixed = lambda shape, at: pl.BlockSpec(shape, lambda i: (0, at), pipeline_mode=pl.Buffered(1))
    out = lambda cols, kind: jax.ShapeDtypeStruct((length, cols), kind)
    steps = CHUNK // 8
    return pl.pallas_call(
        backward_kernel,
        grid=(chunks,),
        in_specs=[
            pl.BlockSpec(memory_space=pltpu.SMEM),
            row(width),
            fixed((width, 1536), 0),
            fixed((width, LANES), 16),
            fixed((width, VAL), 3),
            fixed((4, CONV_CH), 0),
            fixed((1, VAL), 0),
            row(CONV_CH),
            pl.BlockSpec((8, CONV_CH), lambda i: (jnp.maximum((back - i) * steps - 1, 0), 0)),
            row(VAL), row(LANES), row(CHUNK), row(VAL), row(VAL),
            pl.BlockSpec((None, KEY, VAL), lambda i: (back - i, 0, 0)),
        ],
        out_specs=[
            row(width), row(1536), row(LANES),
            pl.BlockSpec((4, CONV_CH), lambda i: (0, 0)),
            pl.BlockSpec((1, VAL), lambda i: (0, 0)),
            pl.BlockSpec((8, LANES), lambda i: (0, 0)),
        ],
        out_shape=[
            out(width, BF16), out(1536, BF16), out(LANES, BF16),
            jax.ShapeDtypeStruct((4, CONV_CH), F32),
            jax.ShapeDtypeStruct((1, VAL), F32),
            jax.ShapeDtypeStruct((8, LANES), F32),
        ],
        scratch_shapes=[
            pltpu.VMEM((CHUNK + 8, CONV_CH), F32),
            pltpu.VMEM((CHUNK + 8, CONV_CH), F32),
            pltpu.VMEM((KEY, VAL), F32),
        ],
        compiler_params=pltpu.CompilerParams(
            dimension_semantics=("arbitrary",), vmem_limit_bytes=56 * 1024 * 1024
        ),
        name="mixer_backward",
    )(scalars, g, pack, pack, pack, taps, gain, proj, proj, gate_in, rates, inverse, fresh, o, states)


def norm_rows(values, gain_row):
    return values * lax.rsqrt(jnp.mean(values * values, axis=-1, keepdims=True) + 1e-06) * gain_row


def swiglu_rows(paired):
    gate_part, up_part = jnp.split(paired, 2, axis=1)
    return jax.nn.silu(gate_part) * up_part


def gather_rows(values):
    return lax.all_gather(values, "tensor", axis=0, tiled=True)


def scatter_sum(partial):
    return lax.psum_scatter(partial, "tensor", scatter_dimension=0, tiled=True).astype(F32)


def dot32(a, b, dims):
    return lax.dot_general(a, b, dims, preferred_element_type=F32)


def shards(
    tokens, lengths, order, norm_mix, w_query, w_key, w_value, w_gate, w_decay, conv_filter,
    log_rate, step_bias, norm_heads, w_out, norm_ffn, w_ffn_gate, w_ffn_up, w_ffn_down, cotangent,
):
    layer_count = w_query.shape[0]
    heads_total = log_rate.shape[1]
    device_part = lax.axis_index("tensor")
    dp_place = lax.axis_index("dp")
    rows_local, slots_local, width = tokens.shape
    assert slots_local == 1 and w_decay.shape[2] == 1
    slot_total = order.shape[0]
    units = w_ffn_gate.shape[2]
    rows_part = w_query.shape[1]

    packs = []
    for layer in range(layer_count):
        aux = jnp.concatenate([w_decay[layer, :, 0, :], conv_filter[layer, :, 0, :].T], axis=1)
        aux = jnp.pad(aux, ((0, 0), (0, LANES - aux.shape[1])))
        mix = jnp.concatenate(
            [w_query[layer], w_key[layer], w_value[layer], w_gate[layer], w_out[layer].T, aux], axis=1
        )
        ffn = jnp.concatenate([w_ffn_gate[layer], w_ffn_up[layer], w_ffn_down[layer].T], axis=1)
        packs.append(
            (
                lax.all_gather(mix, "dp", axis=0, tiled=True),
                lax.all_gather(ffn, "dp", axis=0, tiled=True),
            )
        )

    spread_in = lax.all_to_all(tokens, "dp", split_axis=2, concat_axis=1, tiled=True)
    picked = jnp.take(spread_in, order, axis=1)
    dealt = lax.all_to_all(picked, "dp", split_axis=1, concat_axis=2, tiled=True)
    residual = dealt[:, 0, :].astype(F32)

    saved = []
    for layer in range(layer_count):
        mix, ffn = packs[layer]
        taps = mix[:, 2050:2054].T.astype(F32)
        gain_heads = norm_heads[layer].astype(F32)[None]
        scalars = jnp.concatenate(
            [
                jnp.exp(lax.dynamic_slice_in_dim(log_rate[layer].astype(F32), device_part, 1)),
                lax.dynamic_slice_in_dim(step_bias[layer].astype(F32), device_part, 1),
            ]
        )
        normed, norm_back = jax.vjp(norm_rows, residual, norm_mix[layer].astype(F32))
        rows_in = gather_rows(normed.astype(BF16))
        part, heads, *kept = mixer_forward(rows_in, mix, taps, gain_heads, scalars)
        residual = residual + scatter_sum(part)
        normed_ffn, ffn_norm_back = jax.vjp(norm_rows, residual, norm_ffn[layer].astype(F32))
        rows_ffn = gather_rows(normed_ffn.astype(BF16))
        paired = dot32(rows_ffn, ffn[:, : 2 * units], NN)
        hidden, swiglu_back = jax.vjp(swiglu_rows, paired)
        hidden = hidden.astype(BF16)
        residual = residual + scatter_sum(dot32(hidden, ffn[:, 2 * units :], NT).astype(BF16))
        saved.append(
            (norm_back, rows_in, taps, gain_heads, scalars, kept, heads, ffn_norm_back, rows_ffn,
             swiglu_back, hidden)
        )

    my_length = lengths[order[dp_place]]
    positions = device_part * rows_local + jnp.arange(rows_local)
    gradient = cotangent[:, 0, :].astype(F32) * (positions < my_length).astype(F32)[:, None]
    weight_grads = [None] * layer_count
    small_terms = [None] * layer_count
    for layer in reversed(range(layer_count)):
        mix, ffn = packs[layer]
        (norm_back, rows_in, taps, gain_heads, scalars, kept, heads, ffn_norm_back, rows_ffn,
         swiglu_back, hidden) = saved[layer]
        grad_rows = gather_rows(gradient.astype(BF16))
        (grad_paired,) = swiglu_back(dot32(grad_rows, ffn[:, 2 * units :], NN))
        paired_low = grad_paired.astype(BF16)
        grad_normed = scatter_sum(dot32(paired_low, ffn[:, : 2 * units], NT).astype(BF16))
        ffn_grads = jnp.concatenate(
            [dot32(rows_ffn, paired_low, TN).astype(BF16), dot32(grad_rows, hidden, TN).astype(BF16)],
            axis=1,
        )
        ffn_grads = lax.psum_scatter(ffn_grads, "dp", scatter_dimension=0, tiled=True)
        grad_residual, grad_gain_ffn = ffn_norm_back(grad_normed)
        gradient = gradient + grad_residual
        grad_rows = gather_rows(gradient.astype(BF16))
        part, dproj, drates, dtaps, dgain, dscalars = mixer_backward(
            grad_rows, mix, taps, gain_heads, scalars, kept
        )
        grad_normed = scatter_sum(part)
        aux = dot32(rows_in, drates, TN) + jnp.pad(dtaps.T, ((0, 0), (2, LANES - 6)))
        mix_grads = jnp.concatenate(
            [
                dot32(rows_in, dproj, TN).astype(BF16),
                dot32(grad_rows, heads, TN).astype(BF16),
                aux.astype(BF16),
            ],
            axis=1,
        )
        mix_grads = lax.psum_scatter(mix_grads, "dp", scatter_dimension=0, tiled=True)
        grad_residual, grad_gain_mix = norm_back(grad_normed)
        gradient = gradient + grad_residual
        weight_grads[layer] = (
            mix_grads[:, :256].astype(F32),
            mix_grads[:, 256:512].astype(F32),
            mix_grads[:, 512:1024].astype(F32),
            mix_grads[:, 1024:1536].astype(F32),
            mix_grads[:, 2048:2050].astype(F32).reshape(rows_part, 1, 2),
            mix_grads[:, 2050:2054].astype(F32).T.reshape(4, 1, rows_part),
            mix_grads[:, 1536:2048].astype(F32).T,
            ffn_grads[:, :units].astype(F32),
            ffn_grads[:, units : 2 * units].astype(F32),
            ffn_grads[:, 2 * units :].astype(F32).T,
        )
        mine = (jnp.arange(heads_total) == device_part).astype(F32)
        small_terms[layer] = jnp.concatenate(
            [grad_gain_mix, grad_gain_ffn, dgain[0], mine * dscalars[0, 0], mine * dscalars[1, 0]]
        )
    small = lax.psum(jnp.stack(small_terms), ("dp", "tensor"))
    spread_back = lax.all_to_all(
        gradient.astype(BF16)[:, None, :], "dp", split_axis=2, concat_axis=1, tiled=True
    )
    inverse_order = (
        jnp.zeros((slot_total,), jnp.int32).at[order].set(jnp.arange(slot_total, dtype=jnp.int32))
    )
    homed = jnp.take(spread_back, inverse_order, axis=1)
    grad_home = lax.all_to_all(homed, "dp", split_axis=1, concat_axis=2, tiled=True).astype(F32)
    members = [jnp.stack([grads[m] for grads in weight_grads]) for m in range(10)]
    ends = 2 * width + VAL
    return (
        residual.astype(BF16)[:, None, :],
        grad_home,
        small[:, :width],
        members[0], members[1], members[2], members[3], members[4], members[5],
        small[:, ends : ends + heads_total],
        small[:, ends + heads_total :],
        small[:, 2 * width : ends],
        members[6],
        small[:, width : 2 * width],
        members[7], members[8], members[9],
    )


def solution(mesh):
    return jax.shard_map(
        shards,
        mesh=mesh,
        in_specs=(
            P("tensor", "dp", None), P(), P(), P(),
            P(None, "dp", "tensor"), P(None, "dp", "tensor"), P(None, "dp", "tensor"),
            P(None, "dp", "tensor"), P(None, "dp", "tensor", None), P(None, None, "tensor", "dp"),
            P(), P(), P(), P(None, "tensor", "dp"), P(),
            P(None, "dp", "tensor"), P(None, "dp", "tensor"), P(None, "tensor", "dp"),
            P("tensor", "dp", None),
        ),
        out_specs=(
            P("tensor", "dp", None), P("tensor", "dp", None), P(),
            P(None, "dp", "tensor"), P(None, "dp", "tensor"), P(None, "dp", "tensor"),
            P(None, "dp", "tensor"), P(None, "dp", "tensor", None), P(None, None, "tensor", "dp"),
            P(), P(), P(), P(None, "tensor", "dp"), P(),
            P(None, "dp", "tensor"), P(None, "dp", "tensor"), P(None, "tensor", "dp"),
        ),
        check_vma=False,
    )
```

time: 3150 us -> 1330 us (0.42)
  matrix products: 705 us -> 85.9 us
  other arithmetic: 628 us -> 65 us
  waiting for transfers between devices: 1220 us -> 903 us
  local copies, waits for them, and re-layouts: 326 us -> 63.7 us
  Pallas kernels: 0 us -> 117 us
  loops' own time: 94 us -> 0 us
  blocking collectives: 115 us -> 47.3 us
    dot_general x760 -> x18, matrix products: 567 us -> 85.9 us  [dot32(): return lax.dot_general(a, b, dims, preferred_element_type=F32)]
    another operation x212 -> x11, other arithmetic: 337 us -> 4.56 us  [the longest x10 4.54 us: shards(): jnp.stack([grads[m] for grads in weight_grads])]
    reduce_scatter x24 -> x12, waiting for transfers between devices: 739 us -> 451 us  [the longest x8 334 us: scatter_sum(): lax.psum_scatter(partial, 'tensor', scatter_dimension=0, tiled=True)]
    all_gather x16 -> x4, waiting for transfers between devices: 270 us -> 105 us  [the longest x2 69.1 us: shards(): lax.all_gather(ffn, 'dp', axis=0, tiled=True)]
    all_gather x4 -> x8, waiting for transfers between devices: 157 us -> 311 us  [gather_rows(): return lax.all_gather(values, 'tensor', axis=0, tiled=True)]
    another operation x256 -> x0, matrix products: 137 us -> none  [the longest x128 85.6 us: block_step(): jax.scipy.linalg.solve_triangular(unit_lower, write_rate[:, None] * value...]
    pallas_call x0 -> x4, Pallas kernels: none -> 117 us  [the longest x2 62.4 us: mixer_forward(): pl.pallas_call(forward_kernel, grid=(chunks,), in_specs=[pl.BlockSpec(mem...]
    reduce_sum x138 -> x0, other arithmetic: 98.7 us -> none  [the longest x32 40.3 us: block_step(): final_decay - log_decay]
  transfers between devices with their start and end apart: 52 -> 28, of which waited for: 36 -> 26; matrix products, arithmetic and copies ran while one was open for 37% -> 11% of each run, Pallas kernels for 0% -> 2%
where the time goes in v1:
time: 1330 us; the launch traced here: 1320 us
  waiting for transfers between devices  903 us (68%)
  Pallas kernels  117 us (9%)
  matrix products  85.9 us (6%)
  other arithmetic  65 us (5%)
  local copies, waits for them, and re-layouts  63.7 us (5%)
  blocking collectives  47.3 us (4%)
  starting transfers between devices  18.3 us (1%)
  between operations  17.8 us (1%)
    reduce_scatter x8, waiting for transfers between devices, scatter_sum(): lax.psum_scatter(partial, 'tensor', scatter_dimension=0, tiled=True)  334 us
    all_gather x8, waiting for transfers between devices, gather_rows(): return lax.all_gather(values, 'tensor', axis=0, tiled=True)  311 us
    dot_general x18, matrix products, dot32(): return lax.dot_general(a, b, dims, preferred_element_type=F32)  85.9 us
    all_gather x2, waiting for transfers between devices, shards(): lax.all_gather(ffn, 'dp', axis=0, tiled=True)  69.1 us
    reduce_scatter x2, waiting for transfers between devices, shards(): lax.psum_scatter(ffn_grads, 'dp', scatter_dimension=0, tiled=True)  65.3 us
    pallas_call x2, Pallas kernels, mixer_forward(): pl.pallas_call(forward_kernel, grid=(chunks,), in_specs=[pl.BlockSpec(mem...  62.4 us
    pallas_call x2, Pallas kernels, mixer_backward(): pl.pallas_call(backward_kernel, grid=(chunks,), in_specs=[pl.BlockSpec(me...  54.4 us
    reduce_scatter x2, waiting for transfers between devices, shards(): lax.psum_scatter(mix_grads, 'dp', scatter_dimension=0, tiled=True)  52.2 us
  transfers between devices with their start and end apart: 28, of which 26 were waited for; matrix products, arithmetic and copies ran while one was open for 11% of the time, Pallas kernels for 2%

profile of v1, /device:TPU:0, one launch (start us, length us, event | category | flops | bytes accessed | tf_op | source)
XLA Modules:
  0.0 1318.1 jit_solution(13048852877741211031)
XLA Ops:
  14.6 3.8 reduce.3
  19.3 5.2 all-to-all-start
  24.5 14.3 %all-to-all-done = bf16[8,2,16384]{2,1,0:T(2,128)(2,1)S(1)} async-done(((bf16[8,2,16384]{2,1,0:T(2,128)(2,1)}), bf16[8,2,16384]{2,1,0:T(2,128)(2,1)S(1)}, u32[]{:S(2)}, u32[]{:S(2)}) %all-to-all-start) | async-done | bytes 524320 | tf_op jit(solution)/shard_map/all_to_all | solution.py:410
  44.9 15.5 %all-to-all-done.1 = bf16[256,8,128]{2,0,1:T(8,128)(2,1)S(1)} async-done(((bf16[256,8,128]{2,0,1:T(8,128)(2,1)}), bf16[256,8,128]{2,0,1:T(8,128)(2,1)S(1)}, u32[]{:S(2)}, u32[]{:S(2)}) %all-to-all-start.1) | async-done | bytes 524320 | tf_op jit(solution)/shard_map/all_to_all | solution.py:412
  65.9 6.5 copy.250.w_in_ref.w_aux_ref.w_out_ref
  73.7 40.3 %all-gather.13.cloned.1.call-done.x_ref = bf16[1024,1024]{1,0:T(8,128)(2,1)} async-done(((bf16[256,1024]{1,0:T(8,128)(2,1)}), bf16[1024,1024]{1,0:T(8,128)(2,1)}) %all-gather.13.cloned.1.call-update) | async-done | bytes 2097168 | tf_op jit(solution)/shard_map/all_gather | solution.py:370
  114.0 31.2 %mixer_forward.2 = (bf16[1024,1024]{1,0:T(8,128)(2,1)}, bf16[1024,512]{1,0:T(8,128)(2,1)}, f32[1024,1024]{1,0:T(8,128)}, f32[1024,512]{1,0:T(8,128)}, f32[1024,1...) custom-call(f32[2]{0:T(128)} %pad_maximum_fusion.13.scalars_ref, ...), custom_call_target="tpu_custom_call" | custom-call | tf_op jit(solution)/shard_map/mixer_forward/pallas_call | solution.py:156
  147.3 40.7 %reduce-scatter.13.cloned.1.call-done = bf16[256,1024]{1,0:T(8,128)(2,1)} async-done(((bf16[1024,1024]{1,0:T(8,128)(2,1)}), bf16[256,1024]{1,0:T(8,128)(2,1)}) %reduce-scatter.13.cloned.1.call-update) | async-done | bytes 524304 | tf_op jit(solution)/shard_map/reduce_scatter | solution.py:374
  190.3 37.5 %all-gather.19.cloned.1.call-done = bf16[1024,2112]{0,1:T(8,128)(2,1)} async-done(((bf16[128,2112]{0,1:T(8,128)(2,1)}), bf16[1024,2112]{0,1:T(8,128)(2,1)}) %all-gather.19.cloned.1.call-update) | async-done | bytes 4325392 | tf_op jit(solution)/shard_map/all_gather | solution.py:406
  227.8 48.0 %all-gather.17.cloned.1.call-done = bf16[1024,1024]{1,0:T(8,128)(2,1)} async-done(((bf16[256,1024]{1,0:T(8,128)(2,1)}), bf16[1024,1024]{1,0:T(8,128)(2,1)}) %all-gather.17.cloned.1.call-update) | async-done | bytes 2097168 | tf_op jit(solution)/shard_map/all_gather | solution.py:370
  275.9 5.9 fusion.14
  285.5 4.5 convolution_convert_fusion.5
  290.9 41.8 %reduce-scatter.15.cloned.1.call-done = bf16[256,1024]{1,0:T(8,128)(2,1)} async-done(((bf16[1024,1024]{1,0:T(8,128)(2,1)}), bf16[256,1024]{1,0:T(8,128)(2,1)}) %reduce-scatter.15.cloned.1.call-update) | async-done | bytes 524304 | tf_op jit(solution)/shard_map/reduce_scatter | solution.py:374
  337.9 35.2 %all-gather.23.cloned.1.call-done = bf16[1024,2176]{0,1:T(8,128)(2,1)} async-done(((bf16[128,2176]{0,1:T(8,128)(2,1)}), bf16[1024,2176]{0,1:T(8,128)(2,1)}) %all-gather.23.cloned.1.call-update) | async-done | bytes 4456464 | tf_op jit(solution)/shard_map/all_gather | solution.py:405
  373.1 6.5 copy.257.w_in_ref.w_aux_ref.w_out_ref
  380.9 40.3 %all-gather.21.cloned.1.call-done.x_ref = bf16[1024,1024]{1,0:T(8,128)(2,1)} async-done(((bf16[256,1024]{1,0:T(8,128)(2,1)}), bf16[1024,1024]{1,0:T(8,128)(2,1)}) %all-gather.21.cloned.1.call-update) | async-done | bytes 2097168 | tf_op jit(solution)/shard_map/all_gather | solution.py:370
  421.2 31.2 %mixer_forward.3 = (bf16[1024,1024]{1,0:T(8,128)(2,1)}, bf16[1024,512]{1,0:T(8,128)(2,1)}, f32[1024,1024]{1,0:T(8,128)}, f32[1024,512]{1,0:T(8,128)}, f32[1024,1...) custom-call(f32[2]{0:T(128)} %pad_maximum_fusion.14.scalars_ref, ...), custom_call_target="tpu_custom_call" | custom-call | tf_op jit(solution)/shard_map/mixer_forward/pallas_call | solution.py:156
  453.6 41.5 %reduce-scatter.17.cloned.1.call-done = bf16[256,1024]{1,0:T(8,128)(2,1)} async-done(((bf16[1024,1024]{1,0:T(8,128)(2,1)}), bf16[256,1024]{1,0:T(8,128)(2,1)}) %reduce-scatter.17.cloned.1.call-update) | async-done | bytes 524304 | tf_op jit(solution)/shard_map/reduce_scatter | solution.py:374
  503.4 31.6 %all-gather.27.cloned.1.call-done = bf16[1024,2112]{0,1:T(8,128)(2,1)} async-done(((bf16[128,2112]{0,1:T(8,128)(2,1)}), bf16[1024,2112]{0,1:T(8,128)(2,1)}) %all-gather.27.cloned.1.call-update) | async-done | bytes 4325392 | tf_op jit(solution)/shard_map/all_gather | solution.py:406
  535.0 48.2 %all-gather.25.cloned.1.call-done = bf16[1024,1024]{1,0:T(8,128)(2,1)} async-done(((bf16[256,1024]{1,0:T(8,128)(2,1)}), bf16[1024,1024]{1,0:T(8,128)(2,1)}) %all-gather.25.cloned.1.call-update) | async-done | bytes 2097168 | tf_op jit(solution)/shard_map/all_gather | solution.py:370
  583.2 8.3 fusion.10
  591.5 38.4 %all-gather.29.cloned.1.call-done = bf16[1024,1024]{1,0:T(8,128)(2,1)} async-done(((bf16[256,1024]{1,0:T(8,128)(2,1)}), bf16[1024,1024]{1,0:T(8,128)(2,1)}) %all-gather.29.cloned.1.call-update) | async-done | bytes 2097168 | tf_op jit(solution)/shard_map/all_gather | solution.py:370
  630.0 7.7 fusion.2
  639.4 4.8 fusion.19
  644.2 4.9 convolution_convert_fusion.4
  649.2 37.7 %reduce-scatter.21.cloned.1.call-done = bf16[256,1024]{1,0:T(8,128)(2,1)} async-done(((bf16[1024,1024]{1,0:T(8,128)(2,1)}), bf16[256,1024]{1,0:T(8,128)(2,1)}) %reduce-scatter.21.cloned.1.call-update) | async-done | bytes 524304 | tf_op jit(solution)/shard_map/reduce_scatter | solution.py:374
  688.3 44.0 %reduce-scatter.19.cloned.1.call-done = bf16[256,1024]{1,0:T(8,128)(2,1)} async-done(((bf16[1024,1024]{1,0:T(8,128)(2,1)}), bf16[256,1024]{1,0:T(8,128)(2,1)}) %reduce-scatter.19.cloned.1.call-update) | async-done | bytes 524304 | tf_op jit(solution)/shard_map/reduce_scatter | solution.py:374
  735.9 45.0 %all-gather.31.cloned.1.call-done.g_ref = bf16[1024,1024]{1,0:T(8,128)(2,1)} async-done(((bf16[256,1024]{1,0:T(8,128)(2,1)}), bf16[1024,1024]{1,0:T(8,128)(2,1)}) %all-gather.31.cloned.1.call-update) | async-done | bytes 2097168 | tf_op jit(solution)/shard_map/all_gather | solution.py:370
  780.8 27.2 %mixer_backward.2 = (bf16[1024,1024]{1,0:T(8,128)(2,1)}, bf16[1024,1536]{1,0:T(8,128)(2,1)}, bf16[1024,128]{1,0:T(8,128)(2,1)}, f32[4,1024]{1,0:T(4,128)}, f32[1,512]{1,0:T(1,128)}, /*index=5*/f32[8,128]{1,0:T(8,128)}) custom-call(f32[2]{0:T(128)} %pad_maximum_fusion.14.scalars_ref, bf16[1024,1024]{1,0:T(8,128)(2,1)} %all-gather.31.cloned.1.call-done.g_ref, ...), custom_call_target="tpu_custom_call" | custom-call | tf_op jit(solution)/shard_map/mixer_backward/pallas_call | solution.py:320
  808.1 42.7 %reduce-scatter.23.cloned.1.call-done = bf16[256,1024]{1,0:T(8,128)(2,1)} async-done(((bf16[1024,1024]{1,0:T(8,128)(2,1)}), bf16[256,1024]{1,0:T(8,128)(2,1)}) %reduce-scatter.23.cloned.1.call-update) | async-done | bytes 524304 | tf_op jit(solution)/shard_map/reduce_scatter | solution.py:374
  854.5 45.4 %all-gather.33.cloned.1.call-done = bf16[1024,1024]{1,0:T(8,128)(2,1)} async-done(((bf16[256,1024]{1,0:T(8,128)(2,1)}), bf16[1024,1024]{1,0:T(8,128)(2,1)}) %all-gather.33.cloned.1.call-update) | async-done | bytes 2097168 | tf_op jit(solution)/shard_map/all_gather | solution.py:370
  899.9 6.6 fusion.5
  908.2 6.5 fusion.16
  914.7 42.7 %reduce-scatter.25.cloned.1.call-done = bf16[256,1024]{1,0:T(8,128)(2,1)} async-done(((bf16[1024,1024]{1,0:T(8,128)(2,1)}), bf16[256,1024]{1,0:T(8,128)(2,1)}) %reduce-scatter.25.cloned.1.call-update) | async-done | bytes 524304 | tf_op jit(solution)/shard_map/reduce_scatter | solution.py:374
  962.6 3.7 convolution_convert_fusion.6
  967.0 6.3 convolution_convert_fusion
  981.8 3.8 convolution_convert_fusion.2
  993.4 6.0 convolution_convert_fusion.1
  1001.9 5.9 all-gather.35.cloned.1.call-done.g_ref
  1007.8 27.2 %mixer_backward.3 = (bf16[1024,1024]{1,0:T(8,128)(2,1)}, bf16[1024,1536]{1,0:T(8,128)(2,1)}, bf16[1024,128]{1,0:T(8,128)(2,1)}, f32[4,1024]{1,0:T(4,128)}, f32[1,512]{1,0:T(1,128)}, /*index=5*/f32[8,128]{1,0:T(8,128)}) custom-call(f32[2]{0:T(128)} %pad_maximum_fusion.13.scalars_ref, bf16[1024,1024]{1,0:T(8,128)(2,1)} %all-gather.35.cloned.1.call-done.g_ref, ...), custom_call_target="tpu_custom_call" | custom-call | tf_op jit(solution)/shard_map/mixer_backward/pallas_call | solution.py:320
  1040.8 3.8 convolution_convert_fusion.3
  1048.6 14.2 %reduce-scatter.35.cloned.1.call-done = bf16[128,2112]{1,0:T(8,128)(2,1)} async-done(((bf16[1024,2112]{1,0:T(8,128)(2,1)}), bf16[128,2112]{1,0:T(8,128)(2,1)}) %reduce-scatter.35.cloned.1.call-update) | async-done | bytes 540688 | tf_op jit(solution)/shard_map/reduce_scatter | solution.py:458
  1066.8 52.2 %reduce-scatter.31.cloned.1.call-done = bf16[128,2176]{1,0:T(8,128)(2,1)} async-done(((bf16[1024,2176]{1,0:T(8,128)(2,1)}), bf16[128,2176]{1,0:T(8,128)(2,1)}) %reduce-scatter.31.cloned.1.call-update) | async-done | bytes 557072 | tf_op jit(solution)/shard_map/reduce_scatter | solution.py:475
  1124.5 51.1 %reduce-scatter.33.cloned.1.call-done = bf16[128,2112]{1,0:T(8,128)(2,1)} async-done(((bf16[1024,2112]{1,0:T(8,128)(2,1)}), bf16[128,2112]{1,0:T(8,128)(2,1)}) %reduce-scatter.33.cloned.1.call-update) | async-done | bytes 540688 | tf_op jit(solution)/shard_map/reduce_scatter | solution.py:458
  1179.2 42.5 %reduce-scatter.27.cloned.1.call-done = bf16[256,1024]{1,0:T(8,128)(2,1)} async-done(((bf16[1024,1024]{1,0:T(8,128)(2,1)}), bf16[256,1024]{1,0:T(8,128)(2,1)}) %reduce-scatter.27.cloned.1.call-update) | async-done | bytes 524304 | tf_op jit(solution)/shard_map/reduce_scatter | solution.py:374
  1226.2 3.8 reduce.4
  1238.5 5.8 all-to-all-done.2
  1250.4 47.3 %psum.7 = f32[2,2568]{1,0:T(2,128)S(1)} all-reduce(f32[2,2568]{1,0:T(2,128)S(1)} %pad_maximum_fusion.12), channel_id=1, replica_groups=mesh['dp'=8,'tensor'=4] {'dp','tensor'}, use_global_device_ids=true, to_apply=%region_21.23 | all-reduce | flops 5136 | bytes 41088 | tf_op jit(solution)/shard_map/psum | solution.py:494
  (292 shorter events, 135.1 us)
Async XLA Ops:
  7.2 58.6 %all-gather.15.cloned.1.call-start = ((), (), s32[]{:S(2)}) async-start(), calls=%async_computation.17 | async-start | bytes 5013504 | tf_op jit(solution)/shard_map/all_gather | solution.py:405
  12.4 12.1 copy-start.39
  19.3 19.5 %all-to-all-start = ((bf16[8,2,16384]{2,1,0:T(2,128)(2,1)}), bf16[8,2,16384]{2,1,0:T(2,128)(2,1)S(1)}, u32[]{:S(2)}, u32[]{:S(2)}) async-start(bf16[8,2,16384]{2,1,0:T(2,128)(2,1)} %reshape.205), calls=%async_computation | async-start | bytes 1048576 | tf_op jit(solution)/shard_map/all_to_all | solution.py:410
  39.7 22.0 %copy-start.30 = (bf16[2,4]{1,0:T(2,128)(2,1)S(1)}, bf16[2,4]{1,0:T(2,128)(2,1)}, u32[]{:S(2)}) copy-start(bf16[2,4]{1,0:T(2,128)(2,1)} %param.31) | copy-start | bytes 52
  39.7 22.6 %copy-start.31 = (bf16[2,4]{1,0:T(2,128)(2,1)S(1)}, bf16[2,4]{1,0:T(2,128)(2,1)}, u32[]{:S(2)}) copy-start(bf16[2,4]{1,0:T(2,128)(2,1)} %param.32) | copy-start | bytes 52
  39.7 25.1 %copy-start.24 = (bf16[2,512]{1,0:T(2,128)(2,1)S(1)}, bf16[2,512]{1,0:T(2,128)(2,1)}, u32[]{:S(2)}) copy-start(bf16[2,512]{1,0:T(2,128)(2,1)} %param.33) | copy-start | bytes 6148
  41.3 19.2 %all-to-all-start.1 = ((bf16[256,8,128]{2,0,1:T(8,128)(2,1)}), bf16[256,8,128]{2,0,1:T(8,128)(2,1)S(1)}, u32[]{:S(2)}, u32[]{:S(2)}) async-start(bf16[256,8,128]{2,0,1:T(8,128)(2,1)} %select_bitcast_fusion.1), calls=%async_computation.1 | async-start | bytes 1048576 | tf_op jit(solution)/shard_map/all_to_all | solution.py:412
  44.8 69.2 %all-gather.13.cloned.1.call-start = ((), (), s32[]{:S(2)}) async-start(), calls=%async_computation.16 | async-start | bytes 2621440 | tf_op jit(solution)/shard_map/all_gather | solution.py:370
  60.6 11.8 copy-start.23
  60.6 11.8 copy-start.22
  61.6 126.4 %reduce-scatter.13.cloned.1.call-start = ((), (), s32[]{:S(2)}) async-start(), calls=%async_computation.18 | async-start | bytes 2621440 | tf_op jit(solution)/shard_map/reduce_scatter | solution.py:374
  114.0 31.5 %copy-start.13 = (bf16[2,704,128]{2,1,0:T(8,128)(2,1)S(1)}, bf16[2,704,128]{2,1,0:T(8,128)(2,1)}, u32[]{:S(2)}) copy-start(bf16[2,704,128]{2,1,0:T(8,128)(2,1)} %param.38) | copy-start | bytes 1081348
  145.3 82.6 %all-gather.19.cloned.1.call-start = ((), (), s32[]{:S(2)}) async-start(), calls=%async_computation.20 | async-start | bytes 4866048 | tf_op jit(solution)/shard_map/all_gather | solution.py:406
  147.2 128.7 %all-gather.17.cloned.1.call-start = ((), (), s32[]{:S(2)}) async-start(), calls=%async_computation.19 | async-start | bytes 2621440 | tf_op jit(solution)/shard_map/all_gather | solution.py:370
  190.3 142.4 %reduce-scatter.15.cloned.1.call-start = ((), (), s32[]{:S(2)}) async-start(), calls=%async_computation.21 | async-start | bytes 2621440 | tf_op jit(solution)/shard_map/reduce_scatter | solution.py:374
  290.0 83.1 %all-gather.23.cloned.1.call-start = ((), (), s32[]{:S(2)}) async-start(), calls=%async_computation.23 | async-start | bytes 5013504 | tf_op jit(solution)/shard_map/all_gather | solution.py:405
  290.9 130.3 %all-gather.21.cloned.1.call-start = ((), (), s32[]{:S(2)}) async-start(), calls=%async_computation.22 | async-start | bytes 2621440 | tf_op jit(solution)/shard_map/all_gather | solution.py:370
  336.0 159.2 %reduce-scatter.17.cloned.1.call-start = ((), (), s32[]{:S(2)}) async-start(), calls=%async_computation.24 | async-start | bytes 2621440 | tf_op jit(solution)/shard_map/reduce_scatter | solution.py:374
  452.4 42.8 %copy-start = (bf16[256,1024]{1,0:T(8,128)(2,1)S(1)}, bf16[256,1024]{1,0:T(8,128)(2,1)}, u32[]{:S(2)}) copy-start(bf16[256,1024]{1,0:T(8,128)(2,1)} %reduce-scatter.15.cloned.1.call-done) | copy-start | bytes 1572868
  452.5 82.6 %all-gather.27.cloned.1.call-start = ((), (), s32[]{:S(2)}) async-start(), calls=%async_computation.26 | async-start | bytes 4866048 | tf_op jit(solution)/shard_map/all_gather | solution.py:406
  453.3 46.7 %copy-start.40 = (s32[8]{0:T(128)S(1)}, s32[8]{0:T(128)}, u32[]{:S(2)}) copy-start(s32[8]{0:T(128)} %param.22) | copy-start | bytes 100
  453.4 129.8 %all-gather.25.cloned.1.call-start = ((), (), s32[]{:S(2)}) async-start(), calls=%async_computation.25 | async-start | bytes 2621440 | tf_op jit(solution)/shard_map/all_gather | solution.py:370
  497.5 132.5 %all-gather.29.cloned.1.call-start = ((), (), s32[]{:S(2)}) async-start(), calls=%async_computation.28 | async-start | bytes 2621440 | tf_op jit(solution)/shard_map/all_gather | solution.py:370
  503.3 183.6 %reduce-scatter.21.cloned.1.call-start = ((), (), s32[]{:S(2)}) async-start(), calls=%async_computation.29 | async-start | bytes 2621440 | tf_op jit(solution)/shard_map/reduce_scatter | solution.py:374
  630.0 9.4 copy-start.34
  644.2 88.1 %reduce-scatter.19.cloned.1.call-start = ((), (), s32[]{:S(2)}) async-start(), calls=%async_computation.27 | async-start | bytes 2621440 | tf_op jit(solution)/shard_map/reduce_scatter | solution.py:374
  649.2 131.6 %all-gather.31.cloned.1.call-start = ((), (), s32[]{:S(2)}) async-start(), calls=%async_computation.30 | async-start | bytes 2621440 | tf_op jit(solution)/shard_map/all_gather | solution.py:370
  735.4 115.4 %reduce-scatter.23.cloned.1.call-start = ((), (), s32[]{:S(2)}) async-start(), calls=%async_computation.31 | async-start | bytes 2621440 | tf_op jit(solution)/shard_map/reduce_scatter | solution.py:374
  808.0 44.3 %copy-start.1 = (f32[256,1024]{1,0:T(8,128)S(1)}, f32[256,1024]{1,0:T(8,128)}, u32[]{:S(2)}) copy-start(f32[256,1024]{1,0:T(8,128)} %get-tuple-element.191) | copy-start | bytes 3145732
  808.1 91.9 %all-gather.33.cloned.1.call-start = ((), (), s32[]{:S(2)}) async-start(), calls=%async_computation.32 | async-start | bytes 2621440 | tf_op jit(solution)/shard_map/all_gather | solution.py:370
  854.5 102.9 %reduce-scatter.25.cloned.1.call-start = ((), (), s32[]{:S(2)}) async-start(), calls=%async_computation.33 | async-start | bytes 2621440 | tf_op jit(solution)/shard_map/reduce_scatter | solution.py:374
  914.7 93.1 %all-gather.35.cloned.1.call-start = ((), (), s32[]{:S(2)}) async-start(), calls=%async_computation.34 | async-start | bytes 2621440 | tf_op jit(solution)/shard_map/all_gather | solution.py:370
  962.3 100.5 %reduce-scatter.35.cloned.1.call-start = ((), (), s32[]{:S(2)}) async-start(), calls=%async_computation.39 | async-start | bytes 5013504 | tf_op jit(solution)/shard_map/reduce_scatter | solution.py:458
  975.8 143.3 %reduce-scatter.31.cloned.1.call-start = ((), (), s32[]{:S(2)}) async-start(), calls=%async_computation.37 | async-start | bytes 5013504 | tf_op jit(solution)/shard_map/reduce_scatter | solution.py:475
  988.0 187.6 %reduce-scatter.33.cloned.1.call-start = ((), (), s32[]{:S(2)}) async-start(), calls=%async_computation.38 | async-start | bytes 5013504 | tf_op jit(solution)/shard_map/reduce_scatter | solution.py:458
  1001.8 219.9 %reduce-scatter.27.cloned.1.call-start = ((), (), s32[]{:S(2)}) async-start(), calls=%async_computation.35 | async-start | bytes 2621440 | tf_op jit(solution)/shard_map/reduce_scatter | solution.py:374
  1035.0 266.7 %reduce-scatter.29.cloned.1.call-start = ((), (), s32[]{:S(2)}) async-start(), calls=%async_computation.36 | async-start | bytes 5013504 | tf_op jit(solution)/shard_map/reduce_scatter | solution.py:475
  1046.9 19.9 %copy-start.27 = (f32[1,512]{1,0:T(1,128)S(1)}, f32[1,512]{1,0:T(1,128)}, u32[]{:S(2)}) copy-start(f32[1,512]{1,0:T(1,128)} %get-tuple-element.68) | copy-start | bytes 6148
  1176.9 47.0 %copy-start.3 = (f32[256,1024]{1,0:T(8,128)S(1)}, f32[256,1024]{1,0:T(8,128)}, u32[]{:S(2)}) copy-start(f32[256,1024]{1,0:T(8,128)} %get-tuple-element.189) | copy-start | bytes 3145732
  1226.2 12.2 copy-start.19
  1226.2 12.2 copy-start.28
  1230.9 13.4 %all-to-all-start.2 = ((bf16[8,2,16384]{2,1,0:T(2,128)(2,1)}), bf16[8,2,16384]{2,1,0:T(2,128)(2,1)S(1)}, u32[]{:S(2)}, u32[]{:S(2)}) async-start(bf16[8,2,16384]{2,1,0:T(2,128)(2,1)} %reshape.207), calls=%async_computation.10 | async-start | bytes 1048576 | tf_op jit(solution)/shard_map/all_to_all | solution.py:495
  1235.7 10.2 copy-start.33
  1246.9 52.7 %all-to-all-start.3 = ((bf16[256,8,128]{2,0,1:T(8,128)(2,1)}), bf16[256,8,128]{2,0,1:T(8,128)(2,1)S(1)}, u32[]{:S(2)}, u32[]{:S(2)}) async-start(bf16[256,8,128]{2,0,1:T(8,128)(2,1)} %select_bitcast_fusion), calls=%async_computation.11 | async-start | bytes 1048576 | tf_op jit(solution)/shard_map/all_to_all | solution.py:502
  1299.6 6.0 copy-start.25
  1299.6 6.7 copy-start.26
  1299.8 9.6 copy-start.18
  1301.7 8.4 copy-start.17
  (25 other events, 62.0 us)
Sparse Core Ops, SparseCore 0:
  13.3 52.5 all-gather.14
  68.0 45.9 all-gather.12
  145.4 42.5 reduce-scatter.12
  190.5 37.3 all-gather.18
  229.9 45.9 all-gather.16
  290.1 42.5 reduce-scatter.14
  335.2 37.8 all-gather.22
  375.2 45.9 all-gather.20
  452.6 42.5 reduce-scatter.16
  497.6 37.3 all-gather.26
  537.2 45.9 all-gather.24
  585.3 44.6 all-gather.28
  644.3 42.5 reduce-scatter.20
  689.1 43.1 reduce-scatter.18
  735.5 45.2 all-gather.30
  808.2 42.5 reduce-scatter.22
  854.6 45.2 all-gather.32
  914.8 42.5 reduce-scatter.24
  962.5 45.2 all-gather.34
  1011.5 51.3 reduce-scatter.34
  1066.3 52.6 reduce-scatter.30
  1122.9 52.6 reduce-scatter.32
  1177.9 43.8 reduce-scatter.26
  1225.5 58.1 reduce-scatter.28

commit v2 on v1

--- a/solution.py
+++ b/solution.py
@@ -3,8 +3,9 @@
 import jax.numpy as jnp
 from jax import lax
 from jax.experimental import pallas as pl
+from jax.experimental.layout import Layout, with_layout_constraint
 from jax.experimental.pallas import tpu as pltpu
-from jax.sharding import PartitionSpec as P
+from jax.sharding import Mesh, PartitionSpec as P
 
 CHUNK = 256
 LANES = 128
@@ -177,6 +178,9 @@
         scratch_shapes=[pltpu.VMEM((CHUNK + 8, CONV_CH), F32), pltpu.VMEM((KEY, VAL), F32)],
         compiler_params=pltpu.CompilerParams(
             dimension_semantics=("arbitrary",), vmem_limit_bytes=56 * 1024 * 1024
+        ),
+        cost_estimate=pl.CostEstimate(
+            flops=16 * 10**9, bytes_accessed=80 * 10**6, transcendentals=4 * 10**6
         ),
         name="mixer_forward",
     )(scalars, x, pack, pack, pack, taps, gain)
@@ -353,12 +357,296 @@
         compiler_params=pltpu.CompilerParams(
             dimension_semantics=("arbitrary",), vmem_limit_bytes=56 * 1024 * 1024
         ),
+        cost_estimate=pl.CostEstimate(
+            flops=16 * 10**9, bytes_accessed=80 * 10**6, transcendentals=4 * 10**6
+        ),
         name="mixer_backward",
     )(scalars, g, pack, pack, pack, taps, gain, proj, proj, gate_in, rates, inverse, fresh, o, states)
 
 
-def norm_rows(values, gain_row):
-    return values * lax.rsqrt(jnp.mean(values * values, axis=-1, keepdims=True) + 1e-06) * gain_row
+PIECES = 4
+AXES = ("chip", "core", "zp", "zl")
+
+
+def partners():
+    core, zl = lax.axis_index("core"), lax.axis_index("zl")
+    return core, zl, {"core": 1 - core}, {"zl": 1 - zl}
+
+
+def greet():
+    _, _, beside, across = partners()
+    barrier = pltpu.get_barrier_semaphore()
+    for device in (beside, across):
+        pl.semaphore_signal(
+            barrier, inc=1, device_id=device, device_id_type=pl.DeviceIdType.MESH
+        )
+    pl.semaphore_wait(barrier, 2)
+
+
+class Block:
+    def __init__(self, zl, core, rows):
+        self.first = (zl * 2 + core) * rows
+        self.size = rows // PIECES
+
+    def piece(self, p):
+        return pl.ds(pl.multiple_of(self.first + p * self.size, self.size), self.size)
+
+
+def remote(src, dst, send, recv, device):
+    return pltpu.make_async_remote_copy(
+        src_ref=src, dst_ref=dst, send_sem=send, recv_sem=recv,
+        device_id=device, device_id_type=pl.DeviceIdType.MESH,
+    )
+
+
+class Scatter:
+    def __init__(self, partial, beside_far, beside_own, sums, far, send, recv):
+        core, zl, beside, across = partners()
+        rows = far.shape[0]
+        self.partial, self.beside_far, self.beside_own = partial, beside_far, beside_own
+        self.sums, self.far = sums, far
+        self.size = rows // PIECES
+        self.own = Block(zl, core, rows)
+        self.away = Block(1 - zl, core, rows)
+        own_beside, away_beside = Block(zl, 1 - core, rows), Block(1 - zl, 1 - core, rows)
+        self.to_far = [
+            remote(partial.at[away_beside.piece(p)], beside_far.at[self.local(p)],
+                   send.at[0, p], recv.at[0, p], beside)
+            for p in range(PIECES)
+        ]
+        self.to_own = [
+            remote(partial.at[own_beside.piece(p)], beside_own.at[self.local(p)],
+                   send.at[1, p], recv.at[1, p], beside)
+            for p in range(PIECES)
+        ]
+        self.cross = [
+            remote(sums.at[self.local(p)], far.at[self.local(p)],
+                   send.at[2, p], recv.at[2, p], across)
+            for p in range(PIECES)
+        ]
+
+    def local(self, p):
+        return pl.ds(p * self.size, self.size)
+
+    def start(self):
+        for copy in self.to_far:
+            copy.start()
+        for copy in self.to_own:
+            copy.start()
+        for p in range(PIECES):
+            self.to_far[p].wait_recv()
+            at = self.local(p)
+            self.sums[at, :] = (
+                self.partial[self.away.piece(p), :].astype(F32) + self.beside_far[at, :].astype(F32)
+            ).astype(BF16)
+            self.cross[p].start()
+
+    def total(self, p):
+        self.to_own[p].wait_recv()
+        self.cross[p].wait_recv()
+        at = self.local(p)
+        return (
+            self.partial[self.own.piece(p), :].astype(F32)
+            + self.beside_own[at, :].astype(F32)
+            + self.far[at, :].astype(F32)
+        )
+
+    def finish(self):
+        for copies in (self.to_far, self.to_own, self.cross):
+            for copy in copies:
+                copy.wait_send()
+
+
+class Gather:
+    def __init__(self, gathered, send, recv, first):
+        core, zl, beside, across = partners()
+        rows = gathered.shape[0] // 4
+        self.gathered = gathered
+        self.own = Block(zl, core, rows)
+        other = Block(1 - zl, core, rows)
+        make = lambda block, at, device: [
+            remote(gathered.at[block.piece(p)], gathered.at[block.piece(p)],
+                   send.at[first + at, p], recv.at[first + at, p], device)
+            for p in range(PIECES)
+        ]
+        self.across = make(self.own, 0, across)
+        self.beside = make(self.own, 1, beside)
+        self.forward = make(other, 2, beside)
+
+    def put(self, p, rows):
+        self.gathered[self.own.piece(p), :] = rows
+        self.across[p].start()
+        self.beside[p].start()
+
+    def finish(self):
+        for p in range(PIECES):
+            self.across[p].wait_recv()
+            self.forward[p].start()
+        for p in range(PIECES):
+            self.beside[p].wait_recv()
+            self.forward[p].wait_recv()
+        for copies in (self.across, self.beside, self.forward):
+            for copy in copies:
+                copy.wait_send()
+
+
+def normed_of(x, gain):
+    return x * lax.rsqrt(jnp.mean(x * x, axis=1, keepdims=True) + 1e-6) * gain
+
+
+def first_kernel(x_ref, gain_ref, out_ref, send, recv):
+    greet()
+    gather = Gather(out_ref, send, recv, 0)
+    size = x_ref.shape[0] // PIECES
+    for p in range(PIECES):
+        x = x_ref[p * size : (p + 1) * size, :].astype(F32)
+        gather.put(p, normed_of(x, gain_ref[...]).astype(BF16))
+    gather.finish()
+
+
+def forward_bridge_kernel(
+    partial, x_ref, gain_ref, new_ref, out_ref, beside_far, beside_own, sums, far, send, recv
+):
+    greet()
+    scatter = Scatter(partial, beside_far, beside_own, sums, far, send, recv)
+    gather = Gather(out_ref, send, recv, 3)
+    scatter.start()
+    for p in range(PIECES):
+        at = scatter.local(p)
+        x = x_ref[at, :].astype(F32) + scatter.total(p)
+        new_ref[at, :] = x
+        gather.put(p, normed_of(x, gain_ref[...]).astype(BF16))
+    scatter.finish()
+    gather.finish()
+
+
+def norm_back(total, x, gain):
+    inv = lax.rsqrt(jnp.mean(x * x, axis=1, keepdims=True) + 1e-6)
+    unit = x * inv
+    scaled = total * gain
+    grad = inv * (scaled - unit * jnp.mean(scaled * unit, axis=1, keepdims=True))
+    return grad, jnp.sum(total * unit, axis=0, keepdims=True)
+
+
+def backward_bridge_kernel(
+    partial, x_ref, gain_ref, grad_ref, new_ref, out_ref, dgain_ref,
+    beside_far, beside_own, sums, far, send, recv
+):
+    greet()
+    scatter = Scatter(partial, beside_far, beside_own, sums, far, send, recv)
+    gather = Gather(out_ref, send, recv, 3)
+    scatter.start()
+    dgain = jnp.zeros_like(dgain_ref)
+    for p in range(PIECES):
+        at = scatter.local(p)
+        grad, part = norm_back(scatter.total(p), x_ref[at, :].astype(F32), gain_ref[...])
+        dgain = dgain + part
+        grad = grad + grad_ref[at, :].astype(F32)
+        new_ref[at, :] = grad
+        gather.put(p, grad.astype(BF16))
+    dgain_ref[...] = dgain
+    scatter.finish()
+    gather.finish()
+
+
+def forward_last_kernel(partial, x_ref, new_ref, beside_far, beside_own, sums, far, send, recv):
+    greet()
+    scatter = Scatter(partial, beside_far, beside_own, sums, far, send, recv)
+    scatter.start()
+    for p in range(PIECES):
+        at = scatter.local(p)
+        new_ref[at, :] = (x_ref[at, :] + scatter.total(p)).astype(BF16)
+    scatter.finish()
+
+
+def backward_last_kernel(
+    partial, x_ref, gain_ref, grad_ref, new_ref, dgain_ref,
+    beside_far, beside_own, sums, far, send, recv
+):
+    greet()
+    scatter = Scatter(partial, beside_far, beside_own, sums, far, send, recv)
+    scatter.start()
+    dgain = jnp.zeros_like(dgain_ref)
+    for p in range(PIECES):
+        at = scatter.local(p)
+        grad, part = norm_back(scatter.total(p), x_ref[at, :].astype(F32), gain_ref[...])
+        dgain = dgain + part
+        new_ref[at, :] = (grad + grad_ref[at, :]).astype(BF16)
+    dgain_ref[...] = dgain
+    scatter.finish()
+
+
+def comm_call(kernel, number, outs, args, scatters, gathers):
+    rows = args[1].shape[0] if scatters else args[0].shape[0]
+    width = args[0].shape[1]
+    vmem = pl.BlockSpec(memory_space=pltpu.VMEM)
+    block = lambda: pltpu.VMEM((rows, width), BF16)
+    hops = 3 * scatters + 3 * gathers
+    kinds = sum(1 << at for at, arg in enumerate(args[1:]) if arg.dtype == BF16)
+    return pl.pallas_call(
+        kernel,
+        in_specs=[vmem] * len(args),
+        out_specs=[vmem] * len(outs),
+        out_shape=[jax.ShapeDtypeStruct(shape, kind) for shape, kind in outs],
+        scratch_shapes=[block() for _ in range(4 * scatters)]
+        + [pltpu.SemaphoreType.DMA((hops, PIECES)), pltpu.SemaphoreType.DMA((hops, PIECES))],
+        compiler_params=pltpu.CompilerParams(
+            collective_id=number + 6 * min(kinds, 2), has_side_effects=True, vmem_limit_bytes=48 * 1024 * 1024
+        ),
+        cost_estimate=pl.CostEstimate(
+            flops=rows * width * 20, bytes_accessed=40 * 1024 * 1024, transcendentals=0
+        ),
+        name=kernel.__name__.replace("_kernel", ""),
+    )(*args)
+
+
+def first_gather(x, gain):
+    rows, width = x.shape
+    return comm_call(first_kernel, 0, [((4 * rows, width), BF16)], (x, gain), 0, 1)[0]
+
+
+def forward_bridge(partial, x, gain):
+    rows, width = x.shape
+    return comm_call(
+        forward_bridge_kernel, 1, [((rows, width), F32), ((4 * rows, width), BF16)],
+        (partial, x, gain), 1, 1,
+    )
+
+
+def backward_bridge(partial, x, gain, grad):
+    rows, width = x.shape
+    return comm_call(
+        backward_bridge_kernel, 2,
+        [((rows, width), F32), ((4 * rows, width), BF16), ((1, width), F32)],
+        (partial, x, gain, grad), 1, 1,
+    )
+
+
+def forward_last(partial, x):
+    rows, width = x.shape
+    return comm_call(forward_last_kernel, 3, [((rows, width), BF16)], (partial, x), 1, 0)[0]
+
+
+def backward_last(partial, x, gain, grad):
+    rows, width = x.shape
+    return comm_call(
+        backward_last_kernel, 4, [((rows, width), BF16), ((1, width), F32)],
+        (partial, x, gain, grad), 1, 0,
+    )
+
+
+def gather_plain_kernel(x_ref, out_ref, send, recv):
+    greet()
+    gather = Gather(out_ref, send, recv, 0)
+    size = x_ref.shape[0] // PIECES
+    for p in range(PIECES):
+        gather.put(p, x_ref[p * size : (p + 1) * size, :])
+    gather.finish()
+
+
+def gather_plain(x):
+    rows, width = x.shape
+    return comm_call(gather_plain_kernel, 5, [((4 * rows, width), BF16)], (x,), 0, 1)[0]
 
 
 def swiglu_rows(paired):
@@ -366,31 +654,100 @@
     return jax.nn.silu(gate_part) * up_part
 
 
-def gather_rows(values):
-    return lax.all_gather(values, "tensor", axis=0, tiled=True)
-
-
-def scatter_sum(partial):
-    return lax.psum_scatter(partial, "tensor", scatter_dimension=0, tiled=True).astype(F32)
-
-
 def dot32(a, b, dims):
     return lax.dot_general(a, b, dims, preferred_element_type=F32)
+
+
+def row_major(x):
+    return with_layout_constraint(x, Layout(major_to_minor=tuple(range(x.ndim))))
+
+
+def linear(sizes, index):
+    place = 0
+    for size, at in zip(sizes, index):
+        place = place * size + at
+    return place
+
+
+class Roles:
+    def __init__(self):
+        self.sizes = tuple(lax.axis_size(name) for name in AXES)
+        self.chips, self.cores, self.zps, self.zls = self.sizes
+        assert self.cores == 2 and self.zps == 2 and self.zls == 2
+
+    def every(self):
+        for chip in range(self.chips):
+            for core in range(2):
+                for zp in range(2):
+                    for zl in range(2):
+                        yield chip, core, zp, zl
+
+    def rows_pairs(self):
+        pairs = []
+        for chip, core, zp, zl in self.every():
+            slot, part = zp * self.chips + chip, zl * 2 + core
+            source = linear(self.sizes, (slot // 2, slot % 2, part // 2, part % 2))
+            pairs.append((source, linear(self.sizes, (chip, core, zp, zl))))
+        return pairs
+
+    def weight_pairs(self, which):
+        pairs = []
+        for chip, core, zp, zl in self.every():
+            head = zp * 2 + zl
+            to = (chip, head % 2, core ^ which, head // 2)
+            pairs.append(
+                (linear(self.sizes, (chip, core, zp, zl)), linear(self.sizes, to))
+            )
+        return pairs
+
+
+def flipped(pairs):
+    return [(b, a) for a, b in pairs]
+
+
+def weights_in(pack, roles):
+    halves = [lax.ppermute(pack, AXES, roles.weight_pairs(which)) for which in range(2)]
+    swap = lax.axis_index("zp") == 1
+    ordered = jnp.concatenate(
+        [jnp.where(swap, halves[1], halves[0]), jnp.where(swap, halves[0], halves[1])], axis=0
+    )
+    return row_major(lax.all_gather(row_major(ordered), "chip", axis=0, tiled=True))
+
+
+def weights_out(grads, roles):
+    mine = lax.psum_scatter(grads, "chip", scatter_dimension=0, tiled=True)
+    rows = mine.shape[0] // 2
+    swap = lax.axis_index("zp") == 1
+    low, high = mine[:rows], mine[rows:]
+    halves = [jnp.where(swap, high, low), jnp.where(swap, low, high)]
+    back = [
+        lax.ppermute(half, AXES, flipped(roles.weight_pairs(which)))
+        for which, half in enumerate(halves)
+    ]
+    return back[0].astype(F32) + back[1].astype(F32)
+
+
+def deal(values, order):
+    spread = lax.all_to_all(values, ("chip", "core"), split_axis=2, concat_axis=1, tiled=True)
+    picked = jnp.take(spread, order, axis=1)
+    return lax.all_to_all(picked, ("chip", "core"), split_axis=1, concat_axis=2, tiled=True)
 
 
 def shards(
     tokens, lengths, order, norm_mix, w_query, w_key, w_value, w_gate, w_decay, conv_filter,
     log_rate, step_bias, norm_heads, w_out, norm_ffn, w_ffn_gate, w_ffn_up, w_ffn_down, cotangent,
 ):
+    roles = Roles()
     layer_count = w_query.shape[0]
     heads_total = log_rate.shape[1]
-    device_part = lax.axis_index("tensor")
-    dp_place = lax.axis_index("dp")
+    chip, core, zp, zl = (lax.axis_index(name) for name in AXES)
+    head = zl * 2 + core
     rows_local, slots_local, width = tokens.shape
     assert slots_local == 1 and w_decay.shape[2] == 1
     slot_total = order.shape[0]
     units = w_ffn_gate.shape[2]
     rows_part = w_query.shape[1]
+    to_roles = roles.rows_pairs()
 
     packs = []
     for layer in range(layer_count):
@@ -400,69 +757,67 @@
             [w_query[layer], w_key[layer], w_value[layer], w_gate[layer], w_out[layer].T, aux], axis=1
         )
         ffn = jnp.concatenate([w_ffn_gate[layer], w_ffn_up[layer], w_ffn_down[layer].T], axis=1)
-        packs.append(
-            (
-                lax.all_gather(mix, "dp", axis=0, tiled=True),
-                lax.all_gather(ffn, "dp", axis=0, tiled=True),
-            )
-        )
-
-    spread_in = lax.all_to_all(tokens, "dp", split_axis=2, concat_axis=1, tiled=True)
-    picked = jnp.take(spread_in, order, axis=1)
-    dealt = lax.all_to_all(picked, "dp", split_axis=1, concat_axis=2, tiled=True)
-    residual = dealt[:, 0, :].astype(F32)
+        packs.append((weights_in(row_major(mix), roles), weights_in(row_major(ffn), roles)))
+
+    dealt = deal(tokens, order)[:, 0, :]
+    residual = lax.ppermute(dealt, AXES, to_roles)
+
+    positions = (zp * 2 + zl) * rows_local + jnp.arange(rows_local)
+    my_length = lengths[order[chip * 2 + core]]
+    start = cotangent[:, 0, :] * (positions < my_length).astype(BF16)[:, None]
+    gradient = lax.ppermute(start, AXES, to_roles)
+    grad_rows = gather_plain(gradient)
 
     saved = []
+    gains = [
+        (norm_mix[layer].astype(F32)[None], norm_ffn[layer].astype(F32)[None])
+        for layer in range(layer_count)
+    ]
+    rows_in = first_gather(residual, gains[0][0])
     for layer in range(layer_count):
         mix, ffn = packs[layer]
         taps = mix[:, 2050:2054].T.astype(F32)
         gain_heads = norm_heads[layer].astype(F32)[None]
         scalars = jnp.concatenate(
             [
-                jnp.exp(lax.dynamic_slice_in_dim(log_rate[layer].astype(F32), device_part, 1)),
-                lax.dynamic_slice_in_dim(step_bias[layer].astype(F32), device_part, 1),
+                jnp.exp(lax.dynamic_slice_in_dim(log_rate[layer].astype(F32), head, 1)),
+                lax.dynamic_slice_in_dim(step_bias[layer].astype(F32), head, 1),
             ]
         )
-        normed, norm_back = jax.vjp(norm_rows, residual, norm_mix[layer].astype(F32))
-        rows_in = gather_rows(normed.astype(BF16))
         part, heads, *kept = mixer_forward(rows_in, mix, taps, gain_heads, scalars)
-        residual = residual + scatter_sum(part)
-        normed_ffn, ffn_norm_back = jax.vjp(norm_rows, residual, norm_ffn[layer].astype(F32))
-        rows_ffn = gather_rows(normed_ffn.astype(BF16))
+        middle, rows_ffn = forward_bridge(part, residual, gains[layer][1])
         paired = dot32(rows_ffn, ffn[:, : 2 * units], NN)
         hidden, swiglu_back = jax.vjp(swiglu_rows, paired)
         hidden = hidden.astype(BF16)
-        residual = residual + scatter_sum(dot32(hidden, ffn[:, 2 * units :], NT).astype(BF16))
+        part = dot32(hidden, ffn[:, 2 * units :], NT).astype(BF16)
         saved.append(
-            (norm_back, rows_in, taps, gain_heads, scalars, kept, heads, ffn_norm_back, rows_ffn,
+            (residual, rows_in, taps, gain_heads, scalars, kept, heads, middle, rows_ffn,
              swiglu_back, hidden)
         )
-
-    my_length = lengths[order[dp_place]]
-    positions = device_part * rows_local + jnp.arange(rows_local)
-    gradient = cotangent[:, 0, :].astype(F32) * (positions < my_length).astype(F32)[:, None]
+        if layer + 1 < layer_count:
+            residual, rows_in = forward_bridge(part, middle, gains[layer + 1][0])
+        else:
+            mixed = forward_last(part, middle)
+    mixed = lax.ppermute(mixed, AXES, flipped(to_roles))
+
     weight_grads = [None] * layer_count
     small_terms = [None] * layer_count
     for layer in reversed(range(layer_count)):
         mix, ffn = packs[layer]
-        (norm_back, rows_in, taps, gain_heads, scalars, kept, heads, ffn_norm_back, rows_ffn,
+        (residual, rows_in, taps, gain_heads, scalars, kept, heads, middle, rows_ffn,
          swiglu_back, hidden) = saved[layer]
-        grad_rows = gather_rows(gradient.astype(BF16))
         (grad_paired,) = swiglu_back(dot32(grad_rows, ffn[:, 2 * units :], NN))
         paired_low = grad_paired.astype(BF16)
-        grad_normed = scatter_sum(dot32(paired_low, ffn[:, : 2 * units], NT).astype(BF16))
+        part = dot32(paired_low, ffn[:, : 2 * units], NT).astype(BF16)
         ffn_grads = jnp.concatenate(
             [dot32(rows_ffn, paired_low, TN).astype(BF16), dot32(grad_rows, hidden, TN).astype(BF16)],
             axis=1,
         )
-        ffn_grads = lax.psum_scatter(ffn_grads, "dp", scatter_dimension=0, tiled=True)
-        grad_residual, grad_gain_ffn = ffn_norm_back(grad_normed)
-        gradient = gradient + grad_residual
-        grad_rows = gather_rows(gradient.astype(BF16))
+        ffn_grads = weights_out(ffn_grads, roles)
+        gradient, grad_rows, dgain_ffn = backward_bridge(part, middle, gains[layer][1], gradient)
         part, dproj, drates, dtaps, dgain, dscalars = mixer_backward(
             grad_rows, mix, taps, gain_heads, scalars, kept
         )
-        grad_normed = scatter_sum(part)
         aux = dot32(rows_in, drates, TN) + jnp.pad(dtaps.T, ((0, 0), (2, LANES - 6)))
         mix_grads = jnp.concatenate(
             [
@@ -472,38 +827,37 @@
             ],
             axis=1,
         )
-        mix_grads = lax.psum_scatter(mix_grads, "dp", scatter_dimension=0, tiled=True)
-        grad_residual, grad_gain_mix = norm_back(grad_normed)
-        gradient = gradient + grad_residual
+        mix_grads = weights_out(mix_grads, roles)
+        if layer:
+            gradient, grad_rows, dgain_mix = backward_bridge(part, residual, gains[layer][0], gradient)
+        else:
+            gradient, dgain_mix = backward_last(part, residual, gains[layer][0], gradient)
         weight_grads[layer] = (
-            mix_grads[:, :256].astype(F32),
-            mix_grads[:, 256:512].astype(F32),
-            mix_grads[:, 512:1024].astype(F32),
-            mix_grads[:, 1024:1536].astype(F32),
-            mix_grads[:, 2048:2050].astype(F32).reshape(rows_part, 1, 2),
-            mix_grads[:, 2050:2054].astype(F32).T.reshape(4, 1, rows_part),
-            mix_grads[:, 1536:2048].astype(F32).T,
-            ffn_grads[:, :units].astype(F32),
-            ffn_grads[:, units : 2 * units].astype(F32),
-            ffn_grads[:, 2 * units :].astype(F32).T,
-        )
-        mine = (jnp.arange(heads_total) == device_part).astype(F32)
+            mix_grads[:, :256],
+            mix_grads[:, 256:512],
+            mix_grads[:, 512:1024],
+            mix_grads[:, 1024:1536],
+            mix_grads[:, 2048:2050].reshape(rows_part, 1, 2),
+            mix_grads[:, 2050:2054].T.reshape(4, 1, rows_part),
+            mix_grads[:, 1536:2048].T,
+            ffn_grads[:, :units],
+            ffn_grads[:, units : 2 * units],
+            ffn_grads[:, 2 * units :].T,
+        )
+        mine = (jnp.arange(heads_total) == head).astype(F32)
         small_terms[layer] = jnp.concatenate(
-            [grad_gain_mix, grad_gain_ffn, dgain[0], mine * dscalars[0, 0], mine * dscalars[1, 0]]
-        )
-    small = lax.psum(jnp.stack(small_terms), ("dp", "tensor"))
-    spread_back = lax.all_to_all(
-        gradient.astype(BF16)[:, None, :], "dp", split_axis=2, concat_axis=1, tiled=True
-    )
+            [dgain_mix[0], dgain_ffn[0], dgain[0], mine * dscalars[0, 0], mine * dscalars[1, 0]]
+        )
+    small = lax.psum(jnp.stack(small_terms), AXES)
+    dealt_grad = lax.ppermute(gradient, AXES, flipped(to_roles))
     inverse_order = (
         jnp.zeros((slot_total,), jnp.int32).at[order].set(jnp.arange(slot_total, dtype=jnp.int32))
     )
-    homed = jnp.take(spread_back, inverse_order, axis=1)
-    grad_home = lax.all_to_all(homed, "dp", split_axis=1, concat_axis=2, tiled=True).astype(F32)
+    grad_home = deal(dealt_grad[:, None, :], inverse_order).astype(F32)
     members = [jnp.stack([grads[m] for grads in weight_grads]) for m in range(10)]
     ends = 2 * width + VAL
     return (
-        residual.astype(BF16)[:, None, :],
+        mixed[:, None, :],
         grad_home,
         small[:, :width],
         members[0], members[1], members[2], members[3], members[4], members[5],
@@ -517,23 +871,22 @@
 
 
 def solution(mesh):
+    dp, tensor = mesh.devices.shape
+    mesh = Mesh(mesh.devices.reshape(dp // 2, 2, tensor // 2, 2), AXES)
+    d, t = ("chip", "core"), ("zp", "zl")
+    rows = P(t, d, None)
+    by_rows, by_columns = P(None, d, t), P(None, t, d)
+    heads, filters = P(None, d, t, None), P(None, None, t, d)
     return jax.shard_map(
         shards,
         mesh=mesh,
         in_specs=(
-            P("tensor", "dp", None), P(), P(), P(),
-            P(None, "dp", "tensor"), P(None, "dp", "tensor"), P(None, "dp", "tensor"),
-            P(None, "dp", "tensor"), P(None, "dp", "tensor", None), P(None, None, "tensor", "dp"),
-            P(), P(), P(), P(None, "tensor", "dp"), P(),
-            P(None, "dp", "tensor"), P(None, "dp", "tensor"), P(None, "tensor", "dp"),
-            P("tensor", "dp", None),
+            rows, P(), P(), P(), by_rows, by_rows, by_rows, by_rows, heads, filters,
+            P(), P(), P(), by_columns, P(), by_rows, by_rows, by_columns, rows,
         ),
         out_specs=(
-            P("tensor", "dp", None), P("tensor", "dp", None), P(),
-            P(None, "dp", "tensor"), P(None, "dp", "tensor"), P(None, "dp", "tensor"),
-            P(None, "dp", "tensor"), P(None, "dp", "tensor", None), P(None, None, "tensor", "dp"),
-            P(), P(), P(), P(None, "tensor", "dp"), P(),
-            P(None, "dp", "tensor"), P(None, "dp", "tensor"), P(None, "tensor", "dp"),
+            rows, rows, P(), by_rows, by_rows, by_rows, by_rows, heads, filters,
+            P(), P(), P(), by_columns, P(), by_rows, by_rows, by_columns,
         ),
         check_vma=False,
     )

time: 1330 us -> 888 us (0.67)
  the two profiles are of different devices: /device:TPU:0 before, /device:TPU:1 now
where the time goes in v2:
time: 888 us; the launch traced here: 877 us
  Pallas kernels  379 us (43%)
  waiting for transfers between devices  121 us (14%)
  starting transfers between devices  114 us (13%)
  matrix products  80.1 us (9%)
  local copies, waits for them, and re-layouts  68.7 us (8%)
  other arithmetic  51.7 us (6%)
  blocking collectives  45.6 us (5%)
  between operations  17.9 us (2%)
    pallas_call x10, Pallas kernels, comm_call(): pl.pallas_call(kernel, in_specs=[vmem] * len(args), out_specs=[vmem] * le...  260 us
    dot_general x18, matrix products, dot32(): return lax.dot_general(a, b, dims, preferred_element_type=F32)  80.1 us
    ppermute x8, waiting for transfers between devices, weights_out(): lax.ppermute(half, AXES, flipped(roles.weight_pairs(which)))  66 us
    pallas_call x2, Pallas kernels, mixer_forward(): pl.pallas_call(forward_kernel, grid=(chunks,), in_specs=[pl.BlockSpec(mem...  63.6 us
    pallas_call x2, Pallas kernels, mixer_backward(): pl.pallas_call(backward_kernel, grid=(chunks,), in_specs=[pl.BlockSpec(me...  56 us
    psum x1, blocking collectives, shards(): small = lax.psum(jnp.stack(small_terms), AXES)  45.6 us
    unnamed x135, local copies, waits for them, and re-layouts  41 us
    ppermute x8, starting transfers between devices, weights_in(): lax.ppermute(pack, AXES, roles.weight_pairs(which))  40.2 us
  transfers between devices with their start and end apart: 32, of which 12 were waited for; matrix products, arithmetic and copies ran while one was open for 15% of the time, Pallas kernels for 43%

profile of v2, /device:TPU:1, one launch (start us, length us, event | category | flops | bytes accessed | tf_op | source)
XLA Modules:
  0.0 877.3 jit_solution(16685609343331000781)
XLA Ops:
  16.3 7.1 collective-permute-start.6
  27.5 8.5 collective-permute-done.6
  35.9 9.1 %collective-permute-done.2 = bf16[128,2176]{1,0:T(8,128)(2,1)S(1)} collective-permute-done((bf16[128,2176]{1,0:T(8,128)(2,1)}, bf16[128,2176]{1,0:T(8,128)(2,1)S(1)}, u32[]{:S(2)}, u32[]{:S(2)}) %collective-permute-start.2) | collective-permute-done | bytes 557088 | tf_op jit(solution)/shard_map/ppermute | solution.py:709
  48.9 25.6 %collective-permute-start.8 = (bf16[128,2112]{0,1:T(8,128)(2,1)S(1)}, bf16[128,2112]{0,1:T(8,128)(2,1)S(1)}, u32[]{:S(2)}, u32[]{:S(2)}) collective-permute-start(bf16[128,2112]{0,1:T(8,128)(2,1)S(1)} %copy.256), channel_id=1, source_target_pairs={{0,0},{1,4},{2,1},{3,5},{4,2},{5,6},{6,3},{7,7},{8,8},{9,12},{10,9... | collective-permute-start | bytes 1622024 | tf_op jit(solution)/shard_map/ppermute | solution.py:709
  76.4 5.3 collective-permute-start.4
  82.1 4.6 collective-permute-done.8
  87.0 10.0 %collective-permute-done.4 = bf16[128,2112]{0,1:T(8,128)(2,1)} collective-permute-done((bf16[128,2112]{0,1:T(8,128)(2,1)}, bf16[128,2112]{0,1:T(8,128)(2,1)}, u32[]{:S(2)}, u32[]{:S(2)}) %collective-permute-start.4) | collective-permute-done | bytes 540704 | tf_op jit(solution)/shard_map/ppermute | solution.py:709
  104.6 3.9 reduce
  109.4 3.8 all-to-all-start
  117.9 3.5 collective-permute-start.10
  127.7 25.8 %all-to-all-start.1 = ((bf16[256,8,128]{2,0,1:T(8,128)(2,1)}), bf16[256,8,128]{2,0,1:T(8,128)(2,1)S(1)}, u32[]{:S(2)}, u32[]{:S(2)}) async-start(bf16[256,8,128]{2,0,1:T(8,128)(2,1)} %select_bitcast_fusion.1), calls=%async_computation.1 | async-start | bytes 1048576 | tf_op jit(solution)/shard_map/all_to_all | solution.py:733
  158.4 7.1 all-to-all-done.1
  165.6 4.3 collective-permute-start
  171.9 29.4 %gather_plain.1 = bf16[1024,1024]{1,0:T(8,128)(2,1)S(1)} custom-call(bf16[256,1024]{1,0:T(8,128)(2,1)S(1)} %collective-permute-done.10.x_ref.grad_ref), custom_call_target="tpu_custom_call" | custom-call | flops 5242880 | bytes 41943040 | tf_op jit(solution)/shard_map/gather_plain/pallas_call | solution.py:586
  202.6 15.5 %first.1.x_ref = bf16[1024,1024]{1,0:T(8,128)(2,1)S(1)} custom-call(bf16[256,1024]{1,0:T(8,128)(2,1)S(1)} %collective-permute-done.x_ref, f32[1,1024]{1,0:T(1,128)S(1)} %get-tuple-element.278.gain_ref), custom_call_target="tpu_custom_call" | custom-call | flops 5242880 | bytes 41943040 | tf_op jit(solution)/shard_map/first/pallas_call | solution.py:586
  223.3 32.2 %mixer_forward.2 = (bf16[1024,1024]{1,0:T(8,128)(2,1)}, bf16[1024,512]{1,0:T(8,128)(2,1)}, f32[1024,1024]{1,0:T(8,128)}, f32[1024,512]{1,0:T(8,128)}, f32[1024,1...) custom-call(f32[2]{0:T(128)} %pad_maximum_fusion.28.scalars_ref, ...), custom_call_target="tpu_custom_call" | custom-call | flops 16000000000 | bytes 80000000 | tf_op jit(solution)/shard_map/mixer_forward/pallas_call | solution.py:157
  257.1 28.2 %forward_bridge.3 = (f32[256,1024]{1,0:T(8,128)S(1)}, bf16[1024,1024]{1,0:T(8,128)(2,1)S(1)}) custom-call(bf16[1024,1024]{1,0:T(8,128)(2,1)S(1)} %copy-done.7, bf16[256,1024]{1,0:T(8,128)(2,1)S(1)} %collective-permute-done.x_ref, f32[1,1024]{1,0:T(1,128)S(1)} %get-tuple-element.276.gain_ref), custom_call_target="tpu_custom_call" | custom-call | flops 5242880 | bytes 41943040 | tf_op jit(solution)/shard_map/forward_bridge/pallas_call | solution.py:586
  286.6 5.8 fusion.14
  294.9 5.1 convolution_convert_fusion.5.partial
  300.0 29.7 %forward_bridge.4 = (f32[256,1024]{1,0:T(8,128)S(1)}, bf16[1024,1024]{1,0:T(8,128)(2,1)S(1)}) custom-call(bf16[1024,1024]{1,0:T(8,128)(2,1)} %convolution_convert_fusion.5.partial, f32[256,1024]{1,0:T(8,128)S(1)} %get-tuple-element.67.x_ref, f32[1,1024]{1,0:T(1,128)S(1)} %get-tuple-element.277.gain_ref), custom_call_target="tpu_custom_call" | custom-call | flops 5242880 | bytes 41943040 | tf_op jit(solution)/shard_map/forward_bridge/pallas_call | solution.py:586
  331.1 31.4 %mixer_forward.3 = (bf16[1024,1024]{1,0:T(8,128)(2,1)}, bf16[1024,512]{1,0:T(8,128)(2,1)}, f32[1024,1024]{1,0:T(8,128)}, f32[1024,512]{1,0:T(8,128)}, f32[1024,1...) custom-call(f32[2]{0:T(128)} %pad_maximum_fusion.27.scalars_ref, ...), custom_call_target="tpu_custom_call" | custom-call | flops 16000000000 | bytes 80000000 | tf_op jit(solution)/shard_map/mixer_forward/pallas_call | solution.py:157
  362.5 29.8 %forward_bridge.5 = (f32[256,1024]{1,0:T(8,128)S(1)}, bf16[1024,1024]{1,0:T(8,128)(2,1)S(1)}) custom-call(bf16[1024,1024]{1,0:T(8,128)(2,1)} %get-tuple-element.69.partial, f32[256,1024]{1,0:T(8,128)S(1)} %get-tuple-element.70.x_ref, f32[1,1024]{1,0:T(1,128)S(1)} %get-tuple-element.275.gain_ref), custom_call_target="tpu_custom_call" | custom-call | flops 5242880 | bytes 41943040 | tf_op jit(solution)/shard_map/forward_bridge/pallas_call | solution.py:586
  394.6 6.0 fusion.10
  400.6 5.4 fusion.2
  412.8 6.1 convolution_convert_fusion
  421.4 7.6 fusion.19.partial
  429.0 30.1 %backward_bridge.3 = (f32[256,1024]{1,0:T(8,128)S(1)}, bf16[1024,1024]{1,0:T(8,128)(2,1)S(1)}, f32[1,1024]{1,0:T(1,128)S(1)}) custom-call(bf16[1024,1024]{1,0:T(8,128)(2,1)} %fusion.19.partial, f32[256,1024]{1,0:T(8,128)S(1)} %copy-done.1, f32[1,1024]{1,0:T(1,128)S(1)} %get-tuple-element.275.gain_ref, ...), custom_call_target="tpu_custom_call" | custom-call | flops 5242880 | bytes 41943040 | tf_op jit(solution)/shard_map/backward_bridge/pallas_call | solution.py:586
  460.5 28.4 %mixer_backward.2 = (bf16[1024,1024]{1,0:T(8,128)(2,1)}, bf16[1024,1536]{1,0:T(8,128)(2,1)}, bf16[1024,128]{1,0:T(8,128)(2,1)}, f32[4,1024]{1,0:T(4,128)}, f32[1,512]{1,0:T(1,128)}, /*index=5*/f32[8,128]{1,0:T(8,128)}) custom-call(f32[2]{0:T(128)} %pad_maximum_fusion.27.scalars_ref, bf16[1024,1024]{1,0:T(8,128)(2,1)} %copy-done.19, ...), custom_call_target="tpu_custom_call" | custom-call | flops 16000000000 | bytes 80000000 | tf_op jit(solution)/shard_map/mixer_backward/pallas_call | solution.py:324
  488.9 29.9 %backward_bridge.4 = (f32[256,1024]{1,0:T(8,128)S(1)}, bf16[1024,1024]{1,0:T(8,128)(2,1)S(1)}, f32[1,1024]{1,0:T(1,128)S(1)}) custom-call(bf16[1024,1024]{1,0:T(8,128)(2,1)} %get-tuple-element.81.partial, f32[256,1024]{1,0:T(8,128)S(1)} %get-tuple-element.70.x_ref, f32[1,1024]{1,0:T(1,128)S(1)} %get-tuple-element.277.gain_ref, ...), custom_call_target="tpu_custom_call" | custom-call | flops 5242880 | bytes 41943040 | tf_op jit(solution)/shard_map/backward_bridge/pallas_call | solution.py:586
  524.4 6.7 fusion.5
  532.8 4.2 convolution_convert_fusion.1
  545.9 3.8 convolution_convert_fusion.2
  552.1 7.7 fusion.16.partial
  559.8 29.9 %backward_bridge.5 = (f32[256,1024]{1,0:T(8,128)S(1)}, bf16[1024,1024]{1,0:T(8,128)(2,1)S(1)}, f32[1,1024]{1,0:T(1,128)S(1)}) custom-call(bf16[1024,1024]{1,0:T(8,128)(2,1)} %fusion.16.partial, f32[256,1024]{1,0:T(8,128)S(1)} %get-tuple-element.67.x_ref, f32[1,1024]{1,0:T(1,128)S(1)} %get-tuple-element.276.gain_ref, f32[256,1024]{1,0:T(8,128)S(1)} %copy-done.10), custom_call_target="tpu_custom_call" | custom-call | flops 5242880 | bytes 41943040 | tf_op jit(solution)/shard_map/backward_bridge/pallas_call | solution.py:586
  592.1 27.6 %mixer_backward.3 = (bf16[1024,1024]{1,0:T(8,128)(2,1)}, bf16[1024,1536]{1,0:T(8,128)(2,1)}, bf16[1024,128]{1,0:T(8,128)(2,1)}, f32[4,1024]{1,0:T(4,128)}, f32[1,512]{1,0:T(1,128)}, /*index=5*/f32[8,128]{1,0:T(8,128)}) custom-call(f32[2]{0:T(128)} %pad_maximum_fusion.28.scalars_ref, bf16[1024,1024]{1,0:T(8,128)(2,1)} %copy-done.20, ...), custom_call_target="tpu_custom_call" | custom-call | flops 16000000000 | bytes 80000000 | tf_op jit(solution)/shard_map/mixer_backward/pallas_call | solution.py:324
  624.7 3.9 convolution_convert_fusion.3
  633.7 15.6 %backward_last.1 = (bf16[256,1024]{1,0:T(8,128)(2,1)S(1)}, f32[1,1024]{1,0:T(1,128)S(1)}) custom-call(bf16[1024,1024]{1,0:T(8,128)(2,1)S(1)} %copy-done.8, bf16[256,1024]{1,0:T(8,128)(2,1)S(1)} %collective-permute-done.x_ref, f32[1,1024]{1,0:T(1,128)S(1)} %copy-done.14, f32[256,1024]{1,0:T(8,128)S(1)} %copy-done.12), custom_call_target="tpu_custom_call" | custom-call | flops 5242880 | bytes 41943040 | tf_op jit(solution)/shard_map/backward_last/pallas_call | solution.py:586
  655.4 21.6 %forward_last.1 = bf16[256,1024]{1,0:T(8,128)(2,1)S(1)} custom-call(bf16[1024,1024]{1,0:T(8,128)(2,1)S(1)} %convolution_convert_fusion.4.partial, f32[256,1024]{1,0:T(8,128)S(1)} %copy-done.2), custom_call_target="tpu_custom_call" | custom-call | flops 5242880 | bytes 41943040 | tf_op jit(solution)/shard_map/forward_last/pallas_call | solution.py:586
  681.1 3.9 reduce.1
  685.9 4.2 all-to-all-start.2
  694.2 11.4 %all-to-all-done.2 = bf16[8,2,16384]{2,1,0:T(2,128)(2,1)S(1)} async-done(((bf16[8,2,16384]{2,1,0:T(2,128)(2,1)}), bf16[8,2,16384]{2,1,0:T(2,128)(2,1)S(1)}, u32[]{:S(2)}, u32[]{:S(2)}) %all-to-all-start.2) | async-done | bytes 524320 | tf_op jit(solution)/shard_map/all_to_all | solution.py:731
  708.0 5.8 all-to-all-start.3
  713.9 45.6 %psum.7 = f32[2,2568]{1,0:T(2,128)S(1)} all-reduce(f32[2,2568]{1,0:T(2,128)S(1)} %pad_maximum_fusion.22), channel_id=1, replica_groups=mesh['chip'=4,'core'=2,'zp'=2,'zl'=2] {'chip','core','zp','zl'}, use_global_device_ids=true, to_apply=%region_1.3 | all-reduce | flops 5136 | bytes 41088 | tf_op jit(solution)/shard_map/psum | solution.py:851
  782.8 11.7 %collective-permute-done.18 = bf16[128,2112]{0,1:T(8,128)(2,1)} collective-permute-done((bf16[128,2112]{0,1:T(8,128)(2,1)S(1)}, bf16[128,2112]{0,1:T(8,128)(2,1)}, u32[]{:S(2)}, u32[]{:S(2)}) %collective-permute-start.18) | collective-permute-done | bytes 540704 | tf_op jit(solution)/shard_map/ppermute | solution.py:724
  796.0 8.6 collective-permute-start.12
  804.5 13.2 %collective-permute-done.16 = bf16[128,2112]{0,1:T(8,128)(2,1)} collective-permute-done((bf16[128,2112]{0,1:T(8,128)(2,1)S(1)}, bf16[128,2112]{0,1:T(8,128)(2,1)}, u32[]{:S(2)}, u32[]{:S(2)}) %collective-permute-start.16) | collective-permute-done | bytes 540704 | tf_op jit(solution)/shard_map/ppermute | solution.py:724
  821.8 19.6 %collective-permute-done.14 = bf16[128,2176]{1,0:T(8,128)(2,1)S(1)} collective-permute-done((bf16[128,2176]{1,0:T(8,128)(2,1)S(1)}, bf16[128,2176]{1,0:T(8,128)(2,1)S(1)}, u32[]{:S(2)}, u32[]{:S(2)}) %collective-permute-start.14) | collective-permute-done | bytes 557088 | tf_op jit(solution)/shard_map/ppermute | solution.py:724
  841.7 21.4 %collective-permute-done.12 = bf16[128,2176]{1,0:T(8,128)(2,1)S(1)} collective-permute-done((bf16[128,2176]{1,0:T(8,128)(2,1)S(1)}, bf16[128,2176]{1,0:T(8,128)(2,1)S(1)}, u32[]{:S(2)}, u32[]{:S(2)}) %collective-permute-start.12) | collective-permute-done | bytes 557088 | tf_op jit(solution)/shard_map/ppermute | solution.py:724
  (311 shorter events, 153.8 us)
Async XLA Ops:
  7.2 212.3 %all-gather.5.cloned.1.call-start = ((), (), s32[]{:S(2)}) async-start(), calls=%async_computation.8 | async-start | bytes 5570560 | tf_op jit(solution)/shard_map/all_gather | solution.py:714
  16.2 11.2 %collective-permute-start.5 = (bf16[128,2176]{1,0:T(8,128)(2,1)S(1)}, bf16[128,2176]{1,0:T(8,128)(2,1)S(1)}, u32[]{:S(2)}, u32[]{:S(2)}) collective-permute-start(bf16[128,2176]{1,0:T(8,128)(2,1)S(1)} %pad_dynamic-update-slice_fusion), channel_id=1, source_target_pairs={{0,2},{1,6},{2,3},{3,7},{4,0},{5,4},{6,1},{7,5},{8,10},{9,14},{10,... | collective-permute-start | bytes 1671176 | tf_op jit(solution)/shard_map/ppermute | solution.py:709
  16.3 19.6 %collective-permute-start.6 = (bf16[128,2176]{1,0:T(8,128)(2,1)S(1)}, bf16[128,2176]{1,0:T(8,128)(2,1)S(1)}, u32[]{:S(2)}, u32[]{:S(2)}) collective-permute-start(bf16[128,2176]{1,0:T(8,128)(2,1)S(1)} %pad_dynamic-update-slice_fusion), channel_id=1, source_target_pairs={{0,0},{1,4},{2,1},{3,5},{4,2},{5,6},{6,3},{7,7},{8,8},{9,12},{10,9... | collective-permute-start | bytes 1671176 | tf_op jit(solution)/shard_map/ppermute | solution.py:709
  25.0 20.1 %collective-permute-start.2 = (bf16[128,2176]{1,0:T(8,128)(2,1)}, bf16[128,2176]{1,0:T(8,128)(2,1)S(1)}, u32[]{:S(2)}, u32[]{:S(2)}) collective-permute-start(bf16[128,2176]{1,0:T(8,128)(2,1)} %pad_dynamic-update-slice_fusion.1), channel_id=1, source_target_pairs={{0,0},{1,4},{2,1},{3,5},{4,2},{5,6},{6,3},{7,7},{8,8},{9,12},{10,9... | collective-permute-start | bytes 1671176 | tf_op jit(solution)/shard_map/ppermute | solution.py:709
  26.9 18.2 %collective-permute-start.1 = (bf16[128,2176]{1,0:T(8,128)(2,1)}, bf16[128,2176]{1,0:T(8,128)(2,1)S(1)}, u32[]{:S(2)}, u32[]{:S(2)}) collective-permute-start(bf16[128,2176]{1,0:T(8,128)(2,1)} %pad_dynamic-update-slice_fusion.1), channel_id=1, source_target_pairs={{0,2},{1,6},{2,3},{3,7},{4,0},{5,4},{6,1},{7,5},{8,10},{9,14},{10,... | collective-permute-start | bytes 1671176 | tf_op jit(solution)/shard_map/ppermute | solution.py:709
  46.4 175.0 %all-gather.9.cloned.1.call-start = ((), (), s32[]{:S(2)}) async-start(), calls=%async_computation.10 | async-start | bytes 5570560 | tf_op jit(solution)/shard_map/all_gather | solution.py:714
  47.6 239.0 %all-gather.7.cloned.1.call-start = ((), (), s32[]{:S(2)}) async-start(), calls=%async_computation.9 | async-start | bytes 5570560 | tf_op jit(solution)/shard_map/all_gather | solution.py:714
  48.9 32.9 %collective-permute-start.7 = (bf16[128,2112]{0,1:T(8,128)(2,1)S(1)}, bf16[128,2112]{0,1:T(8,128)(2,1)S(1)}, u32[]{:S(2)}, u32[]{:S(2)}) collective-permute-start(bf16[128,2112]{0,1:T(8,128)(2,1)S(1)} %copy.256), channel_id=1, source_target_pairs={{0,2},{1,6},{2,3},{3,7},{4,0},{5,4},{6,1},{7,5},{8,10},{9,14},{10,... | collective-permute-start | bytes 1622024 | tf_op jit(solution)/shard_map/ppermute | solution.py:709
  48.9 37.8 %collective-permute-start.8 = (bf16[128,2112]{0,1:T(8,128)(2,1)S(1)}, bf16[128,2112]{0,1:T(8,128)(2,1)S(1)}, u32[]{:S(2)}, u32[]{:S(2)}) collective-permute-start(bf16[128,2112]{0,1:T(8,128)(2,1)S(1)} %copy.256), channel_id=1, source_target_pairs={{0,0},{1,4},{2,1},{3,5},{4,2},{5,6},{6,3},{7,7},{8,8},{9,12},{10,9... | collective-permute-start | bytes 1622024 | tf_op jit(solution)/shard_map/ppermute | solution.py:709
  76.4 20.6 %collective-permute-start.4 = (bf16[128,2112]{0,1:T(8,128)(2,1)}, bf16[128,2112]{0,1:T(8,128)(2,1)}, u32[]{:S(2)}, u32[]{:S(2)}) collective-permute-start(bf16[128,2112]{0,1:T(8,128)(2,1)} %copy.244), channel_id=1, source_target_pairs={{0,0},{1,4},{2,1},{3,5},{4,2},{5,6},{6,3},{7,7},{8,8},{9,12},{10,9... | collective-permute-start | bytes 1622024 | tf_op jit(solution)/shard_map/ppermute | solution.py:709
  81.7 16.7 %collective-permute-start.3 = (bf16[128,2112]{0,1:T(8,128)(2,1)}, bf16[128,2112]{0,1:T(8,128)(2,1)}, u32[]{:S(2)}, u32[]{:S(2)}) collective-permute-start(bf16[128,2112]{0,1:T(8,128)(2,1)} %copy.244), channel_id=1, source_target_pairs={{0,2},{1,6},{2,3},{3,7},{4,0},{5,4},{6,1},{7,5},{8,10},{9,14},{10,... | collective-permute-start | bytes 1622024 | tf_op jit(solution)/shard_map/ppermute | solution.py:709
  104.0 9.3 %copy-start.44 = (s32[8]{0:T(128)S(1)}, s32[8]{0:T(128)}, u32[]{:S(2)}) copy-start(s32[8]{0:T(128)} %param.23) | copy-start | bytes 100
  104.0 11.8 %copy-start.43 = (s32[8]{0:T(128)S(1)}, s32[8]{0:T(128)}, u32[]{:S(2)}) copy-start(s32[8]{0:T(128)} %param.22) | copy-start | bytes 100
  104.0 13.0 %copy-start.31 = (bf16[256,1,1024]{2,0,1:T(8,128)(2,1)S(1)}, bf16[256,1,1024]{2,0,1:T(8,128)(2,1)}, u32[]{:S(2)}) copy-start(bf16[256,1,1024]{2,0,1:T(8,128)(2,1)} %param.39) | copy-start | bytes 1572868
  104.6 16.9 %copy-start.40 = (bf16[2,4]{1,0:T(2,128)(2,1)S(1)}, bf16[2,4]{1,0:T(2,128)(2,1)}, u32[]{:S(2)}) copy-start(bf16[2,4]{1,0:T(2,128)(2,1)} %param.32) | copy-start | bytes 52
  109.4 15.8 %all-to-all-start = ((bf16[8,2,16384]{2,1,0:T(2,128)(2,1)}), bf16[8,2,16384]{2,1,0:T(2,128)(2,1)S(1)}, u32[]{:S(2)}, u32[]{:S(2)}) async-start(bf16[8,2,16384]{2,1,0:T(2,128)(2,1)} %reshape.116), calls=%async_computation | async-start | bytes 1048576 | tf_op jit(solution)/shard_map/all_to_all | solution.py:731
  117.9 53.9 %collective-permute-start.10 = (bf16[256,1024]{1,0:T(8,128)(2,1)}, bf16[256,1024]{1,0:T(8,128)(2,1)S(1)}, u32[]{:S(2)}, u32[]{:S(2)}) collective-permute-start(bf16[256,1024]{1,0:T(8,128)(2,1)} %bitcast_multiply_fusion), channel_id=1, source_target_pairs={{0,0},{2,1},{16,2},{18,3},{1,4},{3,5},{17,6},{19,7},{4,8},{6,9},{2... | collective-permute-start | bytes 1572872 | tf_op jit(solution)/shard_map/ppermute | solution.py:768
  127.7 27.0 %copy-start.41 = (bf16[2,4]{1,0:T(2,128)(2,1)S(1)}, bf16[2,4]{1,0:T(2,128)(2,1)}, u32[]{:S(2)}) copy-start(bf16[2,4]{1,0:T(2,128)(2,1)} %param.31) | copy-start | bytes 52
  127.7 30.1 %copy-start.37 = (bf16[2,512]{1,0:T(2,128)(2,1)S(1)}, bf16[2,512]{1,0:T(2,128)(2,1)}, u32[]{:S(2)}) copy-start(bf16[2,512]{1,0:T(2,128)(2,1)} %param.33) | copy-start | bytes 6148
  127.7 37.8 %all-to-all-start.1 = ((bf16[256,8,128]{2,0,1:T(8,128)(2,1)}), bf16[256,8,128]{2,0,1:T(8,128)(2,1)S(1)}, u32[]{:S(2)}, u32[]{:S(2)}) async-start(bf16[256,8,128]{2,0,1:T(8,128)(2,1)} %select_bitcast_fusion.1), calls=%async_computation.1 | async-start | bytes 1048576 | tf_op jit(solution)/shard_map/all_to_all | solution.py:733
  153.6 18.2 %copy-start.35 = (bf16[2,1024]{1,0:T(2,128)(2,1)S(1)}, bf16[2,1024]{1,0:T(2,128)(2,1)}, u32[]{:S(2)}) copy-start(bf16[2,1024]{1,0:T(2,128)(2,1)} %param.24) | copy-start | bytes 12292
  153.6 241.0 %all-gather.11.cloned.1.call-start = ((), (), s32[]{:S(2)}) async-start(), calls=%async_computation.11 | async-start | bytes 5570560 | tf_op jit(solution)/shard_map/all_gather | solution.py:714
  153.6 18.3 %copy-start.36 = (bf16[2,1024]{1,0:T(2,128)(2,1)S(1)}, bf16[2,1024]{1,0:T(2,128)(2,1)}, u32[]{:S(2)}) copy-start(bf16[2,1024]{1,0:T(2,128)(2,1)} %param.35) | copy-start | bytes 12292
  154.7 608.8 %reduce-scatter.11.cloned.1.call-start = ((), (), s32[]{:S(2)}) async-start(), calls=%async_computation.15 | async-start | bytes 5570560 | tf_op jit(solution)/shard_map/reduce_scatter | solution.py:718
  165.6 37.0 %collective-permute-start = (bf16[256,1024]{1,0:T(8,128)(2,1)S(1)}, bf16[256,1024]{1,0:T(8,128)(2,1)S(1)}, u32[]{:S(2)}, u32[]{:S(2)}) collective-permute-start(bf16[256,1024]{1,0:T(8,128)(2,1)S(1)} %copy_bitcast_fusion), channel_id=1, source_target_pairs={{0,0},{2,1},{16,2},{18,3},{1,4},{3,5},{17,6},{19,7},{4,8},{6,9},{2... | collective-permute-start | bytes 1572872 | tf_op jit(solution)/shard_map/ppermute | solution.py:763
  171.8 30.8 %copy-start.13 = (f32[1,1024]{1,0:T(1,128)}, f32[1,1024]{1,0:T(1,128)S(1)}, u32[]{:S(2)}) copy-start(f32[1,1024]{1,0:T(1,128)S(1)} %get-tuple-element.278.gain_ref) | copy-start | bytes 12292
  421.4 347.7 %reduce-scatter.9.cloned.1.call-start = ((), (), s32[]{:S(2)}) async-start(), calls=%async_computation.14 | async-start | bytes 5570560 | tf_op jit(solution)/shard_map/reduce_scatter | solution.py:718
  488.9 32.2 %copy-start.27 = (bf16[1024,704]{1,0:T(8,128)(2,1)S(1)}, bf16[1024,704]{1,0:T(8,128)(2,1)}, u32[]{:S(2)}) copy-start(bf16[1024,704]{1,0:T(8,128)(2,1)} %copy-done.26) | copy-start | bytes 4325380
  524.4 8.4 copy-start.18
  539.4 237.0 %reduce-scatter.7.cloned.1.call-start = ((), (), s32[]{:S(2)}) async-start(), calls=%async_computation.13 | async-start | bytes 5570560 | tf_op jit(solution)/shard_map/reduce_scatter | solution.py:718
  552.0 7.8 copy-start.10
  552.0 227.0 %reduce-scatter.5.cloned.1.call-start = ((), (), s32[]{:S(2)}) async-start(), calls=%async_computation.12 | async-start | bytes 5570560 | tf_op jit(solution)/shard_map/reduce_scatter | solution.py:718
  592.1 27.6 %copy-start.4 = (bf16[1024,1024]{1,0:T(8,128)(2,1)S(1)}, bf16[1024,1024]{1,0:T(8,128)(2,1)}, u32[]{:S(2)}) copy-start(bf16[1024,1024]{1,0:T(8,128)(2,1)} %copy-done.3) | copy-start | bytes 6291460
  633.7 18.5 %copy-start.50 = (bf16[1024,704]{1,0:T(8,128)(2,1)S(1)}, bf16[1024,704]{1,0:T(8,128)(2,1)}, u32[]{:S(2)}) copy-start(bf16[1024,704]{1,0:T(8,128)(2,1)} %copy-done.49) | copy-start | bytes 4325380
  649.2 31.0 %collective-permute-start.11 = (bf16[256,1024]{1,0:T(8,128)(2,1)S(1)}, bf16[256,1024]{1,0:T(8,128)(2,1)S(1)}, u32[]{:S(2)}, u32[]{:S(2)}) collective-permute-start(bf16[256,1024]{1,0:T(8,128)(2,1)S(1)} %get-tuple-element.95), channel_id=1, source_target_pairs={{0,0},{1,2},{2,16},{3,18},{4,1},{5,3},{6,17},{7,19},{8,4},{9,6},{1... | collective-permute-start | bytes 1572872 | tf_op jit(solution)/shard_map/ppermute | solution.py:852
  677.0 84.3 %collective-permute-start.9 = (bf16[256,1024]{1,0:T(8,128)(2,1)S(1)}, bf16[256,1024]{1,0:T(8,128)(2,1)S(1)}, u32[]{:S(2)}, u32[]{:S(2)}) collective-permute-start(bf16[256,1024]{1,0:T(8,128)(2,1)S(1)} %forward_last.1), channel_id=1, source_target_pairs={{0,0},{1,2},{2,16},{3,18},{4,1},{5,3},{6,17},{7,19},{8,4},{9,6},{1... | collective-permute-start | bytes 1572872 | tf_op jit(solution)/shard_map/ppermute | solution.py:801
  681.1 10.3 %copy-start.38 = (f32[1,512]{1,0:T(1,128)S(1)}, f32[1,512]{1,0:T(1,128)}, u32[]{:S(2)}) copy-start(f32[1,512]{1,0:T(1,128)} %get-tuple-element.102) | copy-start | bytes 6148
  681.1 13.0 %copy-start.39 = (f32[1,512]{1,0:T(1,128)S(1)}, f32[1,512]{1,0:T(1,128)}, u32[]{:S(2)}) copy-start(f32[1,512]{1,0:T(1,128)} %get-tuple-element.98) | copy-start | bytes 6148
  685.9 19.7 %all-to-all-start.2 = ((bf16[8,2,16384]{2,1,0:T(2,128)(2,1)}), bf16[8,2,16384]{2,1,0:T(2,128)(2,1)S(1)}, u32[]{:S(2)}, u32[]{:S(2)}) async-start(bf16[8,2,16384]{2,1,0:T(2,128)(2,1)} %reshape.118), calls=%async_computation.2 | async-start | bytes 1048576 | tf_op jit(solution)/shard_map/all_to_all | solution.py:731
  708.0 53.3 %all-to-all-start.3 = ((bf16[256,8,128]{2,0,1:T(8,128)(2,1)}), bf16[256,8,128]{2,0,1:T(8,128)(2,1)S(1)}, u32[]{:S(2)}, u32[]{:S(2)}) async-start(bf16[256,8,128]{2,0,1:T(8,128)(2,1)} %select_bitcast_fusion), calls=%async_computation.3 | async-start | bytes 1048576 | tf_op jit(solution)/shard_map/all_to_all | solution.py:733
  765.8 14.5 %collective-permute-start.19 = (bf16[128,2112]{0,1:T(8,128)(2,1)}, bf16[128,2112]{0,1:T(8,128)(2,1)}, u32[]{:S(2)}, u32[]{:S(2)}) collective-permute-start(bf16[128,2112]{0,1:T(8,128)(2,1)} %copy.282), channel_id=1, source_target_pairs={{2,0},{6,1},{3,2},{7,3},{0,4},{4,5},{1,6},{5,7},{10,8},{14,9},{11,... | collective-permute-start | bytes 1622024 | tf_op jit(solution)/shard_map/ppermute | solution.py:724
  766.1 28.5 %collective-permute-start.18 = (bf16[128,2112]{0,1:T(8,128)(2,1)S(1)}, bf16[128,2112]{0,1:T(8,128)(2,1)}, u32[]{:S(2)}, u32[]{:S(2)}) collective-permute-start(bf16[128,2112]{0,1:T(8,128)(2,1)S(1)} %copy.281), channel_id=1, source_target_pairs={{0,0},{4,1},{1,2},{5,3},{2,4},{6,5},{3,6},{7,7},{8,8},{12,9},{9,10... | collective-permute-start | bytes 1622024 | tf_op jit(solution)/shard_map/ppermute | solution.py:724
  770.7 25.3 %collective-permute-start.17 = (bf16[128,2112]{0,1:T(8,128)(2,1)S(1)}, bf16[128,2112]{0,1:T(8,128)(2,1)}, u32[]{:S(2)}, u32[]{:S(2)}) collective-permute-start(bf16[128,2112]{0,1:T(8,128)(2,1)S(1)} %copy.279), channel_id=1, source_target_pairs={{2,0},{6,1},{3,2},{7,3},{0,4},{4,5},{1,6},{5,7},{10,8},{14,9},{11,... | collective-permute-start | bytes 1622024 | tf_op jit(solution)/shard_map/ppermute | solution.py:724
  773.6 44.2 %collective-permute-start.16 = (bf16[128,2112]{0,1:T(8,128)(2,1)S(1)}, bf16[128,2112]{0,1:T(8,128)(2,1)}, u32[]{:S(2)}, u32[]{:S(2)}) collective-permute-start(bf16[128,2112]{0,1:T(8,128)(2,1)S(1)} %copy.278), channel_id=1, source_target_pairs={{0,0},{4,1},{1,2},{5,3},{2,4},{6,5},{3,6},{7,7},{8,8},{12,9},{9,10... | collective-permute-start | bytes 1622024 | tf_op jit(solution)/shard_map/ppermute | solution.py:724
  777.8 44.1 %collective-permute-start.15 = (bf16[128,2176]{1,0:T(8,128)(2,1)S(1)}, bf16[128,2176]{1,0:T(8,128)(2,1)S(1)}, u32[]{:S(2)}, u32[]{:S(2)}) collective-permute-start(bf16[128,2176]{1,0:T(8,128)(2,1)S(1)} %get-tuple-element.236), channel_id=1, source_target_pairs={{2,0},{6,1},{3,2},{7,3},{0,4},{4,5},{1,6},{5,7},{10,8},{14,9},{11,... | collective-permute-start | bytes 1671176 | tf_op jit(solution)/shard_map/ppermute | solution.py:724
  780.4 61.1 %collective-permute-start.14 = (bf16[128,2176]{1,0:T(8,128)(2,1)S(1)}, bf16[128,2176]{1,0:T(8,128)(2,1)S(1)}, u32[]{:S(2)}, u32[]{:S(2)}) collective-permute-start(bf16[128,2176]{1,0:T(8,128)(2,1)S(1)} %get-tuple-element.235), channel_id=1, source_target_pairs={{0,0},{4,1},{1,2},{5,3},{2,4},{6,5},{3,6},{7,7},{8,8},{12,9},{9,10... | collective-permute-start | bytes 1671176 | tf_op jit(solution)/shard_map/ppermute | solution.py:724
  794.5 47.2 %collective-permute-start.13 = (bf16[128,2176]{1,0:T(8,128)(2,1)S(1)}, bf16[128,2176]{1,0:T(8,128)(2,1)S(1)}, u32[]{:S(2)}, u32[]{:S(2)}) collective-permute-start(bf16[128,2176]{1,0:T(8,128)(2,1)S(1)} %get-tuple-element.234), channel_id=1, source_target_pairs={{2,0},{6,1},{3,2},{7,3},{0,4},{4,5},{1,6},{5,7},{10,8},{14,9},{11,... | collective-permute-start | bytes 1671176 | tf_op jit(solution)/shard_map/ppermute | solution.py:724
  796.0 67.2 %collective-permute-start.12 = (bf16[128,2176]{1,0:T(8,128)(2,1)S(1)}, bf16[128,2176]{1,0:T(8,128)(2,1)S(1)}, u32[]{:S(2)}, u32[]{:S(2)}) collective-permute-start(bf16[128,2176]{1,0:T(8,128)(2,1)S(1)} %get-tuple-element.233), channel_id=1, source_target_pairs={{0,0},{4,1},{1,2},{5,3},{2,4},{6,5},{3,6},{7,7},{8,8},{12,9},{9,10... | collective-permute-start | bytes 1671176 | tf_op jit(solution)/shard_map/ppermute | solution.py:724
  (38 other events, 89.8 us)
Sparse Core Ops, SparseCore 0:
  46.5 83.7 all-gather.4
  132.2 78.0 all-gather.8
  212.1 58.8 all-gather.6
  272.7 54.8 all-gather.10
  421.5 55.7 reduce-scatter.10
  539.6 54.7 reduce-scatter.8
  597.4 54.8 reduce-scatter.6
  655.3 80.9 reduce-scatter.4

commit v3 on v2

--- a/solution.py
+++ b/solution.py
@@ -102,12 +102,16 @@
 
 
 def forward_kernel(
-    scalars_ref, x_ref, w_in_ref, w_aux_ref, w_out_ref, taps_ref, gain_ref,
+    chips, scalars_ref, x_ref, w_in_ref, w_aux_ref, w_out_ref, taps_ref, gain_ref, pack_ref,
     part_ref, heads_ref, proj_ref, gate_ref, rates_ref, inverse_ref, fresh_ref, o_ref, state_ref,
-    padded, memory,
+    wide_ref, padded, memory, send, recv,
 ):
+    weights = Weights(pack_ref, wide_ref, send, recv, chips)
+
     @pl.when(pl.program_id(0) == 0)
     def _():
+        wait_greetings(weights.greet())
+        weights.start()
         memory[...] = jnp.zeros_like(memory)
         padded[0:8, :] = jnp.zeros((8, CONV_CH), F32)
 
@@ -147,15 +151,19 @@
     heads_ref[...] = heads
     part_ref[...] = mm(heads, w_out_ref[...], NT).astype(BF16)
 
-
-def mixer_forward(x, pack, taps, gain, scalars):
+    @pl.when(pl.program_id(0) == pl.num_programs(0) - 1)
+    def _():
+        weights.finish()
+
+
+def mixer_forward(x, pack, taps, gain, scalars, moved, chips, number):
     length, width = x.shape
     chunks = length // CHUNK
     row = lambda cols: pl.BlockSpec((CHUNK, cols), lambda i: (i, 0))
     fixed = lambda shape, at: pl.BlockSpec(shape, lambda i: (0, at), pipeline_mode=pl.Buffered(1))
     out = lambda cols, kind: jax.ShapeDtypeStruct((length, cols), kind)
     return pl.pallas_call(
-        forward_kernel,
+        functools.partial(forward_kernel, chips),
         grid=(chunks,),
         in_specs=[
             pl.BlockSpec(memory_space=pltpu.SMEM),
@@ -165,25 +173,32 @@
             fixed((width, VAL), 3),
             fixed((4, CONV_CH), 0),
             fixed((1, VAL), 0),
+            pl.BlockSpec(memory_space=pl.ANY),
         ],
         out_specs=[
             row(width), row(VAL), row(CONV_CH), row(VAL), row(LANES), row(CHUNK), row(VAL), row(VAL),
             pl.BlockSpec((None, KEY, VAL), lambda i: (i, 0, 0)),
+            pl.BlockSpec(memory_space=pl.ANY),
         ],
         out_shape=[
             out(width, BF16), out(VAL, BF16), out(CONV_CH, F32), out(VAL, F32), out(LANES, F32),
             out(CHUNK, BF16), out(VAL, F32), out(VAL, F32),
             jax.ShapeDtypeStruct((chunks, KEY, VAL), F32),
+            jax.ShapeDtypeStruct((2 * moved.shape[0], moved.shape[1]), BF16),
         ],
-        scratch_shapes=[pltpu.VMEM((CHUNK + 8, CONV_CH), F32), pltpu.VMEM((KEY, VAL), F32)],
+        scratch_shapes=[
+            pltpu.VMEM((CHUNK + 8, CONV_CH), F32), pltpu.VMEM((KEY, VAL), F32),
+            pltpu.SemaphoreType.DMA((3,)), pltpu.SemaphoreType.DMA((2,)),
+        ],
         compiler_params=pltpu.CompilerParams(
-            dimension_semantics=("arbitrary",), vmem_limit_bytes=56 * 1024 * 1024
+            dimension_semantics=("arbitrary",), vmem_limit_bytes=56 * 1024 * 1024,
+            collective_id=number, has_side_effects=True,
         ),
         cost_estimate=pl.CostEstimate(
             flops=16 * 10**9, bytes_accessed=80 * 10**6, transcendentals=4 * 10**6
         ),
         name="mixer_forward",
-    )(scalars, x, pack, pack, pack, taps, gain)
+    )(scalars, x, pack, pack, pack, taps, gain, moved)
 
 
 def unit_back(grad, vector, scale):
@@ -635,18 +650,386 @@
     )
 
 
-def gather_plain_kernel(x_ref, out_ref, send, recv):
-    greet()
+def place(chips):
+    chip, core, zp, zl = (lax.axis_index(name) for name in AXES)
+    return chip, core, zp, zl, chip * 2 + core
+
+
+def at_device(chip, core, zp, zl):
+    return {"chip": chip, "core": core, "zp": zp, "zl": zl}
+
+
+def signal(device):
+    pl.semaphore_signal(
+        pltpu.get_barrier_semaphore(), inc=1, device_id=device,
+        device_id_type=pl.DeviceIdType.MESH,
+    )
+
+
+def unless(condition, action):
+    pl.when(jnp.logical_not(condition))(action)
+
+
+class Weights:
+    def __init__(self, source, target, send, recv, chips):
+        chip, core, zp, zl, _ = place(chips)
+        rows = source.shape[0]
+        at = pl.ds(pl.multiple_of(core * rows, rows), rows)
+        self.fixed = (zp == zl) & (zl == core)
+        self.mine = [self.fixed & (zp == to) for to in range(2)]
+        self.targets = [at_device(chip, zl, to, zp) for to in range(2)]
+        self.sources = [at_device(chip, co, zl, core) for co in range(2)]
+        self.source_mine = [self.fixed & (core == co) for co in range(2)]
+        self.copies = [
+            remote(source, target.at[at], send.at[to], recv.at[core], self.targets[to])
+            for to in range(2)
+        ]
+        self.arrivals = [
+            remote(source, target.at[pl.ds(co * rows, rows)], send.at[0], recv.at[co], self.sources[co])
+            for co in range(2)
+        ]
+        self.local = pltpu.make_async_copy(source, target.at[at], send.at[2])
+
+    def greet(self):
+        for device, mine in zip(self.sources, self.source_mine):
+            unless(mine, functools.partial(signal, device))
+        return 2 - self.fixed.astype(jnp.int32)
+
+    def start(self):
+        for copy, mine in zip(self.copies, self.mine):
+            unless(mine, copy.start)
+        pl.when(self.fixed)(self.local.start)
+
+    def finish(self):
+        for arrival, mine in zip(self.arrivals, self.source_mine):
+            unless(mine, arrival.wait_recv)
+        for copy, mine in zip(self.copies, self.mine):
+            unless(mine, copy.wait_send)
+        pl.when(self.fixed)(self.local.wait)
+
+
+class Plane:
+    def __init__(self, chips):
+        self.count = 2 * chips
+        _, _, self.zp, self.zl, self.own = place(chips)
+
+    def device(self, index):
+        return at_device(index // 2, index % 2, self.zp, self.zl)
+
+    def to(self, j):
+        return lax.rem(self.own + j, self.count)
+
+    def source(self, j):
+        return lax.rem(self.own + self.count - j, self.count)
+
+    def greet(self):
+        for j in range(1, self.count):
+            signal(self.device(self.to(j)))
+        return self.count - 1
+
+
+class Trade:
+    def __init__(self, chips):
+        self.chips, self.count = chips, 2 * chips
+        self.chip, self.core, self.zp, self.zl, self.own = place(chips)
+        self.fixed = (self.zp == self.zl) & (self.zl == self.core)
+        self.slot = self.zp * chips + self.chip
+
+    def role(self, slot):
+        return at_device(slot % self.chips, self.zl, slot // self.chips, self.zp)
+
+    def role_mine(self, slot):
+        return self.fixed & (self.slot == slot)
+
+    def home(self, index):
+        return at_device(index // 2, index % 2, self.zl, self.core)
+
+    def home_mine(self, index):
+        return self.fixed & (self.own == index)
+
+    def greet_homes(self):
+        for index in range(self.count):
+            unless(self.home_mine(index), functools.partial(signal, self.home(index)))
+        return self.count - self.fixed.astype(jnp.int32)
+
+    def greet_roles(self):
+        for slot in range(self.count):
+            unless(self.role_mine(slot), functools.partial(signal, self.role(slot)))
+        return self.count - self.fixed.astype(jnp.int32)
+
+
+def greet_group():
+    _, _, beside, across = partners()
+    signal(beside)
+    signal(across)
+    return 2
+
+
+def wait_greetings(count):
+    pl.semaphore_wait(pltpu.get_barrier_semaphore(), count)
+
+
+def deal_kernel(
+    chips, order_ref, x_ref, gain_ref, pack_ref, next_ref, new_ref, out_ref, wide_ref, wide_next_ref,
+    spread, picked, send, recv, weight_send, weight_recv, next_send, next_recv, plane_send, plane_recv, role_send, role_recv,
+):
+    plane, trade = Plane(chips), Trade(chips)
+    weights = Weights(pack_ref, wide_ref, weight_send, weight_recv, chips)
+    weights_next = Weights(next_ref, wide_next_ref, next_send, next_recv, chips)
     gather = Gather(out_ref, send, recv, 0)
+    count = plane.count
+    part = x_ref.shape[0] // count
+    rows = lambda index: pl.ds(pl.multiple_of(index * part, part), part)
+    wait_greetings(plane.greet() + trade.greet_homes() + weights.greet() + greet_group())
+    outward, inward = [], []
+    for j in range(1, count):
+        to, source = plane.to(j), plane.source(j)
+        outward.append(
+            remote(x_ref.at[rows(to)], spread.at[plane.own], plane_send.at[j], plane_recv.at[j],
+                   plane.device(to))
+        )
+        inward.append(
+            remote(x_ref.at[rows(to)], spread.at[source], plane_send.at[j], plane_recv.at[j],
+                   plane.device(source))
+        )
+    for copy in outward:
+        copy.start()
+    weights.start()
+    weights_next.start()
+    spread[plane.own] = x_ref[rows(plane.own), :]
+    for copy in inward:
+        copy.wait_recv()
+    to_roles = []
+    for slot in range(count):
+        picked[slot] = spread[order_ref[slot]]
+        copy = remote(picked.at[slot], new_ref.at[rows(plane.own)], role_send.at[slot],
+                      role_recv.at[plane.own], trade.role(slot))
+        mine = trade.role_mine(slot)
+        unless(mine, copy.start)
+
+        @pl.when(mine)
+        def _():
+            new_ref[rows(plane.own), :] = picked[slot]
+
+        to_roles.append((copy, mine))
     size = x_ref.shape[0] // PIECES
+    parts = max(size // part, 1)
     for p in range(PIECES):
-        gather.put(p, x_ref[p * size : (p + 1) * size, :])
+        for index in range(p * parts, (p + 1) * parts):
+            arrival = remote(picked.at[0], new_ref.at[rows(index)], role_send.at[0],
+                             role_recv.at[index], trade.home(index))
+            unless(trade.home_mine(index), arrival.wait_recv)
+        x = new_ref[p * size : (p + 1) * size, :].astype(F32)
+        gather.put(p, normed_of(x, gain_ref[...]).astype(BF16))
+    for copy in outward:
+        copy.wait_send()
+    for copy, mine in to_roles:
+        unless(mine, copy.wait_send)
     gather.finish()
-
-
-def gather_plain(x):
+    weights.finish()
+    weights_next.finish()
+
+
+def deal_and_gather(order, x, gain, pack, pack_next, chips):
     rows, width = x.shape
-    return comm_call(gather_plain_kernel, 5, [((4 * rows, width), BF16)], (x,), 0, 1)[0]
+    vmem = pl.BlockSpec(memory_space=pltpu.VMEM)
+    hbm = pl.BlockSpec(memory_space=pl.ANY)
+    count = 2 * chips
+    buffer = pltpu.VMEM((count, rows // count, width), BF16)
+    sems = lambda *shape: [pltpu.SemaphoreType.DMA(shape), pltpu.SemaphoreType.DMA(shape)]
+    return pl.pallas_call(
+        functools.partial(deal_kernel, chips),
+        in_specs=[pl.BlockSpec(memory_space=pltpu.SMEM), vmem, vmem, hbm, hbm],
+        out_specs=[vmem, vmem, hbm, hbm],
+        out_shape=[
+            jax.ShapeDtypeStruct((rows, width), BF16),
+            jax.ShapeDtypeStruct((4 * rows, width), BF16),
+            jax.ShapeDtypeStruct((2 * pack.shape[0], pack.shape[1]), BF16),
+            jax.ShapeDtypeStruct((2 * pack_next.shape[0], pack_next.shape[1]), BF16),
+        ],
+        scratch_shapes=[buffer, buffer]
+        + sems(3, PIECES) + sems(3) + sems(3) + sems(count) + sems(count),
+        compiler_params=pltpu.CompilerParams(
+            collective_id=20, has_side_effects=True, vmem_limit_bytes=48 * 1024 * 1024
+        ),
+        cost_estimate=pl.CostEstimate(
+            flops=rows * width * 20, bytes_accessed=100 * 1024 * 1024, transcendentals=0
+        ),
+        name="deal_and_gather",
+    )(order, x, gain, pack, pack_next)
+
+
+def final_kernel(
+    chips, inverse_ref, partial, x_ref, gain_ref, grad_ref, small_ref, home_ref, total_ref,
+    beside_far, beside_own, sums, far, last, back, picked, small, by_plane, by_z, plane_sum,
+    send, recv, role_send, role_recv, plane_send, plane_recv, small_send, small_recv, z_send, z_recv,
+):
+    plane, trade = Plane(chips), Trade(chips)
+    count = plane.count
+    part = x_ref.shape[0] // count
+    rows = lambda index: pl.ds(pl.multiple_of(index * part, part), part)
+    tier = trade.zp * 2 + trade.zl
+    tier_device = lambda at: at_device(trade.chip, trade.core, at // 2, at % 2)
+    for k in range(1, 4):
+        signal(tier_device(lax.rem(tier + k, 4)))
+    wait_greetings(plane.greet() + trade.greet_roles() + greet_group() + 3)
+    scatter = Scatter(partial, beside_far, beside_own, sums, far, send, recv)
+    scatter.start()
+    dgain = jnp.zeros_like(gain_ref)
+    to_homes = []
+    size = x_ref.shape[0] // PIECES
+    parts = max(size // part, 1)
+    for p in range(PIECES):
+        at = scatter.local(p)
+        grad, piece = norm_back(scatter.total(p), x_ref[at, :].astype(F32), gain_ref[...])
+        dgain = dgain + piece
+        last[at, :] = (grad + grad_ref[at, :]).astype(BF16)
+        for index in range(p * parts, (p + 1) * parts):
+            copy = remote(last.at[rows(index)], back.at[trade.slot], role_send.at[index],
+                          role_recv.at[trade.slot], trade.home(index))
+            mine = trade.home_mine(index)
+            unless(mine, copy.start)
+
+            @pl.when(mine)
+            def _():
+                back[trade.slot] = last[rows(index), :]
+
+            to_homes.append((copy, mine))
+    small[...] = small_ref[...]
+    for r in range(x_ref.shape[1] // LANES):
+        small[r : r + 1, :] = dgain[:, r * LANES : (r + 1) * LANES]
+    small_out, small_in = [], []
+    for j in range(1, count):
+        to, source = plane.to(j), plane.source(j)
+        small_out.append(
+            remote(small, by_plane.at[plane.own], small_send.at[j], small_recv.at[j], plane.device(to))
+        )
+        small_in.append(
+            remote(small, by_plane.at[source], small_send.at[j], small_recv.at[j], plane.device(source))
+        )
+    for copy in small_out:
+        copy.start()
+    by_plane[plane.own] = small[...]
+    for slot in range(count):
+        arrival = remote(last.at[rows(0)], back.at[slot], role_send.at[0], role_recv.at[slot],
+                         trade.role(slot))
+        unless(trade.role_mine(slot), arrival.wait_recv)
+    outward, inward = [], []
+    for j in range(count):
+        to, source = plane.to(j), plane.source(j)
+        picked[j] = back[inverse_ref[to]]
+        if j == 0:
+            home_ref[rows(plane.own), :] = picked[0]
+            continue
+        copy = remote(picked.at[j], home_ref.at[rows(plane.own)], plane_send.at[j], plane_recv.at[j],
+                      plane.device(to))
+        copy.start()
+        outward.append(copy)
+        inward.append(
+            remote(picked.at[j], home_ref.at[rows(source)], plane_send.at[j], plane_recv.at[j],
+                   plane.device(source))
+        )
+    for copy in small_in:
+        copy.wait_recv()
+    total = by_plane[0]
+    for index in range(1, count):
+        total = total + by_plane[index]
+    plane_sum[...] = total
+    z_out, z_in = [], []
+    for k in range(1, 4):
+        to, source = lax.rem(tier + k, 4), lax.rem(tier + 4 - k, 4)
+        z_out.append(remote(plane_sum, by_z.at[tier], z_send.at[k], z_recv.at[k], tier_device(to)))
+        z_in.append(remote(plane_sum, by_z.at[source], z_send.at[k], z_recv.at[k], tier_device(source)))
+    for copy in z_out:
+        copy.start()
+    by_z[tier] = total
+    for copy in z_in:
+        copy.wait_recv()
+    total_ref[...] = (by_z[0] + by_z[1]) + (by_z[2] + by_z[3])
+    for copy in inward:
+        copy.wait_recv()
+    scatter.finish()
+    for copy, mine in to_homes:
+        unless(mine, copy.wait_send)
+    for copy in small_out + z_out + outward:
+        copy.wait_send()
+
+
+def final_step(inverse, partial, x, gain, grad, small, chips):
+    rows, width = x.shape
+    vmem = pl.BlockSpec(memory_space=pltpu.VMEM)
+    count = 2 * chips
+    block = pltpu.VMEM((rows, width), BF16)
+    parted = pltpu.VMEM((count, rows // count, width), BF16)
+    sems = lambda *shape: [pltpu.SemaphoreType.DMA(shape), pltpu.SemaphoreType.DMA(shape)]
+    return pl.pallas_call(
+        functools.partial(final_kernel, chips),
+        in_specs=[pl.BlockSpec(memory_space=pltpu.SMEM)] + [vmem] * 5,
+        out_specs=[vmem, vmem],
+        out_shape=[
+            jax.ShapeDtypeStruct((rows, width), BF16),
+            jax.ShapeDtypeStruct(small.shape, F32),
+        ],
+        scratch_shapes=[block] * 5 + [parted] * 2
+        + [
+            pltpu.VMEM(small.shape, F32), pltpu.VMEM((count,) + small.shape, F32),
+            pltpu.VMEM((4,) + small.shape, F32), pltpu.VMEM(small.shape, F32),
+        ]
+        + sems(3, PIECES) + sems(count) + sems(count) + sems(count) + sems(4),
+        compiler_params=pltpu.CompilerParams(
+            collective_id=21, has_side_effects=True, vmem_limit_bytes=48 * 1024 * 1024
+        ),
+        cost_estimate=pl.CostEstimate(
+            flops=rows * width * 20, bytes_accessed=100 * 1024 * 1024, transcendentals=0
+        ),
+        name="final_step",
+    )(inverse, partial, x, gain, grad, small)
+
+
+def weights_back_kernel(chips, grads_ref, out_ref, halves, send, recv):
+    chip, core, zp, zl, _ = place(chips)
+    rows = out_ref.shape[0]
+    fixed = (zp == zl) & (zl == core)
+    sources = [at_device(chip, zl, at, zp) for at in range(2)]
+    source_mine = [fixed & (zp == at) for at in range(2)]
+    for device, mine in zip(sources, source_mine):
+        unless(mine, functools.partial(signal, device))
+    wait_greetings(2 - fixed.astype(jnp.int32))
+    sent = []
+    for co in range(2):
+        mine = fixed & (core == co)
+        src = grads_ref.at[pl.ds(co * rows, rows)]
+        copy = remote(src, halves.at[zp], send.at[co], recv.at[zp], at_device(chip, co, zl, core))
+        local = pltpu.make_async_copy(src, halves.at[zp], send.at[2])
+        unless(mine, copy.start)
+        pl.when(mine)(local.start)
+        sent.append((copy, local, mine))
+    for at in range(2):
+        arrival = remote(grads_ref.at[pl.ds(0, rows)], halves.at[at], send.at[0], recv.at[at], sources[at])
+        unless(source_mine[at], arrival.wait_recv)
+    for copy, local, mine in sent:
+        unless(mine, copy.wait_send)
+        pl.when(mine)(local.wait)
+    out_ref[...] = halves[0].astype(F32) + halves[1].astype(F32)
+
+
+def weights_back(grads, chips):
+    rows, width = grads.shape
+    return pl.pallas_call(
+        functools.partial(weights_back_kernel, chips),
+        in_specs=[pl.BlockSpec(memory_space=pl.ANY)],
+        out_specs=pl.BlockSpec(memory_space=pltpu.VMEM),
+        out_shape=jax.ShapeDtypeStruct((rows // 2, width), F32),
+        scratch_shapes=[
+            pltpu.VMEM((2, rows // 2, width), BF16),
+            pltpu.SemaphoreType.DMA((3,)), pltpu.SemaphoreType.DMA((2,)),
+        ],
+        compiler_params=pltpu.CompilerParams(
+            collective_id=22, has_side_effects=True, vmem_limit_bytes=48 * 1024 * 1024
+        ),
+        cost_estimate=pl.CostEstimate(flops=0, bytes_accessed=60 * 1024 * 1024, transcendentals=0),
+        name="weights_back",
+    )(grads)
 
 
 def swiglu_rows(paired):
@@ -705,17 +1088,28 @@
     return [(b, a) for a, b in pairs]
 
 
+def tie(value, after):
+    return lax.optimization_barrier((value, after))[0]
+
+
+def chip_gather(ordered):
+    return row_major(lax.all_gather(row_major(ordered), "chip", axis=0, tiled=True))
+
+
 def weights_in(pack, roles):
     halves = [lax.ppermute(pack, AXES, roles.weight_pairs(which)) for which in range(2)]
     swap = lax.axis_index("zp") == 1
     ordered = jnp.concatenate(
         [jnp.where(swap, halves[1], halves[0]), jnp.where(swap, halves[0], halves[1])], axis=0
     )
-    return row_major(lax.all_gather(row_major(ordered), "chip", axis=0, tiled=True))
-
-
-def weights_out(grads, roles):
-    mine = lax.psum_scatter(grads, "chip", scatter_dimension=0, tiled=True)
+    return chip_gather(ordered)
+
+
+def chip_scatter(grads):
+    return lax.psum_scatter(grads, "chip", scatter_dimension=0, tiled=True)
+
+
+def weights_home(mine, roles):
     rows = mine.shape[0] // 2
     swap = lax.axis_index("zp") == 1
     low, high = mine[:rows], mine[rows:]
@@ -725,6 +1119,10 @@
         for which, half in enumerate(halves)
     ]
     return back[0].astype(F32) + back[1].astype(F32)
+
+
+def together(*values):
+    return lax.optimization_barrier(values)
 
 
 def deal(values, order):
@@ -757,23 +1155,41 @@
             [w_query[layer], w_key[layer], w_value[layer], w_gate[layer], w_out[layer].T, aux], axis=1
         )
         ffn = jnp.concatenate([w_ffn_gate[layer], w_ffn_up[layer], w_ffn_down[layer].T], axis=1)
-        packs.append((weights_in(row_major(mix), roles), weights_in(row_major(ffn), roles)))
-
-    dealt = deal(tokens, order)[:, 0, :]
-    residual = lax.ppermute(dealt, AXES, to_roles)
-
-    positions = (zp * 2 + zl) * rows_local + jnp.arange(rows_local)
-    my_length = lengths[order[chip * 2 + core]]
-    start = cotangent[:, 0, :] * (positions < my_length).astype(BF16)[:, None]
-    gradient = lax.ppermute(start, AXES, to_roles)
-    grad_rows = gather_plain(gradient)
-
-    saved = []
+        packs.append([row_major(mix), row_major(ffn)])
     gains = [
         (norm_mix[layer].astype(F32)[None], norm_ffn[layer].astype(F32)[None])
         for layer in range(layer_count)
     ]
-    rows_in = first_gather(residual, gains[0][0])
+    inverse_order = jnp.sum(
+        jnp.where(
+            order[None, :] == jnp.arange(slot_total, dtype=jnp.int32)[:, None],
+            jnp.arange(slot_total, dtype=jnp.int32)[None, :],
+            0,
+        ),
+        axis=1,
+    ).astype(jnp.int32)
+    kernel_deal = rows_local % (16 * slot_total) == 0
+    if kernel_deal:
+        residual, rows_in, ordered, ordered_ffn = deal_and_gather(
+            order, tokens[:, 0, :], gains[0][0], packs[0][0], packs[0][1], roles.chips
+        )
+        packs[0][0] = chip_gather(ordered)
+        packs[0][1] = chip_gather(ordered_ffn)
+    else:
+        dealt = deal(tokens, order)[:, 0, :]
+        residual = lax.ppermute(dealt, AXES, to_roles)
+        rows_in = first_gather(residual, gains[0][0])
+        packs[0][0] = weights_in(packs[0][0], roles)
+        packs[0][1] = weights_in(tie(packs[0][1], rows_in), roles)
+
+    positions = (zp * 2 + zl) * rows_local + jnp.arange(rows_local)
+    my_slot = jnp.sum(jnp.where(jnp.arange(slot_total) == chip * 2 + core, order, 0))
+    my_length = jnp.sum(jnp.where(jnp.arange(slot_total) == my_slot, lengths, 0))
+    start = cotangent[:, 0, :] * (positions < my_length).astype(BF16)[:, None]
+    gradient = lax.ppermute(tie(start, rows_in), AXES, to_roles)
+    grad_rows = lax.all_gather(gradient, ("zl", "core"), axis=0, tiled=True)
+
+    saved = []
     for layer in range(layer_count):
         mix, ffn = packs[layer]
         taps = mix[:, 2050:2054].T.astype(F32)
@@ -784,7 +1200,12 @@
                 lax.dynamic_slice_in_dim(step_bias[layer].astype(F32), head, 1),
             ]
         )
-        part, heads, *kept = mixer_forward(rows_in, mix, taps, gain_heads, scalars)
+        member = layer
+        part, heads, *kept, ordered = mixer_forward(
+            rows_in, mix, taps, gain_heads, scalars, packs[1][member], roles.chips, 30 + member
+        )
+        packs[1][member] = chip_gather(ordered)
+        ffn = packs[layer][1]
         middle, rows_ffn = forward_bridge(part, residual, gains[layer][1])
         paired = dot32(rows_ffn, ffn[:, : 2 * units], NN)
         hidden, swiglu_back = jax.vjp(swiglu_rows, paired)
@@ -797,11 +1218,13 @@
         if layer + 1 < layer_count:
             residual, rows_in = forward_bridge(part, middle, gains[layer + 1][0])
         else:
-            mixed = forward_last(part, middle)
+            total = lax.psum_scatter(part, ("zl", "core"), scatter_dimension=0, tiled=True)
+            mixed = (middle + total.astype(F32)).astype(BF16)
     mixed = lax.ppermute(mixed, AXES, flipped(to_roles))
 
-    weight_grads = [None] * layer_count
     small_terms = [None] * layer_count
+    scattered = [[None] * 3 for _ in range(layer_count)]
+    homed = [[None] * 3 for _ in range(layer_count)]
     for layer in reversed(range(layer_count)):
         mix, ffn = packs[layer]
         (residual, rows_in, taps, gain_heads, scalars, kept, heads, middle, rows_ffn,
@@ -813,59 +1236,94 @@
             [dot32(rows_ffn, paired_low, TN).astype(BF16), dot32(grad_rows, hidden, TN).astype(BF16)],
             axis=1,
         )
-        ffn_grads = weights_out(ffn_grads, roles)
+        part, ffn_grads = together(part, ffn_grads)
+        scattered[layer][2] = chip_scatter(ffn_grads)
+        if layer + 1 < layer_count:
+            part, scattered[layer + 1][0], scattered[layer + 1][1] = together(
+                part, scattered[layer + 1][0], scattered[layer + 1][1]
+            )
         gradient, grad_rows, dgain_ffn = backward_bridge(part, middle, gains[layer][1], gradient)
+        out_grads = dot32(grad_rows, heads, TN).astype(BF16)
+        grad_rows, out_grads = together(grad_rows, out_grads)
+        scattered[layer][1] = chip_scatter(out_grads)
+        if layer + 1 < layer_count:
+            for member in range(3):
+                homed[layer + 1][member] = weights_home(scattered[layer + 1][member], roles)
         part, dproj, drates, dtaps, dgain, dscalars = mixer_backward(
             grad_rows, mix, taps, gain_heads, scalars, kept
         )
         aux = dot32(rows_in, drates, TN) + jnp.pad(dtaps.T, ((0, 0), (2, LANES - 6)))
-        mix_grads = jnp.concatenate(
-            [
-                dot32(rows_in, dproj, TN).astype(BF16),
-                dot32(grad_rows, heads, TN).astype(BF16),
-                aux.astype(BF16),
-            ],
-            axis=1,
-        )
-        mix_grads = weights_out(mix_grads, roles)
+        in_grads = jnp.concatenate(
+            [dot32(rows_in, dproj, TN).astype(BF16), aux.astype(BF16)], axis=1
+        )
+        part, in_grads, scattered[layer][1], scattered[layer][2] = together(
+            part, in_grads, scattered[layer][1], scattered[layer][2]
+        )
+        if layer + 1 < layer_count:
+            part, *homed[layer + 1] = together(part, *homed[layer + 1])
+        scattered[layer][0] = chip_scatter(in_grads)
+        mine = (jnp.arange(heads_total) == head).astype(F32)
+        small_terms[layer] = [
+            dgain_ffn[0], dgain[0], mine * dscalars[0, 0], mine * dscalars[1, 0]
+        ]
         if layer:
             gradient, grad_rows, dgain_mix = backward_bridge(part, residual, gains[layer][0], gradient)
-        else:
-            gradient, dgain_mix = backward_last(part, residual, gains[layer][0], gradient)
-        weight_grads[layer] = (
-            mix_grads[:, :256],
-            mix_grads[:, 256:512],
-            mix_grads[:, 512:1024],
-            mix_grads[:, 1024:1536],
-            mix_grads[:, 2048:2050].reshape(rows_part, 1, 2),
-            mix_grads[:, 2050:2054].T.reshape(4, 1, rows_part),
-            mix_grads[:, 1536:2048].T,
-            ffn_grads[:, :units],
-            ffn_grads[:, units : 2 * units],
-            ffn_grads[:, 2 * units :].T,
-        )
-        mine = (jnp.arange(heads_total) == head).astype(F32)
-        small_terms[layer] = jnp.concatenate(
-            [dgain_mix[0], dgain_ffn[0], dgain[0], mine * dscalars[0, 0], mine * dscalars[1, 0]]
-        )
-    small = lax.psum(jnp.stack(small_terms), AXES)
-    dealt_grad = lax.ppermute(gradient, AXES, flipped(to_roles))
-    inverse_order = (
-        jnp.zeros((slot_total,), jnp.int32).at[order].set(jnp.arange(slot_total, dtype=jnp.int32))
-    )
-    grad_home = deal(dealt_grad[:, None, :], inverse_order).astype(F32)
+            small_terms[layer].insert(0, dgain_mix[0])
+    small_terms[0].insert(0, jnp.zeros((width,), F32))
+    flat = jnp.concatenate(
+        [small_terms[layer][member] for member in range(5) for layer in range(layer_count)]
+    )
+    flat = jnp.pad(flat, (0, -flat.shape[0] % (8 * LANES))).reshape(-1, LANES)
+    if kernel_deal:
+        home, flat = final_step(
+            inverse_order, part, residual, gains[0][0], gradient, flat, roles.chips
+        )
+        grad_home = home[:, None, :].astype(F32)
+    else:
+        gradient, dgain_mix = backward_last(part, residual, gains[0][0], gradient)
+        flat = flat.at[: width // LANES].set(dgain_mix.reshape(-1, LANES))
+        flat = lax.psum(flat, AXES)
+        dealt_grad = lax.ppermute(gradient, AXES, flipped(to_roles))
+        grad_home = deal(dealt_grad[:, None, :], inverse_order).astype(F32)
+    flat = flat.reshape(-1)
+    if kernel_deal:
+        scattered[0][0], _ = together(scattered[0][0], home)
+        homed[0][0] = weights_back(scattered[0][0], roles.chips)
+    else:
+        homed[0][0] = weights_home(scattered[0][0], roles)
+    for member in (1, 2):
+        homed[0][member] = weights_home(scattered[0][member], roles)
+    weight_grads = []
+    for in_grads, out_grads, ffn_grads in homed:
+        weight_grads.append(
+            (
+                in_grads[:, :256],
+                in_grads[:, 256:512],
+                in_grads[:, 512:1024],
+                in_grads[:, 1024:1536],
+                in_grads[:, 1536:1538].reshape(rows_part, 1, 2),
+                in_grads[:, 1538:1542].T.reshape(4, 1, rows_part),
+                out_grads.T,
+                ffn_grads[:, :units],
+                ffn_grads[:, units : 2 * units],
+                ffn_grads[:, 2 * units :].T,
+            )
+        )
+    small, at = [], 0
+    for size in (width, width, VAL, heads_total, heads_total):
+        small.append(flat[at : at + layer_count * size].reshape(layer_count, size))
+        at += layer_count * size
     members = [jnp.stack([grads[m] for grads in weight_grads]) for m in range(10)]
-    ends = 2 * width + VAL
     return (
         mixed[:, None, :],
         grad_home,
-        small[:, :width],
+        small[0],
         members[0], members[1], members[2], members[3], members[4], members[5],
-        small[:, ends : ends + heads_total],
-        small[:, ends + heads_total :],
-        small[:, 2 * width : ends],
+        small[3],
+        small[4],
+        small[2],
         members[6],
-        small[:, width : 2 * width],
+        small[1],
         members[7], members[8], members[9],
     )
 

time: 888 us -> 898 us (1.011)
  the two profiles are of different devices: /device:TPU:1 before, /device:TPU:0 now
where the time goes in v3:
time: 898 us; the launch traced here: 883 us
  Pallas kernels  483 us (54%)
  waiting for transfers between devices  142 us (16%)
  matrix products  85.6 us (10%)
  local copies, waits for them, and re-layouts  63.4 us (7%)
  other arithmetic  46.7 us (5%)
  starting transfers between devices  45.7 us (5%)
  between operations  15.4 us (2%)
    pallas_call x6, Pallas kernels, comm_call(): pl.pallas_call(kernel, in_specs=[vmem] * len(args), out_specs=[vmem] * le...  222 us
    dot_general x18, matrix products, dot32(): return lax.dot_general(a, b, dims, preferred_element_type=F32)  85.6 us
    pallas_call x1, Pallas kernels, deal_and_gather(): pl.pallas_call(functools.partial(deal_kernel, chips), in_specs=[pl.BlockS...  74.7 us
    pallas_call x2, Pallas kernels, mixer_forward(): pl.pallas_call(functools.partial(forward_kernel, chips), grid=(chunks,),...  67.6 us
    pallas_call x2, Pallas kernels, mixer_backward(): pl.pallas_call(backward_kernel, grid=(chunks,), in_specs=[pl.BlockSpec(me...  55.4 us
    all_gather x4, waiting for transfers between devices, chip_gather(): lax.all_gather(row_major(ordered), 'chip', axis=0, tiled=True)  53.7 us
    reduce_scatter x6, waiting for transfers between devices, chip_scatter(): return lax.psum_scatter(grads, 'chip', scatter_dimension=0, tiled=True)  46.7 us
    ppermute x10, starting transfers between devices, weights_home(): lax.ppermute(half, AXES, flipped(roles.weight_pairs(which)))  42.4 us
  transfers between devices with their start and end apart: 24, of which 7 were waited for; matrix products, arithmetic and copies ran while one was open for 14% of the time, Pallas kernels for 36%

profile of v3, /device:TPU:0, one launch (start us, length us, event | category | flops | bytes accessed | tf_op | source)
XLA Modules:
  0.0 882.5 jit_solution(18356419638902682826)
XLA Ops:
  19.2 74.7 %deal_and_gather.1 = (bf16[256,1024]{1,0:T(8,128)(2,1)S(1)}, bf16[1024,1024]{1,0:T(8,128)(2,1)}, bf16[256,2176]{1,0:T(8,128)(2,1)}, bf16[256,2112]{1,0:T(8,128)(2,1)}) custom-call(s32[8]{0:T(128)S(1)} %copy-done.22, bf16[256,1024]{1,0:T(8,128)(2,1)S(1)} %bitcast.148, f32[1,1024]{1,0:T(1,128)S(1)} %get-tuple-element.314.gain_ref, ...), custom_call_target="tpu_custom_call" | custom-call | flops 5242880 | bytes 104857600 | tf_op jit(solution)/shard_map/deal_and_gather/pallas_call | solution.py:840
  100.0 51.9 %all-gather.6.cloned.1.call-done.w_in_ref.w_aux_ref.w_out_ref = bf16[1024,2176]{1,0:T(8,128)(2,1)} async-done(((bf16[256,2176]{1,0:T(8,128)(2,1)}), bf16[1024,2176]{1,0:T(8,128)(2,1)}) %all-gather.6.cloned.1.call-update) | async-done | bytes 4456464 | tf_op jit(solution)/shard_map/all_gather | solution.py:1096
  153.8 34.2 %mixer_forward.2 = (bf16[1024,1024]{1,0:T(8,128)(2,1)}, bf16[1024,512]{1,0:T(8,128)(2,1)}, f32[1024,1024]{1,0:T(8,128)}, f32[1024,512]{1,0:T(8,128)}, f32[1024,1...) custom-call(f32[2]{0:T(128)} %pad_maximum_fusion.23.scalars_ref, ...), custom_call_target="tpu_custom_call" | custom-call | flops 16000000000 | bytes 80000000 | tf_op jit(solution)/shard_map/mixer_forward/pallas_call | solution.py:165
  193.2 28.1 %forward_bridge.3 = (f32[256,1024]{1,0:T(8,128)S(1)}, bf16[1024,1024]{1,0:T(8,128)(2,1)S(1)}) custom-call(bf16[1024,1024]{1,0:T(8,128)(2,1)S(1)} %copy-done.8, bf16[256,1024]{1,0:T(8,128)(2,1)S(1)} %get-tuple-element.98.x_ref, f32[1,1024]{1,0:T(1,128)S(1)} %get-tuple-element.312.gain_ref), custom_call_target="tpu_custom_call" | custom-call | flops 5242880 | bytes 41943040 | tf_op jit(solution)/shard_map/forward_bridge/pallas_call | solution.py:601
  222.7 5.8 fusion.14
  229.4 5.8 convolution_convert_fusion.5.partial
  235.2 29.7 %forward_bridge.4 = (f32[256,1024]{1,0:T(8,128)S(1)}, bf16[1024,1024]{1,0:T(8,128)(2,1)S(1)}) custom-call(bf16[1024,1024]{1,0:T(8,128)(2,1)} %convolution_convert_fusion.5.partial, f32[256,1024]{1,0:T(8,128)S(1)} %get-tuple-element.101.x_ref, f32[1,1024]{1,0:T(1,128)S(1)} %get-tuple-element.313.gain_ref), custom_call_target="tpu_custom_call" | custom-call | flops 5242880 | bytes 41943040 | tf_op jit(solution)/shard_map/forward_bridge/pallas_call | solution.py:601
  268.4 33.5 %mixer_forward.3 = (bf16[1024,1024]{1,0:T(8,128)(2,1)}, bf16[1024,512]{1,0:T(8,128)(2,1)}, f32[1024,1024]{1,0:T(8,128)}, f32[1024,512]{1,0:T(8,128)}, f32[1024,1...) custom-call(f32[2]{0:T(128)} %pad_maximum_fusion.22.scalars_ref, ...), custom_call_target="tpu_custom_call" | custom-call | flops 16000000000 | bytes 80000000 | tf_op jit(solution)/shard_map/mixer_forward/pallas_call | solution.py:165
  306.5 55.2 %forward_bridge.5 = (f32[256,1024]{1,0:T(8,128)S(1)}, bf16[1024,1024]{1,0:T(8,128)(2,1)S(1)}) custom-call(bf16[1024,1024]{1,0:T(8,128)(2,1)} %get-tuple-element.104.partial, f32[256,1024]{1,0:T(8,128)S(1)} %get-tuple-element.105.x_ref, f32[1,1024]{1,0:T(1,128)S(1)} %get-tuple-element.311.gain_ref), custom_call_target="tpu_custom_call" | custom-call | flops 5242880 | bytes 41943040 | tf_op jit(solution)/shard_map/forward_bridge/pallas_call | solution.py:601
  364.8 8.4 fusion.10
  373.2 20.0 %all-gather.14.cloned.1.call-done = bf16[1024,1024]{1,0:T(8,128)(2,1)} async-done(((bf16[256,1024]{1,0:T(8,128)(2,1)}), bf16[1024,1024]{1,0:T(8,128)(2,1)}) %all-gather.14.cloned.1.call-update) | async-done | bytes 2097168 | tf_op jit(solution)/shard_map/all_gather | solution.py:1190
  393.2 8.3 fusion.2
  402.7 2.9 convolution_convert_fusion.7
  405.6 3.0 copy.178
  408.6 6.1 convolution_convert_fusion.3
  414.7 2.4 pad_maximum_fusion
  417.1 7.6 fusion.19.partial
  424.7 29.8 %backward_bridge.3 = (f32[256,1024]{1,0:T(8,128)S(1)}, bf16[1024,1024]{1,0:T(8,128)(2,1)S(1)}, f32[1,1024]{1,0:T(1,128)S(1)}) custom-call(bf16[1024,1024]{1,0:T(8,128)(2,1)} %fusion.19.partial, f32[256,1024]{1,0:T(8,128)S(1)} %get-tuple-element.106.x_ref, f32[1,1024]{1,0:T(1,128)S(1)} %get-tuple-element.311.gain_ref, bf16[256,1024]{1,0:T(8,128)(2,1)S(1)} %copy-done.11), custom_call_target="tpu_custom_call" | custom-call | flops 5242880 | bytes 41943040 | tf_op jit(solution)/shard_map/backward_bridge/pallas_call | solution.py:601
  456.9 2.3 convolution_convert_fusion.9
  460.6 4.6 convolution_convert_fusion.4
  465.2 27.6 %mixer_backward.2 = (bf16[1024,1024]{1,0:T(8,128)(2,1)}, bf16[1024,1536]{1,0:T(8,128)(2,1)}, bf16[1024,128]{1,0:T(8,128)(2,1)}, f32[4,1024]{1,0:T(4,128)}, f32[1,512]{1,0:T(1,128)}, /*index=5*/f32[8,128]{1,0:T(8,128)}) custom-call(f32[2]{0:T(128)} %pad_maximum_fusion.22.scalars_ref, bf16[1024,1024]{1,0:T(8,128)(2,1)} %copy-done.25, ...), custom_call_target="tpu_custom_call" | custom-call | flops 16000000000 | bytes 80000000 | tf_op jit(solution)/shard_map/mixer_backward/pallas_call | solution.py:339
  496.7 3.8 convolution_convert_fusion.2
  502.5 42.9 %reduce-scatter.12.cloned.1.call-done = bf16[256,2112]{1,0:T(8,128)(2,1)} async-done(((bf16[1024,2112]{1,0:T(8,128)(2,1)}), bf16[256,2112]{1,0:T(8,128)(2,1)}) %reduce-scatter.12.cloned.1.call-update) | async-done | bytes 1081360 | tf_op jit(solution)/shard_map/reduce_scatter | solution.py:1109
  545.5 46.7 %backward_bridge.4 = (f32[256,1024]{1,0:T(8,128)S(1)}, bf16[1024,1024]{1,0:T(8,128)(2,1)S(1)}, f32[1,1024]{1,0:T(1,128)S(1)}) custom-call(bf16[1024,1024]{1,0:T(8,128)(2,1)} %get-tuple-element.127.partial, f32[256,1024]{1,0:T(8,128)S(1)} %copy-done.3, f32[1,1024]{1,0:T(1,128)S(1)} %get-tuple-element.313.gain_ref, f32[256,1024]{1,0:T(8,128)S(1)} %copy-done.15), custom_call_target="tpu_custom_call" | custom-call | flops 5242880 | bytes 41943040 | tf_op jit(solution)/shard_map/backward_bridge/pallas_call | solution.py:601
  594.5 2.9 convolution_convert_fusion.6
  597.4 2.9 copy.183
  600.3 5.3 fusion.5
  607.2 4.0 convolution_convert_fusion.1
  611.2 2.5 pad_maximum_fusion.1
  613.7 7.2 fusion.16.partial
  629.3 2.1 broadcast_select_fusion.3
  631.4 2.1 copy.187
  633.5 21.0 %collective-permute-start.7 = (bf16[128,2112]{0,1:T(8,128)(2,1)}, bf16[128,2112]{0,1:T(8,128)(2,1)}, u32[]{:S(2)}, u32[]{:S(2)}) collective-permute-start(bf16[128,2112]{0,1:T(8,128)(2,1)} %copy.187), channel_id=1, source_target_pairs={{2,0},{6,1},{3,2},{7,3},{0,4},{4,5},{1,6},{5,7},{10,8},{14,9},{11,... | collective-permute-start | bytes 1622024 | tf_op jit(solution)/shard_map/ppermute | solution.py:1118
  655.6 6.0 collective-permute-start.6
  661.5 32.2 %backward_bridge.5 = (f32[256,1024]{1,0:T(8,128)S(1)}, bf16[1024,1024]{1,0:T(8,128)(2,1)S(1)}, f32[1,1024]{1,0:T(1,128)S(1)}) custom-call(bf16[1024,1024]{1,0:T(8,128)(2,1)} %fusion.16.partial, f32[256,1024]{1,0:T(8,128)S(1)} %get-tuple-element.101.x_ref, f32[1,1024]{1,0:T(1,128)S(1)} %get-tuple-element.312.gain_ref, f32[256,1024]{1,0:T(8,128)S(1)} %copy-done.17), custom_call_target="tpu_custom_call" | custom-call | flops 5242880 | bytes 41943040 | tf_op jit(solution)/shard_map/backward_bridge/pallas_call | solution.py:601
  696.0 2.3 convolution_convert_fusion.8
  698.4 27.9 %mixer_backward.3 = (bf16[1024,1024]{1,0:T(8,128)(2,1)}, bf16[1024,1536]{1,0:T(8,128)(2,1)}, bf16[1024,128]{1,0:T(8,128)(2,1)}, f32[4,1024]{1,0:T(4,128)}, f32[1,512]{1,0:T(1,128)}, /*index=5*/f32[8,128]{1,0:T(8,128)}) custom-call(f32[2]{0:T(128)} %pad_maximum_fusion.23.scalars_ref, bf16[1024,1024]{1,0:T(8,128)(2,1)} %copy-done.26, ...), custom_call_target="tpu_custom_call" | custom-call | flops 16000000000 | bytes 80000000 | tf_op jit(solution)/shard_map/mixer_backward/pallas_call | solution.py:339
  727.2 5.7 convolution_convert_fusion
  735.7 3.8 reduce-scatter.16.cloned.1.call-done
  739.7 2.5 convert_add_fusion.1
  746.3 3.0 collective-permute-start.5
  749.3 2.2 collective-permute-start.4
  754.2 15.6 %collective-permute-done.5 = bf16[128,512]{1,0:T(8,128)(2,1)S(1)} collective-permute-done((bf16[128,512]{1,0:T(8,128)(2,1)}, bf16[128,512]{1,0:T(8,128)(2,1)S(1)}, u32[]{:S(2)}, u32[]{:S(2)}) %collective-permute-start.5) | collective-permute-done | bytes 131104 | tf_op jit(solution)/shard_map/ppermute | solution.py:1118
  771.5 2.1 convert_add_fusion.2
  773.6 39.2 %final_step.1 = (bf16[256,1024]{1,0:T(8,128)(2,1)S(1)}, f32[48,128]{1,0:T(8,128)S(1)}) custom-call(s32[8]{0:T(128)S(1)} %select_reduce_fusion.inverse_ref, bf16[1024,1024]{1,0:T(8,128)(2,1)S(1)} %copy-done.9, bf16[256,1024]{1,0:T(8,128)(2,1)S(1)} %copy-done.7, f32[1,1024]{1,0:T(1,128)S(1)} %copy-done.21, f32[256,1024]{1,0:T(8,128)S(1)} %copy-done.13, ...), custom_call_target="tpu_custom_call" | custom-call | flops 5242880 | bytes 104857600 | tf_op jit(solution)/shard_map/final_step/pallas_call | solution.py:965
  826.0 5.8 collective-permute-start.10
  835.3 4.8 collective-permute-done.11
  845.4 24.7 %weights_back.1 = f32[128,1664]{1,0:T(8,128)S(1)} custom-call(bf16[256,1664]{1,0:T(8,128)(2,1)S(1)} %copy-done.18), custom_call_target="tpu_custom_call" | custom-call | bytes 62914560 | tf_op jit(solution)/shard_map/weights_back/pallas_call | solution.py:1018
  (282 shorter events, 104.4 us)
Async XLA Ops:
  7.2 144.7 %all-gather.6.cloned.1.call-start = ((), (), s32[]{:S(2)}) async-start(), calls=%async_computation.7 | async-start | bytes 5570560 | tf_op jit(solution)/shard_map/all_gather | solution.py:1096
  8.0 11.2 %copy-start.20 = (f32[1,1024]{1,0:T(1,128)}, f32[1,1024]{1,0:T(1,128)S(1)}, u32[]{:S(2)}) copy-start(f32[1,1024]{1,0:T(1,128)S(1)} %get-tuple-element.314.gain_ref) | copy-start | bytes 12292
  18.8 76.2 %copy-start.51 = (bf16[2,4]{1,0:T(2,128)(2,1)S(1)}, bf16[2,4]{1,0:T(2,128)(2,1)}, u32[]{:S(2)}) copy-start(bf16[2,4]{1,0:T(2,128)(2,1)} %param.30) | copy-start | bytes 52
  18.8 76.9 %copy-start.52 = (bf16[2,4]{1,0:T(2,128)(2,1)S(1)}, bf16[2,4]{1,0:T(2,128)(2,1)}, u32[]{:S(2)}) copy-start(bf16[2,4]{1,0:T(2,128)(2,1)} %param.29) | copy-start | bytes 52
  18.8 80.6 %copy-start.48 = (bf16[2,512]{1,0:T(2,128)(2,1)S(1)}, bf16[2,512]{1,0:T(2,128)(2,1)}, u32[]{:S(2)}) copy-start(bf16[2,512]{1,0:T(2,128)(2,1)} %param.31) | copy-start | bytes 6148
  93.9 97.7 %copy-start.6 = (bf16[256,1024]{1,0:T(8,128)(2,1)}, bf16[256,1024]{1,0:T(8,128)(2,1)S(1)}, u32[]{:S(2)}) copy-start(bf16[256,1024]{1,0:T(8,128)(2,1)S(1)} %get-tuple-element.98.x_ref) | copy-start | bytes 1572868
  94.0 128.7 %all-gather.8.cloned.1.call-start = ((), (), s32[]{:S(2)}) async-start(), calls=%async_computation.8 | async-start | bytes 5570560 | tf_op jit(solution)/shard_map/all_gather | solution.py:1096
  94.7 171.6 %all-gather.10.cloned.1.call-start = ((), (), s32[]{:S(2)}) async-start(), calls=%async_computation.9 | async-start | bytes 5570560 | tf_op jit(solution)/shard_map/all_gather | solution.py:1096
  188.0 176.8 %all-gather.12.cloned.1.call-start = ((), (), s32[]{:S(2)}) async-start(), calls=%async_computation.10 | async-start | bytes 5570560 | tf_op jit(solution)/shard_map/all_gather | solution.py:1096
  266.3 40.1 %copy-start.2 = (f32[256,1024]{1,0:T(8,128)}, f32[256,1024]{1,0:T(8,128)S(1)}, u32[]{:S(2)}) copy-start(f32[256,1024]{1,0:T(8,128)S(1)} %get-tuple-element.105.x_ref) | copy-start | bytes 3145732
  268.4 34.2 %copy-start.54 = (s32[8]{0:T(128)S(1)}, s32[8]{0:T(128)}, u32[]{:S(2)}) copy-start(s32[8]{0:T(128)} %param.20) | copy-start | bytes 100
  268.4 36.1 %copy-start.40 = (bf16[256,1,1024]{2,0,1:T(8,128)(2,1)S(1)}, bf16[256,1,1024]{2,0,1:T(8,128)(2,1)}, u32[]{:S(2)}) copy-start(bf16[256,1,1024]{2,0,1:T(8,128)(2,1)} %param.37) | copy-start | bytes 1572868
  301.9 91.3 %all-gather.14.cloned.1.call-start = ((), (), s32[]{:S(2)}) async-start(), calls=%async_computation.12 | async-start | bytes 2621440 | tf_op jit(solution)/shard_map/all_gather | solution.py:1190
  304.6 0.7 collective-permute-start.1
  306.2 196.3 %reduce-scatter.10.cloned.1.call-start = ((), (), s32[]{:S(2)}) async-start(), calls=%async_computation.13 | async-start | bytes 1310720 | tf_op jit(solution)/shard_map/reduce_scatter | solution.py:1109
  363.0 61.7 %copy-start.4 = (f32[256,1024]{1,0:T(8,128)}, f32[256,1024]{1,0:T(8,128)S(1)}, u32[]{:S(2)}) copy-start(f32[256,1024]{1,0:T(8,128)S(1)} %get-tuple-element.106.x_ref) | copy-start | bytes 3145732
  424.7 32.2 %copy-start.61 = (bf16[1024,512]{1,0:T(8,128)(2,1)S(1)}, bf16[1024,512]{1,0:T(8,128)(2,1)}, u32[]{:S(2)}) copy-start(bf16[1024,512]{1,0:T(8,128)(2,1)} %get-tuple-element.112) | copy-start | bytes 3145732
  459.2 86.2 %reduce-scatter.12.cloned.1.call-start = ((), (), s32[]{:S(2)}) async-start(), calls=%async_computation.14 | async-start | bytes 5570560 | tf_op jit(solution)/shard_map/reduce_scatter | solution.py:1109
  460.0 161.0 %reduce-scatter.8.cloned.1.call-start = ((), (), s32[]{:S(2)}) async-start(), calls=%async_computation.11 | async-start | bytes 2621440 | tf_op jit(solution)/shard_map/reduce_scatter | solution.py:1221
  465.2 196.3 %reduce-scatter.14.cloned.1.call-start = ((), (), s32[]{:S(2)}) async-start(), calls=%async_computation.15 | async-start | bytes 4259840 | tf_op jit(solution)/shard_map/reduce_scatter | solution.py:1109
  465.2 29.3 %copy-start.1 = (bf16[1024,1024]{1,0:T(8,128)(2,1)S(1)}, bf16[1024,1024]{1,0:T(8,128)(2,1)}, u32[]{:S(2)}) copy-start(bf16[1024,1024]{1,0:T(8,128)(2,1)} %copy-done) | copy-start | bytes 6291460
  502.5 42.9 %copy-start.3 = (f32[256,1024]{1,0:T(8,128)S(1)}, f32[256,1024]{1,0:T(8,128)}, u32[]{:S(2)}) copy-start(f32[256,1024]{1,0:T(8,128)} %copy-done.2) | copy-start | bytes 3145732
  502.5 43.0 %copy-start.15 = (f32[256,1024]{1,0:T(8,128)S(1)}, f32[256,1024]{1,0:T(8,128)}, u32[]{:S(2)}) copy-start(f32[256,1024]{1,0:T(8,128)} %copy-done.14) | copy-start | bytes 3145732
  545.4 190.3 %reduce-scatter.18.cloned.1.call-start = ((), (), s32[]{:S(2)}) async-start(), calls=%async_computation.17 | async-start | bytes 5570560 | tf_op jit(solution)/shard_map/reduce_scatter | solution.py:1109
  545.4 49.1 %copy-start.37 = (bf16[1024,704]{1,0:T(8,128)(2,1)S(1)}, bf16[1024,704]{1,0:T(8,128)(2,1)}, u32[]{:S(2)}) copy-start(bf16[1024,704]{1,0:T(8,128)(2,1)} %copy-done.36) | copy-start | bytes 4325380
  620.9 40.6 %copy-start.17 = (f32[256,1024]{1,0:T(8,128)S(1)}, f32[256,1024]{1,0:T(8,128)}, u32[]{:S(2)}) copy-start(f32[256,1024]{1,0:T(8,128)} %copy-done.16) | copy-start | bytes 3145732
  620.9 118.6 %reduce-scatter.16.cloned.1.call-start = ((), (), s32[]{:S(2)}) async-start(), calls=%async_computation.16 | async-start | bytes 1310720 | tf_op jit(solution)/shard_map/reduce_scatter | solution.py:1109
  624.1 4.4 collective-permute-start
  633.5 106.1 %collective-permute-start.7 = (bf16[128,2112]{0,1:T(8,128)(2,1)}, bf16[128,2112]{0,1:T(8,128)(2,1)}, u32[]{:S(2)}, u32[]{:S(2)}) collective-permute-start(bf16[128,2112]{0,1:T(8,128)(2,1)} %copy.187), channel_id=1, source_target_pairs={{2,0},{6,1},{3,2},{7,3},{0,4},{4,5},{1,6},{5,7},{10,8},{14,9},{11,... | collective-permute-start | bytes 1622024 | tf_op jit(solution)/shard_map/ppermute | solution.py:1118
  655.6 40.5 %copy-start.60 = (bf16[1024,512]{1,0:T(8,128)(2,1)S(1)}, bf16[1024,512]{1,0:T(8,128)(2,1)}, u32[]{:S(2)}) copy-start(bf16[1024,512]{1,0:T(8,128)(2,1)} %get-tuple-element.136) | copy-start | bytes 3145732
  655.6 84.1 %collective-permute-start.6 = (bf16[128,2112]{0,1:T(8,128)(2,1)}, bf16[128,2112]{0,1:T(8,128)(2,1)}, u32[]{:S(2)}, u32[]{:S(2)}) collective-permute-start(bf16[128,2112]{0,1:T(8,128)(2,1)} %copy.186), channel_id=1, source_target_pairs={{0,0},{4,1},{1,2},{5,3},{2,4},{6,5},{3,6},{7,7},{8,8},{12,9},{9,10... | collective-permute-start | bytes 1622024 | tf_op jit(solution)/shard_map/ppermute | solution.py:1118
  698.3 145.9 %reduce-scatter.20.cloned.1.call-start = ((), (), s32[]{:S(2)}) async-start(), calls=%async_computation.18 | async-start | bytes 4259840 | tf_op jit(solution)/shard_map/reduce_scatter | solution.py:1109
  698.4 28.8 %copy-start.31 = (bf16[1024,1024]{1,0:T(8,128)(2,1)S(1)}, bf16[1024,1024]{1,0:T(8,128)(2,1)}, u32[]{:S(2)}) copy-start(bf16[1024,1024]{1,0:T(8,128)(2,1)} %get-tuple-element.95.x_ref) | copy-start | bytes 6291460
  739.6 14.5 %copy-start.49 = (f32[1,512]{1,0:T(1,128)S(1)}, f32[1,512]{1,0:T(1,128)}, u32[]{:S(2)}) copy-start(f32[1,512]{1,0:T(1,128)} %get-tuple-element.161) | copy-start | bytes 6148
  739.6 14.5 %copy-start.50 = (f32[1,512]{1,0:T(1,128)S(1)}, f32[1,512]{1,0:T(1,128)}, u32[]{:S(2)}) copy-start(f32[1,512]{1,0:T(1,128)} %get-tuple-element.160) | copy-start | bytes 6148
  739.6 34.0 %copy-start.7 = (bf16[256,1024]{1,0:T(8,128)(2,1)S(1)}, bf16[256,1024]{1,0:T(8,128)(2,1)}, u32[]{:S(2)}) copy-start(bf16[256,1024]{1,0:T(8,128)(2,1)} %copy-done.6) | copy-start | bytes 1572868
  739.6 34.0 %copy-start.9 = (bf16[1024,1024]{1,0:T(8,128)(2,1)S(1)}, bf16[1024,1024]{1,0:T(8,128)(2,1)}, u32[]{:S(2)}) copy-start(bf16[1024,1024]{1,0:T(8,128)(2,1)} %get-tuple-element.155.partial) | copy-start | bytes 6291460
  739.6 34.0 %copy-start.21 = (f32[1,1024]{1,0:T(1,128)S(1)}, f32[1,1024]{1,0:T(1,128)}, u32[]{:S(2)}) copy-start(f32[1,1024]{1,0:T(1,128)} %copy-done.20) | copy-start | bytes 12292
  744.1 27.3 %collective-permute-start.3 = (bf16[128,1664]{1,0:T(8,128)(2,1)}, bf16[128,1664]{1,0:T(8,128)(2,1)}, u32[]{:S(2)}, u32[]{:S(2)}) collective-permute-start(bf16[128,1664]{1,0:T(8,128)(2,1)} %get-tuple-element.282), channel_id=1, source_target_pairs={{2,0},{6,1},{3,2},{7,3},{0,4},{4,5},{1,6},{5,7},{10,8},{14,9},{11,... | collective-permute-start | bytes 1277960 | tf_op jit(solution)/shard_map/ppermute | solution.py:1118
  744.1 27.4 %collective-permute-start.2 = (bf16[128,1664]{1,0:T(8,128)(2,1)S(1)}, bf16[128,1664]{1,0:T(8,128)(2,1)}, u32[]{:S(2)}, u32[]{:S(2)}) collective-permute-start(bf16[128,1664]{1,0:T(8,128)(2,1)S(1)} %get-tuple-element.281), channel_id=1, source_target_pairs={{0,0},{4,1},{1,2},{5,3},{2,4},{6,5},{3,6},{7,7},{8,8},{12,9},{9,10... | collective-permute-start | bytes 1277960 | tf_op jit(solution)/shard_map/ppermute | solution.py:1118
  746.3 23.5 %collective-permute-start.5 = (bf16[128,512]{1,0:T(8,128)(2,1)}, bf16[128,512]{1,0:T(8,128)(2,1)S(1)}, u32[]{:S(2)}, u32[]{:S(2)}) collective-permute-start(bf16[128,512]{1,0:T(8,128)(2,1)} %get-tuple-element.294), channel_id=1, source_target_pairs={{2,0},{6,1},{3,2},{7,3},{0,4},{4,5},{1,6},{5,7},{10,8},{14,9},{11,... | collective-permute-start | bytes 393224 | tf_op jit(solution)/shard_map/ppermute | solution.py:1118
  749.3 21.2 %collective-permute-start.4 = (bf16[128,512]{1,0:T(8,128)(2,1)}, bf16[128,512]{1,0:T(8,128)(2,1)}, u32[]{:S(2)}, u32[]{:S(2)}) collective-permute-start(bf16[128,512]{1,0:T(8,128)(2,1)} %get-tuple-element.293), channel_id=1, source_target_pairs={{0,0},{4,1},{1,2},{5,3},{2,4},{6,5},{3,6},{7,7},{8,8},{12,9},{9,10... | collective-permute-start | bytes 393224 | tf_op jit(solution)/shard_map/ppermute | solution.py:1118
  754.1 19.5 %copy-start.13 = (f32[256,1024]{1,0:T(8,128)S(1)}, f32[256,1024]{1,0:T(8,128)}, u32[]{:S(2)}) copy-start(f32[256,1024]{1,0:T(8,128)} %copy-done.12) | copy-start | bytes 3145732
  818.9 14.4 %collective-permute-start.9 = (bf16[128,512]{1,0:T(8,128)(2,1)}, bf16[128,512]{1,0:T(8,128)(2,1)}, u32[]{:S(2)}, u32[]{:S(2)}) collective-permute-start(bf16[128,512]{1,0:T(8,128)(2,1)} %get-tuple-element.292), channel_id=1, source_target_pairs={{2,0},{6,1},{3,2},{7,3},{0,4},{4,5},{1,6},{5,7},{10,8},{14,9},{11,... | collective-permute-start | bytes 393224 | tf_op jit(solution)/shard_map/ppermute | solution.py:1118
  820.0 13.3 %collective-permute-start.8 = (bf16[128,512]{1,0:T(8,128)(2,1)S(1)}, bf16[128,512]{1,0:T(8,128)(2,1)}, u32[]{:S(2)}, u32[]{:S(2)}) collective-permute-start(bf16[128,512]{1,0:T(8,128)(2,1)S(1)} %get-tuple-element.291), channel_id=1, source_target_pairs={{0,0},{4,1},{1,2},{5,3},{2,4},{6,5},{3,6},{7,7},{8,8},{12,9},{9,10... | collective-permute-start | bytes 393224 | tf_op jit(solution)/shard_map/ppermute | solution.py:1118
  821.9 10.0 %copy-start.34 = (f32[128,2112]{0,1:T(8,128)S(1)}, f32[128,2112]{0,1:T(8,128)}, u32[]{:S(2)}) copy-start(f32[128,2112]{0,1:T(8,128)} %convert_add_fusion.1) | copy-start | bytes 3244036
  824.3 15.8 %collective-permute-start.11 = (bf16[128,2112]{0,1:T(8,128)(2,1)}, bf16[128,2112]{0,1:T(8,128)(2,1)}, u32[]{:S(2)}, u32[]{:S(2)}) collective-permute-start(bf16[128,2112]{0,1:T(8,128)(2,1)} %copy.193), channel_id=1, source_target_pairs={{2,0},{6,1},{3,2},{7,3},{0,4},{4,5},{1,6},{5,7},{10,8},{14,9},{11,... | collective-permute-start | bytes 1622024 | tf_op jit(solution)/shard_map/ppermute | solution.py:1118
  826.0 14.2 %collective-permute-start.10 = (bf16[128,2112]{0,1:T(8,128)(2,1)}, bf16[128,2112]{0,1:T(8,128)(2,1)}, u32[]{:S(2)}, u32[]{:S(2)}) collective-permute-start(bf16[128,2112]{0,1:T(8,128)(2,1)} %copy.192), channel_id=1, source_target_pairs={{0,0},{4,1},{1,2},{5,3},{2,4},{6,5},{3,6},{7,7},{8,8},{12,9},{9,10... | collective-permute-start | bytes 1622024 | tf_op jit(solution)/shard_map/ppermute | solution.py:1118
  (39 other events, 135.7 us)
Sparse Core Ops, SparseCore 0:
  94.1 57.7 all-gather.5
  153.7 54.8 all-gather.7
  210.5 54.8 all-gather.9
  302.0 62.7 all-gather.11
  366.7 26.4 all-gather.13
  459.3 27.7 reduce-scatter.9
  490.5 54.8 reduce-scatter.11
  547.8 42.8 reduce-scatter.7
  593.7 56.2 reduce-scatter.13
  652.9 55.9 reduce-scatter.17
  711.8 27.6 reduce-scatter.15
  742.8 46.1 reduce-scatter.19

commit v4 on v3

v4 whole, which is shorter than its diff:
```python
import functools
import jax
import jax.numpy as jnp
from jax import lax
from jax.experimental import pallas as pl
from jax.experimental.layout import Layout, with_layout_constraint
from jax.experimental.pallas import tpu as pltpu
from jax.sharding import Mesh, PartitionSpec as P

CHUNK = 256
LANES = 128
KEY = 256
VAL = 512
CONV_CH = 2 * KEY + VAL
F32 = jnp.float32
BF16 = jnp.bfloat16
NN = (((1,), (0,)), ((), ()))
NT = (((1,), (1,)), ((), ()))
TN = (((0,), (0,)), ((), ()))


def mm(a, b, dims=NN):
    return lax.dot_general(
        a.astype(BF16), b.astype(BF16), dims, preferred_element_type=F32
    )


def split_low(a):
    high = a.astype(BF16)
    return high, (a - high.astype(F32)).astype(BF16)


def mm3(a, b, dims=NN):
    a_high, a_low = split_low(a)
    b_high, b_low = split_low(b)
    dot = functools.partial(
        lax.dot_general, dimension_numbers=dims, preferred_element_type=F32
    )
    return dot(a_high, b_high) + (dot(a_high, b_low) + dot(a_low, b_high))


def mm_exact_left(a, b, dims=NN):
    a = a.astype(BF16)
    high = b.astype(BF16)
    rest = b - high.astype(F32)
    mid = rest.astype(BF16)
    low = (rest - mid.astype(F32)).astype(BF16)
    dot = functools.partial(
        lax.dot_general, dimension_numbers=dims, preferred_element_type=F32
    )
    return dot(a, high) + (dot(a, mid) + dot(a, low))


def iotas():
    rows = lax.broadcasted_iota(jnp.int32, (CHUNK, CHUNK), 0)
    cols = lax.broadcasted_iota(jnp.int32, (CHUNK, CHUNK), 1)
    return rows, cols


def wide(col_block, width):
    return jnp.concatenate([col_block] * (width // LANES), axis=1)


def rates_of(rates, rate, bias):
    write = jax.nn.sigmoid(jnp.broadcast_to(rates[:, 0:1], (CHUNK, LANES)))
    logit = jnp.broadcast_to(rates[:, 1:2], (CHUNK, LANES)) + bias
    soft = jnp.maximum(logit, 0.0) + jnp.log1p(jnp.exp(-jnp.abs(logit)))
    return write, -rate * soft, jax.nn.sigmoid(logit)


def head_scalars(scalars_ref, layer):
    head = lax.axis_index("zl") * 2 + lax.axis_index("core")
    rate_ref, bias_ref = scalars_ref
    here = lax.broadcasted_iota(jnp.int32, (1, rate_ref.shape[1]), 1) == head
    pick = lambda ref: jnp.sum(
        jnp.where(here, ref[layer : layer + 1, :].astype(F32), 0.0), axis=1, keepdims=True
    )
    return jnp.exp(pick(rate_ref)), pick(bias_ref)


def decay_terms(step, rows, cols):
    inclusive = (rows >= cols).astype(BF16)
    total = mm_exact_left(inclusive, step)
    spread = wide(total, CHUNK) - jnp.concatenate([total.T] * (CHUNK // LANES), axis=0)
    decay = jnp.where(rows >= cols, jnp.exp(jnp.minimum(spread, 0.0)), 0.0)
    last = jnp.broadcast_to(total[CHUNK - 1 : CHUNK, :], (CHUNK, LANES))
    return decay, jnp.exp(total), jnp.exp(last - total), jnp.exp(last)


def solve_unit(coupling, rows, cols, product):
    same = ((rows >> 1) == (cols >> 1)) & (rows != cols)
    inverse = jnp.where(rows == cols, 1.0, 0.0) - jnp.where(same, coupling, 0.0)
    for level in range(1, CHUNK.bit_length() - 1):
        between = ((rows >> (level + 1)) == (cols >> (level + 1))) & (
            (rows >> level) != (cols >> level)
        )
        part = jnp.where(between, coupling, 0.0)
        inverse = inverse - product(product(inverse, part), inverse)
    return inverse


def silu_of(x):
    gate = jax.nn.sigmoid(x)
    return x * gate, gate


def conv_rows(padded_ref, taps_ref, start):
    result = padded_ref[pl.ds(start, CHUNK), :] * taps_ref[0:1, :]
    for j in range(1, 4):
        result = result + padded_ref[pl.ds(start + j, CHUNK), :] * taps_ref[j : j + 1, :]
    return result


def forward_kernel(
    layer, jobs, rate_ref, bias_ref, x_ref, w_qkv_ref, w_gate_ref, w_aux_ref, w_out_ref, gain_ref,
    part_ref, heads_ref, proj_ref, gate_ref, rates_ref, inverse_ref, fresh_ref, o_ref, state_ref,
    padded, memory, taps_ref,
):
    begin_jobs(jobs, pl.program_id(0), pl.num_programs(0))
    @pl.when(pl.program_id(0) == 0)
    def _():
        memory[...] = jnp.zeros_like(memory)
        taps_ref[...] = w_aux_ref[...].astype(F32).T[2:6, :]
        padded[0:8, :] = jnp.zeros((8, CONV_CH), F32)

    x = x_ref[...]
    rates = mm(x, w_aux_ref[...])
    rates_ref[...] = rates
    qkv = mm(x, w_qkv_ref[...])
    proj_ref[...] = qkv
    gate_in = mm(x, w_gate_ref[...])
    gate_ref[...] = gate_in
    padded[8 : 8 + CHUNK, :] = qkv
    conv = conv_rows(padded, taps_ref, 5)
    padded[0:8, :] = qkv[CHUNK - 8 :, :]
    act, _ = silu_of(conv)
    q, k, v = act[:, :KEY], act[:, KEY : 2 * KEY], act[:, 2 * KEY :]
    q = q * (lax.rsqrt(jnp.sum(q * q, axis=1, keepdims=True) + 1e-6) * KEY**-0.5)
    k = k * lax.rsqrt(jnp.sum(k * k, axis=1, keepdims=True) + 1e-6)
    rows, cols = iotas()
    write, step, _ = rates_of(rates, *head_scalars((rate_ref, bias_ref), layer))
    decay, growth, rest, final = decay_terms(step, rows, cols)
    coupling = jnp.where(rows > cols, wide(write, CHUNK) * mm3(k, k, NT) * decay, 0.0)
    inverse = solve_unit(coupling, rows, cols, mm3)
    inverse_ref[...] = inverse.astype(BF16)
    within = mm(q, k, NT) * decay
    state = memory[...]
    state_ref[...] = state
    low_state = state.astype(BF16)
    source = wide(write, VAL) * (v - wide(growth, VAL) * mm(k, low_state))
    fresh = mm3(inverse, source)
    fresh_ref[...] = fresh
    o = wide(growth, VAL) * mm(q, low_state) + mm(within, fresh)
    o_ref[...] = o
    memory[...] = wide(final, VAL) * state + mm(k * wide(rest, KEY), fresh, TN)
    scaled = o * lax.rsqrt(jnp.mean(o * o, axis=1, keepdims=True) + 1e-5) * gain_ref[layer : layer + 1, :].astype(F32)
    heads = (scaled * silu_of(gate_in)[0]).astype(BF16)
    heads_ref[...] = heads
    part_ref[...] = mm(heads, w_out_ref[...], NT).astype(BF16)
    end_jobs(jobs, pl.program_id(0), pl.num_programs(0))


def head_spec(value):
    return pl.BlockSpec(value.shape, lambda i: (0, 0))


def weight_specs(width):
    fixed = lambda shape, at: pl.BlockSpec(shape, lambda i: (0, at), pipeline_mode=pl.Buffered(1))
    return [
        fixed((width, CONV_CH), 0),
        fixed((width, VAL), 0),
        fixed((width, LANES), 2 * VAL // LANES),
        fixed((width, VAL), 1),
        fixed((2, VAL), 0),
    ]


def mixer_forward(layer, x, qkv, pack, gain, scalars, jobs, number):
    length, width = x.shape
    chunks = length // CHUNK
    row = lambda cols: pl.BlockSpec((CHUNK, cols), lambda i: (i, 0))
    out = lambda cols, kind: jax.ShapeDtypeStruct((length, cols), kind)
    return carry_call(
        functools.partial(forward_kernel, layer), jobs, (chunks,),
        [head_spec(scalars[0]), head_spec(scalars[1]), row(width)] + weight_specs(width),
        [
            row(width), row(VAL), row(CONV_CH), row(VAL), row(LANES), row(CHUNK), row(VAL), row(VAL),
            pl.BlockSpec((None, KEY, VAL), lambda i: (i, 0, 0)),
        ],
        [
            out(width, BF16), out(VAL, BF16), out(CONV_CH, F32), out(VAL, F32), out(LANES, F32),
            out(CHUNK, BF16), out(VAL, F32), out(VAL, F32),
            jax.ShapeDtypeStruct((chunks, KEY, VAL), F32),
        ],
        [
            pltpu.VMEM((CHUNK + 8, CONV_CH), F32), pltpu.VMEM((KEY, VAL), F32),
            pltpu.VMEM((4, CONV_CH), F32),
        ],
        (*scalars, x, qkv, pack, pack, pack, gain), number, "mixer_forward", 16 * 10**9,
    )


def unit_back(grad, vector, scale):
    inv = lax.rsqrt(jnp.sum(vector * vector, axis=1, keepdims=True) + 1e-6)
    dot = jnp.sum(grad * vector, axis=1, keepdims=True)
    return (grad - vector * (inv * inv * dot)) * (inv * scale)


def backward_kernel(
    layer, jobs, rate_ref, bias_ref, g_ref, x_ref, w_qkv_ref, w_gate_ref, w_aux_ref, w_out_ref, gain_ref,
    proj_ref, halo_ref, gate_ref, rates_ref, inverse_ref, fresh_ref, o_ref, state_ref,
    part_ref, dqkv_ref, dgate_ref, daux_ref, dgain_ref, dscalars_ref,
    padded, dpadded, dmemory, taps_ref, dtaps_ref, daux_sum,
):
    begin_jobs(jobs, pl.program_id(0), pl.num_programs(0))
    at = pl.program_id(0)
    last = pl.num_programs(0) - 1

    @pl.when(at == 0)
    def _():
        dmemory[...] = jnp.zeros_like(dmemory)
        taps_ref[...] = w_aux_ref[...].astype(F32).T[2:6, :]
        dpadded[CHUNK : CHUNK + 8, :] = jnp.zeros((8, CONV_CH), F32)
        dtaps_ref[...] = jnp.zeros_like(dtaps_ref)
        daux_sum[...] = jnp.zeros_like(daux_sum)
        dgain_ref[...] = jnp.zeros_like(dgain_ref)
        dscalars_ref[...] = jnp.zeros_like(dscalars_ref)

    rows, cols = iotas()
    padded[8 : 8 + CHUNK, :] = proj_ref[...]
    padded[0:8, :] = jnp.where(at == last, 0.0, halo_ref[...])
    conv = conv_rows(padded, taps_ref, 5)
    act, sig = silu_of(conv)
    act_q, act_k, v = act[:, :KEY], act[:, KEY : 2 * KEY], act[:, 2 * KEY :]
    q = act_q * (lax.rsqrt(jnp.sum(act_q * act_q, axis=1, keepdims=True) + 1e-6) * KEY**-0.5)
    k = act_k * lax.rsqrt(jnp.sum(act_k * act_k, axis=1, keepdims=True) + 1e-6)
    rates = rates_ref[...]
    write, step, sig_decay = rates_of(rates, *head_scalars((rate_ref, bias_ref), layer))
    decay, growth, rest, final = decay_terms(step, rows, cols)
    growth_v = wide(growth, VAL)
    write_v = wide(write, VAL)
    low_q, low_k = q.astype(BF16), k.astype(BF16)
    below = rows > cols
    strict_decay = jnp.where(below, decay, 0.0)
    keys = mm(low_k, low_k, NT) * strict_decay * wide(write, CHUNK)
    within = mm(low_q, low_k, NT) * decay
    dheads = mm(g_ref[...], w_out_ref[...])
    o = o_ref[...]
    gate_in = gate_ref[...]
    gate, gate_sig = silu_of(gate_in)
    inv = lax.rsqrt(jnp.mean(o * o, axis=1, keepdims=True) + 1e-5)
    normal = o * inv
    gain = gain_ref[layer : layer + 1, :].astype(F32)
    dgate = dheads * normal * gain * (gate_sig * (1.0 + gate_in * (1.0 - gate_sig)))
    dscaled = dheads * gate
    dgain_ref[...] += jnp.sum(dscaled * normal, axis=0, keepdims=True)
    dnormal = dscaled * gain
    do = inv * (dnormal - normal * jnp.mean(dnormal * normal, axis=1, keepdims=True))
    state = state_ref[...]
    low_state = state.astype(BF16)
    fresh = fresh_ref[...]
    low_fresh = fresh.astype(BF16)
    dstate = dmemory[...]
    low_dstate = dstate.astype(BF16)
    low_do = do.astype(BF16)
    k_rest = k * wide(rest, KEY)
    rest_dstate = mm(k_rest, low_dstate)
    dfresh = mm(within, low_do, TN) + rest_dstate
    dsource = mm(inverse_ref[...], dfresh, TN)
    low_dsource = dsource.astype(BF16)
    dv = write_v * dsource
    dread = -(growth_v * dv)
    low_dread = dread.astype(BF16)
    do_growth = growth_v * do
    low_do_growth = do_growth.astype(BF16)
    dwithin = mm(low_do, low_fresh, NT)
    dcoupling = -mm(low_dsource, low_fresh, NT)
    dkeys = dcoupling * strict_decay * wide(write, CHUNK)
    dpairs = dwithin * decay
    dq = mm(low_do_growth, low_state, NT) + mm(dpairs, low_k)
    dk = (
        mm(low_dread, low_state, NT)
        + mm(dpairs, low_q, TN)
        + mm(dkeys + dkeys.T, low_k)
        + wide(rest, KEY) * mm(low_fresh, low_dstate, NT)
    )
    dmemory[...] = (
        wide(final, VAL) * dstate + mm(low_q, low_do_growth, TN) + mm(low_k, low_dread, TN)
    )
    spread = dwithin * within + dcoupling * keys
    straddle = jnp.where(below, mm_exact_left((rows <= cols).astype(BF16), spread), 0.0)
    read_rows = jnp.sum(
        do_growth * mm(low_q, low_state) + dread * mm(low_k, low_state), axis=1, keepdims=True
    )
    rest_rows = jnp.sum(fresh * rest_dstate, axis=1, keepdims=True)
    carried = jnp.sum(dstate * state) * final[0:1, 0:1]
    suffix = mm_exact_left(
        (rows <= cols).astype(BF16), jnp.broadcast_to(read_rows, (CHUNK, LANES))
    ) + mm_exact_left((rows > cols).astype(BF16), jnp.broadcast_to(rest_rows, (CHUNK, LANES)))
    dstep = suffix + jnp.sum(straddle, axis=1, keepdims=True) + carried
    dlogit = dstep * (-head_scalars((rate_ref, bias_ref), layer)[0]) * sig_decay
    dwrite = (1.0 - write) * jnp.sum(dsource * fresh, axis=1, keepdims=True)
    lane = lax.broadcasted_iota(jnp.int32, (CHUNK, LANES), 1)
    drates = jnp.where(lane == 0, dwrite, jnp.where(lane == 1, dlogit, 0.0))
    low_drates = drates.astype(BF16)
    daux_sum[...] += mm(x_ref[...], low_drates, TN)
    dscalars_ref[0:1, :] += jnp.sum(dstep * step, axis=0, keepdims=True)
    dscalars_ref[1:2, :] += jnp.sum(dlogit, axis=0, keepdims=True)
    dact = jnp.concatenate(
        [unit_back(dq, act_q, KEY**-0.5), unit_back(dk, act_k, 1.0), dv], axis=1
    )
    dconv = dact * (sig * (1.0 + conv * (1.0 - sig)))
    dpadded[0:CHUNK, :] = dconv
    dtaps_ref[2:6, :] += jnp.concatenate(
        [
            jnp.sum(dconv * padded[5 + j : 5 + j + CHUNK, :], axis=0, keepdims=True)
            for j in range(4)
        ],
        axis=0,
    )
    dqkv = dconv * taps_ref[3:4, :]
    for j in range(3):
        dqkv = dqkv + dpadded[pl.ds(3 - j, CHUNK), :] * taps_ref[j : j + 1, :]
    dpadded[CHUNK : CHUNK + 8, :] = dconv[0:8, :]
    low_dqkv, low_dgate = dqkv.astype(BF16), dgate.astype(BF16)
    dqkv_ref[...] = low_dqkv
    dgate_ref[...] = low_dgate
    part_ref[...] = (
        mm(low_dqkv, w_qkv_ref[...], NT)
        + mm(low_dgate, w_gate_ref[...], NT)
        + mm(low_drates, w_aux_ref[...], NT)
    ).astype(BF16)

    @pl.when(at == last)
    def _():
        daux_ref[...] = (daux_sum[...] + dtaps_ref[...].T).astype(BF16)

    end_jobs(jobs, pl.program_id(0), pl.num_programs(0))


def mixer_backward(layer, g, x, qkv, pack, gain, scalars, saved, jobs, number):
    proj, gate_in, rates, inverse, fresh, o, states = saved
    length, width = g.shape
    chunks = length // CHUNK
    back = chunks - 1
    row = lambda cols: pl.BlockSpec((CHUNK, cols), lambda i: (back - i, 0))
    out = lambda cols, kind: jax.ShapeDtypeStruct((length, cols), kind)
    steps = CHUNK // 8
    return carry_call(
        functools.partial(backward_kernel, layer), jobs, (chunks,),
        [head_spec(scalars[0]), head_spec(scalars[1]), row(width), row(width)] + weight_specs(width) + [
            row(CONV_CH),
            pl.BlockSpec((8, CONV_CH), lambda i: (jnp.maximum((back - i) * steps - 1, 0), 0)),
            row(VAL), row(LANES), row(CHUNK), row(VAL), row(VAL),
            pl.BlockSpec((None, KEY, VAL), lambda i: (back - i, 0, 0)),
        ],
        [
            row(width), row(CONV_CH), row(VAL),
            pl.BlockSpec((width, LANES), lambda i: (0, 0)),
            pl.BlockSpec((1, VAL), lambda i: (0, 0)),
            pl.BlockSpec((8, LANES), lambda i: (0, 0)),
        ],
        [
            out(width, BF16), out(CONV_CH, BF16), out(VAL, BF16),
            jax.ShapeDtypeStruct((width, LANES), BF16),
            jax.ShapeDtypeStruct((1, VAL), F32),
            jax.ShapeDtypeStruct((8, LANES), F32),
        ],
        [
            pltpu.VMEM((CHUNK + 8, CONV_CH), F32),
            pltpu.VMEM((CHUNK + 8, CONV_CH), F32),
            pltpu.VMEM((KEY, VAL), F32),
            pltpu.VMEM((4, CONV_CH), F32),
            pltpu.VMEM((LANES, CONV_CH), F32),
            pltpu.VMEM((width, LANES), F32),
        ],
        (*scalars, g, x, qkv, pack, pack, pack, gain, proj, proj, gate_in, rates, inverse, fresh, o,
         states),
        number, "mixer_backward", 16 * 10**9,
    )


PIECES = 4
AXES = ("chip", "core", "zp", "zl")


def partners():
    core, zl = lax.axis_index("core"), lax.axis_index("zl")
    return core, zl, {"core": 1 - core}, {"zl": 1 - zl}


class Block:
    def __init__(self, zl, core, rows):
        self.first = (zl * 2 + core) * rows
        self.size = rows // PIECES

    def piece(self, p):
        return pl.ds(pl.multiple_of(self.first + p * self.size, self.size), self.size)


def remote(src, dst, send, recv, device):
    return pltpu.make_async_remote_copy(
        src_ref=src, dst_ref=dst, send_sem=send, recv_sem=recv,
        device_id=device, device_id_type=pl.DeviceIdType.MESH,
    )


class Scatter:
    def __init__(self, partial, beside_far, beside_own, sums, far, send, recv):
        core, zl, beside, across = partners()
        rows = far.shape[0]
        self.partial, self.beside_far, self.beside_own = partial, beside_far, beside_own
        self.sums, self.far = sums, far
        self.size = rows // PIECES
        self.own = Block(zl, core, rows)
        self.away = Block(1 - zl, core, rows)
        own_beside, away_beside = Block(zl, 1 - core, rows), Block(1 - zl, 1 - core, rows)
        self.to_far = [
            remote(partial.at[away_beside.piece(p)], beside_far.at[self.local(p)],
                   send.at[0, p], recv.at[0, p], beside)
            for p in range(PIECES)
        ]
        self.to_own = [
            remote(partial.at[own_beside.piece(p)], beside_own.at[self.local(p)],
                   send.at[1, p], recv.at[1, p], beside)
            for p in range(PIECES)
        ]
        self.cross = [
            remote(sums.at[self.local(p)], far.at[self.local(p)],
                   send.at[2, p], recv.at[2, p], across)
            for p in range(PIECES)
        ]

    def local(self, p):
        return pl.ds(p * self.size, self.size)

    def start(self):
        for copy in self.to_far:
            copy.start()
        for copy in self.to_own:
            copy.start()
        for p in range(PIECES):
            self.to_far[p].wait_recv()
            at = self.local(p)
            self.sums[at, :] = (
                self.partial[self.away.piece(p), :].astype(F32) + self.beside_far[at, :].astype(F32)
            ).astype(BF16)
            self.cross[p].start()

    def total(self, p):
        self.to_own[p].wait_recv()
        self.cross[p].wait_recv()
        at = self.local(p)
        return (
            self.partial[self.own.piece(p), :].astype(F32)
            + self.beside_own[at, :].astype(F32)
            + self.far[at, :].astype(F32)
        )

    def finish(self):
        for copies in (self.to_far, self.to_own, self.cross):
            for copy in copies:
                copy.wait_send()


class Gather:
    def __init__(self, gathered, send, recv, first):
        core, zl, beside, across = partners()
        rows = gathered.shape[0] // 4
        self.gathered = gathered
        self.own = Block(zl, core, rows)
        other = Block(1 - zl, core, rows)
        make = lambda block, at, device: [
            remote(gathered.at[block.piece(p)], gathered.at[block.piece(p)],
                   send.at[first + at, p], recv.at[first + at, p], device)
            for p in range(PIECES)
        ]
        self.across = make(self.own, 0, across)
        self.beside = make(self.own, 1, beside)
        self.forward = make(other, 2, beside)

    def put(self, p, rows):
        self.gathered[self.own.piece(p), :] = rows
        self.across[p].start()
        self.beside[p].start()

    def finish(self):
        for p in range(PIECES):
            self.across[p].wait_recv()
            self.forward[p].start()
        for p in range(PIECES):
            self.beside[p].wait_recv()
            self.forward[p].wait_recv()
        for copies in (self.across, self.beside, self.forward):
            for copy in copies:
                copy.wait_send()


def normed_of(x, gain):
    return x * lax.rsqrt(jnp.mean(x * x, axis=1, keepdims=True) + 1e-6) * gain


def first_kernel(row, jobs, x_ref, gain_ref, out_ref, send, recv):
    wait_greetings(greet_group() + jobs.greet())
    gather = Gather(out_ref, send, recv, 0)
    jobs.start()
    size = x_ref.shape[0] // PIECES
    for p in range(PIECES):
        x = x_ref[p * size : (p + 1) * size, :].astype(F32)
        gather.put(p, normed_of(x, gain_ref[row : row + 1, :].astype(F32)).astype(BF16))
    jobs.middle()
    gather.finish()
    jobs.finish()


def forward_bridge_kernel(
    row, jobs, partial, x_ref, gain_ref, new_ref, out_ref, beside_far, beside_own, sums, far, send, recv
):
    wait_greetings(greet_group() + jobs.greet())
    scatter = Scatter(partial, beside_far, beside_own, sums, far, send, recv)
    gather = Gather(out_ref, send, recv, 3)
    scatter.start()
    jobs.start()
    for p in range(PIECES):
        at = scatter.local(p)
        x = x_ref[at, :].astype(F32) + scatter.total(p)
        new_ref[at, :] = x
        gather.put(p, normed_of(x, gain_ref[row : row + 1, :].astype(F32)).astype(BF16))
    jobs.middle()
    scatter.finish()
    gather.finish()
    jobs.finish()


def norm_back(total, x, gain):
    inv = lax.rsqrt(jnp.mean(x * x, axis=1, keepdims=True) + 1e-6)
    unit = x * inv
    scaled = total * gain
    grad = inv * (scaled - unit * jnp.mean(scaled * unit, axis=1, keepdims=True))
    return grad, jnp.sum(total * unit, axis=0, keepdims=True)


def backward_bridge_kernel(
    row, jobs, partial, x_ref, gain_ref, grad_ref, new_ref, out_ref, dgain_ref,
    beside_far, beside_own, sums, far, send, recv
):
    wait_greetings(greet_group() + jobs.greet())
    scatter = Scatter(partial, beside_far, beside_own, sums, far, send, recv)
    gather = Gather(out_ref, send, recv, 3)
    scatter.start()
    jobs.start()
    dgain = jnp.zeros(dgain_ref.shape, F32)
    for p in range(PIECES):
        at = scatter.local(p)
        grad, part = norm_back(scatter.total(p), x_ref[at, :].astype(F32), gain_ref[row : row + 1, :].astype(F32))
        dgain = dgain + part
        grad = grad + grad_ref[at, :].astype(F32)
        new_ref[at, :] = grad
        gather.put(p, grad.astype(BF16))
    dgain_ref[...] = dgain
    jobs.middle()
    scatter.finish()
    gather.finish()
    jobs.finish()


def backward_last_kernel(
    row, jobs, partial, x_ref, gain_ref, grad_ref, new_ref, dgain_ref,
    beside_far, beside_own, sums, far, send, recv
):
    wait_greetings(greet_group() + jobs.greet())
    scatter = Scatter(partial, beside_far, beside_own, sums, far, send, recv)
    scatter.start()
    jobs.start()
    dgain = jnp.zeros(dgain_ref.shape, F32)
    for p in range(PIECES):
        at = scatter.local(p)
        grad, part = norm_back(scatter.total(p), x_ref[at, :].astype(F32), gain_ref[row : row + 1, :].astype(F32))
        dgain = dgain + part
        new_ref[at, :] = (grad + grad_ref[at, :]).astype(BF16)
    dgain_ref[...] = dgain
    jobs.middle()
    scatter.finish()
    jobs.finish()


def comm_call(kernel, row, number, outs, args, scatters, gathers, jobs):
    rows = args[1].shape[0] if scatters else args[0].shape[0]
    width = args[0].shape[1]
    vmem = pl.BlockSpec(memory_space=pltpu.VMEM)
    hops = 3 * scatters + 3 * gathers
    return carry_call(
        functools.partial(kernel, row), jobs, (), [vmem] * len(args), [vmem] * len(outs),
        [jax.ShapeDtypeStruct(shape, kind) for shape, kind in outs],
        [pltpu.VMEM((rows, width), BF16) for _ in range(4 * scatters)]
        + [pltpu.SemaphoreType.DMA((hops, PIECES)), pltpu.SemaphoreType.DMA((hops, PIECES))],
        args, number, kernel.__name__.replace("_kernel", ""), rows * width * 20,
    )


def first_gather(x, gain, row, jobs, number):
    rows, width = x.shape
    return comm_call(first_kernel, row, number, [((4 * rows, width), BF16)], (x, gain), 0, 1, jobs)


def forward_bridge(partial, x, gain, row, jobs, number):
    rows, width = x.shape
    return comm_call(
        forward_bridge_kernel, row, number, [((rows, width), F32), ((4 * rows, width), BF16)],
        (partial, x, gain), 1, 1, jobs,
    )


def backward_bridge(partial, x, gain, row, grad, jobs, number):
    rows, width = x.shape
    return comm_call(
        backward_bridge_kernel, row, number,
        [((rows, width), F32), ((4 * rows, width), BF16), ((1, width), F32)],
        (partial, x, gain, grad), 1, 1, jobs,
    )


def backward_last(partial, x, gain, row, grad, jobs, number):
    rows, width = x.shape
    return comm_call(
        backward_last_kernel, row, number, [((rows, width), BF16), ((1, width), F32)],
        (partial, x, gain, grad), 1, 0, jobs,
    )


class Job:
    in_vmem = False

    @staticmethod
    def buffers(shape, chips):
        return []

    def __init__(self, source, target, send, recv, chips, buffers=()):
        self.source, self.target, self.send, self.recv = source, target, send, recv
        self.held = buffers
        self.chips = chips
        self.chip, self.core, self.zp, self.zl, self.own = place(chips)
        self.fixed = (self.zp == self.zl) & (self.zl == self.core)
        self.outward, self.inward, self.locals = [], [], []
        self.plan()

    def copy(self, src, dst, send, recv, device):
        return remote(src, dst, self.send.at[send], self.recv.at[recv], device)

    def local(self, src, dst, at, when=None, through=None):
        if through is None:
            self.locals.append((pltpu.make_async_copy(src, dst, self.send.at[at]), None, when))
        else:
            self.locals.append(
                (pltpu.make_async_copy(src, through, self.send.at[at]),
                 pltpu.make_async_copy(through, dst, self.send.at[at]), when)
            )

    def column(self, chip, core, zp, zl):
        return at_device(chip, core, zp, zl)

    def greet(self):
        count = 0
        for copy, device, mine in self.inward:
            if mine is None:
                signal(device)
            else:
                unless(mine, functools.partial(signal, device))
        for copy, mine in self.outward:
            count = count + (1 if mine is None else 1 - mine.astype(jnp.int32))
        return count

    def start(self):
        for copy, mine in self.outward:
            if mine is None:
                copy.start()
            else:
                unless(mine, copy.start)
        for load, _, when in self.locals:
            if when is None:
                load.start()
            else:
                pl.when(when)(load.start)

    def middle(self):
        for load, store, when in self.locals:
            def turn():
                load.wait()
                store.start()

            if store is not None and when is None:
                turn()
            elif store is not None:
                pl.when(when)(turn)

    def arrivals(self):
        for copy, device, mine in self.inward:
            if mine is None:
                copy.wait_recv()
            else:
                unless(mine, copy.wait_recv)

    def departures(self):
        for copy, mine in self.outward:
            if mine is None:
                copy.wait_send()
            else:
                unless(mine, copy.wait_send)
        for load, store, when in self.locals:
            last = load if store is None else store
            if when is None:
                last.wait()
            else:
                pl.when(when)(last.wait)

    def finish(self):
        self.arrivals()
        self.departures()


def block(index, size):
    return pl.ds(pl.multiple_of(index * size, size), size)


class ToPlane(Job):
    @staticmethod
    def result(shape, chips):
        return (2 * shape[0], shape[1])

    @staticmethod
    def buffers(shape, chips):
        return [pltpu.VMEM(shape, BF16)]

    def plan(self):
        rows = self.source.shape[0]
        at = block(self.core, rows)
        for to in range(2):
            self.outward.append(
                (self.copy(self.source, self.target.at[at], to, self.core,
                           at_device(self.chip, self.zl, to, self.zp)),
                 self.fixed & (self.zp == to))
            )
        for co in range(2):
            device = at_device(self.chip, co, self.zl, self.core)
            self.inward.append(
                (self.copy(self.source, self.target.at[block(co, rows)], 0, co, device), device,
                 self.fixed & (self.core == co))
            )
        self.local(self.source, self.target.at[at], 2, self.fixed, self.held[0] if self.held else None)


class FromPlane(Job):
    @staticmethod
    def result(shape, chips):
        return (2, shape[0] // 2, shape[1])

    @staticmethod
    def buffers(shape, chips):
        return [pltpu.VMEM((shape[0] // 2, shape[1]), BF16)]

    def plan(self):
        rows = self.source.shape[0] // 2
        for co in range(2):
            src, mine = self.source.at[block(co, rows)], self.fixed & (self.core == co)
            self.outward.append(
                (self.copy(src, self.target.at[self.zp], co, self.zp,
                           at_device(self.chip, co, self.zl, self.core)), mine)
            )
            self.local(src, self.target.at[self.zp], 2 + co, mine, self.held[0] if self.held else None)
        for at in range(2):
            device = at_device(self.chip, self.zl, at, self.zp)
            self.inward.append(
                (self.copy(self.source.at[block(0, rows)], self.target.at[at], 0, at, device), device,
                 self.fixed & (self.zp == at))
            )


class Spread(Job):
    @staticmethod
    def result(shape, chips):
        return (chips * shape[0], shape[1])

    @staticmethod
    def buffers(shape, chips):
        return [pltpu.VMEM(shape, BF16)]

    def to(self, chip):
        return at_device(chip, self.core, self.zp, self.zl)

    def plan(self):
        rows = self.source.shape[0]
        own = self.target.at[block(self.chip, rows)]
        self.local(self.source, own, 0, None, self.held[0])
        self.onward, self.later = [], []
        if self.chips != 4:
            for j in range(1, self.chips):
                to = lax.rem(self.chip + j, self.chips)
                source = lax.rem(self.chip + self.chips - j, self.chips)
                self.outward.append((self.copy(self.source, own, j, j, self.to(to)), None))
                self.inward.append(
                    (self.copy(self.source, self.target.at[block(source, rows)], j, j,
                               self.to(source)), self.to(source), None)
                )
            return
        y, x = self.chip // 2, lax.rem(self.chip, 2)
        sides = [y * 2 + (1 - x), (1 - y) * 2 + x]
        across = (1 - y) * 2 + (1 - x)
        half = rows // 2
        for side in range(2):
            device = self.to(sides[side])
            self.outward.append((self.copy(self.source, own, 1 + side, 1 + side, device), None))
            self.inward.append(
                (self.copy(self.source, self.target.at[block(sides[side], rows)], 1 + side, 1 + side,
                           device), device, None)
            )
        for side in range(2):
            part = pl.ds(pl.multiple_of(sides[side] * rows + side * half, half), half)
            self.onward.append(
                self.copy(self.target.at[part], self.target.at[part], 3 + side, 3 + side,
                          self.to(sides[1 - side]))
            )
            part = pl.ds(pl.multiple_of(across * rows + side * half, half), half)
            self.later.append(
                self.copy(self.target.at[part], self.target.at[part], 3 + side, 3 + side,
                          self.to(sides[1 - side]))
            )

    def middle(self):
        super().middle()
        if self.onward:
            self.arrivals()
            for copy in self.onward:
                copy.start()

    def finish(self):
        if not self.onward:
            self.arrivals()
        for copy in self.later:
            copy.wait_recv()
        for copy in self.onward:
            copy.wait_send()
        self.departures()


class Reduce(Job):
    in_vmem = True

    @staticmethod
    def result(shape, chips):
        return (shape[0] // chips, shape[1])

    @staticmethod
    def buffers(shape, chips):
        rows, cols = shape[0] // chips, shape[1]
        if chips != 4:
            return [pltpu.VMEM((chips, rows, cols), BF16)]
        return [pltpu.VMEM((rows // 2, cols), BF16)] * 4 + [pltpu.VMEM((rows, cols), BF16)] * 3

    def plan(self):
        rows = self.source.shape[0] // self.chips
        to = lambda chip: at_device(chip, self.core, self.zp, self.zl)
        if self.chips != 4:
            (parts,) = self.held
            self.local(self.source.at[block(self.chip, rows)], parts.at[self.chip], 0)
            for j in range(1, self.chips):
                target = lax.rem(self.chip + j, self.chips)
                source = lax.rem(self.chip + self.chips - j, self.chips)
                src = self.source.at[block(target, rows)]
                self.outward.append((self.copy(src, parts.at[self.chip], j, j, to(target)), None))
                self.inward.append(
                    (self.copy(src, parts.at[source], j, j, to(source)), to(source), None)
                )
            return
        half = rows // 2
        y, x = self.chip // 2, lax.rem(self.chip, 2)
        sides = [y * 2 + (1 - x), (1 - y) * 2 + x]
        across = (1 - y) * 2 + (1 - x)
        passing, staged, blocks, own = self.held[0:2], self.held[2:4], self.held[4:6], self.held[6]
        piece = lambda chip, at: self.source.at[
            pl.ds(pl.multiple_of(chip * rows + at * half, half), half)
        ]
        self.local(self.source.at[block(self.chip, rows)], own, 0)
        self.loads = []
        self.onward, self.later = [], []
        for side in range(2):
            device = to(sides[side])
            copy = self.copy(piece(across, side), passing[side], 1 + side, 1 + side, device)
            self.outward.append((copy, None))
            self.inward.append((copy, device, None))
        self.direct = []
        for side in range(2):
            device = to(sides[side])
            part = pl.ds(side * half, half)
            self.direct.append(
                self.copy(piece(sides[side], side), blocks[side].at[part], 3 + side, 3 + side, device)
            )
            self.loads.append(
                pltpu.make_async_copy(piece(sides[side], 1 - side), staged[side], self.send.at[5 + side])
            )
            part = pl.ds((1 - side) * half, half)
            self.onward.append(
                self.copy(staged[side], blocks[side].at[part], 7 + side, 5 + side, device)
            )

    def start(self):
        super().start()
        if self.chips == 4:
            for copy in self.direct + self.loads:
                copy.start()

    def middle(self):
        if self.chips == 4:
            for side in range(2):
                self.inward[1 - side][0].wait_recv()
                self.loads[side].wait()
                self.held[2 + side][...] = (
                    self.held[2 + side][...].astype(F32) + self.held[1 - side][...].astype(F32)
                ).astype(BF16)
                self.onward[side].start()

    def finish(self):
        if self.chips == 4:
            for copy in self.direct + self.onward:
                copy.wait_recv()
            self.departures()
            for copy in self.direct + self.onward:
                copy.wait_send()
            total = self.held[6][...].astype(F32) + (
                self.held[4][...].astype(F32) + self.held[5][...].astype(F32)
            )
        else:
            super().finish()
            total = self.held[0][0].astype(F32)
            for chip in range(1, self.chips):
                total = total + self.held[0][chip].astype(F32)
        self.target[...] = total.astype(BF16)


class ToRole(Job):
    @staticmethod
    def result(shape, chips):
        return shape

    @staticmethod
    def buffers(shape, chips):
        return [pltpu.VMEM(shape, BF16)]

    def ends(self):
        role = at_device(self.chip, self.zl, self.core, self.zp)
        home = at_device(self.chip, self.zp, self.zl, self.core)
        return role, home, self.fixed & (self.zp == self.core)

    def plan(self):
        to, source, mine = self.ends()
        self.outward.append((self.copy(self.source, self.target, 0, 0, to), mine))
        self.inward.append((self.copy(self.source, self.target, 0, 0, source), source, mine))
        self.local(self.source, self.target, 1, mine, self.held[0])


class FromRole(ToRole):
    def ends(self):
        role, home, mine = super().ends()
        return home, role, mine


class Share(Job):
    @staticmethod
    def result(shape, chips):
        return (4 * shape[0], shape[1])

    @staticmethod
    def buffers(shape, chips):
        return [pltpu.VMEM(shape, BF16)]

    def plan(self):
        rows = self.source.shape[0]
        own = self.target.at[block(self.zl * 2 + self.core, rows)]
        beside = at_device(self.chip, 1 - self.core, self.zp, self.zl)
        across = at_device(self.chip, self.core, self.zp, 1 - self.zl)
        self.local(self.source, own, 0, None, self.held[0])
        for at, device, zl, core in ((1, beside, self.zl, 1 - self.core), (2, across, 1 - self.zl, self.core)):
            self.outward.append((self.copy(self.source, own, at, at, device), None))
            self.inward.append(
                (self.copy(self.source, self.target.at[block(zl * 2 + core, rows)], at, at, device),
                 device, None)
            )
        other = self.target.at[block((1 - self.zl) * 2 + self.core, rows)]
        self.onward = self.copy(other, other, 3, 3, beside)
        last = self.target.at[block((1 - self.zl) * 2 + 1 - self.core, rows)]
        self.later = self.copy(last, last, 3, 3, beside)

    def middle(self):
        super().middle()
        self.arrivals()
        self.onward.start()

    def finish(self):
        self.later.wait_recv()
        self.onward.wait_send()
        self.departures()


class ShareSum(Job):
    in_vmem = True

    @staticmethod
    def result(shape, chips):
        return (shape[0] // 4, shape[1])

    @staticmethod
    def buffers(shape, chips):
        return [pltpu.VMEM((shape[0] // 4, shape[1]), BF16)] * 5

    def plan(self):
        rows = self.target.shape[0]
        beside = at_device(self.chip, 1 - self.core, self.zp, self.zl)
        across = at_device(self.chip, self.core, self.zp, 1 - self.zl)
        part = lambda zl, core: self.source.at[block(zl * 2 + core, rows)]
        self.far, self.near, self.staged, self.own, self.other = self.held
        for at, src, dst in (
            (0, part(1 - self.zl, 1 - self.core), self.far), (1, part(self.zl, 1 - self.core), self.near)
        ):
            copy = self.copy(src, dst, at, at, beside)
            self.outward.append((copy, None))
            self.inward.append((copy, beside, None))
        self.local(part(1 - self.zl, self.core), self.staged, 2)
        self.local(part(self.zl, self.core), self.own, 3)
        self.onward = self.copy(self.staged, self.other, 4, 2, across)
        self.across = across

    def greet(self):
        signal(self.across)
        return super().greet() + 1

    def middle(self):
        self.arrivals()
        for load, _, _ in self.locals:
            load.wait()
        self.staged[...] = (
            self.staged[...].astype(F32) + self.far[...].astype(F32)
        ).astype(BF16)
        self.onward.start()

    def finish(self):
        for copy, _ in self.outward:
            copy.wait_send()
        self.onward.wait()
        self.target[...] = (
            self.own[...].astype(F32) + self.near[...].astype(F32) + self.other[...].astype(F32)
        ).astype(BF16)


class Jobs:
    def __init__(self, jobs, chips):
        self.kinds = [kind for kind, _ in jobs]
        self.values = [value for _, value in jobs]
        self.chips = chips
        count = max(9, chips + 1)
        any_space = pl.BlockSpec(memory_space=pl.ANY)
        self.in_specs = [any_space] * len(jobs)
        self.out_shape = [
            jax.ShapeDtypeStruct(kind.result(value.shape, chips), BF16) for kind, value in jobs
        ]
        self.buffers = [kind.buffers(value.shape, chips) for kind, value in jobs]
        self.scratch = [pltpu.SemaphoreType.DMA((count,))] * (2 * len(jobs))
        self.scratch += [buffer for buffers in self.buffers for buffer in buffers]

    def out_specs(self, grid):
        specs = []
        for kind, shape in zip(self.kinds, self.out_shape):
            if not kind.in_vmem:
                specs.append(pl.BlockSpec(memory_space=pl.ANY))
            elif grid:
                specs.append(pl.BlockSpec(shape.shape, lambda i: (0, 0)))
            else:
                specs.append(pl.BlockSpec(memory_space=pltpu.VMEM))
        return specs

    def bind(self, sources, targets, scratch):
        sems, scratch = scratch[: 2 * len(self.kinds)], scratch[2 * len(self.kinds) :]
        self.bound = []
        for at, (kind, source, target) in enumerate(zip(self.kinds, sources, targets)):
            held, scratch = scratch[: len(self.buffers[at])], scratch[len(self.buffers[at]) :]
            self.bound.append(
                kind(source, target, sems[2 * at], sems[2 * at + 1], self.chips, held)
            )

    def greet(self):
        count = 0
        for job in self.bound:
            count = count + job.greet()
        return count

    def start(self):
        for job in self.bound:
            job.start()

    def middle(self):
        for job in self.bound:
            job.middle()

    def finish(self):
        for job in self.bound:
            job.finish()


def carrying(body, jobs, ins, outs):
    extra = len(jobs.kinds)

    def kernel(*refs):
        operands, refs = refs[:ins], refs[ins:]
        sources, refs = refs[:extra], refs[extra:]
        results, refs = refs[:outs], refs[outs:]
        targets, refs = refs[:extra], refs[extra:]
        own = len(refs) - len(jobs.scratch)
        scratch = refs[:own]
        jobs.bind(sources, targets, refs[own:])
        body(jobs, *operands, *results, *scratch)

    return kernel


def carry_call(body, jobs, grid, in_specs, out_specs, out_shape, scratch, args, number, name, work):
    outs = len(out_shape)
    results = pl.pallas_call(
        carrying(body, jobs, len(args), outs),
        grid=grid,
        in_specs=list(in_specs) + jobs.in_specs,
        out_specs=list(out_specs) + jobs.out_specs(grid),
        out_shape=list(out_shape) + jobs.out_shape,
        scratch_shapes=list(scratch) + jobs.scratch,
        compiler_params=pltpu.CompilerParams(
            collective_id=number, has_side_effects=True, vmem_limit_bytes=56 * 1024 * 1024
        ),
        cost_estimate=pl.CostEstimate(
            flops=work, bytes_accessed=80 * 1024 * 1024, transcendentals=0
        ),
        name=name,
    )(*args, *jobs.values)
    return list(results[:outs]), list(results[outs:])


def place(chips):
    chip, core, zp, zl = (lax.axis_index(name) for name in AXES)
    return chip, core, zp, zl, chip * 2 + core


def at_device(chip, core, zp, zl):
    return {"chip": chip, "core": core, "zp": zp, "zl": zl}


def signal(device):
    pl.semaphore_signal(
        pltpu.get_barrier_semaphore(), inc=1, device_id=device,
        device_id_type=pl.DeviceIdType.MESH,
    )


def unless(condition, action):
    pl.when(jnp.logical_not(condition))(action)


class Plane:
    def __init__(self, chips):
        self.count = 2 * chips
        _, _, self.zp, self.zl, self.own = place(chips)

    def device(self, index):
        return at_device(index // 2, index % 2, self.zp, self.zl)

    def to(self, j):
        return lax.rem(self.own + j, self.count)

    def source(self, j):
        return lax.rem(self.own + self.count - j, self.count)

    def greet(self):
        for j in range(1, self.count):
            signal(self.device(self.to(j)))
        return self.count - 1


class Trade:
    def __init__(self, chips):
        self.chips, self.count = chips, 2 * chips
        self.chip, self.core, self.zp, self.zl, self.own = place(chips)
        self.fixed = (self.zp == self.zl) & (self.zl == self.core)
        self.slot = self.chip * 2 + self.zp

    def role(self, slot):
        return at_device(slot // 2, self.zl, slot % 2, self.zp)

    def role_mine(self, slot):
        return self.fixed & (self.slot == slot)

    def home(self, index):
        return at_device(index // 2, index % 2, self.zl, self.core)

    def home_mine(self, index):
        return self.fixed & (self.own == index)

    def greet_homes(self):
        for index in range(self.count):
            unless(self.home_mine(index), functools.partial(signal, self.home(index)))
        return self.count - self.fixed.astype(jnp.int32)

    def greet_roles(self):
        for slot in range(self.count):
            unless(self.role_mine(slot), functools.partial(signal, self.role(slot)))
        return self.count - self.fixed.astype(jnp.int32)


def greet_group():
    _, _, beside, across = partners()
    signal(beside)
    signal(across)
    return 2


def wait_greetings(count):
    pl.semaphore_wait(pltpu.get_barrier_semaphore(), count)


class Raw:
    def __init__(self, refs, square):
        (self.query, self.key, self.value, self.gate, self.decay, self.conv, self.out,
         self.ffn_gate, self.ffn_up, self.ffn_down) = refs
        self.square = square

    @staticmethod
    def turned(value):
        return value.astype(F32).T.astype(BF16)

    def qkv(self, layer, ref):
        ref[:, 0:KEY] = self.query[layer]
        ref[:, KEY : 2 * KEY] = self.key[layer]
        ref[:, 2 * KEY :] = self.value[layer]

    def mix(self, layer, ref):
        ref[:, 0:VAL] = self.gate[layer]
        ref[:, VAL : 2 * VAL] = self.turned(self.out[layer])
        self.square[...] = jnp.zeros(self.square.shape, F32)
        self.square[0:2, :] = self.decay[layer].astype(F32)
        self.square[2:6, :] = self.conv[layer].astype(F32)
        ref[:, 2 * VAL :] = self.square[...].T.astype(BF16)

    def pair(self, layer, ref):
        ref[...] = self.turned(
            jnp.concatenate([self.ffn_gate[layer], self.ffn_up[layer]], axis=0)
        )

    def down(self, layer, ref):
        ref[...] = self.turned(self.ffn_down[layer])


def deal_kernel(chips, jobs, order_ref, lengths_ref, x_ref, gain_ref, cotangent_ref, *refs):
    raw, refs = refs[:10], refs[10:]
    (new_ref, out_ref, start_ref, qkv_next, mix_next, pair_ref, pair_next, down_ref, down_next,
     first_full, second_full, first_wide, second_wide), refs = refs[:13], refs[13:]
    (spread, picked, square, first, second, held_first, held_second, send, recv, plane_send,
     plane_recv, role_send, role_recv, *sems) = refs
    raw = Raw(raw, square)
    plane, trade = Plane(chips), Trade(chips)
    first_column = ToPlane(first, first_wide, sems[0], sems[1], chips)
    first_across = Spread(first_wide, first_full, sems[2], sems[3], chips, [held_first])
    second_column = ToPlane(second, second_wide, sems[4], sems[5], chips)
    second_across = Spread(second_wide, second_full, sems[6], sems[7], chips, [held_second])
    gather = Gather(out_ref, send, recv, 0)
    count = plane.count
    part = x_ref.shape[0] // count
    rows = lambda index: pl.ds(pl.multiple_of(index * part, part), part)
    expected = plane.greet() + trade.greet_homes() + greet_group()
    for job in (first_column, first_across, second_column, second_across):
        expected = expected + job.greet()
    raw.qkv(0, first)
    raw.mix(0, second)
    wait_greetings(expected)
    outward, inward = [], []
    for j in range(1, count):
        to, source = plane.to(j), plane.source(j)
        outward.append(
            remote(x_ref.at[rows(to)], spread.at[plane.own], plane_send.at[j], plane_recv.at[j],
                   plane.device(to))
        )
        inward.append(
            remote(x_ref.at[rows(to)], spread.at[source], plane_send.at[j], plane_recv.at[j],
                   plane.device(source))
        )
    for copy in outward:
        copy.start()
    first_column.start()
    spread[plane.own] = x_ref[rows(plane.own), :]
    for copy in inward:
        copy.wait_recv()
    to_roles = []
    for slot in range(count):
        picked[slot] = spread[order_ref[slot]]
        copy = remote(picked.at[slot], new_ref.at[rows(plane.own)], role_send.at[slot],
                      role_recv.at[plane.own], trade.role(slot))
        mine = trade.role_mine(slot)
        unless(mine, copy.start)

        @pl.when(mine)
        def _():
            new_ref[rows(plane.own), :] = picked[slot]

        to_roles.append((copy, mine))
    first_column.finish()
    first_across.start()
    second_column.start()
    size = x_ref.shape[0] // PIECES
    parts = max(size // part, 1)
    for p in range(PIECES):
        for index in range(p * parts, (p + 1) * parts):
            arrival = remote(picked.at[0], new_ref.at[rows(index)], role_send.at[0],
                             role_recv.at[index], trade.home(index))
            unless(trade.home_mine(index), arrival.wait_recv)
        x = new_ref[p * size : (p + 1) * size, :].astype(F32)
        gather.put(p, normed_of(x, gain_ref[0:1, :].astype(F32)).astype(BF16))
    second_column.finish()
    second_across.start()
    first_across.middle()
    length = lengths_ref[order_ref[plane.own]]
    at = (trade.zp * 2 + trade.zl) * x_ref.shape[0]
    positions = lax.broadcasted_iota(jnp.int32, x_ref.shape, 0) + at
    start_ref[...] = jnp.where(positions < length, cotangent_ref[...], jnp.zeros(x_ref.shape, BF16))
    raw.qkv(1, qkv_next)
    raw.mix(1, mix_next)
    raw.pair(0, pair_ref)
    raw.pair(1, pair_next)
    raw.down(0, down_ref)
    raw.down(1, down_next)
    for copy in outward:
        copy.wait_send()
    for copy, mine in to_roles:
        unless(mine, copy.wait_send)
    gather.finish()
    second_across.middle()
    first_across.finish()
    second_across.finish()


def deal_and_gather(order, lengths, x, gain, cotangent, raw, chips, number):
    rows, width = x.shape
    part, units = raw[0].shape[1], raw[7].shape[1]
    vmem = pl.BlockSpec(memory_space=pltpu.VMEM)
    smem = pl.BlockSpec(memory_space=pltpu.SMEM)
    hbm = pl.BlockSpec(memory_space=pl.ANY)
    count = 2 * chips
    buffer = pltpu.VMEM((count, rows // count, width), BF16)
    sems = lambda *shape: [pltpu.SemaphoreType.DMA(shape), pltpu.SemaphoreType.DMA(shape)]
    qkv, mix = CONV_CH, 2 * VAL + LANES
    pair = (part, 2 * units)
    held = [(part, qkv), (part, mix), pair, pair, (part, units), (part, units)]
    spread = [(2 * chips * part, qkv), (2 * chips * part, mix)]
    moved = [(2 * part, qkv), (2 * part, mix)]
    shapes = [(rows, width), (4 * rows, width), (rows, width)] + held + spread + moved
    return carry_call(
        functools.partial(deal_kernel, chips), Jobs([], chips), (),
        [smem, smem] + [vmem] * 13,
        [vmem] * 9 + [hbm] * 4,
        [jax.ShapeDtypeStruct(shape, BF16) for shape in shapes],
        [buffer, buffer, pltpu.VMEM((LANES, LANES), F32)]
        + [pltpu.VMEM(shape, BF16) for shape in (held[0], held[1], moved[0], moved[1])]
        + sems(3, PIECES) + sems(count) + sems(count)
        + [pltpu.SemaphoreType.DMA((max(9, chips + 1),))] * 8,
        (order, lengths, x, gain, cotangent, *raw), number, "deal_and_gather", rows * width * 20,
    )[0]


def small_rows(width):
    rows = (4 * width + 2 * VAL) // LANES + 1
    return rows + -rows % 8


def assemble(small, mix0, mix1, ffn0, ffn1, heads0, heads1, scalars0, scalars1):
    small[...] = jnp.zeros(small.shape, F32)
    at = 0
    for term in (mix0, mix1, ffn0, ffn1, heads0, heads1):
        for r in range(term.shape[1] // LANES):
            small[at : at + 1, :] = term[:, r * LANES : (r + 1) * LANES]
            at += 1
    head = lax.axis_index("zl") * 2 + lax.axis_index("core")
    lane = lax.broadcasted_iota(jnp.int32, (1, LANES), 1)
    row = jnp.zeros((1, LANES), F32)
    values = (scalars0[0:1, :], scalars1[0:1, :], scalars0[1:2, :], scalars1[1:2, :])
    for place, value in enumerate(values):
        row = row + jnp.where(lane == place * 4 + head, value, 0.0)
    small[at : at + 1, :] = row


def final_kernel(
    chips, jobs, order_ref, partial, x_ref, gain_ref, grad_ref, *refs
):
    terms, refs = refs[:7], refs[7:]
    grads, refs = refs[:3], refs[3:]
    home_ref, total_ref, homes, refs = refs[0], refs[1], refs[2:5], refs[5:]
    (beside_far, beside_own, sums, far, last, back, picked, small, by_plane, by_z, plane_sum,
     send, recv, role_send, role_recv, plane_send, plane_recv, small_send, small_recv, z_send,
     z_recv), refs = refs[:21], refs[21:]
    reduces, returns = [], []
    for at in range(3):
        summed, four, refs = refs[0], refs[1:5], refs[5:]
        buffers = len(Reduce.buffers(grads[at].shape, chips))
        reduces.append(Reduce(grads[at], summed, four[0], four[1], chips, refs[:buffers]))
        returns.append(FromPlane(summed, homes[at], four[2], four[3], chips))
        refs = refs[buffers:]
    plane, trade = Plane(chips), Trade(chips)
    count = plane.count
    part = x_ref.shape[0] // count
    rows = lambda index: pl.ds(pl.multiple_of(index * part, part), part)
    tier = trade.zp * 2 + trade.zl
    tier_device = lambda at: at_device(trade.chip, trade.core, at // 2, at % 2)
    for k in range(1, 4):
        signal(tier_device(lax.rem(tier + k, 4)))
    expected = plane.greet() + trade.greet_roles() + greet_group() + jobs.greet() + 3
    for job in reduces + returns:
        expected = expected + job.greet()
    wait_greetings(expected)
    scatter = Scatter(partial, beside_far, beside_own, sums, far, send, recv)
    scatter.start()
    for job in reduces:
        job.start()
    jobs.start()
    dgain = jnp.zeros((1, x_ref.shape[1]), F32)
    to_homes = []
    size = x_ref.shape[0] // PIECES
    parts = max(size // part, 1)
    for p in range(PIECES):
        at = scatter.local(p)
        grad, piece = norm_back(scatter.total(p), x_ref[at, :].astype(F32), gain_ref[0:1, :].astype(F32))
        dgain = dgain + piece
        last[at, :] = (grad + grad_ref[at, :]).astype(BF16)
        for index in range(p * parts, (p + 1) * parts):
            copy = remote(last.at[rows(index)], back.at[trade.slot], role_send.at[index],
                          role_recv.at[trade.slot], trade.home(index))
            mine = trade.home_mine(index)
            unless(mine, copy.start)

            @pl.when(mine)
            def _():
                back[trade.slot] = last[rows(index), :]

            to_homes.append((copy, mine))
    assemble(small, dgain, *terms)
    small_out, small_in = [], []
    for j in range(1, count):
        to, source = plane.to(j), plane.source(j)
        small_out.append(
            remote(small, by_plane.at[plane.own], small_send.at[j], small_recv.at[j], plane.device(to))
        )
        small_in.append(
            remote(small, by_plane.at[source], small_send.at[j], small_recv.at[j], plane.device(source))
        )
    for copy in small_out:
        copy.start()
    by_plane[plane.own] = small[...]
    for job in reduces:
        job.middle()
    for slot in range(count):
        arrival = remote(last.at[rows(0)], back.at[slot], role_send.at[0], role_recv.at[slot],
                         trade.role(slot))
        unless(trade.role_mine(slot), arrival.wait_recv)
    outward, inward = [], []
    for j in range(count):
        to, source = plane.to(j), plane.source(j)
        at = jnp.int32(0)
        for slot in range(count):
            at = jnp.where(order_ref[slot] == to, slot, at)
        picked[j] = back[at]
        if j == 0:
            home_ref[rows(plane.own), :] = picked[0]
            continue
        copy = remote(picked.at[j], home_ref.at[rows(plane.own)], plane_send.at[j], plane_recv.at[j],
                      plane.device(to))
        copy.start()
        outward.append(copy)
        inward.append(
            remote(picked.at[j], home_ref.at[rows(source)], plane_send.at[j], plane_recv.at[j],
                   plane.device(source))
        )
    for reduce, back_home in zip(reduces, returns):
        reduce.finish()
        back_home.start()
    jobs.middle()
    for copy in small_in:
        copy.wait_recv()
    total = by_plane[0]
    for index in range(1, count):
        total = total + by_plane[index]
    plane_sum[...] = total
    z_out, z_in = [], []
    for k in range(1, 4):
        to, source = lax.rem(tier + k, 4), lax.rem(tier + 4 - k, 4)
        z_out.append(remote(plane_sum, by_z.at[tier], z_send.at[k], z_recv.at[k], tier_device(to)))
        z_in.append(remote(plane_sum, by_z.at[source], z_send.at[k], z_recv.at[k], tier_device(source)))
    for copy in z_out:
        copy.start()
    by_z[tier] = total
    for copy in z_in:
        copy.wait_recv()
    total_ref[...] = (by_z[0] + by_z[1]) + (by_z[2] + by_z[3])
    for copy in inward:
        copy.wait_recv()
    scatter.finish()
    for copy, mine in to_homes:
        unless(mine, copy.wait_send)
    for copy in small_out + z_out + outward:
        copy.wait_send()
    jobs.finish()
    for job in returns:
        job.finish()


def final_step(order, partial, x, gain, grad, terms, grads, chips, jobs, number):
    rows, width = x.shape
    small = jax.ShapeDtypeStruct((small_rows(width), LANES), F32)
    vmem = pl.BlockSpec(memory_space=pltpu.VMEM)
    count = 2 * chips
    block = pltpu.VMEM((rows, width), BF16)
    parted = pltpu.VMEM((count, rows // count, width), BF16)
    hbm = pl.BlockSpec(memory_space=pl.ANY)
    chained = []
    for a in grads:
        chained.append(pltpu.VMEM(Reduce.result(a.shape, chips), BF16))
        chained += [pltpu.SemaphoreType.DMA((max(9, chips + 1),))] * 4
        chained += Reduce.buffers(a.shape, chips)
    sems = lambda *shape: [pltpu.SemaphoreType.DMA(shape), pltpu.SemaphoreType.DMA(shape)]
    return carry_call(
        functools.partial(final_kernel, chips), jobs, (),
        [pl.BlockSpec(memory_space=pltpu.SMEM)] + [vmem] * 11 + [hbm] * 3,
        [vmem, vmem] + [hbm] * 3,
        [
            jax.ShapeDtypeStruct((rows, width), BF16),
            jax.ShapeDtypeStruct(small.shape, F32),
        ]
        + [
            jax.ShapeDtypeStruct(FromPlane.result(Reduce.result(a.shape, chips), chips), BF16)
            for a in grads
        ],
        [block] * 5 + [parted] * 2
        + [
            pltpu.VMEM(small.shape, F32), pltpu.VMEM((count,) + small.shape, F32),
            pltpu.VMEM((4,) + small.shape, F32), pltpu.VMEM(small.shape, F32),
        ]
        + sems(3, PIECES) + sems(count) + sems(count) + sems(count) + sems(4) + chained,
        (order, partial, x, gain, grad, *terms, *grads), number, "final_step", rows * width * 20,
    )


def only_jobs_kernel(jobs):
    wait_greetings(jobs.greet())
    jobs.start()
    jobs.middle()
    jobs.finish()


def only_jobs(jobs, number):
    return carry_call(only_jobs_kernel, jobs, (), [], [], [], [], (), number, "weights_back", 0)[1]


def weights_out_kernel(small_ref, home_ref, *refs):
    ins, outs = refs[:12], refs[12:]
    for layer in range(2):
        total = lambda ref: ref[0].astype(F32) + ref[1].astype(F32)
        qkv, gate, aux, out, pair, down = (total(ref) for ref in ins[6 * layer : 6 * layer + 6])
        units = down.shape[1]
        outs[0][layer] = qkv[:, :KEY]
        outs[1][layer] = qkv[:, KEY : 2 * KEY]
        outs[2][layer] = qkv[:, 2 * KEY :]
        outs[3][layer] = gate
        turned = aux.T
        outs[4][layer] = turned[0:2, :]
        outs[14][layer] = turned[2:6, :]
        outs[5][layer] = out.T
        turned = pair.T
        outs[6][layer] = turned[:units, :]
        outs[7][layer] = turned[units:, :]
        outs[8][layer] = down.T
    outs[15][...] = home_ref[...].astype(F32)
    at = 0
    for ref in outs[9:12]:
        for layer in range(2):
            for r in range(ref.shape[1] // LANES):
                ref[layer : layer + 1, r * LANES : (r + 1) * LANES] = small_ref[at : at + 1, :]
                at += 1
    heads = outs[12].shape[1]
    for member in range(2):
        for layer in range(2):
            first = (2 * member + layer) * heads
            outs[12 + member][layer : layer + 1, :] = small_ref[at : at + 1, first : first + heads]


def weights_out(small, home, first, second, heads):
    width = home.shape[1]
    rows, units = first[0].shape[1], first[5].shape[2]
    shapes = [
        (2, rows, KEY), (2, rows, KEY), (2, rows, VAL), (2, rows, VAL), (2, 2, rows), (2, VAL, rows),
        (2, units, rows), (2, units, rows), (2, units, rows),
        (2, width), (2, width), (2, VAL), (2, heads), (2, heads), (2, 4, rows), home.shape,
    ]
    vmem = pl.BlockSpec(memory_space=pltpu.VMEM)
    return pl.pallas_call(
        weights_out_kernel,
        in_specs=[vmem] * 14,
        out_specs=[vmem] * 16,
        out_shape=[jax.ShapeDtypeStruct(shape, F32) for shape in shapes],
        compiler_params=pltpu.CompilerParams(vmem_limit_bytes=56 * 1024 * 1024),
        name="weights_out",
    )(small, home, *first, *second)


def ffn_parts(x, pair):
    paired = mm(x, pair)
    units = paired.shape[1] // 2
    gate, up = paired[:, :units], paired[:, units:]
    act, sig = silu_of(gate)
    return gate, up, act, sig


def begin_jobs(jobs, at, steps):
    if jobs.kinds:
        @pl.when(at == 0)
        def _():
            wait_greetings(jobs.greet())
            jobs.start()

        @pl.when(at == steps // 2)
        def _():
            jobs.middle()


def end_jobs(jobs, at, steps):
    if jobs.kinds:
        @pl.when(at == steps - 1)
        def _():
            jobs.finish()


def ffn_forward_kernel(jobs, x_ref, pair_ref, down_ref, part_ref):
    at, steps = pl.program_id(0), pl.num_programs(0)
    begin_jobs(jobs, at, steps)
    _, up, act, _ = ffn_parts(x_ref[...], pair_ref[...])
    part_ref[...] = mm((act * up).astype(BF16), down_ref[...], NT).astype(BF16)
    end_jobs(jobs, at, steps)


def whole(shape):
    return pl.BlockSpec(shape, lambda i: (0, 0), pipeline_mode=pl.Buffered(1))


def ffn_forward(x, pair, down, jobs, number):
    length, width = x.shape
    rows = pl.BlockSpec((CHUNK, width), lambda i: (i, 0))
    return carry_call(
        ffn_forward_kernel, jobs, (length // CHUNK,),
        [rows, whole(pair.shape), whole(down.shape)], [rows],
        [jax.ShapeDtypeStruct((length, width), BF16)], [], (x, pair, down), number, "ffn_forward",
        4 * 10**9,
    )


def ffn_backward_kernel(both, jobs, x_ref, g_ref, pair_ref, down_ref, *refs):
    outs, (low_ref, hidden_ref) = refs[:-2], refs[-2:]
    part_ref, dpair_ref, ddown_ref = outs[:3]
    at, steps = pl.program_id(0), pl.num_programs(0)
    chunks = steps // 2
    begin_jobs(jobs, at, steps)

    @pl.when(at < chunks)
    def _():
        rows = pl.ds(pl.multiple_of(at * CHUNK, CHUNK), CHUNK)
        gate, up, act, sig = ffn_parts(x_ref[rows, :], pair_ref[...])
        hidden = (act * up).astype(BF16)
        hidden_ref[rows, :] = hidden
        if both:
            outs[3][...] = mm(hidden, down_ref[...], NT).astype(BF16)
        dhidden = mm(g_ref[rows, :], down_ref[...])
        dgate = dhidden * up * (sig * (1.0 + gate * (1.0 - sig)))
        low = jnp.concatenate([dgate, dhidden * act], axis=1).astype(BF16)
        low_ref[rows, :] = low
        part_ref[...] = mm(low, pair_ref[...], NT).astype(BF16)

    @pl.when(at >= chunks)
    def _():
        columns = pl.ds(pl.multiple_of((at - chunks) * CHUNK, CHUNK), CHUNK)
        dpair_ref[...] = mm(x_ref[:, columns], low_ref[...], TN).astype(BF16)
        ddown_ref[...] = mm(g_ref[:, columns], hidden_ref[...], TN).astype(BF16)

    end_jobs(jobs, at, steps)


def ffn_backward(x, g, pair, down, jobs, number, both=False):
    length, width = x.shape
    chunks = length // CHUNK
    assert length == width
    rows = pl.BlockSpec((CHUNK, width), lambda i: (jnp.minimum(i, chunks - 1), 0))
    late = lambda cols: pl.BlockSpec((CHUNK, cols), lambda i: (jnp.maximum(i - chunks, 0), 0))
    out = lambda cols: jax.ShapeDtypeStruct((length, cols), BF16)
    return carry_call(
        functools.partial(ffn_backward_kernel, both), jobs, (2 * chunks,),
        [whole(x.shape), whole(g.shape), whole(pair.shape), whole(down.shape)],
        [rows, late(pair.shape[1]), late(down.shape[1])] + [rows] * both,
        [out(width), out(pair.shape[1]), out(down.shape[1])] + [out(width)] * both,
        [pltpu.VMEM((length, pair.shape[1]), BF16), pltpu.VMEM((length, down.shape[1]), BF16)],
        (x, g, pair, down), number, "ffn_backward", 12 * 10**9,
    )


def dot32(a, b, dims):
    return lax.dot_general(a, b, dims, preferred_element_type=F32)


def row_major(x):
    return with_layout_constraint(x, Layout(major_to_minor=tuple(range(x.ndim))))


def linear(sizes, index):
    place = 0
    for size, at in zip(sizes, index):
        place = place * size + at
    return place


class Roles:
    def __init__(self):
        self.sizes = tuple(lax.axis_size(name) for name in AXES)
        self.chips, self.cores, self.zps, self.zls = self.sizes
        assert self.cores == 2 and self.zps == 2 and self.zls == 2

    def every(self):
        for chip in range(self.chips):
            for core in range(2):
                for zp in range(2):
                    for zl in range(2):
                        yield chip, core, zp, zl

    def rows_pairs(self):
        pairs = []
        for chip, core, zp, zl in self.every():
            slot, part = chip * 2 + zp, zl * 2 + core
            source = linear(self.sizes, (slot // 2, slot % 2, part // 2, part % 2))
            pairs.append((source, linear(self.sizes, (chip, core, zp, zl))))
        return pairs

    def weight_pairs(self, which):
        pairs = []
        for chip, core, zp, zl in self.every():
            head = zp * 2 + zl
            to = (chip, head % 2, core ^ which, head // 2)
            pairs.append(
                (linear(self.sizes, (chip, core, zp, zl)), linear(self.sizes, to))
            )
        return pairs


def flipped(pairs):
    return [(b, a) for a, b in pairs]


def chip_gather(ordered):
    return lax.all_gather(ordered, "chip", axis=0, tiled=True)


def to_plane(pack, roles):
    halves = [lax.ppermute(pack, AXES, roles.weight_pairs(which)) for which in range(2)]
    swap = lax.axis_index("zp") == 1
    return jnp.concatenate(
        [jnp.where(swap, halves[1], halves[0]), jnp.where(swap, halves[0], halves[1])], axis=0
    )


def summed(parts, kind):
    return jnp.sum(parts.astype(F32), axis=0).astype(kind)


def deal(values, order):
    spread = lax.all_to_all(values, ("chip", "core"), split_axis=2, concat_axis=1, tiled=True)
    picked = jnp.take(spread, order, axis=1)
    return lax.all_to_all(picked, ("chip", "core"), split_axis=1, concat_axis=2, tiled=True)


def shards(
    tokens, lengths, order, norm_mix, w_query, w_key, w_value, w_gate, w_decay, conv_filter,
    log_rate, step_bias, norm_heads, w_out, norm_ffn, w_ffn_gate, w_ffn_up, w_ffn_down, cotangent,
):
    roles = Roles()
    layer_count = w_query.shape[0]
    assert layer_count == 2
    heads_total = log_rate.shape[1]
    chip, core, zp, zl = (lax.axis_index(name) for name in AXES)
    head = zl * 2 + core
    rows_local, slots_local, width = tokens.shape
    assert slots_local == 1 and w_decay.shape[2] == 1
    slot_total = order.shape[0]
    units = w_ffn_gate.shape[2]
    rows_part = w_query.shape[1]
    to_roles = roles.rows_pairs()

    def carry(*jobs):
        return Jobs(list(jobs), roles.chips)

    scalars = (log_rate, step_bias)
    kernel_deal = rows_local % (16 * slot_total) == 0
    if kernel_deal:
        turned = lambda w: w.transpose(0, 2, 1)
        raw = (
            w_query, w_key, w_value, w_gate, turned(w_decay[:, :, 0, :]), conv_filter[:, :, 0, :],
            w_out, turned(w_ffn_gate), turned(w_ffn_up), w_ffn_down,
        )
        (residual, rows_in, start, qkv_next, mix_next, pair_first, pair_next, down_first, down_next,
         qkv, mix, _, _) = deal_and_gather(
            order, lengths, tokens[:, 0, :], norm_mix, cotangent[:, 0, :], raw, roles.chips, 1
        )
    else:
        qkv_packs, mix_packs, pair_packs, down_packs = [], [], [], []
        for layer in range(layer_count):
            aux = jnp.concatenate([w_decay[layer, :, 0, :], conv_filter[layer, :, 0, :].T], axis=1)
            aux = jnp.pad(aux, ((0, 0), (0, LANES - aux.shape[1])))
            qkv_packs.append(
                row_major(jnp.concatenate([w_query[layer], w_key[layer], w_value[layer]], axis=1))
            )
            mix_packs.append(
                row_major(jnp.concatenate([w_gate[layer], w_out[layer].T, aux], axis=1))
            )
            pair_packs.append(
                row_major(jnp.concatenate([w_ffn_gate[layer], w_ffn_up[layer]], axis=1))
            )
            down_packs.append(row_major(w_ffn_down[layer].T))
        qkv_next, mix_next = qkv_packs[1], mix_packs[1]
        (pair_first, pair_next), (down_first, down_next) = pair_packs, down_packs
        positions = (zp * 2 + zl) * rows_local + jnp.arange(rows_local)
        start = cotangent[:, 0, :] * (positions < lengths[order[chip * 2 + core]]).astype(BF16)[:, None]
        residual = lax.ppermute(deal(tokens, order)[:, 0, :], AXES, to_roles)
        (rows_in,), _ = first_gather(residual, norm_mix, 0, carry(), 1)
        qkv = chip_gather(to_plane(qkv_packs[0], roles))
        mix = chip_gather(to_plane(mix_packs[0], roles))

    def in_gradients(rows_in, dqkv, dgate):
        return dot32(rows_in, dqkv, TN).astype(BF16), dot32(rows_in, dgate, TN).astype(BF16)

    (part, heads0, *kept0), (pair_wide, down_wide) = mixer_forward(
        0, rows_in, qkv, mix, norm_heads, scalars,
        carry((ToPlane, pair_first), (ToPlane, down_first)), 2,
    )
    rows_in0, qkv0, mix0, residual0 = rows_in, qkv, mix, residual
    (middle0, rows_ffn0), (pair0, down0, qkv_wide, mix_wide) = forward_bridge(
        part, residual0, norm_ffn, 0,
        carry((Spread, pair_wide), (Spread, down_wide), (ToPlane, qkv_next), (ToPlane, mix_next)), 3,
    )
    (part,), _ = ffn_forward(rows_ffn0, pair0, down0, carry(), None)
    (residual1, rows_in1), (qkv1, mix1, down_wide) = forward_bridge(
        part, middle0, norm_mix, 1,
        carry((Spread, qkv_wide), (Spread, mix_wide), (ToPlane, down_next)), 4,
    )
    (part, heads1, *kept1), (down1, pair_wide, gradient) = mixer_forward(
        1, rows_in1, qkv1, mix1, norm_heads, scalars,
        carry((Spread, down_wide), (ToPlane, pair_next), (ToRole, start)), 5,
    )
    (middle1, rows_ffn1), (pair1, grad_rows) = forward_bridge(
        part, residual1, norm_ffn, 1, carry((Spread, pair_wide), (Share, gradient)), 6
    )
    (part, dpair1, ddown1, part_out), _ = ffn_backward(
        rows_ffn1, grad_rows, pair1, down1, carry(), None, both=True
    )

    (gradient, grad_rows, dgain_ffn1), (dpair1,) = backward_bridge(
        part, middle1, norm_ffn, 1, gradient, carry((Reduce, dpair1)), 7
    )
    dout1 = dot32(grad_rows, heads1, TN).astype(BF16)
    (part, dqkv, dgate, daux1, dgain1, dscalars1), jobs_results = mixer_backward(
        1, grad_rows, rows_in1, qkv1, mix1, norm_heads, scalars, kept1,
        carry((Reduce, ddown1), (Reduce, dout1), (FromPlane, dpair1), (ShareSum, part_out)), 8,
    )
    ddown1, dout1, pair_home1, total = jobs_results
    mixed = (middle1 + total.astype(F32)).astype(BF16)
    dqkv1, dgate1 = in_gradients(rows_in1, dqkv, dgate)
    results, jobs_results = backward_bridge(
        part, residual1, norm_mix, 1, gradient,
        carry((Reduce, dqkv1), (Reduce, dgate1), (Reduce, daux1), (FromRole, mixed)), 9,
    )
    gradient, grad_rows, dgain_mix1 = results
    dqkv1, dgate1, daux1, mixed = jobs_results
    (part, dpair0, ddown0), (qkv_home1, gate_home1, aux_home1) = ffn_backward(
        rows_ffn0, grad_rows, pair0, down0,
        carry((FromPlane, dqkv1), (FromPlane, dgate1), (FromPlane, daux1)), 14,
    )
    results, jobs_results = backward_bridge(
        part, middle0, norm_ffn, 0, gradient,
        carry((Reduce, dpair0)), 10,
    )
    gradient, grad_rows, dgain_ffn0 = results
    (dpair0,) = jobs_results
    dout0 = dot32(grad_rows, heads0, TN).astype(BF16)
    results, jobs_results = mixer_backward(
        0, grad_rows, rows_in0, qkv0, mix0, norm_heads, scalars, kept0,
        carry((Reduce, ddown0), (Reduce, dout0), (FromPlane, dpair0), (FromPlane, ddown1),
              (FromPlane, dout1)),
        11,
    )
    part, dqkv, dgate, daux0, dgain0, dscalars0 = results
    ddown0, dout0, pair_home0, down_home1, out_home1 = jobs_results
    dqkv0, dgate0 = in_gradients(rows_in0, dqkv, dgate)
    terms = (dgain_mix1, dgain_ffn0, dgain_ffn1, dgain0, dgain1, dscalars0, dscalars1)
    last = (dqkv0, dgate0, daux0)
    last_jobs = carry((FromPlane, ddown0), (FromPlane, dout0))
    if kernel_deal:
        (home, flat, *last), results = final_step(
            order, part, residual0, norm_mix, gradient, terms, last, roles.chips, last_jobs, 12
        )
    else:
        (gradient, dgain_mix), results = backward_last(
            part, residual0, norm_mix, 0, gradient, last_jobs, 12
        )
        mine = (jnp.arange(heads_total) == head).astype(F32)
        flat = jnp.concatenate(
            [dgain_mix[0], *(term[0] for term in terms[:5])]
            + [mine * term[row, 0] for row in range(2) for term in terms[5:]]
        )
        flat = jnp.pad(flat, (0, small_rows(width) * LANES - flat.shape[0])).reshape(-1, LANES)
        flat = lax.psum(flat, AXES)
        dealt_grad = lax.ppermute(gradient, AXES, flipped(to_roles))
        places = jnp.arange(slot_total, dtype=jnp.int32)
        inverse = jnp.sum(jnp.where(order[None, :] == places[:, None], places[None, :], 0), axis=1)
        home = deal(dealt_grad[:, None, :], inverse)[:, 0, :]
        last = only_jobs(carry(*[(Reduce, a) for a in last]), 13)
        last = only_jobs(carry(*[(FromPlane, a) for a in last]), 15)
    down_home0, out_home0 = results
    qkv_home0, gate_home0, aux_home0 = last
    first = (qkv_home0, gate_home0, aux_home0, out_home0, pair_home0, down_home0)
    second = (qkv_home1, gate_home1, aux_home1, out_home1, pair_home1, down_home1)
    if rows_part % LANES == 0:
        outs = weights_out(flat, home, first, second, heads_total)
    else:
        flat = flat.reshape(-1)
        small, at = [], 0
        for size in (width, width, VAL, heads_total, heads_total):
            small.append(flat[at : at + layer_count * size].reshape(layer_count, size))
            at += layer_count * size
        qkv, gate, aux, out, pair, down = (
            jnp.stack([summed(a, F32), summed(b, F32)]) for a, b in zip(first, second)
        )
        turned = lambda a: a.transpose(0, 2, 1)
        outs = [
            qkv[:, :, :KEY], qkv[:, :, KEY : 2 * KEY], qkv[:, :, 2 * KEY :], gate, turned(aux)[:, :2],
            turned(out), turned(pair)[:, :units], turned(pair)[:, units:], turned(down), *small,
            turned(aux)[:, 2:6], home.astype(F32),
        ]
    return (
        mixed[:, None, :],
        outs[15][:, None, :],
        outs[9],
        outs[0], outs[1], outs[2], outs[3],
        outs[4].transpose(0, 2, 1)[:, :, None, :],
        outs[14][:, :, None, :],
        outs[12],
        outs[13],
        outs[11],
        outs[5],
        outs[10],
        outs[6].transpose(0, 2, 1), outs[7].transpose(0, 2, 1), outs[8],
    )


def solution(mesh):
    dp, tensor = mesh.devices.shape
    mesh = Mesh(mesh.devices.reshape(dp // 2, 2, tensor // 2, 2), AXES)
    d, t = ("chip", "core"), ("zp", "zl")
    rows = P(t, d, None)
    by_rows, by_columns = P(None, d, t), P(None, t, d)
    heads, filters = P(None, d, t, None), P(None, None, t, d)
    return jax.shard_map(
        shards,
        mesh=mesh,
        in_specs=(
            rows, P(), P(), P(), by_rows, by_rows, by_rows, by_rows, heads, filters,
            P(), P(), P(), by_columns, P(), by_rows, by_rows, by_columns, rows,
        ),
        out_specs=(
            rows, rows, P(), by_rows, by_rows, by_rows, by_rows, heads, filters,
            P(), P(), P(), by_columns, P(), by_rows, by_rows, by_columns,
        ),
        check_vma=False,
    )
```

time: 898 us -> 629 us (0.70)
  waiting for transfers between devices: 142 us -> 0 us
  Pallas kernels: 483 us -> 591 us
  matrix products: 85.6 us -> 22.4 us
  local copies, waits for them, and re-layouts: 63.4 us -> 4.16 us
  starting transfers between devices: 45.7 us -> 0 us
  other arithmetic: 46.7 us -> 2.13 us
  between operations: 15.4 us -> 1.29 us
    pallas_call x13 -> x16, Pallas kernels: 483 us -> 591 us  [the longest x15 586 us: carry_call(): pl.pallas_call(carrying(body, jobs, len(args), outs), grid=grid, in_specs...]
    all_gather x5 -> x0, waiting for transfers between devices: 73.7 us -> none  [the longest x4 53.7 us: chip_gather(): lax.all_gather(row_major(ordered), 'chip', axis=0, tiled=True)]
    dot_general x18 -> x6, matrix products: 85.6 us -> 22.4 us  [dot32(): return lax.dot_general(a, b, dims, preferred_element_type=F32)]
    reduce_scatter x7 -> x0, waiting for transfers between devices: 46.7 us -> none  [the longest x6 46.7 us: chip_scatter(): return lax.psum_scatter(grads, 'chip', scatter_dimension=0, tiled=True)]
    ppermute x12 -> x0, starting transfers between devices: 44.8 us -> none  [the longest x10 42.4 us: weights_home(): lax.ppermute(half, AXES, flipped(roles.weight_pairs(which)))]
    unnamed x145 -> x18, local copies, waits for them, and re-layouts: 33.4 us -> 4.16 us
    ppermute x12 -> x0, waiting for transfers between devices: 20.4 us -> none  [the longest x10 20.4 us: weights_home(): lax.ppermute(half, AXES, flipped(roles.weight_pairs(which)))]
    concatenate x7 -> x0, other arithmetic: 12.7 us -> none  [the longest x2 4.88 us: shards(): jnp.concatenate([dot32(rows_ffn, paired_low, TN).astype(BF16), dot32(grad...]
  transfers between devices with their start and end apart: 24 -> 0, of which waited for: 7 -> 0; matrix products, arithmetic and copies ran while one was open for 14% -> 0% of each run, Pallas kernels for 36% -> 0%
where the time goes in v4:
time: 629 us; the launch traced here: 621 us
  Pallas kernels  591 us (94%)
  matrix products  22.4 us (4%)
    pallas_call x15, Pallas kernels, carry_call(): pl.pallas_call(carrying(body, jobs, len(args), outs), grid=grid, in_specs...  586 us
    dot_general x6, matrix products, dot32(): return lax.dot_general(a, b, dims, preferred_element_type=F32)  22.4 us

profile of v4, /device:TPU:0, one launch (start us, length us, event | category | flops | bytes accessed | tf_op | source)
XLA Modules:
  0.0 621.2 jit_solution(6794637346982850584)
XLA Ops:
  0.7 63.0 %deal_and_gather.1 = (bf16[256,1024]{1,0:T(8,128)(2,1)}, bf16[1024,1024]{1,0:T(8,128)(2,1)}, bf16[256,1024]{1,0:T(8,128)(2,1)}, bf16[128,1024]{1,0:T(8,128)(2,1)...) custom-call(s32[8]{0:T(128)} %refs_0_.11, ...), custom_call_target="tpu_custom_call" | custom-call | flops 5242880 | bytes 83886080 | tf_op jit(solution)/shard_map/deal_and_gather/pallas_call | solution.py:1125
  63.7 45.0 %mixer_forward.2 = (bf16[1024,1024]{1,0:T(8,128)(2,1)}, bf16[1024,512]{1,0:T(8,128)(2,1)}, f32[1024,1024]{1,0:T(8,128)}, f32[1024,512]{1,0:T(8,128)}, f32[1024,1...) custom-call(bf16[2,4]{1,0:T(2,128)(2,1)} %refs_0_.10, ...), custom_call_target="tpu_custom_call" | custom-call | flops 16000000000 | bytes 83886080 | tf_op jit(solution)/shard_map/mixer_forward/pallas_call | solution.py:1125
  108.7 46.7 %forward_bridge.3 = (f32[256,1024]{1,0:T(8,128)}, bf16[1024,1024]{1,0:T(8,128)(2,1)}, bf16[1024,1408]{1,0:T(8,128)(2,1)}, bf16[1024,704]{1,0:T(8,128)(2,1)}, bf1...) custom-call(bf16[1024,1024]{1,0:T(8,128)(2,1)} %get-tuple-element.140.refs_0_, ...), custom_call_target="tpu_custom_call" | custom-call | flops 5242880 | bytes 83886080 | tf_op jit(solution)/shard_map/forward_bridge/pallas_call | solution.py:1125
  155.3 9.3 %ffn_forward.1.refs_0_ = bf16[1024,1024]{1,0:T(8,128)(2,1)} custom-call(bf16[1024,1024]{1,0:T(8,128)(2,1)} %get-tuple-element.146.refs_0_, bf16[1024,1408]{1,0:T(8,128)(2,1)} %get-tuple-element.147.refs_1_.refs_2_, bf16[1024,704]{1,0:T(8,128)(2,1)} %get-tuple-element.148.refs_2_.refs_3_), custom_call_target="tpu_custom_call" | custom-call | flops 4000000000 | bytes 83886080 | tf_op jit(solution)/shard_map/ffn_forward/pallas_call | solution.py:1125
  164.6 45.5 %forward_bridge.4 = (f32[256,1024]{1,0:T(8,128)}, bf16[1024,1024]{1,0:T(8,128)(2,1)}, bf16[1024,1024]{1,0:T(8,128)(2,1)}, bf16[1024,1152]{1,0:T(8,128)(2,1)}, bf16[256,704]{1,0:T(8,128)(2,1)}) custom-call(bf16[1024,1024]{1,0:T(8,128)(2,1)} %ffn_forward.1.refs_0_, f32[256,1024]{1,0:T(8,128)} %get-tuple-element.149.refs_1_, bf16[2,1024]{1,0:T(2,128)(2,1)} %refs_3_.3, ...), custom_call_target="tpu_custom_call" | custom-call | flops 5242880 | bytes 83886080 | tf_op jit(solution)/shard_map/forward_bridge/pallas_call | solution.py:1125
  210.1 33.4 %mixer_forward.3 = (bf16[1024,1024]{1,0:T(8,128)(2,1)}, bf16[1024,512]{1,0:T(8,128)(2,1)}, f32[1024,1024]{1,0:T(8,128)}, f32[1024,512]{1,0:T(8,128)}, f32[1024,1...) custom-call(bf16[2,4]{1,0:T(2,128)(2,1)} %refs_0_.10, ...), custom_call_target="tpu_custom_call" | custom-call | flops 16000000000 | bytes 83886080 | tf_op jit(solution)/shard_map/mixer_forward/pallas_call | solution.py:1125
  243.5 45.0 %forward_bridge.5 = (f32[256,1024]{1,0:T(8,128)}, bf16[1024,1024]{1,0:T(8,128)(2,1)}, bf16[1024,1408]{1,0:T(8,128)(2,1)}, bf16[1024,1024]{1,0:T(8,128)(2,1)}) custom-call(bf16[1024,1024]{1,0:T(8,128)(2,1)} %get-tuple-element.159.refs_0_, f32[256,1024]{1,0:T(8,128)} %get-tuple-element.160.refs_1_, bf16[2,1024]{1,0:T(2,128)(2,1)} %refs_2_.11, ...), custom_call_target="tpu_custom_call" | custom-call | flops 5242880 | bytes 83886080 | tf_op jit(solution)/shard_map/forward_bridge/pallas_call | solution.py:1125
  288.5 23.5 %ffn_backward.2 = (bf16[1024,1024]{1,0:T(8,128)(2,1)}, bf16[1024,1408]{1,0:T(8,128)(2,1)}, bf16[1024,704]{1,0:T(8,128)(2,1)}, bf16[1024,1024]{1,0:T(8,128)(2,1)}) custom-call(bf16[1024,1024]{1,0:T(8,128)(2,1)} %get-tuple-element.163.refs_0_, bf16[1024,1024]{1,0:T(8,128)(2,1)} %get-tuple-element.164.refs_1_, bf16[1024,1408]{1,0:T(8,128)(2,1)} %get-tuple-element.165.refs_2_, ...), custom_call_target="tpu_custom_call" | custom-call | flops 12000000000 | bytes 83886080 | tf_op jit(solution)/shard_map/ffn_backward/pallas_call | solution.py:1125
  312.0 0.0 copy-start.5
  312.0 32.8 %backward_bridge.3 = (f32[256,1024]{1,0:T(8,128)}, bf16[1024,1024]{1,0:T(8,128)(2,1)}, f32[1,1024]{1,0:T(1,128)}, bf16[256,1408]{1,0:T(8,128)(2,1)}) custom-call(bf16[1024,1024]{1,0:T(8,128)(2,1)} %get-tuple-element.167.refs_0_, f32[256,1024]{1,0:T(8,128)} %get-tuple-element.168.refs_1_, bf16[2,1024]{1,0:T(2,128)(2,1)} %refs_2_.11, ...), custom_call_target="tpu_custom_call" | custom-call | flops 5242880 | bytes 83886080 | tf_op jit(solution)/shard_map/backward_bridge/pallas_call | solution.py:1125
  344.8 0.0 copy-done.5
  344.8 3.8 convolution_convert_fusion.5.refs_18_
  348.7 0.0 copy-start
  348.7 36.4 %mixer_backward.2 = (bf16[1024,1024]{1,0:T(8,128)(2,1)}, bf16[1024,1024]{1,0:T(8,128)(2,1)}, bf16[1024,512]{1,0:T(8,128)(2,1)}, bf16[1024,128]{1,0:T(8,128)(2,1)...) custom-call(bf16[2,4]{1,0:T(2,128)(2,1)} %refs_0_.10, ...), custom_call_target="tpu_custom_call" | custom-call | flops 16000000000 | bytes 83886080 | tf_op jit(solution)/shard_map/mixer_backward/pallas_call | solution.py:1125
  385.1 0.0 copy-start.3
  385.1 0.0 copy-done
  385.1 2.1 add_convert_fusion.refs_7_
  387.2 0.0 copy-done.3
  387.2 0.0 copy-start.6
  387.2 3.6 convolution_convert_fusion.4.refs_5_
  390.9 0.0 copy-done.6
  390.9 3.7 convolution_convert_fusion.1.refs_4_
  394.6 38.8 %backward_bridge.4 = (f32[256,1024]{1,0:T(8,128)}, bf16[1024,1024]{1,0:T(8,128)(2,1)}, f32[1,1024]{1,0:T(1,128)}, bf16[256,1024]{1,0:T(8,128)(2,1)}, bf16[256,51...) custom-call(bf16[1024,1024]{1,0:T(8,128)(2,1)} %get-tuple-element.182.refs_0_, ...), custom_call_target="tpu_custom_call" | custom-call | flops 5242880 | bytes 83886080 | tf_op jit(solution)/shard_map/backward_bridge/pallas_call | solution.py:1125
  433.5 26.7 %ffn_backward.3 = (bf16[1024,1024]{1,0:T(8,128)(2,1)}, bf16[1024,1408]{1,0:T(8,128)(2,1)}, bf16[1024,704]{1,0:T(8,128)(2,1)}, bf16[2,128,1024]{2,1,0:T(8,128)(2,...) custom-call(bf16[1024,1024]{1,0:T(8,128)(2,1)} %get-tuple-element.146.refs_0_, ...), custom_call_target="tpu_custom_call" | custom-call | flops 12000000000 | bytes 83886080 | tf_op jit(solution)/shard_map/ffn_backward/pallas_call | solution.py:1125
  460.2 0.0 copy-start.4
  460.2 33.1 %backward_bridge.5 = (f32[256,1024]{1,0:T(8,128)}, bf16[1024,1024]{1,0:T(8,128)(2,1)}, f32[1,1024]{1,0:T(1,128)}, bf16[256,1408]{1,0:T(8,128)(2,1)}) custom-call(bf16[1024,1024]{1,0:T(8,128)(2,1)} %get-tuple-element.193.refs_0_, f32[256,1024]{1,0:T(8,128)} %get-tuple-element.149.refs_1_, bf16[2,1024]{1,0:T(2,128)(2,1)} %refs_2_.11, ...), custom_call_target="tpu_custom_call" | custom-call | flops 5242880 | bytes 83886080 | tf_op jit(solution)/shard_map/backward_bridge/pallas_call | solution.py:1125
  493.3 0.0 copy-done.4
  493.3 3.8 convolution_convert_fusion.3.refs_18_
  497.2 0.0 copy-start.2
  497.2 38.1 %mixer_backward.3 = (bf16[1024,1024]{1,0:T(8,128)(2,1)}, bf16[1024,1024]{1,0:T(8,128)(2,1)}, bf16[1024,512]{1,0:T(8,128)(2,1)}, bf16[1024,128]{1,0:T(8,128)(2,1)...) custom-call(bf16[2,4]{1,0:T(2,128)(2,1)} %refs_0_.10, ...), custom_call_target="tpu_custom_call" | custom-call | flops 16000000000 | bytes 83886080 | tf_op jit(solution)/shard_map/mixer_backward/pallas_call | solution.py:1125
  535.2 0.0 copy-done.2
  535.3 0.0 copy-start.7
  535.3 3.6 convolution_convert_fusion.2.refs_13_
  538.9 0.0 copy-done.7
  538.9 3.7 convolution_convert_fusion.refs_12_
  542.6 68.6 %final_step.1 = (bf16[256,1024]{1,0:T(8,128)(2,1)}, f32[48,128]{1,0:T(8,128)}, bf16[2,128,1024]{2,1,0:T(8,128)(2,1)}, bf16[2,128,512]{2,1,0:T(8,128)(2,1)}, bf16...) custom-call(s32[8]{0:T(128)} %refs_0_.11, ...), custom_call_target="tpu_custom_call" | custom-call | flops 5242880 | bytes 83886080 | tf_op jit(solution)/shard_map/final_step/pallas_call | solution.py:1125
  611.2 5.4 weights_out.1
  616.7 0.0 copy-start.1
  616.7 3.3 copy.36
  620.0 0.0 copy-done.1
  620.0 0.8 copy.40
Async XLA Ops:
  312.0 32.8 %copy-start.5 = (bf16[1024,512]{1,0:T(8,128)(2,1)S(1)}, bf16[1024,512]{1,0:T(8,128)(2,1)}, u32[]{:S(2)}) copy-start(bf16[1024,512]{1,0:T(8,128)(2,1)} %get-tuple-element.179) | copy-start | bytes 3145732
  348.7 36.4 %copy-start = (f32[256,1024]{1,0:T(8,128)S(1)}, f32[256,1024]{1,0:T(8,128)}, u32[]{:S(2)}) copy-start(f32[256,1024]{1,0:T(8,128)} %get-tuple-element.168.refs_1_) | copy-start | bytes 3145732
  385.1 2.2 copy-start.3
  387.2 3.6 copy-start.6
  460.2 33.1 %copy-start.4 = (bf16[1024,512]{1,0:T(8,128)(2,1)S(1)}, bf16[1024,512]{1,0:T(8,128)(2,1)}, u32[]{:S(2)}) copy-start(bf16[1024,512]{1,0:T(8,128)(2,1)} %get-tuple-element.205) | copy-start | bytes 3145732
  497.2 38.1 %copy-start.2 = (bf16[1024,1024]{1,0:T(8,128)(2,1)S(1)}, bf16[1024,1024]{1,0:T(8,128)(2,1)}, u32[]{:S(2)}) copy-start(bf16[1024,1024]{1,0:T(8,128)(2,1)} %get-tuple-element.135.refs_2_.refs_3_) | copy-start | bytes 6291460
  535.3 3.6 copy-start.7
  616.7 3.3 copy-start.1

commit v5 on v4

--- a/solution.py
+++ b/solution.py
@@ -87,16 +87,17 @@
     return decay, jnp.exp(total), jnp.exp(last - total), jnp.exp(last)
 
 
-def solve_unit(coupling, rows, cols, product):
+def solve_unit(coupling, rows, cols):
+    unit = jnp.where(rows == cols, 1.0, 0.0)
     same = ((rows >> 1) == (cols >> 1)) & (rows != cols)
-    inverse = jnp.where(rows == cols, 1.0, 0.0) - jnp.where(same, coupling, 0.0)
+    inverse = unit - jnp.where(same, coupling, 0.0)
     for level in range(1, CHUNK.bit_length() - 1):
         between = ((rows >> (level + 1)) == (cols >> (level + 1))) & (
             (rows >> level) != (cols >> level)
         )
         part = jnp.where(between, coupling, 0.0)
-        inverse = inverse - product(product(inverse, part), inverse)
-    return inverse
+        inverse = inverse - mm(mm(inverse, part), inverse)
+    return inverse + mm(inverse, unit - inverse - mm3(coupling, inverse))
 
 
 def silu_of(x):
@@ -112,8 +113,8 @@
 
 
 def forward_kernel(
-    layer, jobs, rate_ref, bias_ref, x_ref, w_qkv_ref, w_gate_ref, w_aux_ref, w_out_ref, gain_ref,
-    part_ref, heads_ref, proj_ref, gate_ref, rates_ref, inverse_ref, fresh_ref, o_ref, state_ref,
+    layer, jobs, rate_ref, bias_ref, x_ref, w_qkv_ref, w_gate_ref, w_aux_ref, gain_ref,
+    heads_ref, proj_ref, conv_ref, gate_ref, rates_ref, inverse_ref, fresh_ref, o_ref, state_ref,
     padded, memory, taps_ref,
 ):
     begin_jobs(jobs, pl.program_id(0), pl.num_programs(0))
@@ -133,6 +134,7 @@
     padded[8 : 8 + CHUNK, :] = qkv
     conv = conv_rows(padded, taps_ref, 5)
     padded[0:8, :] = qkv[CHUNK - 8 :, :]
+    conv_ref[...] = conv
     act, _ = silu_of(conv)
     q, k, v = act[:, :KEY], act[:, KEY : 2 * KEY], act[:, 2 * KEY :]
     q = q * (lax.rsqrt(jnp.sum(q * q, axis=1, keepdims=True) + 1e-6) * KEY**-0.5)
@@ -141,7 +143,7 @@
     write, step, _ = rates_of(rates, *head_scalars((rate_ref, bias_ref), layer))
     decay, growth, rest, final = decay_terms(step, rows, cols)
     coupling = jnp.where(rows > cols, wide(write, CHUNK) * mm3(k, k, NT) * decay, 0.0)
-    inverse = solve_unit(coupling, rows, cols, mm3)
+    inverse = solve_unit(coupling, rows, cols)
     inverse_ref[...] = inverse.astype(BF16)
     within = mm(q, k, NT) * decay
     state = memory[...]
@@ -156,7 +158,6 @@
     scaled = o * lax.rsqrt(jnp.mean(o * o, axis=1, keepdims=True) + 1e-5) * gain_ref[layer : layer + 1, :].astype(F32)
     heads = (scaled * silu_of(gate_in)[0]).astype(BF16)
     heads_ref[...] = heads
-    part_ref[...] = mm(heads, w_out_ref[...], NT).astype(BF16)
     end_jobs(jobs, pl.program_id(0), pl.num_programs(0))
 
 
@@ -169,8 +170,7 @@
     return [
         fixed((width, CONV_CH), 0),
         fixed((width, VAL), 0),
-        fixed((width, LANES), 2 * VAL // LANES),
-        fixed((width, VAL), 1),
+        fixed((width, LANES), VAL // LANES),
         fixed((2, VAL), 0),
     ]
 
@@ -184,11 +184,11 @@
         functools.partial(forward_kernel, layer), jobs, (chunks,),
         [head_spec(scalars[0]), head_spec(scalars[1]), row(width)] + weight_specs(width),
         [
-            row(width), row(VAL), row(CONV_CH), row(VAL), row(LANES), row(CHUNK), row(VAL), row(VAL),
+            row(VAL), row(CONV_CH), row(CONV_CH), row(VAL), row(LANES), row(CHUNK), row(VAL), row(VAL),
             pl.BlockSpec((None, KEY, VAL), lambda i: (i, 0, 0)),
         ],
         [
-            out(width, BF16), out(VAL, BF16), out(CONV_CH, F32), out(VAL, F32), out(LANES, F32),
+            out(VAL, BF16), out(CONV_CH, F32), out(CONV_CH, F32), out(VAL, F32), out(LANES, F32),
             out(CHUNK, BF16), out(VAL, F32), out(VAL, F32),
             jax.ShapeDtypeStruct((chunks, KEY, VAL), F32),
         ],
@@ -196,7 +196,7 @@
             pltpu.VMEM((CHUNK + 8, CONV_CH), F32), pltpu.VMEM((KEY, VAL), F32),
             pltpu.VMEM((4, CONV_CH), F32),
         ],
-        (*scalars, x, qkv, pack, pack, pack, gain), number, "mixer_forward", 16 * 10**9,
+        (*scalars, x, qkv, pack, pack, gain), number, "mixer_forward", 16 * 10**9,
     )
 
 
@@ -207,14 +207,15 @@
 
 
 def backward_kernel(
-    layer, jobs, rate_ref, bias_ref, g_ref, x_ref, w_qkv_ref, w_gate_ref, w_aux_ref, w_out_ref, gain_ref,
-    proj_ref, halo_ref, gate_ref, rates_ref, inverse_ref, fresh_ref, o_ref, state_ref,
-    part_ref, dqkv_ref, dgate_ref, daux_ref, dgain_ref, dscalars_ref,
-    padded, dpadded, dmemory, taps_ref, dtaps_ref, daux_sum,
+    layer, jobs, rate_ref, bias_ref, g_ref, x_ref, w_out_ref, w_qkv_ref, w_gate_ref, w_aux_ref, gain_ref,
+    proj_ref, halo_ref, conv_ref, gate_ref, rates_ref, inverse_ref, fresh_ref, o_ref, state_ref,
+    part_ref, din_ref, daux_ref, dgain_ref, dscalars_ref,
+    padded, dpadded, dmemory, taps_ref, dtaps_ref, daux_sum, x_held, dproj_ref,
 ):
-    begin_jobs(jobs, pl.program_id(0), pl.num_programs(0))
-    at = pl.program_id(0)
-    last = pl.num_programs(0) - 1
+    at, steps = pl.program_id(0), pl.num_programs(0)
+    chunks = steps // 2
+    last = chunks - 1
+    begin_jobs(jobs, at, steps, (chunks // 2, chunks - 1))
 
     @pl.when(at == 0)
     def _():
@@ -226,142 +227,154 @@
         dgain_ref[...] = jnp.zeros_like(dgain_ref)
         dscalars_ref[...] = jnp.zeros_like(dscalars_ref)
 
-    rows, cols = iotas()
-    padded[8 : 8 + CHUNK, :] = proj_ref[...]
-    padded[0:8, :] = jnp.where(at == last, 0.0, halo_ref[...])
-    conv = conv_rows(padded, taps_ref, 5)
-    act, sig = silu_of(conv)
-    act_q, act_k, v = act[:, :KEY], act[:, KEY : 2 * KEY], act[:, 2 * KEY :]
-    q = act_q * (lax.rsqrt(jnp.sum(act_q * act_q, axis=1, keepdims=True) + 1e-6) * KEY**-0.5)
-    k = act_k * lax.rsqrt(jnp.sum(act_k * act_k, axis=1, keepdims=True) + 1e-6)
-    rates = rates_ref[...]
-    write, step, sig_decay = rates_of(rates, *head_scalars((rate_ref, bias_ref), layer))
-    decay, growth, rest, final = decay_terms(step, rows, cols)
-    growth_v = wide(growth, VAL)
-    write_v = wide(write, VAL)
-    low_q, low_k = q.astype(BF16), k.astype(BF16)
-    below = rows > cols
-    strict_decay = jnp.where(below, decay, 0.0)
-    keys = mm(low_k, low_k, NT) * strict_decay * wide(write, CHUNK)
-    within = mm(low_q, low_k, NT) * decay
-    dheads = mm(g_ref[...], w_out_ref[...])
-    o = o_ref[...]
-    gate_in = gate_ref[...]
-    gate, gate_sig = silu_of(gate_in)
-    inv = lax.rsqrt(jnp.mean(o * o, axis=1, keepdims=True) + 1e-5)
-    normal = o * inv
-    gain = gain_ref[layer : layer + 1, :].astype(F32)
-    dgate = dheads * normal * gain * (gate_sig * (1.0 + gate_in * (1.0 - gate_sig)))
-    dscaled = dheads * gate
-    dgain_ref[...] += jnp.sum(dscaled * normal, axis=0, keepdims=True)
-    dnormal = dscaled * gain
-    do = inv * (dnormal - normal * jnp.mean(dnormal * normal, axis=1, keepdims=True))
-    state = state_ref[...]
-    low_state = state.astype(BF16)
-    fresh = fresh_ref[...]
-    low_fresh = fresh.astype(BF16)
-    dstate = dmemory[...]
-    low_dstate = dstate.astype(BF16)
-    low_do = do.astype(BF16)
-    k_rest = k * wide(rest, KEY)
-    rest_dstate = mm(k_rest, low_dstate)
-    dfresh = mm(within, low_do, TN) + rest_dstate
-    dsource = mm(inverse_ref[...], dfresh, TN)
-    low_dsource = dsource.astype(BF16)
-    dv = write_v * dsource
-    dread = -(growth_v * dv)
-    low_dread = dread.astype(BF16)
-    do_growth = growth_v * do
-    low_do_growth = do_growth.astype(BF16)
-    dwithin = mm(low_do, low_fresh, NT)
-    dcoupling = -mm(low_dsource, low_fresh, NT)
-    dkeys = dcoupling * strict_decay * wide(write, CHUNK)
-    dpairs = dwithin * decay
-    dq = mm(low_do_growth, low_state, NT) + mm(dpairs, low_k)
-    dk = (
-        mm(low_dread, low_state, NT)
-        + mm(dpairs, low_q, TN)
-        + mm(dkeys + dkeys.T, low_k)
-        + wide(rest, KEY) * mm(low_fresh, low_dstate, NT)
-    )
-    dmemory[...] = (
-        wide(final, VAL) * dstate + mm(low_q, low_do_growth, TN) + mm(low_k, low_dread, TN)
-    )
-    spread = dwithin * within + dcoupling * keys
-    straddle = jnp.where(below, mm_exact_left((rows <= cols).astype(BF16), spread), 0.0)
-    read_rows = jnp.sum(
-        do_growth * mm(low_q, low_state) + dread * mm(low_k, low_state), axis=1, keepdims=True
-    )
-    rest_rows = jnp.sum(fresh * rest_dstate, axis=1, keepdims=True)
-    carried = jnp.sum(dstate * state) * final[0:1, 0:1]
-    suffix = mm_exact_left(
-        (rows <= cols).astype(BF16), jnp.broadcast_to(read_rows, (CHUNK, LANES))
-    ) + mm_exact_left((rows > cols).astype(BF16), jnp.broadcast_to(rest_rows, (CHUNK, LANES)))
-    dstep = suffix + jnp.sum(straddle, axis=1, keepdims=True) + carried
-    dlogit = dstep * (-head_scalars((rate_ref, bias_ref), layer)[0]) * sig_decay
-    dwrite = (1.0 - write) * jnp.sum(dsource * fresh, axis=1, keepdims=True)
-    lane = lax.broadcasted_iota(jnp.int32, (CHUNK, LANES), 1)
-    drates = jnp.where(lane == 0, dwrite, jnp.where(lane == 1, dlogit, 0.0))
-    low_drates = drates.astype(BF16)
-    daux_sum[...] += mm(x_ref[...], low_drates, TN)
-    dscalars_ref[0:1, :] += jnp.sum(dstep * step, axis=0, keepdims=True)
-    dscalars_ref[1:2, :] += jnp.sum(dlogit, axis=0, keepdims=True)
-    dact = jnp.concatenate(
-        [unit_back(dq, act_q, KEY**-0.5), unit_back(dk, act_k, 1.0), dv], axis=1
-    )
-    dconv = dact * (sig * (1.0 + conv * (1.0 - sig)))
-    dpadded[0:CHUNK, :] = dconv
-    dtaps_ref[2:6, :] += jnp.concatenate(
-        [
-            jnp.sum(dconv * padded[5 + j : 5 + j + CHUNK, :], axis=0, keepdims=True)
-            for j in range(4)
-        ],
-        axis=0,
-    )
-    dqkv = dconv * taps_ref[3:4, :]
-    for j in range(3):
-        dqkv = dqkv + dpadded[pl.ds(3 - j, CHUNK), :] * taps_ref[j : j + 1, :]
-    dpadded[CHUNK : CHUNK + 8, :] = dconv[0:8, :]
-    low_dqkv, low_dgate = dqkv.astype(BF16), dgate.astype(BF16)
-    dqkv_ref[...] = low_dqkv
-    dgate_ref[...] = low_dgate
-    part_ref[...] = (
-        mm(low_dqkv, w_qkv_ref[...], NT)
-        + mm(low_dgate, w_gate_ref[...], NT)
-        + mm(low_drates, w_aux_ref[...], NT)
-    ).astype(BF16)
+    @pl.when(at < chunks)
+    def _():
+        rows, cols = iotas()
+        padded[8 : 8 + CHUNK, :] = proj_ref[...]
+        padded[0:8, :] = jnp.where(at == last, 0.0, halo_ref[...])
+        conv = conv_ref[...]
+        act, sig = silu_of(conv)
+        act_q, act_k, v = act[:, :KEY], act[:, KEY : 2 * KEY], act[:, 2 * KEY :]
+        q = act_q * (lax.rsqrt(jnp.sum(act_q * act_q, axis=1, keepdims=True) + 1e-6) * KEY**-0.5)
+        k = act_k * lax.rsqrt(jnp.sum(act_k * act_k, axis=1, keepdims=True) + 1e-6)
+        rates = rates_ref[...]
+        write, step, sig_decay = rates_of(rates, *head_scalars((rate_ref, bias_ref), layer))
+        decay, growth, rest, final = decay_terms(step, rows, cols)
+        growth_v = wide(growth, VAL)
+        write_v = wide(write, VAL)
+        low_q, low_k = q.astype(BF16), k.astype(BF16)
+        below = rows > cols
+        strict_decay = jnp.where(below, decay, 0.0)
+        keys = mm(low_k, low_k, NT) * strict_decay * wide(write, CHUNK)
+        within = mm(low_q, low_k, NT) * decay
+        dheads = mm(g_ref[...], w_out_ref[...])
+        o = o_ref[...]
+        gate_in = gate_ref[...]
+        gate, gate_sig = silu_of(gate_in)
+        inv = lax.rsqrt(jnp.mean(o * o, axis=1, keepdims=True) + 1e-5)
+        normal = o * inv
+        gain = gain_ref[layer : layer + 1, :].astype(F32)
+        dgate = dheads * normal * gain * (gate_sig * (1.0 + gate_in * (1.0 - gate_sig)))
+        dscaled = dheads * gate
+        dgain_ref[...] += jnp.sum(dscaled * normal, axis=0, keepdims=True)
+        dnormal = dscaled * gain
+        do = inv * (dnormal - normal * jnp.mean(dnormal * normal, axis=1, keepdims=True))
+        state = state_ref[...]
+        low_state = state.astype(BF16)
+        fresh = fresh_ref[...]
+        low_fresh = fresh.astype(BF16)
+        dstate = dmemory[...]
+        low_dstate = dstate.astype(BF16)
+        low_do = do.astype(BF16)
+        k_rest = k * wide(rest, KEY)
+        rest_dstate = mm(k_rest, low_dstate)
+        dfresh = mm(within, low_do, TN) + rest_dstate
+        dsource = mm(inverse_ref[...], dfresh, TN)
+        low_dsource = dsource.astype(BF16)
+        dv = write_v * dsource
+        dread = -(growth_v * dv)
+        low_dread = dread.astype(BF16)
+        do_growth = growth_v * do
+        low_do_growth = do_growth.astype(BF16)
+        dwithin = mm(low_do, low_fresh, NT)
+        dcoupling = -mm(low_dsource, low_fresh, NT)
+        dkeys = dcoupling * strict_decay * wide(write, CHUNK)
+        dpairs = dwithin * decay
+        dq = mm(low_do_growth, low_state, NT) + mm(dpairs, low_k)
+        dk = (
+            mm(low_dread, low_state, NT)
+            + mm(dpairs, low_q, TN)
+            + mm(dkeys + dkeys.T, low_k)
+            + wide(rest, KEY) * mm(low_fresh, low_dstate, NT)
+        )
+        dmemory[...] = (
+            wide(final, VAL) * dstate + mm(low_q, low_do_growth, TN) + mm(low_k, low_dread, TN)
+        )
+        spread = dwithin * within + dcoupling * keys
+        straddle = jnp.where(below, mm_exact_left((rows <= cols).astype(BF16), spread), 0.0)
+        read_rows = jnp.sum(
+            do_growth * mm(low_q, low_state) + dread * mm(low_k, low_state), axis=1, keepdims=True
+        )
+        rest_rows = jnp.sum(fresh * rest_dstate, axis=1, keepdims=True)
+        carried = jnp.sum(dstate * state) * final[0:1, 0:1]
+        suffix = mm_exact_left(
+            (rows <= cols).astype(BF16), jnp.broadcast_to(read_rows, (CHUNK, LANES))
+        ) + mm_exact_left((rows > cols).astype(BF16), jnp.broadcast_to(rest_rows, (CHUNK, LANES)))
+        dstep = suffix + jnp.sum(straddle, axis=1, keepdims=True) + carried
+        dlogit = dstep * (-head_scalars((rate_ref, bias_ref), layer)[0]) * sig_decay
+        dwrite = (1.0 - write) * jnp.sum(dsource * fresh, axis=1, keepdims=True)
+        lane = lax.broadcasted_iota(jnp.int32, (CHUNK, LANES), 1)
+        drates = jnp.where(lane == 0, dwrite, jnp.where(lane == 1, dlogit, 0.0))
+        low_drates = drates.astype(BF16)
+        daux_sum[...] += mm(low_drates, x_ref[...], TN)
+        dscalars_ref[0:1, :] += jnp.sum(dstep * step, axis=0, keepdims=True)
+        dscalars_ref[1:2, :] += jnp.sum(dlogit, axis=0, keepdims=True)
+        dact = jnp.concatenate(
+            [unit_back(dq, act_q, KEY**-0.5), unit_back(dk, act_k, 1.0), dv], axis=1
+        )
+        dconv = dact * (sig * (1.0 + conv * (1.0 - sig)))
+        dpadded[0:CHUNK, :] = dconv
+        dtaps_ref[2:6, :] += jnp.concatenate(
+            [
+                jnp.sum(dconv * padded[5 + j : 5 + j + CHUNK, :], axis=0, keepdims=True)
+                for j in range(4)
+            ],
+            axis=0,
+        )
+        dqkv = dconv * taps_ref[3:4, :]
+        for j in range(3):
+            dqkv = dqkv + dpadded[pl.ds(3 - j, CHUNK), :] * taps_ref[j : j + 1, :]
+        dpadded[CHUNK : CHUNK + 8, :] = dconv[0:8, :]
+        low_dqkv, low_dgate = dqkv.astype(BF16), dgate.astype(BF16)
+        place = block(last - at, CHUNK)
+        dproj_ref[place, :CONV_CH] = low_dqkv
+        dproj_ref[place, CONV_CH:] = low_dgate
+        x_held[place, :] = x_ref[...]
+        part_ref[...] = (
+            mm(low_dqkv, w_qkv_ref[...], NT)
+            + mm(low_dgate, w_gate_ref[...], NT)
+            + mm(low_drates, w_aux_ref[...], NT)
+        ).astype(BF16)
 
     @pl.when(at == last)
     def _():
-        daux_ref[...] = (daux_sum[...] + dtaps_ref[...].T).astype(BF16)
-
-    end_jobs(jobs, pl.program_id(0), pl.num_programs(0))
-
-
-def mixer_backward(layer, g, x, qkv, pack, gain, scalars, saved, jobs, number):
-    proj, gate_in, rates, inverse, fresh, o, states = saved
+        daux_ref[...] = (daux_sum[...] + dtaps_ref[...]).T.astype(BF16)
+
+    @pl.when(at >= chunks)
+    def _():
+        columns = block(at - chunks, CHUNK)
+        din_ref[...] = mm(x_held[:, columns], dproj_ref[...], TN).astype(BF16)
+
+    end_jobs(jobs, at, steps)
+
+
+def mixer_backward(layer, g, x, qkv, pack, w_out, gain, scalars, saved, jobs, number):
+    proj, conv, gate_in, rates, inverse, fresh, o, states = saved
     length, width = g.shape
     chunks = length // CHUNK
     back = chunks - 1
-    row = lambda cols: pl.BlockSpec((CHUNK, cols), lambda i: (back - i, 0))
+    at = lambda i: jnp.maximum(back - i, 0)
+    row = lambda cols: pl.BlockSpec((CHUNK, cols), lambda i: (at(i), 0))
     out = lambda cols, kind: jax.ShapeDtypeStruct((length, cols), kind)
     steps = CHUNK // 8
     return carry_call(
-        functools.partial(backward_kernel, layer), jobs, (chunks,),
-        [head_spec(scalars[0]), head_spec(scalars[1]), row(width), row(width)] + weight_specs(width) + [
+        functools.partial(backward_kernel, layer), jobs, (2 * chunks,),
+        [head_spec(scalars[0]), head_spec(scalars[1]), row(width), row(width), whole(w_out.shape)]
+        + weight_specs(width) + [
             row(CONV_CH),
-            pl.BlockSpec((8, CONV_CH), lambda i: (jnp.maximum((back - i) * steps - 1, 0), 0)),
-            row(VAL), row(LANES), row(CHUNK), row(VAL), row(VAL),
-            pl.BlockSpec((None, KEY, VAL), lambda i: (back - i, 0, 0)),
+            pl.BlockSpec((8, CONV_CH), lambda i: (jnp.maximum(at(i) * steps - 1, 0), 0)),
+            row(CONV_CH), row(VAL), row(LANES), row(CHUNK), row(VAL), row(VAL),
+            pl.BlockSpec((None, KEY, VAL), lambda i: (at(i), 0, 0)),
         ],
         [
-            row(width), row(CONV_CH), row(VAL),
+            row(width),
+            pl.BlockSpec((CHUNK, CONV_CH + VAL), lambda i: (jnp.maximum(i - chunks, 0), 0)),
             pl.BlockSpec((width, LANES), lambda i: (0, 0)),
             pl.BlockSpec((1, VAL), lambda i: (0, 0)),
             pl.BlockSpec((8, LANES), lambda i: (0, 0)),
         ],
         [
-            out(width, BF16), out(CONV_CH, BF16), out(VAL, BF16),
+            out(width, BF16), jax.ShapeDtypeStruct((width, CONV_CH + VAL), BF16),
             jax.ShapeDtypeStruct((width, LANES), BF16),
             jax.ShapeDtypeStruct((1, VAL), F32),
             jax.ShapeDtypeStruct((8, LANES), F32),
@@ -372,9 +385,11 @@
             pltpu.VMEM((KEY, VAL), F32),
             pltpu.VMEM((4, CONV_CH), F32),
             pltpu.VMEM((LANES, CONV_CH), F32),
-            pltpu.VMEM((width, LANES), F32),
+            pltpu.VMEM((LANES, width), F32),
+            pltpu.VMEM((length, width), BF16),
+            pltpu.VMEM((length, CONV_CH + VAL), BF16),
         ],
-        (*scalars, g, x, qkv, pack, pack, pack, gain, proj, proj, gate_in, rates, inverse, fresh, o,
+        (*scalars, g, x, w_out, qkv, pack, pack, gain, proj, proj, conv, gate_in, rates, inverse, fresh, o,
          states),
         number, "mixer_backward", 16 * 10**9,
     )
@@ -396,6 +411,10 @@
 
     def piece(self, p):
         return pl.ds(pl.multiple_of(self.first + p * self.size, self.size), self.size)
+
+    def rows(self):
+        rows = self.size * PIECES
+        return pl.ds(pl.multiple_of(self.first, rows), rows)
 
 
 def remote(src, dst, send, recv, device):
@@ -415,6 +434,7 @@
         self.own = Block(zl, core, rows)
         self.away = Block(1 - zl, core, rows)
         own_beside, away_beside = Block(zl, 1 - core, rows), Block(1 - zl, 1 - core, rows)
+        self.blocks = (away_beside, own_beside, self.away, self.own)
         self.to_far = [
             remote(partial.at[away_beside.piece(p)], beside_far.at[self.local(p)],
                    send.at[0, p], recv.at[0, p], beside)
@@ -434,11 +454,18 @@
     def local(self, p):
         return pl.ds(p * self.size, self.size)
 
-    def start(self):
+    def start(self, make=None):
+        if make is not None:
+            make(self.blocks[0].rows())
         for copy in self.to_far:
             copy.start()
+        if make is not None:
+            make(self.blocks[1].rows())
         for copy in self.to_own:
             copy.start()
+        if make is not None:
+            make(self.blocks[2].rows())
+            make(self.blocks[3].rows())
         for p in range(PIECES):
             self.to_far[p].wait_recv()
             at = self.local(p)
@@ -532,6 +559,30 @@
     jobs.finish()
 
 
+def mixer_bridge_kernel(
+    row, jobs, heads_ref, w_out_ref, x_ref, gain_ref, new_ref, out_ref, partial, beside_far, beside_own,
+    sums, far, send, recv
+):
+    wait_greetings(greet_group() + jobs.greet())
+    scatter = Scatter(partial, beside_far, beside_own, sums, far, send, recv)
+    gather = Gather(out_ref, send, recv, 3)
+
+    def make(rows):
+        partial[rows, :] = mm(heads_ref[rows, :], w_out_ref[...], NT).astype(BF16)
+
+    scatter.start(make)
+    jobs.start()
+    for p in range(PIECES):
+        at = scatter.local(p)
+        x = x_ref[at, :].astype(F32) + scatter.total(p)
+        new_ref[at, :] = x
+        gather.put(p, normed_of(x, gain_ref[row : row + 1, :].astype(F32)).astype(BF16))
+    jobs.middle()
+    scatter.finish()
+    gather.finish()
+    jobs.finish()
+
+
 def norm_back(total, x, gain):
     inv = lax.rsqrt(jnp.mean(x * x, axis=1, keepdims=True) + 1e-6)
     unit = x * inv
@@ -540,10 +591,12 @@
     return grad, jnp.sum(total * unit, axis=0, keepdims=True)
 
 
-def backward_bridge_kernel(
-    row, jobs, partial, x_ref, gain_ref, grad_ref, new_ref, out_ref, dgain_ref,
-    beside_far, beside_own, sums, far, send, recv
-):
+def backward_bridge_kernel(row, last, jobs, partial, x_ref, gain_ref, grad_ref, *refs):
+    if last:
+        heads_ref, new_ref, out_ref, dgain_ref, dout_ref, *refs = refs
+    else:
+        new_ref, out_ref, dgain_ref, *refs = refs
+    beside_far, beside_own, sums, far, send, recv = refs
     wait_greetings(greet_group() + jobs.greet())
     scatter = Scatter(partial, beside_far, beside_own, sums, far, send, recv)
     gather = Gather(out_ref, send, recv, 3)
@@ -561,6 +614,10 @@
     jobs.middle()
     scatter.finish()
     gather.finish()
+    if last:
+        for first in range(0, out_ref.shape[1], 256):
+            columns = slice(first, first + 256)
+            dout_ref[columns, :] = mm(out_ref[:, columns], heads_ref[...], TN).astype(BF16)
     jobs.finish()
 
 
@@ -584,17 +641,17 @@
     jobs.finish()
 
 
-def comm_call(kernel, row, number, outs, args, scatters, gathers, jobs):
+def comm_call(kernel, row, number, outs, args, scatters, gathers, jobs, name=None):
     rows = args[1].shape[0] if scatters else args[0].shape[0]
     width = args[0].shape[1]
     vmem = pl.BlockSpec(memory_space=pltpu.VMEM)
     hops = 3 * scatters + 3 * gathers
     return carry_call(
-        functools.partial(kernel, row), jobs, (), [vmem] * len(args), [vmem] * len(outs),
+        kernel if row is None else functools.partial(kernel, row), jobs, (), [vmem] * len(args), [vmem] * len(outs),
         [jax.ShapeDtypeStruct(shape, kind) for shape, kind in outs],
         [pltpu.VMEM((rows, width), BF16) for _ in range(4 * scatters)]
         + [pltpu.SemaphoreType.DMA((hops, PIECES)), pltpu.SemaphoreType.DMA((hops, PIECES))],
-        args, number, kernel.__name__.replace("_kernel", ""), rows * width * 20,
+        args, number, name or kernel.__name__.replace("_kernel", ""), rows * width * 20,
     )
 
 
@@ -611,12 +668,31 @@
     )
 
 
-def backward_bridge(partial, x, gain, row, grad, jobs, number):
+def mixer_bridge(heads, w_out, x, gain, row, jobs, number):
     rows, width = x.shape
+    vmem = pl.BlockSpec(memory_space=pltpu.VMEM)
+    sems = pltpu.SemaphoreType.DMA((6, PIECES))
+    return carry_call(
+        functools.partial(mixer_bridge_kernel, row), jobs, (), [vmem] * 4, [vmem] * 2,
+        [
+            jax.ShapeDtypeStruct((rows, width), F32),
+            jax.ShapeDtypeStruct((4 * rows, width), BF16),
+        ],
+        [pltpu.VMEM((4 * rows, width), BF16)]
+        + [pltpu.VMEM((rows, width), BF16) for _ in range(4)] + [sems, sems],
+        (heads, w_out, x, gain), number, "mixer_bridge", 10**9,
+    )
+
+
+def backward_bridge(partial, x, gain, row, grad, jobs, number, heads=None):
+    rows, width = x.shape
+    last = heads is not None
+    outs = [((rows, width), F32), ((4 * rows, width), BF16), ((1, width), F32)]
+    if last:
+        outs.append(((width, heads.shape[1]), BF16))
     return comm_call(
-        backward_bridge_kernel, row, number,
-        [((rows, width), F32), ((4 * rows, width), BF16), ((1, width), F32)],
-        (partial, x, gain, grad), 1, 1, jobs,
+        functools.partial(backward_bridge_kernel, row, last), None, number, outs,
+        (partial, x, gain, grad) + ((heads,) if last else ()), 1, 1, jobs, "backward_bridge",
     )
 
 
@@ -630,6 +706,7 @@
 
 class Job:
     in_vmem = False
+    late = False
 
     @staticmethod
     def buffers(shape, chips):
@@ -964,6 +1041,7 @@
 
 
 class Share(Job):
+    late = True
     @staticmethod
     def result(shape, chips):
         return (4 * shape[0], shape[1])
@@ -1001,6 +1079,7 @@
 
 
 class ShareSum(Job):
+    late = True
     in_vmem = True
 
     @staticmethod
@@ -1095,9 +1174,10 @@
         for job in self.bound:
             job.start()
 
-    def middle(self):
+    def middle(self, late=None):
         for job in self.bound:
-            job.middle()
+            if late is None or job.late == late:
+                job.middle()
 
     def finish(self):
         for job in self.bound:
@@ -1227,53 +1307,45 @@
          self.ffn_gate, self.ffn_up, self.ffn_down) = refs
         self.square = square
 
-    @staticmethod
-    def turned(value):
-        return value.astype(F32).T.astype(BF16)
-
     def qkv(self, layer, ref):
         ref[:, 0:KEY] = self.query[layer]
         ref[:, KEY : 2 * KEY] = self.key[layer]
         ref[:, 2 * KEY :] = self.value[layer]
 
-    def mix(self, layer, ref):
+    def side(self, layer, ref):
         ref[:, 0:VAL] = self.gate[layer]
-        ref[:, VAL : 2 * VAL] = self.turned(self.out[layer])
         self.square[...] = jnp.zeros(self.square.shape, F32)
         self.square[0:2, :] = self.decay[layer].astype(F32)
         self.square[2:6, :] = self.conv[layer].astype(F32)
-        ref[:, 2 * VAL :] = self.square[...].T.astype(BF16)
-
-    def pair(self, layer, ref):
-        ref[...] = self.turned(
-            jnp.concatenate([self.ffn_gate[layer], self.ffn_up[layer]], axis=0)
-        )
-
-    def down(self, layer, ref):
-        ref[...] = self.turned(self.ffn_down[layer])
+        ref[:, VAL:] = self.square[...].T.astype(BF16)
+
+    def turn(self, value, ref):
+        ref[...] = value.astype(F32).T.astype(BF16)
 
 
 def deal_kernel(chips, jobs, order_ref, lengths_ref, x_ref, gain_ref, cotangent_ref, *refs):
     raw, refs = refs[:10], refs[10:]
-    (new_ref, out_ref, start_ref, qkv_next, mix_next, pair_ref, pair_next, down_ref, down_next,
-     first_full, second_full, first_wide, second_wide), refs = refs[:13], refs[13:]
-    (spread, picked, square, first, second, held_first, held_second, send, recv, plane_send,
-     plane_recv, role_send, role_recv, *sems) = refs
+    (new_ref, out_ref, start_ref, qkv_next, side_next, out_next, gate_next, up_ref, up_next, down_ref,
+     down_next, first_full, second_full, first_wide, second_wide, third_wide, fourth_wide) = refs[:17]
+    (spread, picked, square, first, second, third, fourth, held_first, held_second, send, recv,
+     plane_send, plane_recv, role_send, role_recv, *sems) = refs[17:]
     raw = Raw(raw, square)
     plane, trade = Plane(chips), Trade(chips)
     first_column = ToPlane(first, first_wide, sems[0], sems[1], chips)
     first_across = Spread(first_wide, first_full, sems[2], sems[3], chips, [held_first])
     second_column = ToPlane(second, second_wide, sems[4], sems[5], chips)
     second_across = Spread(second_wide, second_full, sems[6], sems[7], chips, [held_second])
+    third_column = ToPlane(third, third_wide, sems[8], sems[9], chips)
+    fourth_column = ToPlane(fourth, fourth_wide, sems[10], sems[11], chips)
     gather = Gather(out_ref, send, recv, 0)
     count = plane.count
     part = x_ref.shape[0] // count
     rows = lambda index: pl.ds(pl.multiple_of(index * part, part), part)
     expected = plane.greet() + trade.greet_homes() + greet_group()
-    for job in (first_column, first_across, second_column, second_across):
+    for job in (first_column, first_across, second_column, second_across, third_column, fourth_column):
         expected = expected + job.greet()
     raw.qkv(0, first)
-    raw.mix(0, second)
+    raw.side(0, second)
     wait_greetings(expected)
     outward, inward = [], []
     for j in range(1, count):
@@ -1305,9 +1377,11 @@
             new_ref[rows(plane.own), :] = picked[slot]
 
         to_roles.append((copy, mine))
+    second_column.start()
+    raw.turn(raw.out[0], third)
+    raw.turn(raw.ffn_gate[0], fourth)
     first_column.finish()
     first_across.start()
-    second_column.start()
     size = x_ref.shape[0] // PIECES
     parts = max(size // part, 1)
     for p in range(PIECES):
@@ -1319,17 +1393,21 @@
         gather.put(p, normed_of(x, gain_ref[0:1, :].astype(F32)).astype(BF16))
     second_column.finish()
     second_across.start()
+    third_column.start()
+    fourth_column.start()
     first_across.middle()
     length = lengths_ref[order_ref[plane.own]]
     at = (trade.zp * 2 + trade.zl) * x_ref.shape[0]
     positions = lax.broadcasted_iota(jnp.int32, x_ref.shape, 0) + at
     start_ref[...] = jnp.where(positions < length, cotangent_ref[...], jnp.zeros(x_ref.shape, BF16))
     raw.qkv(1, qkv_next)
-    raw.mix(1, mix_next)
-    raw.pair(0, pair_ref)
-    raw.pair(1, pair_next)
-    raw.down(0, down_ref)
-    raw.down(1, down_next)
+    raw.side(1, side_next)
+    raw.turn(raw.out[1], out_next)
+    raw.turn(raw.ffn_gate[1], gate_next)
+    raw.turn(raw.ffn_up[0], up_ref)
+    raw.turn(raw.ffn_up[1], up_next)
+    raw.turn(raw.ffn_down[0], down_ref)
+    raw.turn(raw.ffn_down[1], down_next)
     for copy in outward:
         copy.wait_send()
     for copy, mine in to_roles:
@@ -1338,6 +1416,8 @@
     second_across.middle()
     first_across.finish()
     second_across.finish()
+    third_column.finish()
+    fourth_column.finish()
 
 
 def deal_and_gather(order, lengths, x, gain, cotangent, raw, chips, number):
@@ -1349,21 +1429,21 @@
     count = 2 * chips
     buffer = pltpu.VMEM((count, rows // count, width), BF16)
     sems = lambda *shape: [pltpu.SemaphoreType.DMA(shape), pltpu.SemaphoreType.DMA(shape)]
-    qkv, mix = CONV_CH, 2 * VAL + LANES
-    pair = (part, 2 * units)
-    held = [(part, qkv), (part, mix), pair, pair, (part, units), (part, units)]
-    spread = [(2 * chips * part, qkv), (2 * chips * part, mix)]
-    moved = [(2 * part, qkv), (2 * part, mix)]
+    qkv, side = CONV_CH, VAL + LANES
+    held = [(part, cols) for cols in (qkv, side, VAL, units, units, units, units, units)]
+    spread = [(2 * chips * part, qkv), (2 * chips * part, side)]
+    moved = [(2 * part, cols) for cols in (qkv, side, VAL, units)]
     shapes = [(rows, width), (4 * rows, width), (rows, width)] + held + spread + moved
+    own = [(part, qkv), (part, side), (part, VAL), (part, units), moved[0], moved[1]]
     return carry_call(
         functools.partial(deal_kernel, chips), Jobs([], chips), (),
         [smem, smem] + [vmem] * 13,
-        [vmem] * 9 + [hbm] * 4,
+        [vmem] * 11 + [hbm] * 6,
         [jax.ShapeDtypeStruct(shape, BF16) for shape in shapes],
         [buffer, buffer, pltpu.VMEM((LANES, LANES), F32)]
-        + [pltpu.VMEM(shape, BF16) for shape in (held[0], held[1], moved[0], moved[1])]
+        + [pltpu.VMEM(shape, BF16) for shape in own]
         + sems(3, PIECES) + sems(count) + sems(count)
-        + [pltpu.SemaphoreType.DMA((max(9, chips + 1),))] * 8,
+        + [pltpu.SemaphoreType.DMA((max(9, chips + 1),))] * 12,
         (order, lengths, x, gain, cotangent, *raw), number, "deal_and_gather", rows * width * 20,
     )[0]
 
@@ -1393,8 +1473,11 @@
     chips, jobs, order_ref, partial, x_ref, gain_ref, grad_ref, *refs
 ):
     terms, refs = refs[:7], refs[7:]
-    grads, refs = refs[:3], refs[3:]
-    home_ref, total_ref, homes, refs = refs[0], refs[1], refs[2:5], refs[5:]
+    (in_ref, aux_ref), refs = refs[:2], refs[2:]
+    home_ref, total_ref, in_home, aux_home, refs = *refs[:4], refs[4:]
+    cut = [pl.ds(0, CONV_CH), pl.ds(CONV_CH, VAL)]
+    grads = [in_ref.at[:, cut[0]], in_ref.at[:, cut[1]], aux_ref]
+    homes = [in_home.at[:, :, cut[0]], in_home.at[:, :, cut[1]], aux_home]
     (beside_far, beside_own, sums, far, last, back, picked, small, by_plane, by_z, plane_sum,
      send, recv, role_send, role_recv, plane_send, plane_recv, small_send, small_recv, z_send,
      z_recv), refs = refs[:21], refs[21:]
@@ -1419,8 +1502,7 @@
     wait_greetings(expected)
     scatter = Scatter(partial, beside_far, beside_own, sums, far, send, recv)
     scatter.start()
-    for job in reduces:
-        job.start()
+    reduces[0].start()
     jobs.start()
     dgain = jnp.zeros((1, x_ref.shape[1]), F32)
     to_homes = []
@@ -1455,12 +1537,15 @@
     for copy in small_out:
         copy.start()
     by_plane[plane.own] = small[...]
-    for job in reduces:
-        job.middle()
+    reduces[0].middle()
+    reduces[1].start()
+    reduces[2].start()
     for slot in range(count):
         arrival = remote(last.at[rows(0)], back.at[slot], role_send.at[0], role_recv.at[slot],
                          trade.role(slot))
         unless(trade.role_mine(slot), arrival.wait_recv)
+    reduces[0].finish()
+    returns[0].start()
     outward, inward = [], []
     for j in range(count):
         to, source = plane.to(j), plane.source(j)
@@ -1479,10 +1564,12 @@
             remote(picked.at[j], home_ref.at[rows(source)], plane_send.at[j], plane_recv.at[j],
                    plane.device(source))
         )
-    for reduce, back_home in zip(reduces, returns):
+    for job in reduces[1:]:
+        job.middle()
+    jobs.middle()
+    for reduce, back_home in zip(reduces[1:], returns[1:]):
         reduce.finish()
         back_home.start()
-    jobs.middle()
     for copy in small_in:
         copy.wait_recv()
     total = by_plane[0]
@@ -1521,15 +1608,15 @@
     parted = pltpu.VMEM((count, rows // count, width), BF16)
     hbm = pl.BlockSpec(memory_space=pl.ANY)
     chained = []
-    for a in grads:
-        chained.append(pltpu.VMEM(Reduce.result(a.shape, chips), BF16))
+    for a in [(grads[0].shape[0], cols) for cols in (CONV_CH, VAL, LANES)]:
+        chained.append(pltpu.VMEM(Reduce.result(a, chips), BF16))
         chained += [pltpu.SemaphoreType.DMA((max(9, chips + 1),))] * 4
-        chained += Reduce.buffers(a.shape, chips)
+        chained += Reduce.buffers(a, chips)
     sems = lambda *shape: [pltpu.SemaphoreType.DMA(shape), pltpu.SemaphoreType.DMA(shape)]
     return carry_call(
         functools.partial(final_kernel, chips), jobs, (),
-        [pl.BlockSpec(memory_space=pltpu.SMEM)] + [vmem] * 11 + [hbm] * 3,
-        [vmem, vmem] + [hbm] * 3,
+        [pl.BlockSpec(memory_space=pltpu.SMEM)] + [vmem] * 11 + [hbm] * 2,
+        [vmem, vmem] + [hbm] * 2,
         [
             jax.ShapeDtypeStruct((rows, width), BF16),
             jax.ShapeDtypeStruct(small.shape, F32),
@@ -1563,21 +1650,19 @@
     ins, outs = refs[:12], refs[12:]
     for layer in range(2):
         total = lambda ref: ref[0].astype(F32) + ref[1].astype(F32)
-        qkv, gate, aux, out, pair, down = (total(ref) for ref in ins[6 * layer : 6 * layer + 6])
-        units = down.shape[1]
-        outs[0][layer] = qkv[:, :KEY]
-        outs[1][layer] = qkv[:, KEY : 2 * KEY]
-        outs[2][layer] = qkv[:, 2 * KEY :]
-        outs[3][layer] = gate
+        proj, aux, out, gate, up, down = (total(ref) for ref in ins[6 * layer : 6 * layer + 6])
+        outs[0][layer] = proj[:, :KEY]
+        outs[1][layer] = proj[:, KEY : 2 * KEY]
+        outs[2][layer] = proj[:, 2 * KEY : CONV_CH]
+        outs[3][layer] = proj[:, CONV_CH:]
         turned = aux.T
         outs[4][layer] = turned[0:2, :]
         outs[14][layer] = turned[2:6, :]
         outs[5][layer] = out.T
-        turned = pair.T
-        outs[6][layer] = turned[:units, :]
-        outs[7][layer] = turned[units:, :]
+        outs[6][layer] = gate.T
+        outs[7][layer] = up.T
         outs[8][layer] = down.T
-    outs[15][...] = home_ref[...].astype(F32)
+    outs[15][...] = home_ref[...].astype(F32)[:, None, :]
     at = 0
     for ref in outs[9:12]:
         for layer in range(2):
@@ -1597,7 +1682,8 @@
     shapes = [
         (2, rows, KEY), (2, rows, KEY), (2, rows, VAL), (2, rows, VAL), (2, 2, rows), (2, VAL, rows),
         (2, units, rows), (2, units, rows), (2, units, rows),
-        (2, width), (2, width), (2, VAL), (2, heads), (2, heads), (2, 4, rows), home.shape,
+        (2, width), (2, width), (2, VAL), (2, heads), (2, heads), (2, 4, rows),
+        (home.shape[0], 1, width),
     ]
     vmem = pl.BlockSpec(memory_space=pltpu.VMEM)
     return pl.pallas_call(
@@ -1610,24 +1696,28 @@
     )(small, home, *first, *second)
 
 
-def ffn_parts(x, pair):
-    paired = mm(x, pair)
-    units = paired.shape[1] // 2
-    gate, up = paired[:, :units], paired[:, units:]
+def ffn_parts(x, gate_ref, up_ref):
+    gate, up = mm(x, gate_ref[...]), mm(x, up_ref[...])
     act, sig = silu_of(gate)
     return gate, up, act, sig
 
 
-def begin_jobs(jobs, at, steps):
+def begin_jobs(jobs, at, steps, turns=None):
     if jobs.kinds:
         @pl.when(at == 0)
         def _():
             wait_greetings(jobs.greet())
             jobs.start()
 
-        @pl.when(at == steps // 2)
+        early, late = turns or (steps // 2, steps - 1)
+
+        @pl.when(at == early)
         def _():
-            jobs.middle()
+            jobs.middle(late=False)
+
+        @pl.when(at == late)
+        def _():
+            jobs.middle(late=True)
 
 
 def end_jobs(jobs, at, steps):
@@ -1637,10 +1727,10 @@
             jobs.finish()
 
 
-def ffn_forward_kernel(jobs, x_ref, pair_ref, down_ref, part_ref):
+def ffn_forward_kernel(jobs, x_ref, gate_ref, up_ref, down_ref, part_ref):
     at, steps = pl.program_id(0), pl.num_programs(0)
     begin_jobs(jobs, at, steps)
-    _, up, act, _ = ffn_parts(x_ref[...], pair_ref[...])
+    _, up, act, _ = ffn_parts(x_ref[...], gate_ref, up_ref)
     part_ref[...] = mm((act * up).astype(BF16), down_ref[...], NT).astype(BF16)
     end_jobs(jobs, at, steps)
 
@@ -1649,20 +1739,22 @@
     return pl.BlockSpec(shape, lambda i: (0, 0), pipeline_mode=pl.Buffered(1))
 
 
-def ffn_forward(x, pair, down, jobs, number):
+def ffn_forward(x, weights, jobs, number):
     length, width = x.shape
     rows = pl.BlockSpec((CHUNK, width), lambda i: (i, 0))
     return carry_call(
         ffn_forward_kernel, jobs, (length // CHUNK,),
-        [rows, whole(pair.shape), whole(down.shape)], [rows],
-        [jax.ShapeDtypeStruct((length, width), BF16)], [], (x, pair, down), number, "ffn_forward",
+        [rows] + [whole(weight.shape) for weight in weights], [rows],
+        [jax.ShapeDtypeStruct((length, width), BF16)], [], (x, *weights), number, "ffn_forward",
         4 * 10**9,
     )
 
 
-def ffn_backward_kernel(both, jobs, x_ref, g_ref, pair_ref, down_ref, *refs):
-    outs, (low_ref, hidden_ref) = refs[:-2], refs[-2:]
-    part_ref, dpair_ref, ddown_ref = outs[:3]
+def ffn_backward_kernel(both, jobs, x_ref, g_ref, gate_ref, up_ref, down_ref, *refs):
+    outs, (low_gate, low_up, hidden_ref, x_held, g_held) = refs[:-5], refs[-5:]
+    if both:
+        residual_ref, outs = outs[0], outs[1:]
+    part_ref, dgate_ref, dup_ref, ddown_ref = outs[:4]
     at, steps = pl.program_id(0), pl.num_programs(0)
     chunks = steps // 2
     begin_jobs(jobs, at, steps)
@@ -1670,45 +1762,51 @@
     @pl.when(at < chunks)
     def _():
         rows = pl.ds(pl.multiple_of(at * CHUNK, CHUNK), CHUNK)
-        gate, up, act, sig = ffn_parts(x_ref[rows, :], pair_ref[...])
+        x, g = x_ref[...], g_ref[...]
+        x_held[rows, :] = x
+        g_held[rows, :] = g
+        gate, up, act, sig = ffn_parts(x, gate_ref, up_ref)
         hidden = (act * up).astype(BF16)
         hidden_ref[rows, :] = hidden
         if both:
-            outs[3][...] = mm(hidden, down_ref[...], NT).astype(BF16)
-        dhidden = mm(g_ref[rows, :], down_ref[...])
-        dgate = dhidden * up * (sig * (1.0 + gate * (1.0 - sig)))
-        low = jnp.concatenate([dgate, dhidden * act], axis=1).astype(BF16)
-        low_ref[rows, :] = low
-        part_ref[...] = mm(low, pair_ref[...], NT).astype(BF16)
+            own = lax.axis_index("zl") * 2 + lax.axis_index("core")
+            outs[4][...] = (
+                mm(hidden, down_ref[...], NT) + jnp.where(at == own, residual_ref[...], 0.0)
+            ).astype(BF16)
+        dhidden = mm(g, down_ref[...])
+        dgate = (dhidden * up * (sig * (1.0 + gate * (1.0 - sig)))).astype(BF16)
+        dup = (dhidden * act).astype(BF16)
+        low_gate[rows, :] = dgate
+        low_up[rows, :] = dup
+        part_ref[...] = (mm(dgate, gate_ref[...], NT) + mm(dup, up_ref[...], NT)).astype(BF16)
 
     @pl.when(at >= chunks)
     def _():
         columns = pl.ds(pl.multiple_of((at - chunks) * CHUNK, CHUNK), CHUNK)
-        dpair_ref[...] = mm(x_ref[:, columns], low_ref[...], TN).astype(BF16)
-        ddown_ref[...] = mm(g_ref[:, columns], hidden_ref[...], TN).astype(BF16)
+        dgate_ref[...] = mm(x_held[:, columns], low_gate[...], TN).astype(BF16)
+        dup_ref[...] = mm(x_held[:, columns], low_up[...], TN).astype(BF16)
+        ddown_ref[...] = mm(g_held[:, columns], hidden_ref[...], TN).astype(BF16)
 
     end_jobs(jobs, at, steps)
 
 
-def ffn_backward(x, g, pair, down, jobs, number, both=False):
+def ffn_backward(x, g, weights, jobs, number, residual=None):
+    both = residual is not None
     length, width = x.shape
     chunks = length // CHUNK
-    assert length == width
+    units = weights[0].shape[1]
+    assert length == width and (not both or residual.shape[0] == CHUNK)
     rows = pl.BlockSpec((CHUNK, width), lambda i: (jnp.minimum(i, chunks - 1), 0))
-    late = lambda cols: pl.BlockSpec((CHUNK, cols), lambda i: (jnp.maximum(i - chunks, 0), 0))
+    late = pl.BlockSpec((CHUNK, units), lambda i: (jnp.maximum(i - chunks, 0), 0))
     out = lambda cols: jax.ShapeDtypeStruct((length, cols), BF16)
     return carry_call(
         functools.partial(ffn_backward_kernel, both), jobs, (2 * chunks,),
-        [whole(x.shape), whole(g.shape), whole(pair.shape), whole(down.shape)],
-        [rows, late(pair.shape[1]), late(down.shape[1])] + [rows] * both,
-        [out(width), out(pair.shape[1]), out(down.shape[1])] + [out(width)] * both,
-        [pltpu.VMEM((length, pair.shape[1]), BF16), pltpu.VMEM((length, down.shape[1]), BF16)],
-        (x, g, pair, down), number, "ffn_backward", 12 * 10**9,
-    )
-
-
-def dot32(a, b, dims):
-    return lax.dot_general(a, b, dims, preferred_element_type=F32)
+        [rows, rows] + [whole(weight.shape) for weight in weights] + [whole((CHUNK, width))] * both,
+        [rows] + [late] * 3 + [rows] * both,
+        [out(width)] + [out(units)] * 3 + [out(width)] * both,
+        [pltpu.VMEM((length, units), BF16)] * 3 + [pltpu.VMEM((length, width), BF16)] * 2,
+        (x, g, *weights) + ((residual,) if both else ()), number, "ffn_backward", 12 * 10**9,
+    )
 
 
 def row_major(x):
@@ -1808,101 +1906,93 @@
             w_query, w_key, w_value, w_gate, turned(w_decay[:, :, 0, :]), conv_filter[:, :, 0, :],
             w_out, turned(w_ffn_gate), turned(w_ffn_up), w_ffn_down,
         )
-        (residual, rows_in, start, qkv_next, mix_next, pair_first, pair_next, down_first, down_next,
-         qkv, mix, _, _) = deal_and_gather(
+        (residual, rows_in, start, qkv_next, side_next, out_next, gate_next, up_first, up_next,
+         down_first, down_next, qkv0, side0, _, _, out_wide, gate_wide) = deal_and_gather(
             order, lengths, tokens[:, 0, :], norm_mix, cotangent[:, 0, :], raw, roles.chips, 1
         )
     else:
-        qkv_packs, mix_packs, pair_packs, down_packs = [], [], [], []
+        packs = []
         for layer in range(layer_count):
             aux = jnp.concatenate([w_decay[layer, :, 0, :], conv_filter[layer, :, 0, :].T], axis=1)
             aux = jnp.pad(aux, ((0, 0), (0, LANES - aux.shape[1])))
-            qkv_packs.append(
-                row_major(jnp.concatenate([w_query[layer], w_key[layer], w_value[layer]], axis=1))
+            packs.append(
+                [
+                    row_major(pack) for pack in (
+                        jnp.concatenate([w_query[layer], w_key[layer], w_value[layer]], axis=1),
+                        jnp.concatenate([w_gate[layer], aux], axis=1),
+                        w_out[layer].T, w_ffn_gate[layer], w_ffn_up[layer], w_ffn_down[layer].T,
+                    )
+                ]
             )
-            mix_packs.append(
-                row_major(jnp.concatenate([w_gate[layer], w_out[layer].T, aux], axis=1))
-            )
-            pair_packs.append(
-                row_major(jnp.concatenate([w_ffn_gate[layer], w_ffn_up[layer]], axis=1))
-            )
-            down_packs.append(row_major(w_ffn_down[layer].T))
-        qkv_next, mix_next = qkv_packs[1], mix_packs[1]
-        (pair_first, pair_next), (down_first, down_next) = pair_packs, down_packs
+        (qkv0, side0, out_wide, gate_wide, up_first, down_first) = packs[0]
+        (qkv_next, side_next, out_next, gate_next, up_next, down_next) = packs[1]
         positions = (zp * 2 + zl) * rows_local + jnp.arange(rows_local)
         start = cotangent[:, 0, :] * (positions < lengths[order[chip * 2 + core]]).astype(BF16)[:, None]
         residual = lax.ppermute(deal(tokens, order)[:, 0, :], AXES, to_roles)
         (rows_in,), _ = first_gather(residual, norm_mix, 0, carry(), 1)
-        qkv = chip_gather(to_plane(qkv_packs[0], roles))
-        mix = chip_gather(to_plane(mix_packs[0], roles))
-
-    def in_gradients(rows_in, dqkv, dgate):
-        return dot32(rows_in, dqkv, TN).astype(BF16), dot32(rows_in, dgate, TN).astype(BF16)
-
-    (part, heads0, *kept0), (pair_wide, down_wide) = mixer_forward(
-        0, rows_in, qkv, mix, norm_heads, scalars,
-        carry((ToPlane, pair_first), (ToPlane, down_first)), 2,
-    )
-    rows_in0, qkv0, mix0, residual0 = rows_in, qkv, mix, residual
-    (middle0, rows_ffn0), (pair0, down0, qkv_wide, mix_wide) = forward_bridge(
-        part, residual0, norm_ffn, 0,
-        carry((Spread, pair_wide), (Spread, down_wide), (ToPlane, qkv_next), (ToPlane, mix_next)), 3,
-    )
-    (part,), _ = ffn_forward(rows_ffn0, pair0, down0, carry(), None)
-    (residual1, rows_in1), (qkv1, mix1, down_wide) = forward_bridge(
+        qkv0, side0 = (chip_gather(to_plane(pack, roles)) for pack in (qkv0, side0))
+        out_wide, gate_wide = (to_plane(pack, roles) for pack in (out_wide, gate_wide))
+
+    (heads0, *kept0), (out0, gate0, up_wide, down_wide, qkv_wide) = mixer_forward(
+        0, rows_in, qkv0, side0, norm_heads, scalars,
+        carry((Spread, out_wide), (Spread, gate_wide), (ToPlane, up_first), (ToPlane, down_first),
+              (ToPlane, qkv_next)),
+        2,
+    )
+    rows_in0, residual0 = rows_in, residual
+    (middle0, rows_ffn0), (up0, down0, side_wide, gradient) = mixer_bridge(
+        heads0, out0, residual0, norm_ffn, 0,
+        carry((Spread, up_wide), (Spread, down_wide), (ToPlane, side_next), (ToRole, start)), 3,
+    )
+    ffn0 = (gate0, up0, down0)
+    (part,), _ = ffn_forward(rows_ffn0, ffn0, carry(), None)
+    (residual1, rows_in1), (qkv1, side1, out_wide, down_wide) = forward_bridge(
         part, middle0, norm_mix, 1,
-        carry((Spread, qkv_wide), (Spread, mix_wide), (ToPlane, down_next)), 4,
-    )
-    (part, heads1, *kept1), (down1, pair_wide, gradient) = mixer_forward(
-        1, rows_in1, qkv1, mix1, norm_heads, scalars,
-        carry((Spread, down_wide), (ToPlane, pair_next), (ToRole, start)), 5,
-    )
-    (middle1, rows_ffn1), (pair1, grad_rows) = forward_bridge(
-        part, residual1, norm_ffn, 1, carry((Spread, pair_wide), (Share, gradient)), 6
-    )
-    (part, dpair1, ddown1, part_out), _ = ffn_backward(
-        rows_ffn1, grad_rows, pair1, down1, carry(), None, both=True
-    )
-
-    (gradient, grad_rows, dgain_ffn1), (dpair1,) = backward_bridge(
-        part, middle1, norm_ffn, 1, gradient, carry((Reduce, dpair1)), 7
-    )
-    dout1 = dot32(grad_rows, heads1, TN).astype(BF16)
-    (part, dqkv, dgate, daux1, dgain1, dscalars1), jobs_results = mixer_backward(
-        1, grad_rows, rows_in1, qkv1, mix1, norm_heads, scalars, kept1,
-        carry((Reduce, ddown1), (Reduce, dout1), (FromPlane, dpair1), (ShareSum, part_out)), 8,
-    )
-    ddown1, dout1, pair_home1, total = jobs_results
-    mixed = (middle1 + total.astype(F32)).astype(BF16)
-    dqkv1, dgate1 = in_gradients(rows_in1, dqkv, dgate)
-    results, jobs_results = backward_bridge(
+        carry((Spread, qkv_wide), (Spread, side_wide), (ToPlane, out_next), (ToPlane, down_next)), 4,
+    )
+    (heads1, *kept1), (out1, down1, gate_wide, up_wide, grad_rows) = mixer_forward(
+        1, rows_in1, qkv1, side1, norm_heads, scalars,
+        carry((Spread, out_wide), (Spread, down_wide), (ToPlane, gate_next), (ToPlane, up_next),
+              (Share, gradient)),
+        5,
+    )
+    (middle1, rows_ffn1), (gate1, up1) = mixer_bridge(
+        heads1, out1, residual1, norm_ffn, 1, carry((Spread, gate_wide), (Spread, up_wide)), 6
+    )
+    ffn1 = (gate1, up1, down1)
+    (part, dgate1, dup1, ddown1, part_out), _ = ffn_backward(
+        rows_ffn1, grad_rows, ffn1, carry(), None, residual=middle1
+    )
+
+    (gradient, grad_rows, dgain_ffn1, dout1), (dgate1, dup1) = backward_bridge(
+        part, middle1, norm_ffn, 1, gradient, carry((Reduce, dgate1), (Reduce, dup1)), 7, heads1
+    )
+    (part, din1, daux1, dgain1, dscalars1), jobs_results = mixer_backward(
+        1, grad_rows, rows_in1, qkv1, side1, out1, norm_heads, scalars, kept1,
+        carry((Reduce, ddown1), (Reduce, dout1), (FromPlane, dgate1), (FromPlane, dup1),
+              (ShareSum, part_out)),
+        8,
+    )
+    ddown1, dout1, gate_home1, up_home1, mixed = jobs_results
+    (gradient, grad_rows, dgain_mix1), (din1, daux1, mixed) = backward_bridge(
         part, residual1, norm_mix, 1, gradient,
-        carry((Reduce, dqkv1), (Reduce, dgate1), (Reduce, daux1), (FromRole, mixed)), 9,
-    )
-    gradient, grad_rows, dgain_mix1 = results
-    dqkv1, dgate1, daux1, mixed = jobs_results
-    (part, dpair0, ddown0), (qkv_home1, gate_home1, aux_home1) = ffn_backward(
-        rows_ffn0, grad_rows, pair0, down0,
-        carry((FromPlane, dqkv1), (FromPlane, dgate1), (FromPlane, daux1)), 14,
-    )
-    results, jobs_results = backward_bridge(
-        part, middle0, norm_ffn, 0, gradient,
-        carry((Reduce, dpair0)), 10,
-    )
-    gradient, grad_rows, dgain_ffn0 = results
-    (dpair0,) = jobs_results
-    dout0 = dot32(grad_rows, heads0, TN).astype(BF16)
-    results, jobs_results = mixer_backward(
-        0, grad_rows, rows_in0, qkv0, mix0, norm_heads, scalars, kept0,
-        carry((Reduce, ddown0), (Reduce, dout0), (FromPlane, dpair0), (FromPlane, ddown1),
-              (FromPlane, dout1)),
+        carry((Reduce, din1), (Reduce, daux1), (FromRole, mixed)), 9,
+    )
+    (part, dgate0, dup0, ddown0), (in_home1, aux_home1) = ffn_backward(
+        rows_ffn0, grad_rows, ffn0, carry((FromPlane, din1), (FromPlane, daux1)), 14,
+    )
+    (gradient, grad_rows, dgain_ffn0, dout0), (dgate0, dup0) = backward_bridge(
+        part, middle0, norm_ffn, 0, gradient, carry((Reduce, dgate0), (Reduce, dup0)), 10, heads0
+    )
+    (part, din0, daux0, dgain0, dscalars0), jobs_results = mixer_backward(
+        0, grad_rows, rows_in0, qkv0, side0, out0, norm_heads, scalars, kept0,
+        carry((Reduce, ddown0), (Reduce, dout0), (FromPlane, dgate0), (FromPlane, dup0),
+              (FromPlane, ddown1), (FromPlane, dout1)),
         11,
     )
-    part, dqkv, dgate, daux0, dgain0, dscalars0 = results
-    ddown0, dout0, pair_home0, down_home1, out_home1 = jobs_results
-    dqkv0, dgate0 = in_gradients(rows_in0, dqkv, dgate)
+    ddown0, dout0, gate_home0, up_home0, down_home1, out_home1 = jobs_results
     terms = (dgain_mix1, dgain_ffn0, dgain_ffn1, dgain0, dgain1, dscalars0, dscalars1)
-    last = (dqkv0, dgate0, daux0)
+    last = (din0, daux0)
     last_jobs = carry((FromPlane, ddown0), (FromPlane, dout0))
     if kernel_deal:
         (home, flat, *last), results = final_step(
@@ -1926,9 +2016,9 @@
         last = only_jobs(carry(*[(Reduce, a) for a in last]), 13)
         last = only_jobs(carry(*[(FromPlane, a) for a in last]), 15)
     down_home0, out_home0 = results
-    qkv_home0, gate_home0, aux_home0 = last
-    first = (qkv_home0, gate_home0, aux_home0, out_home0, pair_home0, down_home0)
-    second = (qkv_home1, gate_home1, aux_home1, out_home1, pair_home1, down_home1)
+    in_home0, aux_home0 = last
+    first = (in_home0, aux_home0, out_home0, gate_home0, up_home0, down_home0)
+    second = (in_home1, aux_home1, out_home1, gate_home1, up_home1, down_home1)
     if rows_part % LANES == 0:
         outs = weights_out(flat, home, first, second, heads_total)
     else:
@@ -1937,18 +2027,18 @@
         for size in (width, width, VAL, heads_total, heads_total):
             small.append(flat[at : at + layer_count * size].reshape(layer_count, size))
             at += layer_count * size
-        qkv, gate, aux, out, pair, down = (
+        proj, aux, out, gate, up, down = (
             jnp.stack([summed(a, F32), summed(b, F32)]) for a, b in zip(first, second)
         )
         turned = lambda a: a.transpose(0, 2, 1)
         outs = [
-            qkv[:, :, :KEY], qkv[:, :, KEY : 2 * KEY], qkv[:, :, 2 * KEY :], gate, turned(aux)[:, :2],
-            turned(out), turned(pair)[:, :units], turned(pair)[:, units:], turned(down), *small,
-            turned(aux)[:, 2:6], home.astype(F32),
+            proj[:, :, :KEY], proj[:, :, KEY : 2 * KEY], proj[:, :, 2 * KEY : CONV_CH],
+            proj[:, :, CONV_CH:], turned(aux)[:, :2], turned(out), turned(gate), turned(up),
+            turned(down), *small, turned(aux)[:, 2:6], home.astype(F32)[:, None, :],
         ]
     return (
         mixed[:, None, :],
-        outs[15][:, None, :],
+        outs[15],
         outs[9],
         outs[0], outs[1], outs[2], outs[3],
         outs[4].transpose(0, 2, 1)[:, :, None, :],

time: 629 us -> 587 us (0.933)
  matrix products: 22.4 us -> 0 us
  Pallas kernels: 591 us -> 576 us
    dot_general x6 -> x0, matrix products: 22.4 us -> none  [dot32(): return lax.dot_general(a, b, dims, preferred_element_type=F32)]
    pallas_call x15, Pallas kernels: 586 us -> 571 us  [carry_call(): pl.pallas_call(carrying(body, jobs, len(args), outs), grid=grid, in_specs...]
where the time goes in v5:
time: 587 us; the launch traced here: 578 us
  Pallas kernels  576 us (98%)
    pallas_call x15, Pallas kernels, carry_call(): pl.pallas_call(carrying(body, jobs, len(args), outs), grid=grid, in_specs...  571 us

profile of v5, /device:TPU:0, one launch (start us, length us, event | category | flops | bytes accessed | tf_op | source)
XLA Modules:
  0.0 578.3 jit_solution(674184673509765995)
XLA Ops:
  0.7 58.0 %deal_and_gather.1 = (bf16[256,1024]{1,0:T(8,128)(2,1)}, bf16[1024,1024]{1,0:T(8,128)(2,1)}, bf16[256,1024]{1,0:T(8,128)(2,1)}, bf16[128,1024]{1,0:T(8,128)(2,1)...) custom-call(s32[8]{0:T(128)} %refs_0_.11, ...), custom_call_target="tpu_custom_call" | custom-call | flops 5242880 | bytes 83886080 | tf_op jit(solution)/shard_map/deal_and_gather/pallas_call | solution.py:1205
  58.7 43.4 %mixer_forward.2 = (bf16[1024,512]{1,0:T(8,128)(2,1)}, f32[1024,1024]{1,0:T(8,128)}, f32[1024,1024]{1,0:T(8,128)}, f32[1024,512]{1,0:T(8,128)}, f32[1024,128]{1,...) custom-call(bf16[2,4]{1,0:T(2,128)(2,1)} %refs_0_.10, ...), custom_call_target="tpu_custom_call" | custom-call | flops 16000000000 | bytes 83886080 | tf_op jit(solution)/shard_map/mixer_forward/pallas_call | solution.py:1205
  102.1 43.7 %mixer_bridge.2 = (f32[256,1024]{1,0:T(8,128)}, bf16[1024,1024]{1,0:T(8,128)(2,1)}, bf16[1024,704]{1,0:T(8,128)(2,1)}, bf16[1024,704]{1,0:T(8,128)(2,1)}, bf16[2...) custom-call(bf16[1024,512]{1,0:T(8,128)(2,1)} %get-tuple-element.156.refs_0_.refs_4_, ...), custom_call_target="tpu_custom_call" | custom-call | flops 1000000000 | bytes 83886080 | tf_op jit(solution)/shard_map/mixer_bridge/pallas_call | solution.py:1205
  145.8 9.0 %ffn_forward.1.refs_0_ = bf16[1024,1024]{1,0:T(8,128)(2,1)} custom-call(bf16[1024,1024]{1,0:T(8,128)(2,1)} %get-tuple-element.163.refs_0_, bf16[1024,704]{1,0:T(8,128)(2,1)} %get-tuple-element.164.refs_1_.refs_2_, bf16[1024,704]{1,0:T(8,128)(2,1)} %get-tuple-element.165.refs_2_.refs_3_, bf16[1024,704]{1,0:T(8,128)(2,1)} %get-tuple-element.166.refs_3_.refs_4_), custom_call_target="tpu_custom_call" | custom-call | flops 4000000000 | bytes 83886080 | tf_op jit(solution)/shard_map/ffn_forward/pallas_call | solution.py:1205
  154.8 39.5 %forward_bridge.1 = (f32[256,1024]{1,0:T(8,128)}, bf16[1024,1024]{1,0:T(8,128)(2,1)}, bf16[1024,1024]{1,0:T(8,128)(2,1)}, bf16[1024,640]{1,0:T(8,128)(2,1)}, bf1...) custom-call(bf16[1024,1024]{1,0:T(8,128)(2,1)} %ffn_forward.1.refs_0_, f32[256,1024]{1,0:T(8,128)} %get-tuple-element.167.refs_1_, ...), custom_call_target="tpu_custom_call" | custom-call | flops 5242880 | bytes 83886080 | tf_op jit(solution)/shard_map/forward_bridge/pallas_call | solution.py:1205
  194.2 33.7 %mixer_forward.3 = (bf16[1024,512]{1,0:T(8,128)(2,1)}, f32[1024,1024]{1,0:T(8,128)}, f32[1024,1024]{1,0:T(8,128)}, f32[1024,512]{1,0:T(8,128)}, f32[1024,128]{1,...) custom-call(bf16[2,4]{1,0:T(2,128)(2,1)} %refs_0_.10, ...), custom_call_target="tpu_custom_call" | custom-call | flops 16000000000 | bytes 83886080 | tf_op jit(solution)/shard_map/mixer_forward/pallas_call | solution.py:1205
  227.9 35.3 %mixer_bridge.3 = (f32[256,1024]{1,0:T(8,128)}, bf16[1024,1024]{1,0:T(8,128)(2,1)}, bf16[1024,704]{1,0:T(8,128)(2,1)}, bf16[1024,704]{1,0:T(8,128)(2,1)}) custom-call(bf16[1024,512]{1,0:T(8,128)(2,1)} %get-tuple-element.180.refs_0_.refs_4_, bf16[1024,512]{1,0:T(8,128)(2,1)} %get-tuple-element.181.refs_1_.refs_4_, ...), custom_call_target="tpu_custom_call" | custom-call | flops 1000000000 | bytes 83886080 | tf_op jit(solution)/shard_map/mixer_bridge/pallas_call | solution.py:1205
  263.3 24.6 %ffn_backward.2 = (bf16[1024,1024]{1,0:T(8,128)(2,1)}, bf16[1024,704]{1,0:T(8,128)(2,1)}, bf16[1024,704]{1,0:T(8,128)(2,1)}, bf16[1024,704]{1,0:T(8,128)(2,1)}, bf16[1024,1024]{1,0:T(8,128)(2,1)}) custom-call(bf16[1024,1024]{1,0:T(8,128)(2,1)} %get-tuple-element.185.refs_0_, bf16[1024,1024]{1,0:T(8,128)(2,1)} %get-tuple-element.186.refs_1_, ...), custom_call_target="tpu_custom_call" | custom-call | flops 12000000000 | bytes 83886080 | tf_op jit(solution)/shard_map/ffn_backward/pallas_call | solution.py:1205
  287.8 35.5 %backward_bridge.3 = (f32[256,1024]{1,0:T(8,128)}, bf16[1024,1024]{1,0:T(8,128)(2,1)}, f32[1,1024]{1,0:T(1,128)}, bf16[1024,512]{1,0:T(8,128)(2,1)}, bf16[256,704]{1,0:T(8,128)(2,1)}, /*index=5*/bf16[256,704]{1,0:T(8,128)(2,1)}) custom-call(bf16[1024,1024]{1,0:T(8,128)(2,1)} %get-tuple-element.191.refs_0_, f32[256,1024]{1,0:T(8,128)} %get-tuple-element.190.refs_5_.refs_1_, ...), custom_call_target="tpu_custom_call" | custom-call | flops 5242880 | bytes 83886080 | tf_op jit(solution)/shard_map/backward_bridge/pallas_call | solution.py:1205
  323.3 41.4 %mixer_backward.2 = (bf16[1024,1024]{1,0:T(8,128)(2,1)}, bf16[1024,1536]{1,0:T(8,128)(2,1)}, bf16[1024,128]{1,0:T(8,128)(2,1)}, f32[1,512]{1,0:T(1,128)}, f32[8,...) custom-call(bf16[2,4]{1,0:T(2,128)(2,1)} %refs_0_.10, ...), custom_call_target="tpu_custom_call" | custom-call | flops 16000000000 | bytes 83886080 | tf_op jit(solution)/shard_map/mixer_backward/pallas_call | solution.py:1205
  364.8 38.2 %backward_bridge.4 = (f32[256,1024]{1,0:T(8,128)}, bf16[1024,1024]{1,0:T(8,128)(2,1)}, f32[1,1024]{1,0:T(1,128)}, bf16[256,1536]{1,0:T(8,128)(2,1)}, bf16[256,12...) custom-call(bf16[1024,1024]{1,0:T(8,128)(2,1)} %get-tuple-element.208.refs_0_, f32[256,1024]{1,0:T(8,128)} %get-tuple-element.182.refs_2_.refs_1_, ...), custom_call_target="tpu_custom_call" | custom-call | flops 5242880 | bytes 83886080 | tf_op jit(solution)/shard_map/backward_bridge/pallas_call | solution.py:1205
  402.9 26.0 %ffn_backward.3 = (bf16[1024,1024]{1,0:T(8,128)(2,1)}, bf16[1024,704]{1,0:T(8,128)(2,1)}, bf16[1024,704]{1,0:T(8,128)(2,1)}, bf16[1024,704]{1,0:T(8,128)(2,1)}, ...) custom-call(bf16[1024,1024]{1,0:T(8,128)(2,1)} %get-tuple-element.163.refs_0_, ...), custom_call_target="tpu_custom_call" | custom-call | flops 12000000000 | bytes 83886080 | tf_op jit(solution)/shard_map/ffn_backward/pallas_call | solution.py:1205
  429.0 35.9 %backward_bridge.5 = (f32[256,1024]{1,0:T(8,128)}, bf16[1024,1024]{1,0:T(8,128)(2,1)}, f32[1,1024]{1,0:T(1,128)}, bf16[1024,512]{1,0:T(8,128)(2,1)}, bf16[256,704]{1,0:T(8,128)(2,1)}, /*index=5*/bf16[256,704]{1,0:T(8,128)(2,1)}) custom-call(bf16[1024,1024]{1,0:T(8,128)(2,1)} %get-tuple-element.217.refs_0_, f32[256,1024]{1,0:T(8,128)} %get-tuple-element.167.refs_1_, ...), custom_call_target="tpu_custom_call" | custom-call | flops 5242880 | bytes 83886080 | tf_op jit(solution)/shard_map/backward_bridge/pallas_call | solution.py:1205
  464.9 40.1 %mixer_backward.3 = (bf16[1024,1024]{1,0:T(8,128)(2,1)}, bf16[1024,1536]{1,0:T(8,128)(2,1)}, bf16[1024,128]{1,0:T(8,128)(2,1)}, f32[1,512]{1,0:T(1,128)}, f32[8,...) custom-call(bf16[2,4]{1,0:T(2,128)(2,1)} %refs_0_.10, ...), custom_call_target="tpu_custom_call" | custom-call | flops 16000000000 | bytes 83886080 | tf_op jit(solution)/shard_map/mixer_backward/pallas_call | solution.py:1205
  504.9 66.6 %final_step.1 = (bf16[256,1024]{1,0:T(8,128)(2,1)}, f32[48,128]{1,0:T(8,128)}, bf16[2,128,1536]{2,1,0:T(8,128)(2,1)}, bf16[2,128,128]{2,1,0:T(8,128)(2,1)}, bf16...) custom-call(s32[8]{0:T(128)} %refs_0_.11, bf16[1024,1024]{1,0:T(8,128)(2,1)} %get-tuple-element.236.refs_1_, ...), custom_call_target="tpu_custom_call" | custom-call | flops 5242880 | bytes 83886080 | tf_op jit(solution)/shard_map/final_step/pallas_call | solution.py:1205
  571.6 0.0 copy-start
  571.6 5.5 weights_out.1
  577.1 0.0 copy-done
  577.1 0.8 copy.39
Async XLA Ops:
  571.6 5.5 copy-start

commit v6 on v5

--- a/solution.py
+++ b/solution.py
@@ -396,12 +396,20 @@
 
 
 PIECES = 4
+TURN = (1, 2)
 AXES = ("chip", "core", "zp", "zl")
 
 
 def partners():
     core, zl = lax.axis_index("core"), lax.axis_index("zl")
     return core, zl, {"core": 1 - core}, {"zl": 1 - zl}
+
+
+def remote(src, dst, send, recv, device):
+    return pltpu.make_async_remote_copy(
+        src_ref=src, dst_ref=dst, send_sem=send, recv_sem=recv,
+        device_id=device, device_id_type=pl.DeviceIdType.MESH,
+    )
 
 
 class Block:
@@ -415,13 +423,6 @@
     def rows(self):
         rows = self.size * PIECES
         return pl.ds(pl.multiple_of(self.first, rows), rows)
-
-
-def remote(src, dst, send, recv, device):
-    return pltpu.make_async_remote_copy(
-        src_ref=src, dst_ref=dst, send_sem=send, recv_sem=recv,
-        device_id=device, device_id_type=pl.DeviceIdType.MESH,
-    )
 
 
 class Scatter:
@@ -434,7 +435,6 @@
         self.own = Block(zl, core, rows)
         self.away = Block(1 - zl, core, rows)
         own_beside, away_beside = Block(zl, 1 - core, rows), Block(1 - zl, 1 - core, rows)
-        self.blocks = (away_beside, own_beside, self.away, self.own)
         self.to_far = [
             remote(partial.at[away_beside.piece(p)], beside_far.at[self.local(p)],
                    send.at[0, p], recv.at[0, p], beside)
@@ -454,18 +454,11 @@
     def local(self, p):
         return pl.ds(p * self.size, self.size)
 
-    def start(self, make=None):
-        if make is not None:
-            make(self.blocks[0].rows())
+    def start(self):
         for copy in self.to_far:
             copy.start()
-        if make is not None:
-            make(self.blocks[1].rows())
         for copy in self.to_own:
             copy.start()
-        if make is not None:
-            make(self.blocks[2].rows())
-            make(self.blocks[3].rows())
         for p in range(PIECES):
             self.to_far[p].wait_recv()
             at = self.local(p)
@@ -490,97 +483,206 @@
                 copy.wait_send()
 
 
-class Gather:
-    def __init__(self, gathered, send, recv, first):
+class Exchange:
+    def __init__(self, partial, near, sums, far, send, recv):
         core, zl, beside, across = partners()
-        rows = gathered.shape[0] // 4
-        self.gathered = gathered
-        self.own = Block(zl, core, rows)
-        other = Block(1 - zl, core, rows)
-        make = lambda block, at, device: [
-            remote(gathered.at[block.piece(p)], gathered.at[block.piece(p)],
-                   send.at[first + at, p], recv.at[first + at, p], device)
-            for p in range(PIECES)
+        rows = far.shape[1]
+        self.near, self.sums, self.far = near, sums, far
+        self.size = rows // PIECES
+        self.blocks = [Block(l, core, rows) for l in range(2)]
+        self.others = [Block(l, 1 - core, rows) for l in range(2)]
+        self.order = [(l, p) for l in range(2) for p in range(PIECES)]
+        self.beside = [
+            [
+                remote(partial.at[self.others[l].piece(p)], near.at[l, self.local(p)],
+                       send.at[l, p], recv.at[l, p], beside)
+                for p in range(PIECES)
+            ]
+            for l in range(2)
         ]
-        self.across = make(self.own, 0, across)
-        self.beside = make(self.own, 1, beside)
-        self.forward = make(other, 2, beside)
-
-    def put(self, p, rows):
-        self.gathered[self.own.piece(p), :] = rows
-        self.across[p].start()
-        self.beside[p].start()
+        self.across = [
+            [
+                remote(sums.at[l, self.local(p)], far.at[l, self.local(p)],
+                       send.at[2 + l, p], recv.at[2 + l, p], across)
+                for p in range(PIECES)
+            ]
+            for l in range(2)
+        ]
+
+    def local(self, p):
+        return pl.ds(p * self.size, self.size)
+
+    def send(self, l):
+        for copy in self.beside[l]:
+            copy.start()
+
+    def pass_on(self, l, mine):
+        for p in range(PIECES):
+            self.beside[l][p].wait_recv()
+            at = self.local(p)
+            self.sums[l, at, :] = (
+                mine(l, p).astype(F32) + self.near[l, at, :].astype(F32)
+            ).astype(BF16)
+            self.across[l][p].start()
+
+    def total(self, l, p):
+        self.across[l][p].wait_recv()
+        at = self.local(p)
+        return self.sums[l, at, :].astype(F32) + self.far[l, at, :].astype(F32)
 
     def finish(self):
-        for p in range(PIECES):
-            self.across[p].wait_recv()
-            self.forward[p].start()
-        for p in range(PIECES):
-            self.beside[p].wait_recv()
-            self.forward[p].wait_recv()
-        for copies in (self.across, self.beside, self.forward):
-            for copy in copies:
+        for l, p in self.order:
+            self.beside[l][p].wait_send()
+            self.across[l][p].wait_send()
+
+
+class Sharing:
+    def __init__(self, held, out, send, recv, stores):
+        core, _, beside, _ = partners()
+        rows = held.shape[0] // 4
+        self.held = held
+        self.blocks = [Block(l, core, rows) for l in range(2)]
+        self.copies = [
+            [
+                remote(held.at[block.piece(p)], held.at[block.piece(p)], send.at[l, p], recv.at[l, p],
+                       beside)
+                for p in range(PIECES)
+            ]
+            for l, block in enumerate(self.blocks)
+        ]
+        others = [Block(l, 1 - core, rows) for l in range(2)]
+        self.stores = [
+            pltpu.make_async_copy(held.at[block.rows()], out.at[block.rows()], stores.at[at])
+            for at, block in enumerate(self.blocks + others)
+        ]
+
+    def put(self, l, p, rows):
+        self.held[self.blocks[l].piece(p), :] = rows
+        self.copies[l][p].start()
+        if p == PIECES - 1:
+            self.stores[l].start()
+
+    def arrive(self):
+        for l in range(2):
+            for copy in self.copies[l]:
+                copy.wait_recv()
+            self.stores[2 + l].start()
+
+    def finish(self):
+        for l in range(2):
+            for copy in self.copies[l]:
                 copy.wait_send()
+        for store in self.stores:
+            store.wait()
 
 
 def normed_of(x, gain):
     return x * lax.rsqrt(jnp.mean(x * x, axis=1, keepdims=True) + 1e-6) * gain
 
 
-def first_kernel(row, jobs, x_ref, gain_ref, out_ref, send, recv):
+def load_all(copies):
+    for copy in copies:
+        copy.start()
+
+
+def first_kernel(row, jobs, x_ref, gain_ref, new_ref, out_ref, raw, held, cross_send, cross_recv, send,
+                 recv, stores):
+    _, zl, _, across = partners()
     wait_greetings(greet_group() + jobs.greet())
-    gather = Gather(out_ref, send, recv, 0)
+    swap = remote(raw.at[zl], raw.at[zl], cross_send.at[0], cross_recv.at[0], across)
+    raw[zl] = x_ref[...]
+    swap.start()
     jobs.start()
-    size = x_ref.shape[0] // PIECES
-    for p in range(PIECES):
-        x = x_ref[p * size : (p + 1) * size, :].astype(F32)
-        gather.put(p, normed_of(x, gain_ref[row : row + 1, :].astype(F32)).astype(BF16))
+    sharing = Sharing(held, out_ref, send, recv, stores)
+    swap.wait()
+    size = raw.shape[1] // PIECES
+    for l in range(2):
+        for p in range(PIECES):
+            x = raw[l, p * size : (p + 1) * size, :].astype(F32)
+            sharing.put(l, p, normed_of(x, gain_ref[row : row + 1, :].astype(F32)).astype(BF16))
+    new_ref[...] = raw[...]
     jobs.middle()
-    gather.finish()
+    sharing.arrive()
+    sharing.finish()
     jobs.finish()
 
 
 def forward_bridge_kernel(
-    row, jobs, partial, x_ref, gain_ref, new_ref, out_ref, beside_far, beside_own, sums, far, send, recv
+    row, jobs, partial, x_ref, gain_ref, new_ref, out_ref, mine, near, sums, far, x, held, send, recv,
+    share_send, share_recv, loads, stores
 ):
+    exchange = Exchange(partial, near, sums, far, send, recv)
+    sharing = Sharing(held, out_ref, share_send, share_recv, stores)
+    own = [
+        pltpu.make_async_copy(partial.at[exchange.blocks[l].rows()], mine.at[l], loads.at[l])
+        for l in range(2)
+    ]
+    old = [pltpu.make_async_copy(x_ref.at[l], x.at[l], loads.at[2 + l]) for l in range(2)]
+    new = [pltpu.make_async_copy(x.at[l], new_ref.at[l], stores.at[4 + l]) for l in range(2)]
+    load_all(own + old)
     wait_greetings(greet_group() + jobs.greet())
-    scatter = Scatter(partial, beside_far, beside_own, sums, far, send, recv)
-    gather = Gather(out_ref, send, recv, 3)
-    scatter.start()
+    for l in range(2):
+        exchange.send(l)
     jobs.start()
-    for p in range(PIECES):
-        at = scatter.local(p)
-        x = x_ref[at, :].astype(F32) + scatter.total(p)
-        new_ref[at, :] = x
-        gather.put(p, normed_of(x, gain_ref[row : row + 1, :].astype(F32)).astype(BF16))
-    jobs.middle()
-    scatter.finish()
-    gather.finish()
+    for l in range(2):
+        own[l].wait()
+        exchange.pass_on(l, lambda l, p: mine[l, exchange.local(p), :])
+    forward_rows(row, jobs, exchange, sharing, old, new, x, gain_ref)
+
+
+def forward_rows(row, jobs, exchange, sharing, old, new, x, gain_ref):
+    gain = gain_ref[row : row + 1, :].astype(F32)
+    for l in range(2):
+        old[l].wait()
+        for p in range(PIECES):
+            if (l, p) == TURN:
+                jobs.middle()
+            at = exchange.local(p)
+            rows = x[l, at, :] + exchange.total(l, p)
+            x[l, at, :] = rows
+            sharing.put(l, p, normed_of(rows, gain).astype(BF16))
+        new[l].start()
+    sharing.arrive()
+    exchange.finish()
+    sharing.finish()
+    for store in new:
+        store.wait()
     jobs.finish()
 
 
 def mixer_bridge_kernel(
-    row, jobs, heads_ref, w_out_ref, x_ref, gain_ref, new_ref, out_ref, partial, beside_far, beside_own,
-    sums, far, send, recv
+    row, jobs, heads_ref, w_out_ref, x_ref, gain_ref, new_ref, out_ref, partial, raw, near, sums, far, x,
+    held, send, recv, share_send, share_recv, loads, stores
 ):
+    exchange = Exchange(partial, near, sums, far, send, recv)
+    sharing = Sharing(held, out_ref, share_send, share_recv, stores)
+    old = [pltpu.make_async_copy(x_ref.at[l], raw.at[l], loads.at[2 + l]) for l in range(2)]
+    new = [pltpu.make_async_copy(x.at[l], new_ref.at[l], stores.at[4 + l]) for l in range(2)]
+    load_all(old)
     wait_greetings(greet_group() + jobs.greet())
-    scatter = Scatter(partial, beside_far, beside_own, sums, far, send, recv)
-    gather = Gather(out_ref, send, recv, 3)
-
-    def make(rows):
+
+    def make(block):
+        rows = block.rows()
         partial[rows, :] = mm(heads_ref[rows, :], w_out_ref[...], NT).astype(BF16)
 
-    scatter.start(make)
+    for l in range(2):
+        make(exchange.others[l])
+        exchange.send(l)
     jobs.start()
-    for p in range(PIECES):
-        at = scatter.local(p)
-        x = x_ref[at, :].astype(F32) + scatter.total(p)
-        new_ref[at, :] = x
-        gather.put(p, normed_of(x, gain_ref[row : row + 1, :].astype(F32)).astype(BF16))
-    jobs.middle()
-    scatter.finish()
-    gather.finish()
-    jobs.finish()
+    for l in range(2):
+        make(exchange.blocks[l])
+        exchange.pass_on(l, lambda l, p: partial[exchange.blocks[l].piece(p), :])
+    for l in range(2):
+        old[l].wait()
+        if x_ref.dtype != F32:
+            x[l] = raw[l].astype(F32)
+        old[l] = Done()
+    forward_rows(row, jobs, exchange, sharing, old, new, x, gain_ref)
+
+
+class Done:
+    def wait(self):
+        pass
 
 
 def norm_back(total, x, gain):
@@ -596,28 +698,55 @@
         heads_ref, new_ref, out_ref, dgain_ref, dout_ref, *refs = refs
     else:
         new_ref, out_ref, dgain_ref, *refs = refs
-    beside_far, beside_own, sums, far, send, recv = refs
+    (mine, near, sums, far, x, grad, new_rows, held, send, recv, share_send, share_recv, loads,
+     stores) = refs
+    exchange = Exchange(partial, near, sums, far, send, recv)
+    sharing = Sharing(held, out_ref, share_send, share_recv, stores)
+    zl = lax.axis_index("zl")
+    place = lambda ref, l: ref.at[exchange.blocks[l].rows()] if len(ref.shape) == 2 else ref.at[l]
+    own, old = [], []
+    for l in range(2):
+        own.append(
+            pltpu.make_async_copy(partial.at[exchange.blocks[l].rows()], mine.at[l], loads.at[l])
+        )
+        old.append(
+            (pltpu.make_async_copy(x_ref.at[l], x.at[l], loads.at[2 + l]),
+             pltpu.make_async_copy(place(grad_ref, l), grad.at[l], loads.at[4 + l]))
+        )
+    new = [pltpu.make_async_copy(new_rows.at[l], new_ref.at[l], stores.at[4 + l]) for l in range(2)]
+    load_all(own + [copy for pair in old for copy in pair])
     wait_greetings(greet_group() + jobs.greet())
-    scatter = Scatter(partial, beside_far, beside_own, sums, far, send, recv)
-    gather = Gather(out_ref, send, recv, 3)
-    scatter.start()
+    for l in range(2):
+        exchange.send(l)
     jobs.start()
+    for l in range(2):
+        own[l].wait()
+        exchange.pass_on(l, lambda l, p: mine[l, exchange.local(p), :])
+    gain = gain_ref[row : row + 1, :].astype(F32)
     dgain = jnp.zeros(dgain_ref.shape, F32)
-    for p in range(PIECES):
-        at = scatter.local(p)
-        grad, part = norm_back(scatter.total(p), x_ref[at, :].astype(F32), gain_ref[row : row + 1, :].astype(F32))
-        dgain = dgain + part
-        grad = grad + grad_ref[at, :].astype(F32)
-        new_ref[at, :] = grad
-        gather.put(p, grad.astype(BF16))
+    for l in range(2):
+        for copy in old[l]:
+            copy.wait()
+        for p in range(PIECES):
+            if (l, p) == TURN:
+                jobs.middle()
+            at = exchange.local(p)
+            rows, part = norm_back(exchange.total(l, p), x[l, at, :].astype(F32), gain)
+            dgain = dgain + jnp.where(zl == l, part, 0.0)
+            rows = rows + grad[l, at, :].astype(F32)
+            new_rows[l, at, :] = rows
+            sharing.put(l, p, rows.astype(BF16))
+        new[l].start()
     dgain_ref[...] = dgain
-    jobs.middle()
-    scatter.finish()
-    gather.finish()
+    sharing.arrive()
     if last:
-        for first in range(0, out_ref.shape[1], 256):
+        for first in range(0, held.shape[1], 256):
             columns = slice(first, first + 256)
-            dout_ref[columns, :] = mm(out_ref[:, columns], heads_ref[...], TN).astype(BF16)
+            dout_ref[columns, :] = mm(held[:, columns], heads_ref[...], TN).astype(BF16)
+    exchange.finish()
+    sharing.finish()
+    for store in new:
+        store.wait()
     jobs.finish()
 
 
@@ -629,78 +758,115 @@
     scatter = Scatter(partial, beside_far, beside_own, sums, far, send, recv)
     scatter.start()
     jobs.start()
+    zl = lax.axis_index("zl")
     dgain = jnp.zeros(dgain_ref.shape, F32)
     for p in range(PIECES):
         at = scatter.local(p)
-        grad, part = norm_back(scatter.total(p), x_ref[at, :].astype(F32), gain_ref[row : row + 1, :].astype(F32))
+        grad, part = norm_back(
+            scatter.total(p), x_ref[zl, at, :].astype(F32), gain_ref[row : row + 1, :].astype(F32)
+        )
         dgain = dgain + part
-        new_ref[at, :] = (grad + grad_ref[at, :]).astype(BF16)
+        new_ref[at, :] = (grad + grad_ref[zl, at, :]).astype(BF16)
     dgain_ref[...] = dgain
     jobs.middle()
     scatter.finish()
     jobs.finish()
 
 
-def comm_call(kernel, row, number, outs, args, scatters, gathers, jobs, name=None):
-    rows = args[1].shape[0] if scatters else args[0].shape[0]
-    width = args[0].shape[1]
-    vmem = pl.BlockSpec(memory_space=pltpu.VMEM)
-    hops = 3 * scatters + 3 * gathers
-    return carry_call(
-        kernel if row is None else functools.partial(kernel, row), jobs, (), [vmem] * len(args), [vmem] * len(outs),
-        [jax.ShapeDtypeStruct(shape, kind) for shape, kind in outs],
-        [pltpu.VMEM((rows, width), BF16) for _ in range(4 * scatters)]
-        + [pltpu.SemaphoreType.DMA((hops, PIECES)), pltpu.SemaphoreType.DMA((hops, PIECES))],
-        args, number, name or kernel.__name__.replace("_kernel", ""), rows * width * 20,
-    )
+VMEM_SPEC = pl.BlockSpec(memory_space=pltpu.VMEM)
+ANY_SPEC = pl.BlockSpec(memory_space=pl.ANY)
+
+
+def pair_scratch(rows, width, kinds):
+    return [pltpu.VMEM((2, rows, width), kind) for kind in kinds]
+
+
+def bridge_sems():
+    many = pltpu.SemaphoreType.DMA((4, PIECES))
+    few = pltpu.SemaphoreType.DMA((2, PIECES))
+    return [many, many, few, few, pltpu.SemaphoreType.DMA((6,)), pltpu.SemaphoreType.DMA((6,))]
+
+
+def bridge_shapes(rows, width):
+    return [
+        jax.ShapeDtypeStruct((2, rows, width), F32),
+        jax.ShapeDtypeStruct((4 * rows, width), BF16),
+    ]
 
 
 def first_gather(x, gain, row, jobs, number):
     rows, width = x.shape
-    return comm_call(first_kernel, row, number, [((4 * rows, width), BF16)], (x, gain), 0, 1, jobs)
-
-
-def forward_bridge(partial, x, gain, row, jobs, number):
-    rows, width = x.shape
-    return comm_call(
-        forward_bridge_kernel, row, number, [((rows, width), F32), ((4 * rows, width), BF16)],
-        (partial, x, gain), 1, 1, jobs,
-    )
-
-
-def mixer_bridge(heads, w_out, x, gain, row, jobs, number):
-    rows, width = x.shape
-    vmem = pl.BlockSpec(memory_space=pltpu.VMEM)
-    sems = pltpu.SemaphoreType.DMA((6, PIECES))
+    few = pltpu.SemaphoreType.DMA((2, PIECES))
+    one = pltpu.SemaphoreType.DMA((1,))
     return carry_call(
-        functools.partial(mixer_bridge_kernel, row), jobs, (), [vmem] * 4, [vmem] * 2,
+        functools.partial(first_kernel, row), jobs, (), [VMEM_SPEC] * 2, [VMEM_SPEC, ANY_SPEC],
         [
-            jax.ShapeDtypeStruct((rows, width), F32),
+            jax.ShapeDtypeStruct((2, rows, width), BF16),
             jax.ShapeDtypeStruct((4 * rows, width), BF16),
         ],
-        [pltpu.VMEM((4 * rows, width), BF16)]
-        + [pltpu.VMEM((rows, width), BF16) for _ in range(4)] + [sems, sems],
+        [pltpu.VMEM((2, rows, width), BF16), pltpu.VMEM((4 * rows, width), BF16), one, one, few, few,
+         pltpu.SemaphoreType.DMA((4,))],
+        (x, gain), number, "first", rows * width * 20,
+    )
+
+
+def forward_bridge(partial, x, gain, row, jobs, number):
+    _, rows, width = x.shape
+    return carry_call(
+        functools.partial(forward_bridge_kernel, row), jobs, (),
+        [ANY_SPEC, ANY_SPEC, VMEM_SPEC], [ANY_SPEC] * 2, bridge_shapes(rows, width),
+        pair_scratch(rows, width, [BF16] * 4 + [F32]) + [pltpu.VMEM((4 * rows, width), BF16)]
+        + bridge_sems(),
+        (partial, x, gain), number, "forward_bridge", rows * width * 20,
+    )
+
+
+def mixer_bridge(heads, w_out, x, gain, row, jobs, number):
+    _, rows, width = x.shape
+    kernel = functools.partial(
+        mixer_bridge_kernel if x.dtype != F32 else mixer_bridge_kernel_f32, row
+    )
+    raw = pair_scratch(rows, width, [BF16]) if x.dtype != F32 else []
+    return carry_call(
+        kernel, jobs, (), [VMEM_SPEC, VMEM_SPEC, ANY_SPEC, VMEM_SPEC], [ANY_SPEC] * 2,
+        bridge_shapes(rows, width),
+        [pltpu.VMEM((4 * rows, width), BF16)] + raw + pair_scratch(rows, width, [BF16] * 3 + [F32])
+        + [pltpu.VMEM((4 * rows, width), BF16)] + bridge_sems(),
         (heads, w_out, x, gain), number, "mixer_bridge", 10**9,
     )
 
 
+def mixer_bridge_kernel_f32(row, jobs, heads_ref, w_out_ref, x_ref, gain_ref, new_ref, out_ref, partial,
+                            near, sums, far, x, *refs):
+    mixer_bridge_kernel(row, jobs, heads_ref, w_out_ref, x_ref, gain_ref, new_ref, out_ref, partial, x,
+                        near, sums, far, x, *refs)
+
+
 def backward_bridge(partial, x, gain, row, grad, jobs, number, heads=None):
-    rows, width = x.shape
+    _, rows, width = x.shape
     last = heads is not None
-    outs = [((rows, width), F32), ((4 * rows, width), BF16), ((1, width), F32)]
+    outs = bridge_shapes(rows, width) + [jax.ShapeDtypeStruct((1, width), F32)]
     if last:
-        outs.append(((width, heads.shape[1]), BF16))
-    return comm_call(
-        functools.partial(backward_bridge_kernel, row, last), None, number, outs,
-        (partial, x, gain, grad) + ((heads,) if last else ()), 1, 1, jobs, "backward_bridge",
+        outs.append(jax.ShapeDtypeStruct((width, heads.shape[1]), BF16))
+    return carry_call(
+        functools.partial(backward_bridge_kernel, row, last), jobs, (),
+        [ANY_SPEC, ANY_SPEC, VMEM_SPEC, ANY_SPEC] + [VMEM_SPEC] * last,
+        [ANY_SPEC, ANY_SPEC, VMEM_SPEC] + [VMEM_SPEC] * last, outs,
+        pair_scratch(rows, width, [BF16] * 4 + [x.dtype, grad.dtype, F32])
+        + [pltpu.VMEM((4 * rows, width), BF16)] + bridge_sems(),
+        (partial, x, gain, grad) + ((heads,) if last else ()), number, "backward_bridge",
+        rows * width * 20,
     )
 
 
 def backward_last(partial, x, gain, row, grad, jobs, number):
-    rows, width = x.shape
-    return comm_call(
-        backward_last_kernel, row, number, [((rows, width), BF16), ((1, width), F32)],
-        (partial, x, gain, grad), 1, 0, jobs,
+    _, rows, width = x.shape
+    hops = pltpu.SemaphoreType.DMA((3, PIECES))
+    return carry_call(
+        functools.partial(backward_last_kernel, row), jobs, (), [VMEM_SPEC] * 4, [VMEM_SPEC] * 2,
+        [jax.ShapeDtypeStruct((rows, width), BF16), jax.ShapeDtypeStruct((1, width), F32)],
+        [pltpu.VMEM((rows, width), BF16) for _ in range(4)] + [hops, hops],
+        (partial, x, gain, grad), number, "backward_last", rows * width * 20,
     )
 
 
@@ -1131,16 +1297,22 @@
 
 class Jobs:
     def __init__(self, jobs, chips):
-        self.kinds = [kind for kind, _ in jobs]
-        self.values = [value for _, value in jobs]
+        self.kinds = [job[0] for job in jobs]
+        self.values = [job[1] for job in jobs]
+        self.columns = [job[2] if len(job) > 2 else None for job in jobs]
+        shapes = [
+            value.shape if columns is None else (value.shape[0], columns[1])
+            for value, columns in zip(self.values, self.columns)
+        ]
         self.chips = chips
         count = max(9, chips + 1)
         any_space = pl.BlockSpec(memory_space=pl.ANY)
         self.in_specs = [any_space] * len(jobs)
         self.out_shape = [
-            jax.ShapeDtypeStruct(kind.result(value.shape, chips), BF16) for kind, value in jobs
+            jax.ShapeDtypeStruct(kind.result(shape, chips), BF16)
+            for kind, shape in zip(self.kinds, shapes)
         ]
-        self.buffers = [kind.buffers(value.shape, chips) for kind, value in jobs]
+        self.buffers = [kind.buffers(shape, chips) for kind, shape in zip(self.kinds, shapes)]
         self.scratch = [pltpu.SemaphoreType.DMA((count,))] * (2 * len(jobs))
         self.scratch += [buffer for buffers in self.buffers for buffer in buffers]
 
@@ -1159,6 +1331,8 @@
         sems, scratch = scratch[: 2 * len(self.kinds)], scratch[2 * len(self.kinds) :]
         self.bound = []
         for at, (kind, source, target) in enumerate(zip(self.kinds, sources, targets)):
+            if self.columns[at] is not None:
+                source = source.at[:, pl.ds(*self.columns[at])]
             held, scratch = scratch[: len(self.buffers[at])], scratch[len(self.buffers[at]) :]
             self.bound.append(
                 kind(source, target, sems[2 * at], sems[2 * at + 1], self.chips, held)
@@ -1327,7 +1501,8 @@
     raw, refs = refs[:10], refs[10:]
     (new_ref, out_ref, start_ref, qkv_next, side_next, out_next, gate_next, up_ref, up_next, down_ref,
      down_next, first_full, second_full, first_wide, second_wide, third_wide, fourth_wide) = refs[:17]
-    (spread, picked, square, first, second, third, fourth, held_first, held_second, send, recv,
+    (spread, picked, square, first, second, third, fourth, held_first, held_second, held, send, recv, stores,
+     cross_send, cross_recv,
      plane_send, plane_recv, role_send, role_recv, *sems) = refs[17:]
     raw = Raw(raw, square)
     plane, trade = Plane(chips), Trade(chips)
@@ -1337,7 +1512,8 @@
     second_across = Spread(second_wide, second_full, sems[6], sems[7], chips, [held_second])
     third_column = ToPlane(third, third_wide, sems[8], sems[9], chips)
     fourth_column = ToPlane(fourth, fourth_wide, sems[10], sems[11], chips)
-    gather = Gather(out_ref, send, recv, 0)
+    sharing = Sharing(held, out_ref, send, recv, stores)
+    across = {"zl": 1 - trade.zl}
     count = plane.count
     part = x_ref.shape[0] // count
     rows = lambda index: pl.ds(pl.multiple_of(index * part, part), part)
@@ -1367,14 +1543,14 @@
     to_roles = []
     for slot in range(count):
         picked[slot] = spread[order_ref[slot]]
-        copy = remote(picked.at[slot], new_ref.at[rows(plane.own)], role_send.at[slot],
+        copy = remote(picked.at[slot], new_ref.at[trade.zp, rows(plane.own)], role_send.at[slot],
                       role_recv.at[plane.own], trade.role(slot))
         mine = trade.role_mine(slot)
         unless(mine, copy.start)
 
         @pl.when(mine)
         def _():
-            new_ref[rows(plane.own), :] = picked[slot]
+            new_ref[trade.zl, rows(plane.own), :] = picked[slot]
 
         to_roles.append((copy, mine))
     second_column.start()
@@ -1384,18 +1560,34 @@
     first_across.start()
     size = x_ref.shape[0] // PIECES
     parts = max(size // part, 1)
+    swaps = []
+    for p in range(PIECES):
+        piece = new_ref.at[trade.zl, pl.ds(p * size, size)]
+        swaps.append(remote(piece, piece, cross_send.at[p], cross_recv.at[p], across))
     for p in range(PIECES):
         for index in range(p * parts, (p + 1) * parts):
-            arrival = remote(picked.at[0], new_ref.at[rows(index)], role_send.at[0],
+            arrival = remote(picked.at[0], new_ref.at[trade.zl, rows(index)], role_send.at[0],
                              role_recv.at[index], trade.home(index))
             unless(trade.home_mine(index), arrival.wait_recv)
-        x = new_ref[p * size : (p + 1) * size, :].astype(F32)
-        gather.put(p, normed_of(x, gain_ref[0:1, :].astype(F32)).astype(BF16))
+        swaps[p].start()
+    gain = gain_ref[0:1, :].astype(F32)
+
+    def share(l):
+        for p in range(PIECES):
+            x = new_ref[l, p * size : (p + 1) * size, :].astype(F32)
+            sharing.put(l, p, normed_of(x, gain).astype(BF16))
+
+    for l in range(2):
+        pl.when(trade.zl == l)(functools.partial(share, l))
     second_column.finish()
     second_across.start()
     third_column.start()
     fourth_column.start()
     first_across.middle()
+    for swap in swaps:
+        swap.wait_recv()
+    for l in range(2):
+        pl.when(trade.zl != l)(functools.partial(share, l))
     length = lengths_ref[order_ref[plane.own]]
     at = (trade.zp * 2 + trade.zl) * x_ref.shape[0]
     positions = lax.broadcasted_iota(jnp.int32, x_ref.shape, 0) + at
@@ -1412,7 +1604,10 @@
         copy.wait_send()
     for copy, mine in to_roles:
         unless(mine, copy.wait_send)
-    gather.finish()
+    for swap in swaps:
+        swap.wait_send()
+    sharing.arrive()
+    sharing.finish()
     second_across.middle()
     first_across.finish()
     second_across.finish()
@@ -1433,16 +1628,17 @@
     held = [(part, cols) for cols in (qkv, side, VAL, units, units, units, units, units)]
     spread = [(2 * chips * part, qkv), (2 * chips * part, side)]
     moved = [(2 * part, cols) for cols in (qkv, side, VAL, units)]
-    shapes = [(rows, width), (4 * rows, width), (rows, width)] + held + spread + moved
+    shapes = [(2, rows, width), (4 * rows, width), (rows, width)] + held + spread + moved
     own = [(part, qkv), (part, side), (part, VAL), (part, units), moved[0], moved[1]]
     return carry_call(
         functools.partial(deal_kernel, chips), Jobs([], chips), (),
         [smem, smem] + [vmem] * 13,
-        [vmem] * 11 + [hbm] * 6,
+        [vmem, hbm] + [vmem] * 9 + [hbm] * 6,
         [jax.ShapeDtypeStruct(shape, BF16) for shape in shapes],
         [buffer, buffer, pltpu.VMEM((LANES, LANES), F32)]
         + [pltpu.VMEM(shape, BF16) for shape in own]
-        + sems(3, PIECES) + sems(count) + sems(count)
+        + [pltpu.VMEM((4 * rows, width), BF16)] + sems(2, PIECES) + [pltpu.SemaphoreType.DMA((4,))]
+        + sems(PIECES) + sems(count) + sems(count)
         + [pltpu.SemaphoreType.DMA((max(9, chips + 1),))] * 12,
         (order, lengths, x, gain, cotangent, *raw), number, "deal_and_gather", rows * width * 20,
     )[0]
@@ -1474,10 +1670,10 @@
 ):
     terms, refs = refs[:7], refs[7:]
     (in_ref, aux_ref), refs = refs[:2], refs[2:]
-    home_ref, total_ref, in_home, aux_home, refs = *refs[:4], refs[4:]
+    home_ref, total_ref, *homes = refs[:5]
+    refs = refs[5:]
     cut = [pl.ds(0, CONV_CH), pl.ds(CONV_CH, VAL)]
     grads = [in_ref.at[:, cut[0]], in_ref.at[:, cut[1]], aux_ref]
-    homes = [in_home.at[:, :, cut[0]], in_home.at[:, :, cut[1]], aux_home]
     (beside_far, beside_own, sums, far, last, back, picked, small, by_plane, by_z, plane_sum,
      send, recv, role_send, role_recv, plane_send, plane_recv, small_send, small_recv, z_send,
      z_recv), refs = refs[:21], refs[21:]
@@ -1490,7 +1686,7 @@
         refs = refs[buffers:]
     plane, trade = Plane(chips), Trade(chips)
     count = plane.count
-    part = x_ref.shape[0] // count
+    part = x_ref.shape[1] // count
     rows = lambda index: pl.ds(pl.multiple_of(index * part, part), part)
     tier = trade.zp * 2 + trade.zl
     tier_device = lambda at: at_device(trade.chip, trade.core, at // 2, at % 2)
@@ -1504,15 +1700,15 @@
     scatter.start()
     reduces[0].start()
     jobs.start()
-    dgain = jnp.zeros((1, x_ref.shape[1]), F32)
+    dgain = jnp.zeros((1, x_ref.shape[2]), F32)
     to_homes = []
-    size = x_ref.shape[0] // PIECES
+    size = x_ref.shape[1] // PIECES
     parts = max(size // part, 1)
     for p in range(PIECES):
         at = scatter.local(p)
-        grad, piece = norm_back(scatter.total(p), x_ref[at, :].astype(F32), gain_ref[0:1, :].astype(F32))
+        grad, piece = norm_back(scatter.total(p), x_ref[trade.zl, at, :].astype(F32), gain_ref[0:1, :].astype(F32))
         dgain = dgain + piece
-        last[at, :] = (grad + grad_ref[at, :]).astype(BF16)
+        last[at, :] = (grad + grad_ref[trade.zl, at, :]).astype(BF16)
         for index in range(p * parts, (p + 1) * parts):
             copy = remote(last.at[rows(index)], back.at[trade.slot], role_send.at[index],
                           role_recv.at[trade.slot], trade.home(index))
@@ -1600,7 +1796,7 @@
 
 
 def final_step(order, partial, x, gain, grad, terms, grads, chips, jobs, number):
-    rows, width = x.shape
+    _, rows, width = x.shape
     small = jax.ShapeDtypeStruct((small_rows(width), LANES), F32)
     vmem = pl.BlockSpec(memory_space=pltpu.VMEM)
     count = 2 * chips
@@ -1608,7 +1804,8 @@
     parted = pltpu.VMEM((count, rows // count, width), BF16)
     hbm = pl.BlockSpec(memory_space=pl.ANY)
     chained = []
-    for a in [(grads[0].shape[0], cols) for cols in (CONV_CH, VAL, LANES)]:
+    pieces = [(grads[0].shape[0], cols) for cols in (CONV_CH, VAL, LANES)]
+    for a in pieces:
         chained.append(pltpu.VMEM(Reduce.result(a, chips), BF16))
         chained += [pltpu.SemaphoreType.DMA((max(9, chips + 1),))] * 4
         chained += Reduce.buffers(a, chips)
@@ -1616,14 +1813,14 @@
     return carry_call(
         functools.partial(final_kernel, chips), jobs, (),
         [pl.BlockSpec(memory_space=pltpu.SMEM)] + [vmem] * 11 + [hbm] * 2,
-        [vmem, vmem] + [hbm] * 2,
+        [vmem, vmem] + [hbm] * 3,
         [
             jax.ShapeDtypeStruct((rows, width), BF16),
             jax.ShapeDtypeStruct(small.shape, F32),
         ]
         + [
-            jax.ShapeDtypeStruct(FromPlane.result(Reduce.result(a.shape, chips), chips), BF16)
-            for a in grads
+            jax.ShapeDtypeStruct(FromPlane.result(Reduce.result(a, chips), chips), BF16)
+            for a in pieces
         ],
         [block] * 5 + [parted] * 2
         + [
@@ -1647,14 +1844,16 @@
 
 
 def weights_out_kernel(small_ref, home_ref, *refs):
-    ins, outs = refs[:12], refs[12:]
+    ins, outs = refs[:14], refs[14:]
     for layer in range(2):
         total = lambda ref: ref[0].astype(F32) + ref[1].astype(F32)
-        proj, aux, out, gate, up, down = (total(ref) for ref in ins[6 * layer : 6 * layer + 6])
-        outs[0][layer] = proj[:, :KEY]
-        outs[1][layer] = proj[:, KEY : 2 * KEY]
-        outs[2][layer] = proj[:, 2 * KEY : CONV_CH]
-        outs[3][layer] = proj[:, CONV_CH:]
+        qkv, head_gate, aux, out, gate, up, down = (
+            total(ref) for ref in ins[7 * layer : 7 * layer + 7]
+        )
+        outs[0][layer] = qkv[:, :KEY]
+        outs[1][layer] = qkv[:, KEY : 2 * KEY]
+        outs[2][layer] = qkv[:, 2 * KEY :]
+        outs[3][layer] = head_gate
         turned = aux.T
         outs[4][layer] = turned[0:2, :]
         outs[14][layer] = turned[2:6, :]
@@ -1678,7 +1877,7 @@
 
 def weights_out(small, home, first, second, heads):
     width = home.shape[1]
-    rows, units = first[0].shape[1], first[5].shape[2]
+    rows, units = first[0].shape[1], first[6].shape[2]
     shapes = [
         (2, rows, KEY), (2, rows, KEY), (2, rows, VAL), (2, rows, VAL), (2, 2, rows), (2, VAL, rows),
         (2, units, rows), (2, units, rows), (2, units, rows),
@@ -1688,7 +1887,7 @@
     vmem = pl.BlockSpec(memory_space=pltpu.VMEM)
     return pl.pallas_call(
         weights_out_kernel,
-        in_specs=[vmem] * 14,
+        in_specs=[vmem] * 16,
         out_specs=[vmem] * 16,
         out_shape=[jax.ShapeDtypeStruct(shape, F32) for shape in shapes],
         compiler_params=pltpu.CompilerParams(vmem_limit_bytes=56 * 1024 * 1024),
@@ -1771,7 +1970,7 @@
         if both:
             own = lax.axis_index("zl") * 2 + lax.axis_index("core")
             outs[4][...] = (
-                mm(hidden, down_ref[...], NT) + jnp.where(at == own, residual_ref[...], 0.0)
+                mm(hidden, down_ref[...], NT) + jnp.where(at == own, residual_ref[lax.axis_index("zl")], 0.0)
             ).astype(BF16)
         dhidden = mm(g, down_ref[...])
         dgate = (dhidden * up * (sig * (1.0 + gate * (1.0 - sig)))).astype(BF16)
@@ -1795,13 +1994,15 @@
     length, width = x.shape
     chunks = length // CHUNK
     units = weights[0].shape[1]
-    assert length == width and (not both or residual.shape[0] == CHUNK)
+    assert length == width and (not both or residual.shape[1] == CHUNK)
     rows = pl.BlockSpec((CHUNK, width), lambda i: (jnp.minimum(i, chunks - 1), 0))
     late = pl.BlockSpec((CHUNK, units), lambda i: (jnp.maximum(i - chunks, 0), 0))
     out = lambda cols: jax.ShapeDtypeStruct((length, cols), BF16)
     return carry_call(
         functools.partial(ffn_backward_kernel, both), jobs, (2 * chunks,),
-        [rows, rows] + [whole(weight.shape) for weight in weights] + [whole((CHUNK, width))] * both,
+        [rows, rows] + [whole(weight.shape) for weight in weights] + [
+            pl.BlockSpec((2, CHUNK, width), lambda i: (0, 0, 0), pipeline_mode=pl.Buffered(1))
+        ] * both,
         [rows] + [late] * 3 + [rows] * both,
         [out(width)] + [out(units)] * 3 + [out(width)] * both,
         [pltpu.VMEM((length, units), BF16)] * 3 + [pltpu.VMEM((length, width), BF16)] * 2,
@@ -1929,7 +2130,7 @@
         positions = (zp * 2 + zl) * rows_local + jnp.arange(rows_local)
         start = cotangent[:, 0, :] * (positions < lengths[order[chip * 2 + core]]).astype(BF16)[:, None]
         residual = lax.ppermute(deal(tokens, order)[:, 0, :], AXES, to_roles)
-        (rows_in,), _ = first_gather(residual, norm_mix, 0, carry(), 1)
+        (residual, rows_in), _ = first_gather(residual, norm_mix, 0, carry(), 1)
         qkv0, side0 = (chip_gather(to_plane(pack, roles)) for pack in (qkv0, side0))
         out_wide, gate_wide = (to_plane(pack, roles) for pack in (out_wide, gate_wide))
 
@@ -1965,7 +2166,7 @@
     )
 
     (gradient, grad_rows, dgain_ffn1, dout1), (dgate1, dup1) = backward_bridge(
-        part, middle1, norm_ffn, 1, gradient, carry((Reduce, dgate1), (Reduce, dup1)), 7, heads1
+        part, middle1, norm_ffn, 1, grad_rows, carry((Reduce, dgate1), (Reduce, dup1)), 7, heads1
     )
     (part, din1, daux1, dgain1, dscalars1), jobs_results = mixer_backward(
         1, grad_rows, rows_in1, qkv1, side1, out1, norm_heads, scalars, kept1,
@@ -1974,12 +2175,15 @@
         8,
     )
     ddown1, dout1, gate_home1, up_home1, mixed = jobs_results
-    (gradient, grad_rows, dgain_mix1), (din1, daux1, mixed) = backward_bridge(
+    (gradient, grad_rows, dgain_mix1), (dqkv1, daux1, mixed) = backward_bridge(
         part, residual1, norm_mix, 1, gradient,
-        carry((Reduce, din1), (Reduce, daux1), (FromRole, mixed)), 9,
-    )
-    (part, dgate0, dup0, ddown0), (in_home1, aux_home1) = ffn_backward(
-        rows_ffn0, grad_rows, ffn0, carry((FromPlane, din1), (FromPlane, daux1)), 14,
+        carry((Reduce, din1, (0, CONV_CH)), (Reduce, daux1), (FromRole, mixed)), 9,
+    )
+    (part, dgate0, dup0, ddown0), (side1, qkv_home1, aux_home1, down_home1) = ffn_backward(
+        rows_ffn0, grad_rows, ffn0,
+        carry((Reduce, din1, (CONV_CH, VAL)), (FromPlane, dqkv1), (FromPlane, daux1),
+              (FromPlane, ddown1)),
+        14,
     )
     (gradient, grad_rows, dgain_ffn0, dout0), (dgate0, dup0) = backward_bridge(
         part, middle0, norm_ffn, 0, gradient, carry((Reduce, dgate0), (Reduce, dup0)), 10, heads0
@@ -1987,10 +2191,10 @@
     (part, din0, daux0, dgain0, dscalars0), jobs_results = mixer_backward(
         0, grad_rows, rows_in0, qkv0, side0, out0, norm_heads, scalars, kept0,
         carry((Reduce, ddown0), (Reduce, dout0), (FromPlane, dgate0), (FromPlane, dup0),
-              (FromPlane, ddown1), (FromPlane, dout1)),
+              (FromPlane, side1), (FromPlane, dout1)),
         11,
     )
-    ddown0, dout0, gate_home0, up_home0, down_home1, out_home1 = jobs_results
+    ddown0, dout0, gate_home0, up_home0, side_home1, out_home1 = jobs_results
     terms = (dgain_mix1, dgain_ffn0, dgain_ffn1, dgain0, dgain1, dscalars0, dscalars1)
     last = (din0, daux0)
     last_jobs = carry((FromPlane, ddown0), (FromPlane, dout0))
@@ -2013,12 +2217,14 @@
         places = jnp.arange(slot_total, dtype=jnp.int32)
         inverse = jnp.sum(jnp.where(order[None, :] == places[:, None], places[None, :], 0), axis=1)
         home = deal(dealt_grad[:, None, :], inverse)[:, 0, :]
-        last = only_jobs(carry(*[(Reduce, a) for a in last]), 13)
+        last = only_jobs(
+            carry((Reduce, din0, (0, CONV_CH)), (Reduce, din0, (CONV_CH, VAL)), (Reduce, daux0)), 13
+        )
         last = only_jobs(carry(*[(FromPlane, a) for a in last]), 15)
     down_home0, out_home0 = results
-    in_home0, aux_home0 = last
-    first = (in_home0, aux_home0, out_home0, gate_home0, up_home0, down_home0)
-    second = (in_home1, aux_home1, out_home1, gate_home1, up_home1, down_home1)
+    qkv_home0, side_home0, aux_home0 = last
+    first = (qkv_home0, side_home0, aux_home0, out_home0, gate_home0, up_home0, down_home0)
+    second = (qkv_home1, side_home1, aux_home1, out_home1, gate_home1, up_home1, down_home1)
     if rows_part % LANES == 0:
         outs = weights_out(flat, home, first, second, heads_total)
     else:
@@ -2027,13 +2233,12 @@
         for size in (width, width, VAL, heads_total, heads_total):
             small.append(flat[at : at + layer_count * size].reshape(layer_count, size))
             at += layer_count * size
-        proj, aux, out, gate, up, down = (
+        qkv, side, aux, out, gate, up, down = (
             jnp.stack([summed(a, F32), summed(b, F32)]) for a, b in zip(first, second)
         )
         turned = lambda a: a.transpose(0, 2, 1)
         outs = [
-            proj[:, :, :KEY], proj[:, :, KEY : 2 * KEY], proj[:, :, 2 * KEY : CONV_CH],
-            proj[:, :, CONV_CH:], turned(aux)[:, :2], turned(out), turned(gate), turned(up),
+            qkv[:, :, :KEY], qkv[:, :, KEY : 2 * KEY], qkv[:, :, 2 * KEY :], side, turned(aux)[:, :2], turned(out), turned(gate), turned(up),
             turned(down), *small, turned(aux)[:, 2:6], home.astype(F32)[:, None, :],
         ]
     return (

time: 587 us -> 583 us (level)
  no operation moved by 1% of the time
where the time goes in v6:
time: 583 us; the launch traced here: 576 us
  Pallas kernels  574 us (98%)
    pallas_call x15, Pallas kernels, carry_call(): pl.pallas_call(carrying(body, jobs, len(args), outs), grid=grid, in_specs...  569 us

profile of v6, /device:TPU:0, one launch (start us, length us, event | category | flops | bytes accessed | tf_op | source)
XLA Modules:
  0.0 576.4 jit_solution(11602586801662501616)
XLA Ops:
  0.7 58.7 %deal_and_gather.1 = (bf16[2,256,1024]{2,1,0:T(8,128)(2,1)}, bf16[1024,1024]{1,0:T(8,128)(2,1)}, bf16[256,1024]{1,0:T(8,128)(2,1)}, bf16[128,1024]{1,0:T(8,128)(...) custom-call(s32[8]{0:T(128)} %refs_0_.11, ...), custom_call_target="tpu_custom_call" | custom-call | flops 5242880 | bytes 83886080 | tf_op jit(solution)/shard_map/deal_and_gather/pallas_call | solution.py:1379
  59.4 42.1 %mixer_forward.2 = (bf16[1024,512]{1,0:T(8,128)(2,1)}, f32[1024,1024]{1,0:T(8,128)}, f32[1024,1024]{1,0:T(8,128)}, f32[1024,512]{1,0:T(8,128)}, f32[1024,128]{1,...) custom-call(bf16[2,4]{1,0:T(2,128)(2,1)} %refs_0_.10, ...), custom_call_target="tpu_custom_call" | custom-call | flops 16000000000 | bytes 83886080 | tf_op jit(solution)/shard_map/mixer_forward/pallas_call | solution.py:1379
  101.5 45.3 %mixer_bridge.2 = (f32[2,256,1024]{2,1,0:T(8,128)}, bf16[1024,1024]{1,0:T(8,128)(2,1)}, bf16[1024,704]{1,0:T(8,128)(2,1)}, bf16[1024,704]{1,0:T(8,128)(2,1)}, bf...) custom-call(bf16[1024,512]{1,0:T(8,128)(2,1)} %get-tuple-element.159.refs_0_.refs_4_, ...), custom_call_target="tpu_custom_call" | custom-call | flops 1000000000 | bytes 83886080 | tf_op jit(solution)/shard_map/mixer_bridge/pallas_call | solution.py:1379
  146.8 9.0 %ffn_forward.1.refs_0_ = bf16[1024,1024]{1,0:T(8,128)(2,1)} custom-call(bf16[1024,1024]{1,0:T(8,128)(2,1)} %get-tuple-element.166.refs_0_, bf16[1024,704]{1,0:T(8,128)(2,1)} %get-tuple-element.167.refs_1_.refs_2_, bf16[1024,704]{1,0:T(8,128)(2,1)} %get-tuple-element.168.refs_2_.refs_3_, bf16[1024,704]{1,0:T(8,128)(2,1)} %get-tuple-element.169.refs_3_.refs_4_), custom_call_target="tpu_custom_call" | custom-call | flops 4000000000 | bytes 83886080 | tf_op jit(solution)/shard_map/ffn_forward/pallas_call | solution.py:1379
  155.8 36.8 %forward_bridge.1 = (f32[2,256,1024]{2,1,0:T(8,128)}, bf16[1024,1024]{1,0:T(8,128)(2,1)}, bf16[1024,1024]{1,0:T(8,128)(2,1)}, bf16[1024,640]{1,0:T(8,128)(2,1)},...) custom-call(bf16[1024,1024]{1,0:T(8,128)(2,1)} %ffn_forward.1.refs_0_, f32[2,256,1024]{2,1,0:T(8,128)} %get-tuple-element.170.refs_1_, ...), custom_call_target="tpu_custom_call" | custom-call | flops 5242880 | bytes 83886080 | tf_op jit(solution)/shard_map/forward_bridge/pallas_call | solution.py:1379
  192.7 36.4 %mixer_forward.3 = (bf16[1024,512]{1,0:T(8,128)(2,1)}, f32[1024,1024]{1,0:T(8,128)}, f32[1024,1024]{1,0:T(8,128)}, f32[1024,512]{1,0:T(8,128)}, f32[1024,128]{1,...) custom-call(bf16[2,4]{1,0:T(2,128)(2,1)} %refs_0_.10, ...), custom_call_target="tpu_custom_call" | custom-call | flops 16000000000 | bytes 83886080 | tf_op jit(solution)/shard_map/mixer_forward/pallas_call | solution.py:1379
  229.1 34.1 %mixer_bridge.3 = (f32[2,256,1024]{2,1,0:T(8,128)}, bf16[1024,1024]{1,0:T(8,128)(2,1)}, bf16[1024,704]{1,0:T(8,128)(2,1)}, bf16[1024,704]{1,0:T(8,128)(2,1)}) custom-call(bf16[1024,512]{1,0:T(8,128)(2,1)} %get-tuple-element.183.refs_0_.refs_4_, bf16[1024,512]{1,0:T(8,128)(2,1)} %get-tuple-element.184.refs_1_.refs_4_, ...), custom_call_target="tpu_custom_call" | custom-call | flops 1000000000 | bytes 83886080 | tf_op jit(solution)/shard_map/mixer_bridge/pallas_call | solution.py:1379
  263.2 25.0 %ffn_backward.2 = (bf16[1024,1024]{1,0:T(8,128)(2,1)}, bf16[1024,704]{1,0:T(8,128)(2,1)}, bf16[1024,704]{1,0:T(8,128)(2,1)}, bf16[1024,704]{1,0:T(8,128)(2,1)}, bf16[1024,1024]{1,0:T(8,128)(2,1)}) custom-call(bf16[1024,1024]{1,0:T(8,128)(2,1)} %get-tuple-element.188.refs_0_, bf16[1024,1024]{1,0:T(8,128)(2,1)} %get-tuple-element.189.refs_1_.refs_3_, ...), custom_call_target="tpu_custom_call" | custom-call | flops 12000000000 | bytes 83886080 | tf_op jit(solution)/shard_map/ffn_backward/pallas_call | solution.py:1379
  288.2 33.9 %backward_bridge.3 = (f32[2,256,1024]{2,1,0:T(8,128)}, bf16[1024,1024]{1,0:T(8,128)(2,1)}, f32[1,1024]{1,0:T(1,128)}, bf16[1024,512]{1,0:T(8,128)(2,1)}, bf16[25...) custom-call(bf16[1024,1024]{1,0:T(8,128)(2,1)} %get-tuple-element.194.refs_0_, ...), custom_call_target="tpu_custom_call" | custom-call | flops 5242880 | bytes 83886080 | tf_op jit(solution)/shard_map/backward_bridge/pallas_call | solution.py:1379
  322.1 41.1 %mixer_backward.2 = (bf16[1024,1024]{1,0:T(8,128)(2,1)}, bf16[1024,1536]{1,0:T(8,128)(2,1)}, bf16[1024,128]{1,0:T(8,128)(2,1)}, f32[1,512]{1,0:T(1,128)}, f32[8,...) custom-call(bf16[2,4]{1,0:T(2,128)(2,1)} %refs_0_.10, ...), custom_call_target="tpu_custom_call" | custom-call | flops 16000000000 | bytes 83886080 | tf_op jit(solution)/shard_map/mixer_backward/pallas_call | solution.py:1379
  363.3 38.9 %backward_bridge.4 = (f32[2,256,1024]{2,1,0:T(8,128)}, bf16[1024,1024]{1,0:T(8,128)(2,1)}, f32[1,1024]{1,0:T(1,128)}, bf16[256,1024]{1,0:T(8,128)(2,1)}, bf16[25...) custom-call(bf16[1024,1024]{1,0:T(8,128)(2,1)} %get-tuple-element.211.refs_0_, ...), custom_call_target="tpu_custom_call" | custom-call | flops 5242880 | bytes 83886080 | tf_op jit(solution)/shard_map/backward_bridge/pallas_call | solution.py:1379
  402.1 25.6 %ffn_backward.3 = (bf16[1024,1024]{1,0:T(8,128)(2,1)}, bf16[1024,704]{1,0:T(8,128)(2,1)}, bf16[1024,704]{1,0:T(8,128)(2,1)}, bf16[1024,704]{1,0:T(8,128)(2,1)}, ...) custom-call(bf16[1024,1024]{1,0:T(8,128)(2,1)} %get-tuple-element.16, ...), custom_call_target="tpu_custom_call" | custom-call | flops 12000000000 | bytes 83886080 | tf_op jit(solution)/shard_map/ffn_backward/pallas_call | solution.py:1379
  427.8 36.7 %backward_bridge.5 = (f32[2,256,1024]{2,1,0:T(8,128)}, bf16[1024,1024]{1,0:T(8,128)(2,1)}, f32[1,1024]{1,0:T(1,128)}, bf16[1024,512]{1,0:T(8,128)(2,1)}, bf16[25...) custom-call(bf16[1024,1024]{1,0:T(8,128)(2,1)} %get-tuple-element.221.refs_0_, f32[2,256,1024]{2,1,0:T(8,128)} %get-tuple-element.170.refs_1_, ...), custom_call_target="tpu_custom_call" | custom-call | flops 5242880 | bytes 83886080 | tf_op jit(solution)/shard_map/backward_bridge/pallas_call | solution.py:1379
  464.5 39.0 %mixer_backward.3 = (bf16[1024,1024]{1,0:T(8,128)(2,1)}, bf16[1024,1536]{1,0:T(8,128)(2,1)}, bf16[1024,128]{1,0:T(8,128)(2,1)}, f32[1,512]{1,0:T(1,128)}, f32[8,...) custom-call(bf16[2,4]{1,0:T(2,128)(2,1)} %refs_0_.10, ...), custom_call_target="tpu_custom_call" | custom-call | flops 16000000000 | bytes 83886080 | tf_op jit(solution)/shard_map/mixer_backward/pallas_call | solution.py:1379
  503.5 66.2 %final_step.1 = (bf16[256,1024]{1,0:T(8,128)(2,1)}, f32[48,128]{1,0:T(8,128)}, bf16[2,128,1024]{2,1,0:T(8,128)(2,1)}, bf16[2,128,512]{2,1,0:T(8,128)(2,1)}, bf16...) custom-call(s32[8]{0:T(128)} %refs_0_.11, ...), custom_call_target="tpu_custom_call" | custom-call | flops 5242880 | bytes 83886080 | tf_op jit(solution)/shard_map/final_step/pallas_call | solution.py:1379
  569.7 0.0 copy-start
  569.7 5.5 weights_out.1
  575.2 0.0 copy-done
  575.2 0.8 copy.39
Async XLA Ops:
  569.7 5.5 copy-start

commit v7 on v6

--- a/solution.py
+++ b/solution.py
@@ -113,23 +113,32 @@
 
 
 def forward_kernel(
-    layer, jobs, rate_ref, bias_ref, x_ref, w_qkv_ref, w_gate_ref, w_aux_ref, gain_ref,
+    layer, jobs, rate_ref, bias_ref, x_ref, qkv_hbm, side_hbm, gain_ref,
     heads_ref, proj_ref, conv_ref, gate_ref, rates_ref, inverse_ref, fresh_ref, o_ref, state_ref,
-    padded, memory, taps_ref,
+    padded, memory, taps_ref, w_qkv_ref, w_side_ref, sems,
 ):
+    at = pl.program_id(0)
+    held = Held(at, (qkv_hbm, side_hbm), (w_qkv_ref, w_side_ref), sems)
+    held.start()
     begin_jobs(jobs, pl.program_id(0), pl.num_programs(0))
     @pl.when(pl.program_id(0) == 0)
     def _():
         memory[...] = jnp.zeros_like(memory)
-        taps_ref[...] = w_aux_ref[...].astype(F32).T[2:6, :]
         padded[0:8, :] = jnp.zeros((8, CONV_CH), F32)
 
     x = x_ref[...]
-    rates = mm(x, w_aux_ref[...])
+    held.ready(0)
+    qkv = mm(x, w_qkv_ref[...])
+    held.ready(1)
+
+    @pl.when(at == 0)
+    def _():
+        taps_ref[...] = w_side_ref[:, VAL:].astype(F32).T[2:6, :]
+
+    rates = mm(x, w_side_ref[:, VAL:])
     rates_ref[...] = rates
-    qkv = mm(x, w_qkv_ref[...])
     proj_ref[...] = qkv
-    gate_in = mm(x, w_gate_ref[...])
+    gate_in = mm(x, w_side_ref[:, :VAL])
     gate_ref[...] = gate_in
     padded[8 : 8 + CHUNK, :] = qkv
     conv = conv_rows(padded, taps_ref, 5)
@@ -165,16 +174,6 @@
     return pl.BlockSpec(value.shape, lambda i: (0, 0))
 
 
-def weight_specs(width):
-    fixed = lambda shape, at: pl.BlockSpec(shape, lambda i: (0, at), pipeline_mode=pl.Buffered(1))
-    return [
-        fixed((width, CONV_CH), 0),
-        fixed((width, VAL), 0),
-        fixed((width, LANES), VAL // LANES),
-        fixed((2, VAL), 0),
-    ]
-
-
 def mixer_forward(layer, x, qkv, pack, gain, scalars, jobs, number):
     length, width = x.shape
     chunks = length // CHUNK
@@ -182,7 +181,7 @@
     out = lambda cols, kind: jax.ShapeDtypeStruct((length, cols), kind)
     return carry_call(
         functools.partial(forward_kernel, layer), jobs, (chunks,),
-        [head_spec(scalars[0]), head_spec(scalars[1]), row(width)] + weight_specs(width),
+        [head_spec(scalars[0]), head_spec(scalars[1]), row(width), ANY_SPEC, ANY_SPEC, head_spec(gain)],
         [
             row(VAL), row(CONV_CH), row(CONV_CH), row(VAL), row(LANES), row(CHUNK), row(VAL), row(VAL),
             pl.BlockSpec((None, KEY, VAL), lambda i: (i, 0, 0)),
@@ -195,8 +194,8 @@
         [
             pltpu.VMEM((CHUNK + 8, CONV_CH), F32), pltpu.VMEM((KEY, VAL), F32),
             pltpu.VMEM((4, CONV_CH), F32),
-        ],
-        (*scalars, x, qkv, pack, pack, gain), number, "mixer_forward", 16 * 10**9,
+        ] + held_scratch((qkv, pack)),
+        (*scalars, x, qkv, pack, gain), number, "mixer_forward", 16 * 10**9,
     )
 
 
@@ -207,20 +206,22 @@
 
 
 def backward_kernel(
-    layer, jobs, rate_ref, bias_ref, g_ref, x_ref, w_out_ref, w_qkv_ref, w_gate_ref, w_aux_ref, gain_ref,
+    layer, jobs, rate_ref, bias_ref, g_ref, x_ref, out_hbm, qkv_hbm, side_hbm, gain_ref,
     proj_ref, halo_ref, conv_ref, gate_ref, rates_ref, inverse_ref, fresh_ref, o_ref, state_ref,
     part_ref, din_ref, daux_ref, dgain_ref, dscalars_ref,
     padded, dpadded, dmemory, taps_ref, dtaps_ref, daux_sum, x_held, dproj_ref,
+    w_out_ref, w_qkv_ref, w_side_ref, sems,
 ):
     at, steps = pl.program_id(0), pl.num_programs(0)
     chunks = steps // 2
     last = chunks - 1
+    held = Held(at, (out_hbm, qkv_hbm, side_hbm), (w_out_ref, w_qkv_ref, w_side_ref), sems)
+    held.start()
     begin_jobs(jobs, at, steps, (chunks // 2, chunks - 1))
 
     @pl.when(at == 0)
     def _():
         dmemory[...] = jnp.zeros_like(dmemory)
-        taps_ref[...] = w_aux_ref[...].astype(F32).T[2:6, :]
         dpadded[CHUNK : CHUNK + 8, :] = jnp.zeros((8, CONV_CH), F32)
         dtaps_ref[...] = jnp.zeros_like(dtaps_ref)
         daux_sum[...] = jnp.zeros_like(daux_sum)
@@ -247,6 +248,7 @@
         strict_decay = jnp.where(below, decay, 0.0)
         keys = mm(low_k, low_k, NT) * strict_decay * wide(write, CHUNK)
         within = mm(low_q, low_k, NT) * decay
+        held.ready(0)
         dheads = mm(g_ref[...], w_out_ref[...])
         o = o_ref[...]
         gate_in = gate_ref[...]
@@ -321,6 +323,13 @@
             ],
             axis=0,
         )
+        held.ready(1)
+        held.ready(2)
+
+        @pl.when(at == 0)
+        def _():
+            taps_ref[...] = w_side_ref[:, VAL:].astype(F32).T[2:6, :]
+
         dqkv = dconv * taps_ref[3:4, :]
         for j in range(3):
             dqkv = dqkv + dpadded[pl.ds(3 - j, CHUNK), :] * taps_ref[j : j + 1, :]
@@ -332,8 +341,8 @@
         x_held[place, :] = x_ref[...]
         part_ref[...] = (
             mm(low_dqkv, w_qkv_ref[...], NT)
-            + mm(low_dgate, w_gate_ref[...], NT)
-            + mm(low_drates, w_aux_ref[...], NT)
+            + mm(low_dgate, w_side_ref[:, :VAL], NT)
+            + mm(low_drates, w_side_ref[:, VAL:], NT)
         ).astype(BF16)
 
     @pl.when(at == last)
@@ -359,8 +368,8 @@
     steps = CHUNK // 8
     return carry_call(
         functools.partial(backward_kernel, layer), jobs, (2 * chunks,),
-        [head_spec(scalars[0]), head_spec(scalars[1]), row(width), row(width), whole(w_out.shape)]
-        + weight_specs(width) + [
+        [head_spec(scalars[0]), head_spec(scalars[1]), row(width), row(width)]
+        + [ANY_SPEC] * 3 + [head_spec(gain),
             row(CONV_CH),
             pl.BlockSpec((8, CONV_CH), lambda i: (jnp.maximum(at(i) * steps - 1, 0), 0)),
             row(CONV_CH), row(VAL), row(LANES), row(CHUNK), row(VAL), row(VAL),
@@ -388,8 +397,8 @@
             pltpu.VMEM((LANES, width), F32),
             pltpu.VMEM((length, width), BF16),
             pltpu.VMEM((length, CONV_CH + VAL), BF16),
-        ],
-        (*scalars, g, x, w_out, qkv, pack, pack, gain, proj, proj, conv, gate_in, rates, inverse, fresh, o,
+        ] + held_scratch((w_out, qkv, pack)),
+        (*scalars, g, x, w_out, qkv, pack, gain, proj, proj, conv, gate_in, rates, inverse, fresh, o,
          states),
         number, "mixer_backward", 16 * 10**9,
     )
@@ -426,8 +435,9 @@
 
 
 class Scatter:
-    def __init__(self, partial, beside_far, beside_own, sums, far, send, recv):
+    def __init__(self, partial, beside_far, beside_own, sums, far, send, recv, held=None):
         core, zl, beside, across = partners()
+        self.held = held
         rows = far.shape[0]
         self.partial, self.beside_far, self.beside_own = partial, beside_far, beside_own
         self.sums, self.far = sums, far
@@ -454,6 +464,22 @@
     def local(self, p):
         return pl.ds(p * self.size, self.size)
 
+    def load(self):
+        away, own, sems = self.held
+        self.loads = [
+            pltpu.make_async_copy(self.partial.at[block.rows()], ref, sems.at[at])
+            for at, (block, ref) in enumerate(((self.away, away), (self.own, own)))
+        ]
+        for copy in self.loads:
+            copy.start()
+
+    def mine(self, which, p):
+        if self.held is None:
+            return self.partial[(self.away, self.own)[which].piece(p), :]
+        if p == 0:
+            self.loads[which].wait()
+        return self.held[which][self.local(p), :]
+
     def start(self):
         for copy in self.to_far:
             copy.start()
@@ -463,7 +489,7 @@
             self.to_far[p].wait_recv()
             at = self.local(p)
             self.sums[at, :] = (
-                self.partial[self.away.piece(p), :].astype(F32) + self.beside_far[at, :].astype(F32)
+                self.mine(0, p).astype(F32) + self.beside_far[at, :].astype(F32)
             ).astype(BF16)
             self.cross[p].start()
 
@@ -472,7 +498,7 @@
         self.cross[p].wait_recv()
         at = self.local(p)
         return (
-            self.partial[self.own.piece(p), :].astype(F32)
+            self.mine(1, p).astype(F32)
             + self.beside_own[at, :].astype(F32)
             + self.far[at, :].astype(F32)
         )
@@ -1501,13 +1527,20 @@
     raw, refs = refs[:10], refs[10:]
     (new_ref, out_ref, start_ref, qkv_next, side_next, out_next, gate_next, up_ref, up_next, down_ref,
      down_next, first_full, second_full, first_wide, second_wide, third_wide, fourth_wide) = refs[:17]
-    (spread, picked, square, first, second, third, fourth, held_first, held_second, held, send, recv, stores,
-     cross_send, cross_recv,
+    (spread, picked, square, first, second, third, fourth, held_first, held_other, held_second, held, send, recv,
+     stores,     cross_send, cross_recv,
      plane_send, plane_recv, role_send, role_recv, *sems) = refs[17:]
     raw = Raw(raw, square)
     plane, trade = Plane(chips), Trade(chips)
-    first_column = ToPlane(first, first_wide, sems[0], sems[1], chips)
-    first_across = Spread(first_wide, first_full, sems[2], sems[3], chips, [held_first])
+    half = CONV_CH // 2
+    halves = []
+    for at, (own, four) in enumerate(((held_first, sems[0:4]), (held_other, sems[12:16]))):
+        cut = pl.ds(at * half, half)
+        wide = first_wide.at[:, cut]
+        halves.append(
+            (ToPlane(first.at[:, cut], wide, four[0], four[1], chips),
+             Spread(wide, first_full.at[:, cut], four[2], four[3], chips, [own]))
+        )
     second_column = ToPlane(second, second_wide, sems[4], sems[5], chips)
     second_across = Spread(second_wide, second_full, sems[6], sems[7], chips, [held_second])
     third_column = ToPlane(third, third_wide, sems[8], sems[9], chips)
@@ -1518,7 +1551,7 @@
     part = x_ref.shape[0] // count
     rows = lambda index: pl.ds(pl.multiple_of(index * part, part), part)
     expected = plane.greet() + trade.greet_homes() + greet_group()
-    for job in (first_column, first_across, second_column, second_across, third_column, fourth_column):
+    for job in (*halves[0], *halves[1], second_column, second_across, third_column, fourth_column):
         expected = expected + job.greet()
     raw.qkv(0, first)
     raw.side(0, second)
@@ -1536,10 +1569,13 @@
         )
     for copy in outward:
         copy.start()
-    first_column.start()
+    for column, _ in halves:
+        column.start()
     spread[plane.own] = x_ref[rows(plane.own), :]
     for copy in inward:
         copy.wait_recv()
+    halves[0][0].finish()
+    halves[0][1].start()
     to_roles = []
     for slot in range(count):
         picked[slot] = spread[order_ref[slot]]
@@ -1556,8 +1592,8 @@
     second_column.start()
     raw.turn(raw.out[0], third)
     raw.turn(raw.ffn_gate[0], fourth)
-    first_column.finish()
-    first_across.start()
+    halves[1][0].finish()
+    halves[1][1].start()
     size = x_ref.shape[0] // PIECES
     parts = max(size // part, 1)
     swaps = []
@@ -1583,7 +1619,8 @@
     second_across.start()
     third_column.start()
     fourth_column.start()
-    first_across.middle()
+    for _, across_chips in halves:
+        across_chips.middle()
     for swap in swaps:
         swap.wait_recv()
     for l in range(2):
@@ -1609,7 +1646,8 @@
     sharing.arrive()
     sharing.finish()
     second_across.middle()
-    first_across.finish()
+    for _, across_chips in halves:
+        across_chips.finish()
     second_across.finish()
     third_column.finish()
     fourth_column.finish()
@@ -1629,7 +1667,8 @@
     spread = [(2 * chips * part, qkv), (2 * chips * part, side)]
     moved = [(2 * part, cols) for cols in (qkv, side, VAL, units)]
     shapes = [(2, rows, width), (4 * rows, width), (rows, width)] + held + spread + moved
-    own = [(part, qkv), (part, side), (part, VAL), (part, units), moved[0], moved[1]]
+    halved = (2 * part, qkv // 2)
+    own = [(part, qkv), (part, side), (part, VAL), (part, units), halved, halved, moved[1]]
     return carry_call(
         functools.partial(deal_kernel, chips), Jobs([], chips), (),
         [smem, smem] + [vmem] * 13,
@@ -1639,7 +1678,7 @@
         + [pltpu.VMEM(shape, BF16) for shape in own]
         + [pltpu.VMEM((4 * rows, width), BF16)] + sems(2, PIECES) + [pltpu.SemaphoreType.DMA((4,))]
         + sems(PIECES) + sems(count) + sems(count)
-        + [pltpu.SemaphoreType.DMA((max(9, chips + 1),))] * 12,
+        + [pltpu.SemaphoreType.DMA((max(9, chips + 1),))] * 16,
         (order, lengths, x, gain, cotangent, *raw), number, "deal_and_gather", rows * width * 20,
     )[0]
 
@@ -1666,7 +1705,7 @@
 
 
 def final_kernel(
-    chips, jobs, order_ref, partial, x_ref, gain_ref, grad_ref, *refs
+    chips, jobs, order_ref, partial, x_hbm, gain_ref, grad_hbm, *refs
 ):
     terms, refs = refs[:7], refs[7:]
     (in_ref, aux_ref), refs = refs[:2], refs[2:]
@@ -1674,9 +1713,10 @@
     refs = refs[5:]
     cut = [pl.ds(0, CONV_CH), pl.ds(CONV_CH, VAL)]
     grads = [in_ref.at[:, cut[0]], in_ref.at[:, cut[1]], aux_ref]
-    (beside_far, beside_own, sums, far, last, back, picked, small, by_plane, by_z, plane_sum,
+    (away_held, own_held, x_ref, grad_ref, loads, beside_far, beside_own, sums, far, last, back,
+     picked, small, by_plane, by_z, plane_sum,
      send, recv, role_send, role_recv, plane_send, plane_recv, small_send, small_recv, z_send,
-     z_recv), refs = refs[:21], refs[21:]
+     z_recv), refs = refs[:26], refs[26:]
     reduces, returns = [], []
     for at in range(3):
         summed, four, refs = refs[0], refs[1:5], refs[5:]
@@ -1685,8 +1725,17 @@
         returns.append(FromPlane(summed, homes[at], four[2], four[3], chips))
         refs = refs[buffers:]
     plane, trade = Plane(chips), Trade(chips)
+    scatter = Scatter(
+        partial, beside_far, beside_own, sums, far, send, recv, (away_held, own_held, loads)
+    )
+    scatter.load()
+    rows_in = [
+        pltpu.make_async_copy(x_hbm.at[trade.zl], x_ref, loads.at[2]),
+        pltpu.make_async_copy(grad_hbm.at[trade.zl], grad_ref, loads.at[3]),
+    ]
+    load_all(rows_in)
     count = plane.count
-    part = x_ref.shape[1] // count
+    part = x_ref.shape[0] // count
     rows = lambda index: pl.ds(pl.multiple_of(index * part, part), part)
     tier = trade.zp * 2 + trade.zl
     tier_device = lambda at: at_device(trade.chip, trade.core, at // 2, at % 2)
@@ -1696,19 +1745,20 @@
     for job in reduces + returns:
         expected = expected + job.greet()
     wait_greetings(expected)
-    scatter = Scatter(partial, beside_far, beside_own, sums, far, send, recv)
     scatter.start()
     reduces[0].start()
     jobs.start()
-    dgain = jnp.zeros((1, x_ref.shape[2]), F32)
+    dgain = jnp.zeros((1, x_ref.shape[1]), F32)
+    for copy in rows_in:
+        copy.wait()
     to_homes = []
-    size = x_ref.shape[1] // PIECES
+    size = x_ref.shape[0] // PIECES
     parts = max(size // part, 1)
     for p in range(PIECES):
         at = scatter.local(p)
-        grad, piece = norm_back(scatter.total(p), x_ref[trade.zl, at, :].astype(F32), gain_ref[0:1, :].astype(F32))
+        grad, piece = norm_back(scatter.total(p), x_ref[at, :].astype(F32), gain_ref[0:1, :].astype(F32))
         dgain = dgain + piece
-        last[at, :] = (grad + grad_ref[trade.zl, at, :]).astype(BF16)
+        last[at, :] = (grad + grad_ref[at, :]).astype(BF16)
         for index in range(p * parts, (p + 1) * parts):
             copy = remote(last.at[rows(index)], back.at[trade.slot], role_send.at[index],
                           role_recv.at[trade.slot], trade.home(index))
@@ -1812,7 +1862,7 @@
     sems = lambda *shape: [pltpu.SemaphoreType.DMA(shape), pltpu.SemaphoreType.DMA(shape)]
     return carry_call(
         functools.partial(final_kernel, chips), jobs, (),
-        [pl.BlockSpec(memory_space=pltpu.SMEM)] + [vmem] * 11 + [hbm] * 2,
+        [pl.BlockSpec(memory_space=pltpu.SMEM), hbm, hbm, vmem, hbm] + [vmem] * 7 + [hbm] * 2,
         [vmem, vmem] + [hbm] * 3,
         [
             jax.ShapeDtypeStruct((rows, width), BF16),
@@ -1822,7 +1872,8 @@
             jax.ShapeDtypeStruct(FromPlane.result(Reduce.result(a, chips), chips), BF16)
             for a in pieces
         ],
-        [block] * 5 + [parted] * 2
+        [block] * 2 + [pltpu.VMEM((rows, width), x.dtype), pltpu.VMEM((rows, width), F32)]
+        + [pltpu.SemaphoreType.DMA((4,))] + [block] * 5 + [parted] * 2
         + [
             pltpu.VMEM(small.shape, F32), pltpu.VMEM((count,) + small.shape, F32),
             pltpu.VMEM((4,) + small.shape, F32), pltpu.VMEM(small.shape, F32),
@@ -2008,6 +2059,30 @@
         [pltpu.VMEM((length, units), BF16)] * 3 + [pltpu.VMEM((length, width), BF16)] * 2,
         (x, g, *weights) + ((residual,) if both else ()), number, "ffn_backward", 12 * 10**9,
     )
+
+
+class Held:
+    def __init__(self, at, sources, held, sems):
+        self.at = at
+        self.copies = [
+            pltpu.make_async_copy(source, ref, sems.at[index])
+            for index, (source, ref) in enumerate(zip(sources, held))
+        ]
+
+    def start(self):
+        @pl.when(self.at == 0)
+        def _():
+            for copy in self.copies:
+                copy.start()
+
+    def ready(self, index):
+        pl.when(self.at == 0)(self.copies[index].wait)
+
+
+def held_scratch(weights):
+    return [pltpu.VMEM(weight.shape, BF16) for weight in weights] + [
+        pltpu.SemaphoreType.DMA((len(weights),))
+    ]
 
 
 def row_major(x):
@@ -2186,7 +2261,8 @@
         14,
     )
     (gradient, grad_rows, dgain_ffn0, dout0), (dgate0, dup0) = backward_bridge(
-        part, middle0, norm_ffn, 0, gradient, carry((Reduce, dgate0), (Reduce, dup0)), 10, heads0
+        part, middle0, norm_ffn, 0, gradient,
+        carry((Reduce, dgate0), (Reduce, dup0)), 10, heads0,
     )
     (part, din0, daux0, dgain0, dscalars0), jobs_results = mixer_backward(
         0, grad_rows, rows_in0, qkv0, side0, out0, norm_heads, scalars, kept0,

time: 583 us -> 579 us (level)
  no operation moved by 1% of the time
where the time goes in v7:
time: 579 us; the launch traced here: 572 us
  Pallas kernels  570 us (98%)
    pallas_call x15, Pallas kernels, carry_call(): pl.pallas_call(carrying(body, jobs, len(args), outs), grid=grid, in_specs...  564 us

profile of v7, /device:TPU:0, one launch (start us, length us, event | category | flops | bytes accessed | tf_op | source)
XLA Modules:
  0.0 571.9 jit_solution(10248153584375466028)
XLA Ops:
  0.7 61.8 %deal_and_gather.1 = (bf16[2,256,1024]{2,1,0:T(8,128)(2,1)}, bf16[1024,1024]{1,0:T(8,128)(2,1)}, bf16[256,1024]{1,0:T(8,128)(2,1)}, bf16[128,1024]{1,0:T(8,128)(...) custom-call(s32[8]{0:T(128)} %refs_0_.11, ...), custom_call_target="tpu_custom_call" | custom-call | flops 5242880 | bytes 83886080 | tf_op jit(solution)/shard_map/deal_and_gather/pallas_call | solution.py:1405
  62.5 38.9 %mixer_forward.2 = (bf16[1024,512]{1,0:T(8,128)(2,1)}, f32[1024,1024]{1,0:T(8,128)}, f32[1024,1024]{1,0:T(8,128)}, f32[1024,512]{1,0:T(8,128)}, f32[1024,128]{1,...) custom-call(bf16[2,4]{1,0:T(2,128)(2,1)} %refs_0_.10, ...), custom_call_target="tpu_custom_call" | custom-call | flops 16000000000 | bytes 83886080 | tf_op jit(solution)/shard_map/mixer_forward/pallas_call | solution.py:1405
  101.4 43.6 %mixer_bridge.2 = (f32[2,256,1024]{2,1,0:T(8,128)}, bf16[1024,1024]{1,0:T(8,128)(2,1)}, bf16[1024,704]{1,0:T(8,128)(2,1)}, bf16[1024,704]{1,0:T(8,128)(2,1)}, bf...) custom-call(bf16[1024,512]{1,0:T(8,128)(2,1)} %get-tuple-element.159.refs_0_.refs_4_, ...), custom_call_target="tpu_custom_call" | custom-call | flops 1000000000 | bytes 83886080 | tf_op jit(solution)/shard_map/mixer_bridge/pallas_call | solution.py:1405
  145.1 9.0 %ffn_forward.1.refs_0_ = bf16[1024,1024]{1,0:T(8,128)(2,1)} custom-call(bf16[1024,1024]{1,0:T(8,128)(2,1)} %get-tuple-element.166.refs_0_, bf16[1024,704]{1,0:T(8,128)(2,1)} %get-tuple-element.167.refs_1_.refs_2_, bf16[1024,704]{1,0:T(8,128)(2,1)} %get-tuple-element.168.refs_2_.refs_3_, bf16[1024,704]{1,0:T(8,128)(2,1)} %get-tuple-element.169.refs_3_.refs_4_), custom_call_target="tpu_custom_call" | custom-call | flops 4000000000 | bytes 83886080 | tf_op jit(solution)/shard_map/ffn_forward/pallas_call | solution.py:1405
  154.1 36.8 %forward_bridge.1 = (f32[2,256,1024]{2,1,0:T(8,128)}, bf16[1024,1024]{1,0:T(8,128)(2,1)}, bf16[1024,1024]{1,0:T(8,128)(2,1)}, bf16[1024,640]{1,0:T(8,128)(2,1)},...) custom-call(bf16[1024,1024]{1,0:T(8,128)(2,1)} %ffn_forward.1.refs_0_, f32[2,256,1024]{2,1,0:T(8,128)} %get-tuple-element.170.refs_1_, ...), custom_call_target="tpu_custom_call" | custom-call | flops 5242880 | bytes 83886080 | tf_op jit(solution)/shard_map/forward_bridge/pallas_call | solution.py:1405
  190.9 37.2 %mixer_forward.3 = (bf16[1024,512]{1,0:T(8,128)(2,1)}, f32[1024,1024]{1,0:T(8,128)}, f32[1024,1024]{1,0:T(8,128)}, f32[1024,512]{1,0:T(8,128)}, f32[1024,128]{1,...) custom-call(bf16[2,4]{1,0:T(2,128)(2,1)} %refs_0_.10, ...), custom_call_target="tpu_custom_call" | custom-call | flops 16000000000 | bytes 83886080 | tf_op jit(solution)/shard_map/mixer_forward/pallas_call | solution.py:1405
  228.1 34.0 %mixer_bridge.3 = (f32[2,256,1024]{2,1,0:T(8,128)}, bf16[1024,1024]{1,0:T(8,128)(2,1)}, bf16[1024,704]{1,0:T(8,128)(2,1)}, bf16[1024,704]{1,0:T(8,128)(2,1)}) custom-call(bf16[1024,512]{1,0:T(8,128)(2,1)} %get-tuple-element.183.refs_0_.refs_4_, bf16[1024,512]{1,0:T(8,128)(2,1)} %get-tuple-element.184.refs_1_.refs_4_, ...), custom_call_target="tpu_custom_call" | custom-call | flops 1000000000 | bytes 83886080 | tf_op jit(solution)/shard_map/mixer_bridge/pallas_call | solution.py:1405
  262.1 25.0 %ffn_backward.2 = (bf16[1024,1024]{1,0:T(8,128)(2,1)}, bf16[1024,704]{1,0:T(8,128)(2,1)}, bf16[1024,704]{1,0:T(8,128)(2,1)}, bf16[1024,704]{1,0:T(8,128)(2,1)}, bf16[1024,1024]{1,0:T(8,128)(2,1)}) custom-call(bf16[1024,1024]{1,0:T(8,128)(2,1)} %get-tuple-element.188.refs_0_, bf16[1024,1024]{1,0:T(8,128)(2,1)} %get-tuple-element.189.refs_1_.refs_3_, ...), custom_call_target="tpu_custom_call" | custom-call | flops 12000000000 | bytes 83886080 | tf_op jit(solution)/shard_map/ffn_backward/pallas_call | solution.py:1405
  287.0 34.0 %backward_bridge.3 = (f32[2,256,1024]{2,1,0:T(8,128)}, bf16[1024,1024]{1,0:T(8,128)(2,1)}, f32[1,1024]{1,0:T(1,128)}, bf16[1024,512]{1,0:T(8,128)(2,1)}, bf16[25...) custom-call(bf16[1024,1024]{1,0:T(8,128)(2,1)} %get-tuple-element.194.refs_0_, ...), custom_call_target="tpu_custom_call" | custom-call | flops 5242880 | bytes 83886080 | tf_op jit(solution)/shard_map/backward_bridge/pallas_call | solution.py:1405
  321.0 40.0 %mixer_backward.2 = (bf16[1024,1024]{1,0:T(8,128)(2,1)}, bf16[1024,1536]{1,0:T(8,128)(2,1)}, bf16[1024,128]{1,0:T(8,128)(2,1)}, f32[1,512]{1,0:T(1,128)}, f32[8,...) custom-call(bf16[2,4]{1,0:T(2,128)(2,1)} %refs_0_.10, ...), custom_call_target="tpu_custom_call" | custom-call | flops 16000000000 | bytes 83886080 | tf_op jit(solution)/shard_map/mixer_backward/pallas_call | solution.py:1405
  361.0 38.0 %backward_bridge.4 = (f32[2,256,1024]{2,1,0:T(8,128)}, bf16[1024,1024]{1,0:T(8,128)(2,1)}, f32[1,1024]{1,0:T(1,128)}, bf16[256,1024]{1,0:T(8,128)(2,1)}, bf16[25...) custom-call(bf16[1024,1024]{1,0:T(8,128)(2,1)} %get-tuple-element.211.refs_0_, ...), custom_call_target="tpu_custom_call" | custom-call | flops 5242880 | bytes 83886080 | tf_op jit(solution)/shard_map/backward_bridge/pallas_call | solution.py:1405
  399.0 26.0 %ffn_backward.3 = (bf16[1024,1024]{1,0:T(8,128)(2,1)}, bf16[1024,704]{1,0:T(8,128)(2,1)}, bf16[1024,704]{1,0:T(8,128)(2,1)}, bf16[1024,704]{1,0:T(8,128)(2,1)}, ...) custom-call(bf16[1024,1024]{1,0:T(8,128)(2,1)} %get-tuple-element.16, ...), custom_call_target="tpu_custom_call" | custom-call | flops 12000000000 | bytes 83886080 | tf_op jit(solution)/shard_map/ffn_backward/pallas_call | solution.py:1405
  425.0 35.8 %backward_bridge.5 = (f32[2,256,1024]{2,1,0:T(8,128)}, bf16[1024,1024]{1,0:T(8,128)(2,1)}, f32[1,1024]{1,0:T(1,128)}, bf16[1024,512]{1,0:T(8,128)(2,1)}, bf16[25...) custom-call(bf16[1024,1024]{1,0:T(8,128)(2,1)} %get-tuple-element.221.refs_0_, f32[2,256,1024]{2,1,0:T(8,128)} %get-tuple-element.170.refs_1_, ...), custom_call_target="tpu_custom_call" | custom-call | flops 5242880 | bytes 83886080 | tf_op jit(solution)/shard_map/backward_bridge/pallas_call | solution.py:1405
  460.7 38.1 %mixer_backward.3 = (bf16[1024,1024]{1,0:T(8,128)(2,1)}, bf16[1024,1536]{1,0:T(8,128)(2,1)}, bf16[1024,128]{1,0:T(8,128)(2,1)}, f32[1,512]{1,0:T(1,128)}, f32[8,...) custom-call(bf16[2,4]{1,0:T(2,128)(2,1)} %refs_0_.10, ...), custom_call_target="tpu_custom_call" | custom-call | flops 16000000000 | bytes 83886080 | tf_op jit(solution)/shard_map/mixer_backward/pallas_call | solution.py:1405
  498.8 66.3 %final_step.1 = (bf16[256,1024]{1,0:T(8,128)(2,1)}, f32[48,128]{1,0:T(8,128)}, bf16[2,128,1024]{2,1,0:T(8,128)(2,1)}, bf16[2,128,512]{2,1,0:T(8,128)(2,1)}, bf16...) custom-call(s32[8]{0:T(128)} %refs_0_.11, ...), custom_call_target="tpu_custom_call" | custom-call | flops 5242880 | bytes 83886080 | tf_op jit(solution)/shard_map/final_step/pallas_call | solution.py:1405
  565.2 0.0 copy-start
  565.2 5.5 weights_out.1
  570.7 0.0 copy-done
  570.7 0.8 copy.39
Async XLA Ops:
  565.2 5.5 copy-start

commit v8 on v7

--- a/solution.py
+++ b/solution.py
@@ -120,7 +120,7 @@
     at = pl.program_id(0)
     held = Held(at, (qkv_hbm, side_hbm), (w_qkv_ref, w_side_ref), sems)
     held.start()
-    begin_jobs(jobs, pl.program_id(0), pl.num_programs(0))
+    begin_jobs(jobs, at, pl.num_programs(0), (pl.num_programs(0) - 1,) * 2)
     @pl.when(pl.program_id(0) == 0)
     def _():
         memory[...] = jnp.zeros_like(memory)
@@ -217,7 +217,7 @@
     last = chunks - 1
     held = Held(at, (out_hbm, qkv_hbm, side_hbm), (w_out_ref, w_qkv_ref, w_side_ref), sems)
     held.start()
-    begin_jobs(jobs, at, steps, (chunks // 2, chunks - 1))
+    begin_jobs(jobs, at, steps, (chunks - 1, chunks // 2))
 
     @pl.when(at == 0)
     def _():
@@ -1746,7 +1746,8 @@
         expected = expected + job.greet()
     wait_greetings(expected)
     scatter.start()
-    reduces[0].start()
+    for job in reduces:
+        job.start()
     jobs.start()
     dgain = jnp.zeros((1, x_ref.shape[1]), F32)
     for copy in rows_in:
@@ -1783,15 +1784,14 @@
     for copy in small_out:
         copy.start()
     by_plane[plane.own] = small[...]
-    reduces[0].middle()
-    reduces[1].start()
-    reduces[2].start()
+    for job in reduces:
+        job.middle()
+    reduces[0].finish()
+    returns[0].start()
     for slot in range(count):
         arrival = remote(last.at[rows(0)], back.at[slot], role_send.at[0], role_recv.at[slot],
                          trade.role(slot))
         unless(trade.role_mine(slot), arrival.wait_recv)
-    reduces[0].finish()
-    returns[0].start()
     outward, inward = [], []
     for j in range(count):
         to, source = plane.to(j), plane.source(j)
@@ -1810,8 +1810,6 @@
             remote(picked.at[j], home_ref.at[rows(source)], plane_send.at[j], plane_recv.at[j],
                    plane.device(source))
         )
-    for job in reduces[1:]:
-        job.middle()
     jobs.middle()
     for reduce, back_home in zip(reduces[1:], returns[1:]):
         reduce.finish()

time: 579 us -> 575 us (level)
  no operation moved by 1% of the time
where the time goes in v8:
time: 575 us; the launch traced here: 569 us
  Pallas kernels  567 us (99%)
    pallas_call x15, Pallas kernels, carry_call(): pl.pallas_call(carrying(body, jobs, len(args), outs), grid=grid, in_specs...  561 us

profile of v8, /device:TPU:0, one launch (start us, length us, event | category | flops | bytes accessed | tf_op | source)
XLA Modules:
  0.0 568.7 jit_solution(11038223581426287124)
XLA Ops:
  0.7 61.8 %deal_and_gather.1 = (bf16[2,256,1024]{2,1,0:T(8,128)(2,1)}, bf16[1024,1024]{1,0:T(8,128)(2,1)}, bf16[256,1024]{1,0:T(8,128)(2,1)}, bf16[128,1024]{1,0:T(8,128)(...) custom-call(s32[8]{0:T(128)} %refs_0_.11, ...), custom_call_target="tpu_custom_call" | custom-call | flops 5242880 | bytes 83886080 | tf_op jit(solution)/shard_map/deal_and_gather/pallas_call | solution.py:1405
  62.5 37.3 %mixer_forward.2 = (bf16[1024,512]{1,0:T(8,128)(2,1)}, f32[1024,1024]{1,0:T(8,128)}, f32[1024,1024]{1,0:T(8,128)}, f32[1024,512]{1,0:T(8,128)}, f32[1024,128]{1,...) custom-call(bf16[2,4]{1,0:T(2,128)(2,1)} %refs_0_.10, ...), custom_call_target="tpu_custom_call" | custom-call | flops 16000000000 | bytes 83886080 | tf_op jit(solution)/shard_map/mixer_forward/pallas_call | solution.py:1405
  99.8 45.3 %mixer_bridge.2 = (f32[2,256,1024]{2,1,0:T(8,128)}, bf16[1024,1024]{1,0:T(8,128)(2,1)}, bf16[1024,704]{1,0:T(8,128)(2,1)}, bf16[1024,704]{1,0:T(8,128)(2,1)}, bf...) custom-call(bf16[1024,512]{1,0:T(8,128)(2,1)} %get-tuple-element.159.refs_0_.refs_4_, ...), custom_call_target="tpu_custom_call" | custom-call | flops 1000000000 | bytes 83886080 | tf_op jit(solution)/shard_map/mixer_bridge/pallas_call | solution.py:1405
  145.1 9.0 %ffn_forward.1.refs_0_ = bf16[1024,1024]{1,0:T(8,128)(2,1)} custom-call(bf16[1024,1024]{1,0:T(8,128)(2,1)} %get-tuple-element.166.refs_0_, bf16[1024,704]{1,0:T(8,128)(2,1)} %get-tuple-element.167.refs_1_.refs_2_, bf16[1024,704]{1,0:T(8,128)(2,1)} %get-tuple-element.168.refs_2_.refs_3_, bf16[1024,704]{1,0:T(8,128)(2,1)} %get-tuple-element.169.refs_3_.refs_4_), custom_call_target="tpu_custom_call" | custom-call | flops 4000000000 | bytes 83886080 | tf_op jit(solution)/shard_map/ffn_forward/pallas_call | solution.py:1405
  154.1 36.8 %forward_bridge.1 = (f32[2,256,1024]{2,1,0:T(8,128)}, bf16[1024,1024]{1,0:T(8,128)(2,1)}, bf16[1024,1024]{1,0:T(8,128)(2,1)}, bf16[1024,640]{1,0:T(8,128)(2,1)},...) custom-call(bf16[1024,1024]{1,0:T(8,128)(2,1)} %ffn_forward.1.refs_0_, f32[2,256,1024]{2,1,0:T(8,128)} %get-tuple-element.170.refs_1_, ...), custom_call_target="tpu_custom_call" | custom-call | flops 5242880 | bytes 83886080 | tf_op jit(solution)/shard_map/forward_bridge/pallas_call | solution.py:1405
  190.9 34.7 %mixer_forward.3 = (bf16[1024,512]{1,0:T(8,128)(2,1)}, f32[1024,1024]{1,0:T(8,128)}, f32[1024,1024]{1,0:T(8,128)}, f32[1024,512]{1,0:T(8,128)}, f32[1024,128]{1,...) custom-call(bf16[2,4]{1,0:T(2,128)(2,1)} %refs_0_.10, ...), custom_call_target="tpu_custom_call" | custom-call | flops 16000000000 | bytes 83886080 | tf_op jit(solution)/shard_map/mixer_forward/pallas_call | solution.py:1405
  225.6 35.5 %mixer_bridge.3 = (f32[2,256,1024]{2,1,0:T(8,128)}, bf16[1024,1024]{1,0:T(8,128)(2,1)}, bf16[1024,704]{1,0:T(8,128)(2,1)}, bf16[1024,704]{1,0:T(8,128)(2,1)}) custom-call(bf16[1024,512]{1,0:T(8,128)(2,1)} %get-tuple-element.183.refs_0_.refs_4_, bf16[1024,512]{1,0:T(8,128)(2,1)} %get-tuple-element.184.refs_1_.refs_4_, ...), custom_call_target="tpu_custom_call" | custom-call | flops 1000000000 | bytes 83886080 | tf_op jit(solution)/shard_map/mixer_bridge/pallas_call | solution.py:1405
  261.1 25.0 %ffn_backward.2 = (bf16[1024,1024]{1,0:T(8,128)(2,1)}, bf16[1024,704]{1,0:T(8,128)(2,1)}, bf16[1024,704]{1,0:T(8,128)(2,1)}, bf16[1024,704]{1,0:T(8,128)(2,1)}, bf16[1024,1024]{1,0:T(8,128)(2,1)}) custom-call(bf16[1024,1024]{1,0:T(8,128)(2,1)} %get-tuple-element.188.refs_0_, bf16[1024,1024]{1,0:T(8,128)(2,1)} %get-tuple-element.189.refs_1_.refs_3_, ...), custom_call_target="tpu_custom_call" | custom-call | flops 12000000000 | bytes 83886080 | tf_op jit(solution)/shard_map/ffn_backward/pallas_call | solution.py:1405
  286.1 34.3 %backward_bridge.3 = (f32[2,256,1024]{2,1,0:T(8,128)}, bf16[1024,1024]{1,0:T(8,128)(2,1)}, f32[1,1024]{1,0:T(1,128)}, bf16[1024,512]{1,0:T(8,128)(2,1)}, bf16[25...) custom-call(bf16[1024,1024]{1,0:T(8,128)(2,1)} %get-tuple-element.194.refs_0_, ...), custom_call_target="tpu_custom_call" | custom-call | flops 5242880 | bytes 83886080 | tf_op jit(solution)/shard_map/backward_bridge/pallas_call | solution.py:1405
  320.4 36.1 %mixer_backward.2 = (bf16[1024,1024]{1,0:T(8,128)(2,1)}, bf16[1024,1536]{1,0:T(8,128)(2,1)}, bf16[1024,128]{1,0:T(8,128)(2,1)}, f32[1,512]{1,0:T(1,128)}, f32[8,...) custom-call(bf16[2,4]{1,0:T(2,128)(2,1)} %refs_0_.10, ...), custom_call_target="tpu_custom_call" | custom-call | flops 16000000000 | bytes 83886080 | tf_op jit(solution)/shard_map/mixer_backward/pallas_call | solution.py:1405
  356.5 38.6 %backward_bridge.4 = (f32[2,256,1024]{2,1,0:T(8,128)}, bf16[1024,1024]{1,0:T(8,128)(2,1)}, f32[1,1024]{1,0:T(1,128)}, bf16[256,1024]{1,0:T(8,128)(2,1)}, bf16[25...) custom-call(bf16[1024,1024]{1,0:T(8,128)(2,1)} %get-tuple-element.211.refs_0_, ...), custom_call_target="tpu_custom_call" | custom-call | flops 5242880 | bytes 83886080 | tf_op jit(solution)/shard_map/backward_bridge/pallas_call | solution.py:1405
  395.1 26.4 %ffn_backward.3 = (bf16[1024,1024]{1,0:T(8,128)(2,1)}, bf16[1024,704]{1,0:T(8,128)(2,1)}, bf16[1024,704]{1,0:T(8,128)(2,1)}, bf16[1024,704]{1,0:T(8,128)(2,1)}, ...) custom-call(bf16[1024,1024]{1,0:T(8,128)(2,1)} %get-tuple-element.16, ...), custom_call_target="tpu_custom_call" | custom-call | flops 12000000000 | bytes 83886080 | tf_op jit(solution)/shard_map/ffn_backward/pallas_call | solution.py:1405
  421.5 36.8 %backward_bridge.5 = (f32[2,256,1024]{2,1,0:T(8,128)}, bf16[1024,1024]{1,0:T(8,128)(2,1)}, f32[1,1024]{1,0:T(1,128)}, bf16[1024,512]{1,0:T(8,128)(2,1)}, bf16[25...) custom-call(bf16[1024,1024]{1,0:T(8,128)(2,1)} %get-tuple-element.221.refs_0_, f32[2,256,1024]{2,1,0:T(8,128)} %get-tuple-element.170.refs_1_, ...), custom_call_target="tpu_custom_call" | custom-call | flops 5242880 | bytes 83886080 | tf_op jit(solution)/shard_map/backward_bridge/pallas_call | solution.py:1405
  458.2 36.1 %mixer_backward.3 = (bf16[1024,1024]{1,0:T(8,128)(2,1)}, bf16[1024,1536]{1,0:T(8,128)(2,1)}, bf16[1024,128]{1,0:T(8,128)(2,1)}, f32[1,512]{1,0:T(1,128)}, f32[8,...) custom-call(bf16[2,4]{1,0:T(2,128)(2,1)} %refs_0_.10, ...), custom_call_target="tpu_custom_call" | custom-call | flops 16000000000 | bytes 83886080 | tf_op jit(solution)/shard_map/mixer_backward/pallas_call | solution.py:1405
  494.3 67.6 %final_step.1 = (bf16[256,1024]{1,0:T(8,128)(2,1)}, f32[48,128]{1,0:T(8,128)}, bf16[2,128,1024]{2,1,0:T(8,128)(2,1)}, bf16[2,128,512]{2,1,0:T(8,128)(2,1)}, bf16...) custom-call(s32[8]{0:T(128)} %refs_0_.11, ...), custom_call_target="tpu_custom_call" | custom-call | flops 5242880 | bytes 83886080 | tf_op jit(solution)/shard_map/final_step/pallas_call | solution.py:1405
  561.9 0.0 copy-start
  561.9 5.5 weights_out.1
  567.4 0.0 copy-done
  567.4 0.8 copy.39
Async XLA Ops:
  561.9 5.5 copy-start

commit v9 on v8

--- a/solution.py
+++ b/solution.py
@@ -677,15 +677,23 @@
 
 
 def mixer_bridge_kernel(
-    row, jobs, heads_ref, w_out_ref, x_ref, gain_ref, new_ref, out_ref, partial, raw, near, sums, far, x,
-    held, send, recv, share_send, share_recv, loads, stores
+    row, jobs, heads_hbm, w_out_hbm, x_ref, gain_ref, new_ref, out_ref, partial, raw, near, sums, far, x,
+    held, heads_ref, w_out_ref, fetch, send, recv, share_send, share_recv, loads, stores
 ):
+    fetches = [
+        pltpu.make_async_copy(w_out_hbm, w_out_ref, fetch.at[0]),
+        pltpu.make_async_copy(heads_hbm, heads_ref, fetch.at[1]),
+    ]
+    load_all(fetches)
     exchange = Exchange(partial, near, sums, far, send, recv)
     sharing = Sharing(held, out_ref, share_send, share_recv, stores)
     old = [pltpu.make_async_copy(x_ref.at[l], raw.at[l], loads.at[2 + l]) for l in range(2)]
     new = [pltpu.make_async_copy(x.at[l], new_ref.at[l], stores.at[4 + l]) for l in range(2)]
     load_all(old)
     wait_greetings(greet_group() + jobs.greet())
+
+    for copy in fetches:
+        copy.wait()
 
     def make(block):
         rows = block.rows()
@@ -721,7 +729,10 @@
 
 def backward_bridge_kernel(row, last, jobs, partial, x_ref, gain_ref, grad_ref, *refs):
     if last:
-        heads_ref, new_ref, out_ref, dgain_ref, dout_ref, *refs = refs
+        heads_hbm, new_ref, out_ref, dgain_ref, dout_ref, *refs = refs
+        heads_ref, fetch, *refs = refs
+        heads_copy = pltpu.make_async_copy(heads_hbm, heads_ref, fetch.at[0])
+        heads_copy.start()
     else:
         new_ref, out_ref, dgain_ref, *refs = refs
     (mine, near, sums, far, x, grad, new_rows, held, send, recv, share_send, share_recv, loads,
@@ -766,6 +777,7 @@
     dgain_ref[...] = dgain
     sharing.arrive()
     if last:
+        heads_copy.wait()
         for first in range(0, held.shape[1], 256):
             columns = slice(first, first + 256)
             dout_ref[columns, :] = mm(held[:, columns], heads_ref[...], TN).astype(BF16)
@@ -854,10 +866,11 @@
     )
     raw = pair_scratch(rows, width, [BF16]) if x.dtype != F32 else []
     return carry_call(
-        kernel, jobs, (), [VMEM_SPEC, VMEM_SPEC, ANY_SPEC, VMEM_SPEC], [ANY_SPEC] * 2,
+        kernel, jobs, (), [ANY_SPEC, ANY_SPEC, ANY_SPEC, VMEM_SPEC], [ANY_SPEC] * 2,
         bridge_shapes(rows, width),
         [pltpu.VMEM((4 * rows, width), BF16)] + raw + pair_scratch(rows, width, [BF16] * 3 + [F32])
-        + [pltpu.VMEM((4 * rows, width), BF16)] + bridge_sems(),
+        + [pltpu.VMEM((4 * rows, width), BF16), pltpu.VMEM(heads.shape, BF16),
+           pltpu.VMEM(w_out.shape, BF16), pltpu.SemaphoreType.DMA((2,))] + bridge_sems(),
         (heads, w_out, x, gain), number, "mixer_bridge", 10**9,
     )
 
@@ -876,9 +889,10 @@
         outs.append(jax.ShapeDtypeStruct((width, heads.shape[1]), BF16))
     return carry_call(
         functools.partial(backward_bridge_kernel, row, last), jobs, (),
-        [ANY_SPEC, ANY_SPEC, VMEM_SPEC, ANY_SPEC] + [VMEM_SPEC] * last,
+        [ANY_SPEC, ANY_SPEC, VMEM_SPEC, ANY_SPEC] + [ANY_SPEC] * last,
         [ANY_SPEC, ANY_SPEC, VMEM_SPEC] + [VMEM_SPEC] * last, outs,
-        pair_scratch(rows, width, [BF16] * 4 + [x.dtype, grad.dtype, F32])
+        ([pltpu.VMEM(heads.shape, BF16), pltpu.SemaphoreType.DMA((1,))] if last else [])
+        + pair_scratch(rows, width, [BF16] * 4 + [x.dtype, grad.dtype, F32])
         + [pltpu.VMEM((4 * rows, width), BF16)] + bridge_sems(),
         (partial, x, gain, grad) + ((heads,) if last else ()), number, "backward_bridge",
         rows * width * 20,
@@ -1524,13 +1538,20 @@
 
 
 def deal_kernel(chips, jobs, order_ref, lengths_ref, x_ref, gain_ref, cotangent_ref, *refs):
-    raw, refs = refs[:10], refs[10:]
+    raw, refs = list(refs[:10]), refs[10:]
     (new_ref, out_ref, start_ref, qkv_next, side_next, out_next, gate_next, up_ref, up_next, down_ref,
      down_next, first_full, second_full, first_wide, second_wide, third_wide, fourth_wide) = refs[:17]
-    (spread, picked, square, first, second, third, fourth, held_first, held_other, held_second, held, send, recv,
+    (late_out, late_gate, late_up, late_down, cotangent, fetch, spread, picked, square, first, second,
+     third, fourth, held_first, held_other, held_second, held, send, recv,
      stores,     cross_send, cross_recv,
      plane_send, plane_recv, role_send, role_recv, *sems) = refs[17:]
-    raw = Raw(raw, square)
+    fetches = [
+        pltpu.make_async_copy(source, ref, fetch.at[at])
+        for at, (source, ref) in enumerate(
+            zip(raw[6:] + [cotangent_ref], (late_out, late_gate, late_up, late_down, cotangent))
+        )
+    ]
+    raw = Raw(raw[:6] + [late_out, late_gate, late_up, late_down], square)
     plane, trade = Plane(chips), Trade(chips)
     half = CONV_CH // 2
     halves = []
@@ -1555,6 +1576,7 @@
         expected = expected + job.greet()
     raw.qkv(0, first)
     raw.side(0, second)
+    load_all(fetches)
     wait_greetings(expected)
     outward, inward = [], []
     for j in range(1, count):
@@ -1590,6 +1612,8 @@
 
         to_roles.append((copy, mine))
     second_column.start()
+    for copy in fetches:
+        copy.wait()
     raw.turn(raw.out[0], third)
     raw.turn(raw.ffn_gate[0], fourth)
     halves[1][0].finish()
@@ -1628,7 +1652,7 @@
     length = lengths_ref[order_ref[plane.own]]
     at = (trade.zp * 2 + trade.zl) * x_ref.shape[0]
     positions = lax.broadcasted_iota(jnp.int32, x_ref.shape, 0) + at
-    start_ref[...] = jnp.where(positions < length, cotangent_ref[...], jnp.zeros(x_ref.shape, BF16))
+    start_ref[...] = jnp.where(positions < length, cotangent[...], jnp.zeros(x_ref.shape, BF16))
     raw.qkv(1, qkv_next)
     raw.side(1, side_next)
     raw.turn(raw.out[1], out_next)
@@ -1671,10 +1695,12 @@
     own = [(part, qkv), (part, side), (part, VAL), (part, units), halved, halved, moved[1]]
     return carry_call(
         functools.partial(deal_kernel, chips), Jobs([], chips), (),
-        [smem, smem] + [vmem] * 13,
+        [smem, smem, vmem, vmem, hbm] + [vmem] * 6 + [hbm] * 4,
         [vmem, hbm] + [vmem] * 9 + [hbm] * 6,
         [jax.ShapeDtypeStruct(shape, BF16) for shape in shapes],
-        [buffer, buffer, pltpu.VMEM((LANES, LANES), F32)]
+        [pltpu.VMEM(value.shape, BF16) for value in (*raw[6:], cotangent)]
+        + [pltpu.SemaphoreType.DMA((5,))]
+        + [buffer, buffer, pltpu.VMEM((LANES, LANES), F32)]
         + [pltpu.VMEM(shape, BF16) for shape in own]
         + [pltpu.VMEM((4 * rows, width), BF16)] + sems(2, PIECES) + [pltpu.SemaphoreType.DMA((4,))]
         + sems(PIECES) + sems(count) + sems(count)

time: 575 us -> 573 us (level)
  no operation moved by 1% of the time
where the time goes in v9:
time: 573 us; the launch traced here: 566 us
  Pallas kernels  564 us (98%)
    pallas_call x15, Pallas kernels, carry_call(): pl.pallas_call(carrying(body, jobs, len(args), outs), grid=grid, in_specs...  559 us

profile of v9, /device:TPU:0, one launch (start us, length us, event | category | flops | bytes accessed | tf_op | source)
XLA Modules:
  0.0 566.4 jit_solution(16030930703707946102)
XLA Ops:
  0.7 61.3 %deal_and_gather.1 = (bf16[2,256,1024]{2,1,0:T(8,128)(2,1)}, bf16[1024,1024]{1,0:T(8,128)(2,1)}, bf16[256,1024]{1,0:T(8,128)(2,1)}, bf16[128,1024]{1,0:T(8,128)(...) custom-call(s32[8]{0:T(128)} %refs_0_.11, ...), custom_call_target="tpu_custom_call" | custom-call | flops 5242880 | bytes 83886080 | tf_op jit(solution)/shard_map/deal_and_gather/pallas_call | solution.py:1419
  62.0 37.3 %mixer_forward.2 = (bf16[1024,512]{1,0:T(8,128)(2,1)}, f32[1024,1024]{1,0:T(8,128)}, f32[1024,1024]{1,0:T(8,128)}, f32[1024,512]{1,0:T(8,128)}, f32[1024,128]{1,...) custom-call(bf16[2,4]{1,0:T(2,128)(2,1)} %refs_0_.10, ...), custom_call_target="tpu_custom_call" | custom-call | flops 16000000000 | bytes 83886080 | tf_op jit(solution)/shard_map/mixer_forward/pallas_call | solution.py:1419
  99.2 44.4 %mixer_bridge.2 = (f32[2,256,1024]{2,1,0:T(8,128)}, bf16[1024,1024]{1,0:T(8,128)(2,1)}, bf16[1024,704]{1,0:T(8,128)(2,1)}, bf16[1024,704]{1,0:T(8,128)(2,1)}, bf...) custom-call(bf16[1024,512]{1,0:T(8,128)(2,1)} %get-tuple-element.159.refs_0_.refs_4_, ...), custom_call_target="tpu_custom_call" | custom-call | flops 1000000000 | bytes 83886080 | tf_op jit(solution)/shard_map/mixer_bridge/pallas_call | solution.py:1419
  143.7 9.0 %ffn_forward.1.refs_0_ = bf16[1024,1024]{1,0:T(8,128)(2,1)} custom-call(bf16[1024,1024]{1,0:T(8,128)(2,1)} %get-tuple-element.166.refs_0_, bf16[1024,704]{1,0:T(8,128)(2,1)} %get-tuple-element.167.refs_1_.refs_2_, bf16[1024,704]{1,0:T(8,128)(2,1)} %get-tuple-element.168.refs_2_.refs_3_, bf16[1024,704]{1,0:T(8,128)(2,1)} %get-tuple-element.169.refs_3_.refs_4_), custom_call_target="tpu_custom_call" | custom-call | flops 4000000000 | bytes 83886080 | tf_op jit(solution)/shard_map/ffn_forward/pallas_call | solution.py:1419
  152.7 36.8 %forward_bridge.1 = (f32[2,256,1024]{2,1,0:T(8,128)}, bf16[1024,1024]{1,0:T(8,128)(2,1)}, bf16[1024,1024]{1,0:T(8,128)(2,1)}, bf16[1024,640]{1,0:T(8,128)(2,1)},...) custom-call(bf16[1024,1024]{1,0:T(8,128)(2,1)} %ffn_forward.1.refs_0_, f32[2,256,1024]{2,1,0:T(8,128)} %get-tuple-element.170.refs_1_, ...), custom_call_target="tpu_custom_call" | custom-call | flops 5242880 | bytes 83886080 | tf_op jit(solution)/shard_map/forward_bridge/pallas_call | solution.py:1419
  189.5 34.7 %mixer_forward.3 = (bf16[1024,512]{1,0:T(8,128)(2,1)}, f32[1024,1024]{1,0:T(8,128)}, f32[1024,1024]{1,0:T(8,128)}, f32[1024,512]{1,0:T(8,128)}, f32[1024,128]{1,...) custom-call(bf16[2,4]{1,0:T(2,128)(2,1)} %refs_0_.10, ...), custom_call_target="tpu_custom_call" | custom-call | flops 16000000000 | bytes 83886080 | tf_op jit(solution)/shard_map/mixer_forward/pallas_call | solution.py:1419
  224.2 34.7 %mixer_bridge.3 = (f32[2,256,1024]{2,1,0:T(8,128)}, bf16[1024,1024]{1,0:T(8,128)(2,1)}, bf16[1024,704]{1,0:T(8,128)(2,1)}, bf16[1024,704]{1,0:T(8,128)(2,1)}) custom-call(bf16[1024,512]{1,0:T(8,128)(2,1)} %get-tuple-element.183.refs_0_.refs_4_, bf16[1024,512]{1,0:T(8,128)(2,1)} %get-tuple-element.184.refs_1_.refs_4_, ...), custom_call_target="tpu_custom_call" | custom-call | flops 1000000000 | bytes 83886080 | tf_op jit(solution)/shard_map/mixer_bridge/pallas_call | solution.py:1419
  258.9 25.0 %ffn_backward.2 = (bf16[1024,1024]{1,0:T(8,128)(2,1)}, bf16[1024,704]{1,0:T(8,128)(2,1)}, bf16[1024,704]{1,0:T(8,128)(2,1)}, bf16[1024,704]{1,0:T(8,128)(2,1)}, bf16[1024,1024]{1,0:T(8,128)(2,1)}) custom-call(bf16[1024,1024]{1,0:T(8,128)(2,1)} %get-tuple-element.188.refs_0_, bf16[1024,1024]{1,0:T(8,128)(2,1)} %get-tuple-element.189.refs_1_.refs_3_, ...), custom_call_target="tpu_custom_call" | custom-call | flops 12000000000 | bytes 83886080 | tf_op jit(solution)/shard_map/ffn_backward/pallas_call | solution.py:1419
  283.9 33.6 %backward_bridge.3 = (f32[2,256,1024]{2,1,0:T(8,128)}, bf16[1024,1024]{1,0:T(8,128)(2,1)}, f32[1,1024]{1,0:T(1,128)}, bf16[1024,512]{1,0:T(8,128)(2,1)}, bf16[25...) custom-call(bf16[1024,1024]{1,0:T(8,128)(2,1)} %get-tuple-element.194.refs_0_, ...), custom_call_target="tpu_custom_call" | custom-call | flops 5242880 | bytes 83886080 | tf_op jit(solution)/shard_map/backward_bridge/pallas_call | solution.py:1419
  317.5 37.7 %mixer_backward.2 = (bf16[1024,1024]{1,0:T(8,128)(2,1)}, bf16[1024,1536]{1,0:T(8,128)(2,1)}, bf16[1024,128]{1,0:T(8,128)(2,1)}, f32[1,512]{1,0:T(1,128)}, f32[8,...) custom-call(bf16[2,4]{1,0:T(2,128)(2,1)} %refs_0_.10, ...), custom_call_target="tpu_custom_call" | custom-call | flops 16000000000 | bytes 83886080 | tf_op jit(solution)/shard_map/mixer_backward/pallas_call | solution.py:1419
  355.1 38.2 %backward_bridge.4 = (f32[2,256,1024]{2,1,0:T(8,128)}, bf16[1024,1024]{1,0:T(8,128)(2,1)}, f32[1,1024]{1,0:T(1,128)}, bf16[256,1024]{1,0:T(8,128)(2,1)}, bf16[25...) custom-call(bf16[1024,1024]{1,0:T(8,128)(2,1)} %get-tuple-element.211.refs_0_, ...), custom_call_target="tpu_custom_call" | custom-call | flops 5242880 | bytes 83886080 | tf_op jit(solution)/shard_map/backward_bridge/pallas_call | solution.py:1419
  393.3 26.4 %ffn_backward.3 = (bf16[1024,1024]{1,0:T(8,128)(2,1)}, bf16[1024,704]{1,0:T(8,128)(2,1)}, bf16[1024,704]{1,0:T(8,128)(2,1)}, bf16[1024,704]{1,0:T(8,128)(2,1)}, ...) custom-call(bf16[1024,1024]{1,0:T(8,128)(2,1)} %get-tuple-element.16, ...), custom_call_target="tpu_custom_call" | custom-call | flops 12000000000 | bytes 83886080 | tf_op jit(solution)/shard_map/ffn_backward/pallas_call | solution.py:1419
  419.7 35.9 %backward_bridge.5 = (f32[2,256,1024]{2,1,0:T(8,128)}, bf16[1024,1024]{1,0:T(8,128)(2,1)}, f32[1,1024]{1,0:T(1,128)}, bf16[1024,512]{1,0:T(8,128)(2,1)}, bf16[25...) custom-call(bf16[1024,1024]{1,0:T(8,128)(2,1)} %get-tuple-element.221.refs_0_, f32[2,256,1024]{2,1,0:T(8,128)} %get-tuple-element.170.refs_1_, ...), custom_call_target="tpu_custom_call" | custom-call | flops 5242880 | bytes 83886080 | tf_op jit(solution)/shard_map/backward_bridge/pallas_call | solution.py:1419
  455.6 36.1 %mixer_backward.3 = (bf16[1024,1024]{1,0:T(8,128)(2,1)}, bf16[1024,1536]{1,0:T(8,128)(2,1)}, bf16[1024,128]{1,0:T(8,128)(2,1)}, f32[1,512]{1,0:T(1,128)}, f32[8,...) custom-call(bf16[2,4]{1,0:T(2,128)(2,1)} %refs_0_.10, ...), custom_call_target="tpu_custom_call" | custom-call | flops 16000000000 | bytes 83886080 | tf_op jit(solution)/shard_map/mixer_backward/pallas_call | solution.py:1419
  491.7 68.0 %final_step.1 = (bf16[256,1024]{1,0:T(8,128)(2,1)}, f32[48,128]{1,0:T(8,128)}, bf16[2,128,1024]{2,1,0:T(8,128)(2,1)}, bf16[2,128,512]{2,1,0:T(8,128)(2,1)}, bf16...) custom-call(s32[8]{0:T(128)} %refs_0_.11, ...), custom_call_target="tpu_custom_call" | custom-call | flops 5242880 | bytes 83886080 | tf_op jit(solution)/shard_map/final_step/pallas_call | solution.py:1419
  559.7 0.0 copy-start
  559.7 5.5 weights_out.1
  565.2 0.0 copy-done
  565.2 0.8 copy.39
Async XLA Ops:
  559.7 5.5 copy-start
